TPU v7x, 32 devices: a whole 2x2x4 slice. The times are simulated.
32 devices in a mesh: dp: 8 (over z, x), head: 4 (over y, core).
Axes of the slice: x: 2, y: 2, z: 4, core: 2. Of those that a mesh axis runs over, the one named last changes fastest.
Arguments:
- images: bfloat16 [64, 32, 32, 384], P('dp', 'head'), may hold values from -6 to 6
- noise: bfloat16 [64, 32, 32, 192], P('dp', 'head'), may hold values from -6 to 6
- timesteps: int32 [64], P('dp'), may hold values from 2 to 3999
- extents: int32 [64, 2], P('dp'), may hold values from 1 to 32, as said below
- film_master: float32 [768, 768], P(('dp', 'head')), may hold values from -0.21875 to 0.21875
- conv_master: float32 [6912, 384], P(('dp', 'head')), may hold values from -0.109375 to 0.109375
- qkv_master: float32 [384, 1152], P(('dp', 'head')), may hold values from -0.3125 to 0.3125
- out_master: float32 [384, 384], P(('dp', 'head')), may hold values from -1.25 to 1.25
- gains: float32 [384, 6], P(('dp', 'head')), may hold values from -3 to 4
- film_first: float32 [768, 768], P(('dp', 'head')), may hold values from -7.1525574e-07 to 7.1525574e-07
- film_second: float32 [768, 768], P(('dp', 'head')), may hold values from 1.0427094e-15 to 4.1708377e-15
- conv_first: float32 [6912, 384], P(('dp', 'head')), may hold values from -7.1525574e-07 to 7.1525574e-07
- conv_second: float32 [6912, 384], P(('dp', 'head')), may hold values from 1.0427094e-15 to 4.1708377e-15
- qkv_first: float32 [384, 1152], P(('dp', 'head')), may hold values from -7.1525574e-07 to 7.1525574e-07
- qkv_second: float32 [384, 1152], P(('dp', 'head')), may hold values from 1.0427094e-15 to 4.1708377e-15
- out_first: float32 [384, 384], P(('dp', 'head')), may hold values from -7.1525574e-07 to 7.1525574e-07
- out_second: float32 [384, 384], P(('dp', 'head')), may hold values from 1.0427094e-15 to 4.1708377e-15
- gain_first: float32 [384, 6], P(('dp', 'head')), may hold values from -6.67572e-06 to 6.67572e-06
- gain_second: float32 [384, 6], P(('dp', 'head')), may hold values from 1.04270935e-13 to 4.1708374e-13
Outputs:
- loss_parts: float32 [2], replicated
- grad_norm: float32 [], replicated
- film_new: float32 [768, 768], P(('dp', 'head'))
- film_first_new: float32 [768, 768], P(('dp', 'head'))
- film_second_new: float32 [768, 768], P(('dp', 'head'))
- conv_new: float32 [6912, 384], P(('dp', 'head'))
- conv_first_new: float32 [6912, 384], P(('dp', 'head'))
- conv_second_new: float32 [6912, 384], P(('dp', 'head'))
- qkv_new: float32 [384, 1152], P(('dp', 'head'))
- qkv_first_new: float32 [384, 1152], P(('dp', 'head'))
- qkv_second_new: float32 [384, 1152], P(('dp', 'head'))
- out_new: float32 [384, 384], P(('dp', 'head'))
- out_first_new: float32 [384, 384], P(('dp', 'head'))
- out_second_new: float32 [384, 384], P(('dp', 'head'))
- gains_new: float32 [384, 6], P(('dp', 'head'))
- gain_first_new: float32 [384, 6], P(('dp', 'head'))
- gain_second_new: float32 [384, 6], P(('dp', 'head'))
Inputs may be any that keep to these rules, and one draw needn't show every extreme that they name: extents[b] = (h, w): the valid region is the last h rows and the first w columns; samples with b >= 32 are valid everywhere.
All inputs are finite; a program needn't handle non-finite values.
Results may differ from a plain program's by a relative error of at most 0.0075.
Values may be sent and summed in bfloat16 or wider, within the bound.
No kernel may reach another device: no remote copies, remote signals or barrier semaphores. Data moves between devices by JAX's collectives and lax.ppermute only.
A program may use at most 192 MiB of HBM per device.

v0:
```python
import math

import jax
import jax.numpy as jnp
from jax import lax
from jax.sharding import PartitionSpec as P

HEADS = 4
GROUPS = 32
STEP = 10
TSTEPS = 4000


EPS_NORM = 1e-05
VLB_WEIGHT = 0.001
BETA_ONE = 0.9
BETA_TWO = 0.999
ADAM_EPS = 1e-08
DECAY = 0.01
RATE_MATRIX = 0.05
RATE_GAIN = 0.4
THRESHOLD = 0.002
OFFSET = 0.008


def extended(shard, sides, width):
    for axis, dim in sides:
        devices, length = (lax.axis_size(axis), shard.shape[dim])
        up = [(i, (i + 1) % devices) for i in range(devices - 1)]
        down = [(j, i) for i, j in up]
        last = lax.slice_in_dim(shard, length - width, length, axis=dim)
        initial = lax.slice_in_dim(shard, 0, width, axis=dim)
        before = lax.ppermute(last, axis, up)
        after = lax.ppermute(initial, axis, down)
        shard = jnp.concatenate([before, shard, after], axis=dim)
    return shard


def plan(step_ids):
    moment = step_ids.astype(jnp.float32)

    def angle(values):
        return (values / TSTEPS + OFFSET) / (1.0 + OFFSET) * (0.5 * math.pi)

    start = angle(jnp.zeros_like(moment))
    before = angle(moment - 1.0)
    later_angle = angle(moment)
    beta_now = jnp.sin(later_angle - before) * jnp.sin(later_angle + before) / jnp.cos(before) ** 2
    fade_now = jnp.sin(later_angle - start) * jnp.sin(later_angle + start) / jnp.cos(start) ** 2
    fade_prev = jnp.sin(before - start) * jnp.sin(before + start) / jnp.cos(start) ** 2
    log_beta = jnp.log(beta_now)
    log_tilde = jnp.log(beta_now * fade_prev / fade_now)
    factor = beta_now * beta_now / ((1.0 - beta_now) * fade_now)
    return (log_beta, log_tilde, factor)


def embed(step_ids, width):
    half_width = width // 2
    frequency = jnp.exp(-math.log(10000.0) * jnp.arange(half_width, dtype=jnp.float32) / half_width)
    phases = step_ids.astype(jnp.float32)[:, None] * frequency[None, :]
    return jnp.concatenate([jnp.cos(phases), jnp.sin(phases)], axis=1)


def silu_slope(values):
    sigmoid_vals = jax.nn.sigmoid(values)
    return sigmoid_vals * (1.0 + values * (1.0 - sigmoid_vals))


def group_norm(values, gain_row, shift_row):
    samples, pixels, channels = values.shape
    grouped_vals = values.reshape(samples, pixels, GROUPS, channels // GROUPS)
    first_sum, second_sum = lax.psum(
        (jnp.sum(grouped_vals, axis=(1, 3)), jnp.sum(grouped_vals * grouped_vals, axis=(1, 3))),
        "head",
    )
    group_count = pixels * lax.axis_size("head") * (channels // GROUPS)
    group_mean = first_sum / group_count
    inverse_std = lax.rsqrt(second_sum / group_count - group_mean * group_mean + EPS_NORM)
    normed = (
        (grouped_vals - group_mean[:, None, :, None]) * inverse_std[:, None, :, None]
    ).reshape(values.shape)
    return (normed * gain_row + shift_row, normed, inverse_std)


def group_norm_back(grad_out, normed, inverse_std, gain_row):
    samples, pixels, channels = grad_out.shape
    scaled = (grad_out * gain_row).reshape(samples, pixels, GROUPS, channels // GROUPS)
    flat_normed = normed.reshape(scaled.shape)
    first_sum, second_sum = lax.psum(
        (jnp.sum(scaled, axis=(1, 3)), jnp.sum(scaled * flat_normed, axis=(1, 3))), "head"
    )
    group_count = pixels * lax.axis_size("head") * (channels // GROUPS)
    back_values = (
        scaled
        - (first_sum / group_count)[:, None, :, None]
        - flat_normed * (second_sum / group_count)[:, None, :, None]
    ) * inverse_std[:, None, :, None]
    return (
        back_values.reshape(grad_out.shape),
        jnp.sum(grad_out * normed, axis=(0, 1)),
        jnp.sum(grad_out, axis=(0, 1)),
    )


def conv_apply(padded, conv_taps, strip_rows, width_px, einsum_form, mirror):
    summed = None
    for tap_index in range(9):
        offset_row = 2 - tap_index // 3 if mirror else tap_index // 3
        offset_col = 2 - tap_index % 3 if mirror else tap_index % 3
        window = padded[
            :, offset_row : offset_row + strip_rows, offset_col : offset_col + width_px, :
        ]
        product = jnp.einsum(
            einsum_form, window, conv_taps[tap_index], preferred_element_type=jnp.float32
        )
        summed = product if summed is None else summed + product
    return summed


def conv_forward(hidden_b, conv_taps):
    samples, strip_rows, width_px, channels = hidden_b.shape
    padded = extended(hidden_b, (("head", 1),), 1)
    padded = jnp.pad(padded, ((0, 0), (0, 0), (1, 1), (0, 0)))
    summed = conv_apply(padded, conv_taps, strip_rows, width_px, "srwc,cd->srwd", False)
    return (padded, summed.reshape(samples, strip_rows * width_px, channels))


def conv_backward(padded, grad_b, conv_taps):
    samples, strip_rows, width_px, channels = grad_b.shape
    tap_rows = []
    for tap_index in range(9):
        offset_row, offset_col = (tap_index // 3, tap_index % 3)
        window = padded[
            :, offset_row : offset_row + strip_rows, offset_col : offset_col + width_px, :
        ]
        tap_rows.append(
            jnp.einsum("srwc,srwd->cd", window, grad_b, preferred_element_type=jnp.float32)
        )
    grad_pad = extended(grad_b, (("head", 1),), 1)
    grad_pad = jnp.pad(grad_pad, ((0, 0), (0, 0), (1, 1), (0, 0)))
    grad_input = conv_apply(grad_pad, conv_taps, strip_rows, width_px, "srwd,cd->srwc", True)
    return (
        jnp.concatenate(tap_rows, axis=0),
        grad_input.reshape(samples, strip_rows * width_px, channels),
    )


def adamw(master, gradient, first, second, step_rate, decay_rate, clip_factor):
    gradient = gradient * clip_factor
    first_new = BETA_ONE * first + (1.0 - BETA_ONE) * gradient
    second_new = BETA_TWO * second + (1.0 - BETA_TWO) * gradient * gradient
    ratio = (
        first_new
        / (1.0 - BETA_ONE**STEP)
        / (jnp.sqrt(second_new / (1.0 - BETA_TWO**STEP)) + ADAM_EPS)
    )
    return (master - step_rate * (ratio + decay_rate * master), first_new, second_new)


def body(
    images,
    noise,
    timesteps,
    extents,
    film_master,
    conv_master,
    qkv_master,
    out_master,
    gains,
    film_first,
    film_second,
    conv_first,
    conv_second,
    qkv_first,
    qkv_second,
    out_first,
    out_second,
    gain_first,
    gain_second,
):
    film_w, conv_w, qkv_w, out_w, gain_all = (
        lax.all_gather(film_master.astype(jnp.bfloat16), ("dp", "head"), axis=0, tiled=True),
        lax.all_gather(conv_master.astype(jnp.bfloat16), ("dp", "head"), axis=0, tiled=True),
        lax.all_gather(qkv_master.astype(jnp.bfloat16), ("dp", "head"), axis=0, tiled=True),
        lax.all_gather(out_master.astype(jnp.bfloat16), ("dp", "head"), axis=0, tiled=True),
        lax.all_gather(gains.astype(jnp.bfloat16), ("dp", "head"), axis=0, tiled=True),
    )
    samples, strip_rows, width_px, channels = images.shape
    pixels = strip_rows * width_px
    half_width = channels // 2
    head_size = channels // HEADS
    factor_att = head_size ** (-0.5)
    gain_f = gain_all.astype(jnp.float32)
    taps_one = conv_w[: 9 * channels].reshape(9, channels, channels)
    taps_two = conv_w[9 * channels :].reshape(9, channels, channels)
    log_beta, log_tilde, factor = plan(timesteps)
    embedded = jax.nn.silu(embed(timesteps, film_w.shape[1])).astype(jnp.bfloat16)
    film_out = lax.dot_general(
        embedded, film_w, (((1,), (1,)), ((), ())), preferred_element_type=jnp.float32
    )
    scale_part = film_out[:, None, :channels]
    shift_part = film_out[:, None, channels:]
    source = images.reshape(samples, pixels, channels).astype(jnp.float32)
    first_out, first_normed, first_std = group_norm(source, gain_f[:, 0], gain_f[:, 1])
    hidden_one = (
        jax.nn.silu(first_out).astype(jnp.bfloat16).reshape(samples, strip_rows, width_px, channels)
    )
    padded_one, inner = conv_forward(hidden_one, taps_one)
    second_out, second_normed, second_std = group_norm(inner, gain_f[:, 2], gain_f[:, 3])
    lifted = second_out * (1.0 + scale_part) + shift_part
    hidden_two = (
        jax.nn.silu(lifted).astype(jnp.bfloat16).reshape(samples, strip_rows, width_px, channels)
    )
    padded_two, conv_out = conv_forward(hidden_two, taps_two)
    middle = source + conv_out
    third_out, third_normed, third_std = group_norm(middle, gain_f[:, 4], gain_f[:, 5])
    normed_b = third_out.astype(jnp.bfloat16)
    local_qkv = jnp.einsum(
        "spc,cf->spf", normed_b, qkv_w, preferred_element_type=jnp.float32
    ).astype(jnp.bfloat16)
    grouped = lax.all_to_all(
        local_qkv.reshape(samples, pixels, HEADS, 3 * head_size),
        "head",
        split_axis=2,
        concat_axis=1,
        tiled=True,
    )

    def attend(sample_block):
        queries = sample_block[..., :head_size]
        key_part = sample_block[..., head_size : 2 * head_size]
        value_part = sample_block[..., 2 * head_size :]
        scores = (
            jnp.einsum("qhd,khd->hqk", queries, key_part, preferred_element_type=jnp.float32)
            * factor_att
        )
        row_max = jnp.max(scores, axis=-1, keepdims=True)
        log_total = jnp.log(jnp.sum(jnp.exp(scores - row_max), axis=-1, keepdims=True)) + row_max
        weights_soft = jnp.exp(scores - log_total).astype(jnp.bfloat16)
        mixed = jnp.einsum(
            "hqk,khd->qhd", weights_soft, value_part, preferred_element_type=jnp.float32
        ).astype(jnp.bfloat16)
        return (mixed, log_total)

    mixed_all, log_totals = lax.map(attend, grouped)
    attn_cat = lax.all_to_all(mixed_all, "head", split_axis=1, concat_axis=2, tiled=True).reshape(
        samples, pixels, channels
    )
    result = middle + jnp.einsum("spc,cd->spd", attn_cat, out_w, preferred_element_type=jnp.float32)
    row_ids = lax.axis_index("head") * strip_rows + jnp.arange(strip_rows, dtype=jnp.int32)
    col_ids = jnp.arange(width_px, dtype=jnp.int32)
    full_rows = strip_rows * lax.axis_size("head")
    valid = (
        (
            (row_ids[None, :, None] >= full_rows - extents[:, 0][:, None, None])
            & (col_ids[None, None, :] < extents[:, 1][:, None, None])
        )
        .astype(jnp.float32)
        .reshape(samples, pixels)
    )
    residue = result[..., :half_width] - noise.reshape(samples, pixels, half_width).astype(
        jnp.float32
    )
    weight = jax.nn.sigmoid(result[..., half_width:])
    beta_log = log_beta[:, None, None]
    tilde_log = log_tilde[:, None, None]
    blended = weight * beta_log + (1.0 - weight) * tilde_log
    spread = jnp.exp(tilde_log - blended)
    damped = factor[:, None, None] * residue * residue * jnp.exp(-blended)
    diverge = 0.5 * (-1.0 + blended - tilde_log + spread + damped)
    loss_local = jnp.sum(
        valid * (jnp.mean(residue * residue, axis=-1) + VLB_WEIGHT * jnp.mean(diverge, axis=-1))
    )
    count_local = jnp.sum(valid)
    divisor = lax.psum(count_local, ("dp", "head"))
    grad_guess = valid[..., None] * 2.0 * residue / (half_width * divisor)
    grad_blend = (
        valid[..., None] * (VLB_WEIGHT / half_width) * 0.5 * (1.0 - spread - damped) / divisor
    )
    grad_raw = grad_blend * (beta_log - tilde_log) * weight * (1.0 - weight)
    grad_result = jnp.concatenate([grad_guess, grad_raw], axis=-1)
    down_b = grad_result.astype(jnp.bfloat16)
    out_grad = jnp.einsum("spc,spd->cd", attn_cat, down_b, preferred_element_type=jnp.float32)
    back_mixed = jnp.einsum(
        "spd,cd->spc", down_b, out_w, preferred_element_type=jnp.float32
    ).astype(jnp.bfloat16)
    back_grouped = lax.all_to_all(
        back_mixed.reshape(samples, pixels, HEADS, head_size),
        "head",
        split_axis=2,
        concat_axis=1,
        tiled=True,
    )

    def attend_back(sample_parts):
        packed, log_total, upstream = sample_parts
        queries = packed[..., :head_size]
        key_part = packed[..., head_size : 2 * head_size]
        value_part = packed[..., 2 * head_size :]
        scores = (
            jnp.einsum("qhd,khd->hqk", queries, key_part, preferred_element_type=jnp.float32)
            * factor_att
        )
        weights_soft = jnp.exp(scores - log_total)
        grad_value = jnp.einsum(
            "hqk,qhd->khd",
            weights_soft.astype(jnp.bfloat16),
            upstream,
            preferred_element_type=jnp.float32,
        )
        grad_soft = jnp.einsum(
            "qhd,khd->hqk", upstream, value_part, preferred_element_type=jnp.float32
        )
        grad_scores = (
            weights_soft * (grad_soft - jnp.sum(weights_soft * grad_soft, axis=-1, keepdims=True))
        ).astype(jnp.bfloat16)
        grad_query = (
            jnp.einsum("hqk,khd->qhd", grad_scores, key_part, preferred_element_type=jnp.float32)
            * factor_att
        )
        grad_key = (
            jnp.einsum("hqk,qhd->khd", grad_scores, queries, preferred_element_type=jnp.float32)
            * factor_att
        )
        return jnp.concatenate([grad_query, grad_key, grad_value], axis=-1).astype(jnp.bfloat16)

    grad_grouped = lax.map(attend_back, (grouped, log_totals, back_grouped))
    grad_local = lax.all_to_all(
        grad_grouped, "head", split_axis=1, concat_axis=2, tiled=True
    ).reshape(samples, pixels, 3 * channels)
    qkv_grad = jnp.einsum("spc,spf->cf", normed_b, grad_local, preferred_element_type=jnp.float32)
    grad_normed = jnp.einsum("spf,cf->spc", grad_local, qkv_w, preferred_element_type=jnp.float32)
    back_middle, gain_three, bias_three = group_norm_back(
        grad_normed, third_normed, third_std, gain_f[:, 4]
    )
    grad_middle = grad_result + back_middle
    grad_two_b = grad_middle.astype(jnp.bfloat16).reshape(samples, strip_rows, width_px, channels)
    conv_two_grad, grad_hidden_two = conv_backward(padded_two, grad_two_b, taps_two)
    grad_lifted = grad_hidden_two * silu_slope(lifted)
    grad_scale = jnp.sum(grad_lifted * second_out, axis=1)
    grad_shift = jnp.sum(grad_lifted, axis=1)
    grad_second = grad_lifted * (1.0 + scale_part)
    back_inner, gain_two, bias_two = group_norm_back(
        grad_second, second_normed, second_std, gain_f[:, 2]
    )
    grad_one_b = back_inner.astype(jnp.bfloat16).reshape(samples, strip_rows, width_px, channels)
    conv_one_grad, grad_hidden_one = conv_backward(padded_one, grad_one_b, taps_one)
    grad_first = grad_hidden_one * silu_slope(first_out)
    gain_one = jnp.sum(grad_first * first_normed, axis=(0, 1))
    bias_one = jnp.sum(grad_first, axis=(0, 1))
    film_grad_b = jnp.concatenate([grad_scale, grad_shift], axis=1).astype(jnp.bfloat16)
    film_grad = jnp.einsum("sf,se->fe", film_grad_b, embedded, preferred_element_type=jnp.float32)
    conv_grad = jnp.concatenate([conv_one_grad, conv_two_grad], axis=0)
    gain_grad = jnp.stack([gain_one, bias_one, gain_two, bias_two, gain_three, bias_three], axis=1)
    reduced = (
        lax.psum_scatter(film_grad, ("dp", "head"), scatter_dimension=0, tiled=True),
        lax.psum_scatter(conv_grad, ("dp", "head"), scatter_dimension=0, tiled=True),
        lax.psum_scatter(qkv_grad, ("dp", "head"), scatter_dimension=0, tiled=True),
        lax.psum_scatter(out_grad, ("dp", "head"), scatter_dimension=0, tiled=True),
        lax.psum_scatter(gain_grad, ("dp", "head"), scatter_dimension=0, tiled=True),
    )
    squares = jnp.zeros((), jnp.float32)
    for gradient in reduced:
        squares = squares + jnp.sum(gradient * gradient)
    square_total, loss_total = lax.psum((squares, loss_local), ("dp", "head"))
    late_divisor = jnp.ones((), jnp.float32)
    film_g, conv_g, qkv_g, out_g, gain_g = [gradient / late_divisor for gradient in reduced]
    grad_norm = jnp.sqrt(square_total) / late_divisor
    clip_factor = jnp.minimum(1.0, THRESHOLD / (grad_norm + 1e-06))
    film_res = adamw(film_master, film_g, film_first, film_second, RATE_MATRIX, DECAY, clip_factor)
    conv_res = adamw(conv_master, conv_g, conv_first, conv_second, RATE_MATRIX, DECAY, clip_factor)
    qkv_res = adamw(qkv_master, qkv_g, qkv_first, qkv_second, RATE_MATRIX, DECAY, clip_factor)
    out_res = adamw(out_master, out_g, out_first, out_second, RATE_MATRIX, DECAY, clip_factor)
    gain_res = adamw(gains, gain_g, gain_first, gain_second, RATE_GAIN, 0.0, clip_factor)
    loss_parts = jnp.stack([loss_total, divisor])
    return (
        loss_parts,
        grad_norm,
        film_res[0],
        film_res[1],
        film_res[2],
        conv_res[0],
        conv_res[1],
        conv_res[2],
        qkv_res[0],
        qkv_res[1],
        qkv_res[2],
        out_res[0],
        out_res[1],
        out_res[2],
        gain_res[0],
        gain_res[1],
        gain_res[2],
    )


def solution(mesh):
    in_specs = (
        P("dp", "head", None, None),
        P("dp", "head", None, None),
        P("dp"),
        P("dp", None),
        P(("dp", "head"), None),
        P(("dp", "head"), None),
        P(("dp", "head"), None),
        P(("dp", "head"), None),
        P(("dp", "head"), None),
        P(("dp", "head"), None),
        P(("dp", "head"), None),
        P(("dp", "head"), None),
        P(("dp", "head"), None),
        P(("dp", "head"), None),
        P(("dp", "head"), None),
        P(("dp", "head"), None),
        P(("dp", "head"), None),
        P(("dp", "head"), None),
        P(("dp", "head"), None),
    )
    out_specs = (
        P(),
        P(),
        P(("dp", "head"), None),
        P(("dp", "head"), None),
        P(("dp", "head"), None),
        P(("dp", "head"), None),
        P(("dp", "head"), None),
        P(("dp", "head"), None),
        P(("dp", "head"), None),
        P(("dp", "head"), None),
        P(("dp", "head"), None),
        P(("dp", "head"), None),
        P(("dp", "head"), None),
        P(("dp", "head"), None),
        P(("dp", "head"), None),
        P(("dp", "head"), None),
        P(("dp", "head"), None),
    )
    return jax.shard_map(body, mesh=mesh, in_specs=in_specs, out_specs=out_specs, check_vma=False)
```

profile of v0, /device:TPU:0, one launch (start us, length us, event | category | flops | bytes accessed | tf_op | source)
XLA Modules:
  0.0 1058.9 jit_solution(12306785958457689695)
XLA Ops:
  11.3 43.4 %all-gather = bf16[32,12,6]{1,2,0:T(8,128)(2,1)S(1)} all-gather(bf16[1,12,6]{1,2,0:T(8,128)(2,1)S(1)} %convert_bitcast_fusion.2), channel_id=1, replica_groups=mesh['dp'=8,'head'=4] {'dp','head'}, dimensions={0}, use_global_device_ids=true | all-gather | bytes 4752 | tf_op jit(solution)/shard_map/all_gather | solution.py:186
  57.5 6.5 all-reduce.15
  69.6 45.2 %all-gather.1 = bf16[32,12,1152]{2,1,0:T(8,128)(2,1)S(1)} all-gather(bf16[1,12,1152]{2,1,0:T(8,128)(2,1)S(1)} %convert_bitcast_fusion), channel_id=1, replica_groups=mesh['dp'=8,'head'=4] {'dp','head'}, dimensions={0}, use_global_device_ids=true | all-gather | bytes 912384 | tf_op jit(solution)/shard_map/all_gather | solution.py:184
  120.5 17.5 %all-gather.6.cloned.1.call-done = bf16[6912,384]{1,0:T(8,128)(2,1)} async-done(((bf16[216,384]{1,0:T(8,128)(2,1)}), bf16[6912,384]{1,0:T(8,128)(2,1)}) %all-gather.6.cloned.1.call-update) | async-done | bytes 5308432 | tf_op jit(solution)/shard_map/all_gather | solution.py:183
  158.0 5.6 fusion.336
  164.1 7.3 all-reduce.14
  200.0 3.9 fusion.70
  203.9 7.4 fusion.335
  211.8 10.3 all-reduce.13
  226.2 4.3 convolution_convert_fusion
  230.6 6.7 copy.290
  237.3 4.8 copy.291
  242.1 5.1 all-to-all-start
  248.1 85.9 %psum.98 = f32[]{:T(128)} all-reduce(f32[]{:T(128)} %convert_reduce_fusion.1), channel_id=1, replica_groups=mesh['dp'=8,'head'=4] {'dp','head'}, use_global_device_ids=true, to_apply=%region_27.28 | all-reduce | flops 1 | bytes 8 | tf_op jit(solution)/shard_map/psum | solution.py:275
  334.0 5.1 copy.389
  339.1 38.0 %while.22 = (s32[]{:T(128)}, bf16[8,1024,1,96]{1,3,2,0:T(8,128)(2,1)}, f32[8,1,1024,1]{2,3,1,0:T(1,128)}, bf16[8,1024,1,288]{1,3,2,0:T(8,128)(2,1)}, s32[]{:T(128)}) while((s32[]{:T(128)}, bf16[8,1024,1,96]{1,3,2,0:T(8,128)(2,1)}, f32[8,1,1024,1]{2,3,1,0:T(1,128)}, bf16[8,1024,1,288]{1,3,2,0:T(8,128)(2,1)}, s32[]{:T(128)}) %tuple.128), condition=%wide.region_21.22_spmd, body=%wide.region_18.21_spmd.sunk | while | flops 411139072 | bytes 14585937 | solution.py:245
  377.1 4.1 copy.294
  381.2 4.5 all-to-all-start.1
  386.4 60.6 %all-gather.2 = bf16[32,12,384]{2,1,0:T(8,128)(2,1)} all-gather(bf16[1,12,384]{2,1,0:T(8,128)(2,1)S(1)} %convert_bitcast_fusion.1), channel_id=1, replica_groups=mesh['dp'=8,'head'=4] {'dp','head'}, dimensions={0}, use_global_device_ids=true | all-gather | bytes 304128 | tf_op jit(solution)/shard_map/all_gather | solution.py:185
  452.0 3.8 copy.385
  459.6 4.8 multiply_reduce_fusion.13
  474.0 4.4 all-to-all-start.2
  478.4 20.1 %all-to-all-done.2 = bf16[8,256,4,96]{1,3,0,2:T(8,128)(2,1)} async-done(((bf16[8,256,4,96]{1,3,0,2:T(8,128)(2,1)}), bf16[8,256,4,96]{1,3,0,2:T(8,128)(2,1)}, u32[]{:S(2)}, u32[]{:S(2)}) %all-to-all-start.2) | async-done | bytes 1572896 | tf_op jit(solution)/shard_map/all_to_all | solution.py:287
  501.3 77.1 %while.23 = (s32[]{:T(128)}, bf16[8,1024,1,288]{1,3,2,0:T(8,128)(2,1)}, bf16[8,1024,1,288]{1,3,2,0:T(8,128)(2,1)}, f32[8,1,1024,1]{2,3,1,0:T(1,128)}, bf16[8,1024,1,96]{1,3,2,0:T(8,128)(2,1)}, /*index=5*/s32[]{:T(128)}) while((s32[]{:T(128)}, bf16[8,1024,1,288]{1,3,2,0:T(8,128)(2,1)}, bf16[8,1024,1,288]{1,3,2,0:T(8,128)(2,1)}, ...), condition=%wide.region_30.31_spmd, body=%wide.region_28.30_spmd.sunk | while | flops 1021475840 | bytes 35811424 | solution.py:327
  578.4 8.6 copy.303
  587.0 5.3 all-to-all-start.3
  592.5 3.8 pad_maximum_fusion.3
  596.3 4.8 fusion.345
  604.0 4.8 fusion.344
  608.8 54.2 %all-to-all-done.3 = bf16[8,1024,1,288]{3,0,2,1:T(8,128)(2,1)} async-done(((bf16[8,1024,1,288]{3,0,2,1:T(8,128)(2,1)}), bf16[8,1024,1,288]{3,0,2,1:T(8,128)(2,1)}, u32[]{:S(2)}, u32[]{:S(2)}) %all-to-all-start.3) | async-done | bytes 4718624 | tf_op jit(solution)/shard_map/all_to_all | solution.py:328
  663.0 8.7 copy.386
  675.2 5.8 multiply_reduce_fusion.2
  681.5 5.9 all-reduce.12
  687.8 4.5 add_convert_fusion
  718.1 4.0 fusion.116
  722.2 9.4 multiply_reduce_fusion.3
  732.1 7.0 all-reduce.11
  741.8 4.0 multiply_convert_fusion.1
  780.7 4.2 convolution_bitcast_fusion.1
  785.0 5.8 convolution_bitcast_fusion
  790.8 79.4 %fusion.337 = (f32[16,1152]{1,0:T(8,128)S(1)}, f32[16,384]{1,0:T(8,128)S(1)}) fusion(f32[384,1152]{1,0:T(8,128)} %convolution_bitcast_fusion, f32[384,384]{1,0:T(8,128)S(1)} %copy-done.21), kind=kCustom, calls=%all-reduce-scatter.2 | all-reduce-scatter fusion | flops 786433 | bytes 2457600
  876.8 8.4 collective-permute-start.13
  895.0 5.1 collective-permute-start.12
  915.6 5.7 collective-permute-start.6
  940.7 4.0 fusion.104
  944.8 6.8 fusion.334
  951.7 43.4 %all-reduce.7 = f32[384,6]{0,1:T(8,128)S(1)} all-reduce(f32[384,6]{0,1:T(8,128)S(1)} %stack.39), channel_id=6, replica_groups=mesh['dp'=8,'head'=4] {'dp','head'}, use_global_device_ids=true, to_apply=%region_59.60.clone | all-reduce | flops 2304 | bytes 18432
  1002.2 40.3 %all-reduce.10 = (f32[1]{0:T(128)}, f32[]{:T(128)}) all-reduce(f32[1]{0:T(128)} %bitcast.73, f32[]{:T(128)S(6)} %add.516), channel_id=1, replica_groups=mesh['dp'=8,'head'=4] {'dp','head'}, use_global_device_ids=true, to_apply=%region_25.26 | all-reduce | flops 2 | bytes 16 | tf_op jit(solution)/shard_map/psum | solution.py:365
  (542 shorter events, 341.5 us)
Async XLA Ops:
  7.2 111.6 %all-gather.8.cloned.1.call-start = ((), (), s32[]{:S(2)}) async-start(), calls=%async_computation.7 | async-start | bytes 1216512 | tf_op jit(solution)/shard_map/all_gather | solution.py:182
  8.9 129.1 %all-gather.6.cloned.1.call-start = ((), (), s32[]{:S(2)}) async-start(), calls=%async_computation.6 | async-start | bytes 5474304 | tf_op jit(solution)/shard_map/all_gather | solution.py:183
  64.6 107.3 %copy-start.79 = (f32[384]{0:T(512)}, f32[384]{0:T(512)S(1)}, u32[]{:S(2)}) copy-start(f32[384]{0:T(512)S(1)} %get-tuple-element.138) | copy-start | bytes 4612
  64.6 107.3 %copy-start.87 = (f32[384]{0:T(512)}, f32[384]{0:T(512)S(1)}, u32[]{:S(2)}) copy-start(f32[384]{0:T(512)S(1)} %get-tuple-element.137) | copy-start | bytes 4612
  66.9 49.2 %collective-permute-start = (bf16[8,1,32,384]{3,2,1,0:T(8,128)(2,1)S(1)}, bf16[8,1,32,384]{3,2,1,0:T(8,128)(2,1)S(1)}, u32[]{:S(2)}, u32[]{:S(2)}) collective-permute-start(bf16[8,1,32,384]{3,2,1,0:T(8,128)(2,1)S(1)} %get-tuple-element.222), channel_id=1, source_target_pairs={{0,1},{1,2},{2,3},{4,5},{5,6},{6,7},{8,9},{9,10},{10,11},{12,13},{... | collective-permute-start | bytes 589832 | tf_op jit(solution)/shard_map/ppermute | solution.py:33
  68.3 47.9 %collective-permute-start.1 = (bf16[8,1,32,384]{3,2,1,0:T(8,128)(2,1)S(1)}, bf16[8,1,32,384]{3,2,1,0:T(8,128)(2,1)S(1)}, u32[]{:S(2)}, u32[]{:S(2)}) collective-permute-start(bf16[8,1,32,384]{3,2,1,0:T(8,128)(2,1)S(1)} %get-tuple-element.223), channel_id=1, source_target_pairs={{1,0},{2,1},{3,2},{5,4},{6,5},{7,6},{9,8},{10,9},{11,10},{13,12},{... | collective-permute-start | bytes 589832 | tf_op jit(solution)/shard_map/ppermute | solution.py:34
  175.7 4.7 collective-permute-start.2
  177.0 4.1 collective-permute-start.3
  242.1 91.9 %all-to-all-start = ((bf16[8,256,4,288]{1,3,0,2:T(8,128)(2,1)}), bf16[8,256,4,288]{1,3,0,2:T(8,128)(2,1)}, u32[]{:S(2)}, u32[]{:S(2)}) async-start(bf16[8,256,4,288]{1,3,0,2:T(8,128)(2,1)} %copy.291), calls=%async_computation | async-start | bytes 9437184 | tf_op jit(solution)/shard_map/all_to_all | solution.py:221
  381.2 70.8 %all-to-all-start.1 = ((bf16[8,1024,1,96]{3,0,2,1:T(8,128)(2,1)}), bf16[8,1024,1,96]{3,0,2,1:T(8,128)(2,1)}, u32[]{:S(2)}, u32[]{:S(2)}) async-start(bf16[8,1024,1,96]{3,0,2,1:T(8,128)(2,1)} %copy.294), calls=%async_computation.1 | async-start | bytes 4194304 | tf_op jit(solution)/shard_map/all_to_all | solution.py:246
  474.0 24.5 %all-to-all-start.2 = ((bf16[8,256,4,96]{1,3,0,2:T(8,128)(2,1)}), bf16[8,256,4,96]{1,3,0,2:T(8,128)(2,1)}, u32[]{:S(2)}, u32[]{:S(2)}) async-start(bf16[8,256,4,96]{1,3,0,2:T(8,128)(2,1)} %copy.299), calls=%async_computation.2 | async-start | bytes 3145728 | tf_op jit(solution)/shard_map/all_to_all | solution.py:287
  587.0 76.0 %all-to-all-start.3 = ((bf16[8,1024,1,288]{3,0,2,1:T(8,128)(2,1)}), bf16[8,1024,1,288]{3,0,2,1:T(8,128)(2,1)}, u32[]{:S(2)}, u32[]{:S(2)}) async-start(bf16[8,1024,1,288]{3,0,2,1:T(8,128)(2,1)} %copy.303), calls=%async_computation.3 | async-start | bytes 12582912 | tf_op jit(solution)/shard_map/all_to_all | solution.py:328
  592.3 403.5 %reduce-scatter.10.cloned.1.call-start = ((), (), s32[]{:S(2)}) async-start(), calls=%async_computation.8 | async-start | bytes 2433024 | tf_op jit(solution)/shard_map/reduce_scatter | solution.py:356
  692.4 9.0 collective-permute-start.5
  693.7 5.6 collective-permute-start.4
  741.6 255.7 %reduce-scatter.12.cloned.1.call-start = ((), (), s32[]{:S(2)}) async-start(), calls=%async_computation.9 | async-start | bytes 10948608
  785.0 125.2 %copy-start.73 = (f32[8,256]{1,0:T(8,128)S(1)}, f32[8,256]{1,0:T(8,128)}, u32[]{:S(2)}) copy-start(f32[8,256]{1,0:T(8,128)} %get-tuple-element.120) | copy-start | bytes 24580
  785.0 125.2 %copy-start.74 = (f32[8,256]{1,0:T(8,128)S(1)}, f32[8,256]{1,0:T(8,128)}, u32[]{:S(2)}) copy-start(f32[8,256]{1,0:T(8,128)} %get-tuple-element.121) | copy-start | bytes 24580
  785.0 125.2 %copy-start.81 = (pred[8,256]{1,0:T(8,128)(4,1)S(1)}, pred[8,256]{1,0:T(8,128)(4,1)}, u32[]{:S(2)}) copy-start(pred[8,256]{1,0:T(8,128)(4,1)} %and.35) | copy-start | bytes 6148
  785.0 125.8 %copy-start.96 = (f32[384]{0:T(512)S(1)}, f32[384]{0:T(512)}, u32[]{:S(2)}) copy-start(f32[384]{0:T(512)} %get-tuple-element.118) | copy-start | bytes 4612
  785.0 125.8 %copy-start.95 = (f32[384]{0:T(512)S(1)}, f32[384]{0:T(512)}, u32[]{:S(2)}) copy-start(f32[384]{0:T(512)} %get-tuple-element.125) | copy-start | bytes 4612
  870.3 6.5 collective-permute-start.23
  871.6 13.6 %collective-permute-start.22 = (f32[16,384]{1,0:T(8,128)S(1)}, f32[16,384]{1,0:T(8,128)S(1)}, u32[]{:S(2)}, u32[]{:S(2)}) collective-permute-start(f32[16,384]{1,0:T(8,128)S(1)} %get-tuple-element.174), channel_id=1, source_target_pairs={{0,7},{1,8},{2,9},{3,10},{4,11},{5,12},{6,13},{7,14},{8,15},{9,16}... | collective-permute-start | bytes 73736
  872.9 13.6 %collective-permute-start.21 = (f32[16,384]{1,0:T(8,128)S(1)}, f32[16,384]{1,0:T(8,128)S(1)}, u32[]{:S(2)}, u32[]{:S(2)}) collective-permute-start(f32[16,384]{1,0:T(8,128)S(1)} %get-tuple-element.174), channel_id=1, source_target_pairs={{0,6},{1,7},{2,8},{3,9},{4,10},{5,11},{6,12},{7,13},{8,14},{9,15},... | collective-permute-start | bytes 73736
  874.2 14.3 %collective-permute-start.20 = (f32[16,384]{1,0:T(8,128)S(1)}, f32[16,384]{1,0:T(8,128)S(1)}, u32[]{:S(2)}, u32[]{:S(2)}) collective-permute-start(f32[16,384]{1,0:T(8,128)S(1)} %get-tuple-element.174), channel_id=1, source_target_pairs={{0,5},{1,6},{2,7},{3,8},{4,9},{5,10},{6,11},{7,12},{8,13},{9,14},{... | collective-permute-start | bytes 73736
  875.5 30.1 %collective-permute-start.14 = (f32[16,1152]{1,0:T(8,128)S(1)}, f32[16,1152]{1,0:T(8,128)S(1)}, u32[]{:S(2)}, u32[]{:S(2)}) collective-permute-start(f32[16,1152]{1,0:T(8,128)S(1)} %get-tuple-element.173), channel_id=1, source_target_pairs={{0,7},{1,8},{2,9},{3,10},{4,11},{5,12},{6,13},{7,14},{8,15},{9,16}... | collective-permute-start | bytes 221192
  876.8 31.3 %collective-permute-start.13 = (f32[16,1152]{1,0:T(8,128)S(1)}, f32[16,1152]{1,0:T(8,128)S(1)}, u32[]{:S(2)}, u32[]{:S(2)}) collective-permute-start(f32[16,1152]{1,0:T(8,128)S(1)} %get-tuple-element.173), channel_id=1, source_target_pairs={{0,6},{1,7},{2,8},{3,9},{4,10},{5,11},{6,12},{7,13},{8,14},{9,15},... | collective-permute-start | bytes 221192
  885.2 17.5 %collective-permute-start.15 = (f32[12,1152]{1,0:T(8,128)S(1)}, f32[12,1152]{1,0:T(8,128)S(1)}, u32[]{:S(2)}, u32[]{:S(2)}) collective-permute-start(f32[12,1152]{1,0:T(8,128)S(1)} %slice.464), channel_id=1, source_target_pairs={{0,8},{1,9},{2,10},{3,11},{4,12},{5,13},{6,14},{7,15},{8,16},{9,17... | collective-permute-start | bytes 165896
  886.5 3.9 collective-permute-start.19
  888.5 4.8 collective-permute-start.18
  890.4 4.6 collective-permute-start.17
  893.3 6.9 collective-permute-start.16
  895.0 17.4 %collective-permute-start.12 = (f32[16,1152]{1,0:T(8,128)S(1)}, f32[16,1152]{1,0:T(8,128)S(1)}, u32[]{:S(2)}, u32[]{:S(2)}) collective-permute-start(f32[16,1152]{1,0:T(8,128)S(1)} %get-tuple-element.173), channel_id=1, source_target_pairs={{0,5},{1,6},{2,7},{3,8},{4,9},{5,10},{6,11},{7,12},{8,13},{9,14},{... | collective-permute-start | bytes 221192
  900.2 12.2 %collective-permute-start.11 = (f32[16,1152]{1,0:T(8,128)S(1)}, f32[16,1152]{1,0:T(8,128)S(1)}, u32[]{:S(2)}, u32[]{:S(2)}) collective-permute-start(f32[16,1152]{1,0:T(8,128)S(1)} %get-tuple-element.173), channel_id=1, source_target_pairs={{0,4},{1,5},{2,6},{3,7},{4,8},{5,9},{6,10},{7,11},{8,12},{9,13},{1... | collective-permute-start | bytes 221192
  902.7 9.7 collective-permute-start.10
  905.6 6.8 collective-permute-start.9
  908.1 4.3 collective-permute-start.8
  914.3 11.3 %collective-permute-start.7 = (bf16[8,1,32,384]{3,2,1,0:T(8,128)(2,1)S(1)}, bf16[8,1,32,384]{3,2,1,0:T(8,128)(2,1)S(1)}, u32[]{:S(2)}, u32[]{:S(2)}) collective-permute-start(bf16[8,1,32,384]{3,2,1,0:T(8,128)(2,1)S(1)} %get-tuple-element.212), channel_id=1, source_target_pairs={{1,0},{2,1},{3,2},{5,4},{6,5},{7,6},{9,8},{10,9},{11,10},{13,12},{... | collective-permute-start | bytes 589832 | tf_op jit(solution)/shard_map/ppermute | solution.py:34
  915.6 7.8 collective-permute-start.6
  944.7 101.9 %copy-start.82 = (f32[12,6]{0,1:T(8,128)S(1)}, f32[12,6]{0,1:T(8,128)}, u32[]{:S(2)}) copy-start(f32[12,6]{0,1:T(8,128)} %param.31) | copy-start | bytes 868
  944.7 101.9 %copy-start.89 = (f32[12,6]{0,1:T(8,128)S(1)}, f32[12,6]{0,1:T(8,128)}, u32[]{:S(2)}) copy-start(f32[12,6]{0,1:T(8,128)} %param.40) | copy-start | bytes 868
  944.7 101.8 %copy-start.90 = (f32[12,6]{0,1:T(8,128)S(1)}, f32[12,6]{0,1:T(8,128)}, u32[]{:S(2)}) copy-start(f32[12,6]{0,1:T(8,128)} %param.41) | copy-start | bytes 868
  944.8 102.5 %copy-start.48 = (f32[24,768]{1,0:T(8,128)S(1)}, f32[24,768]{1,0:T(8,128)}, u32[]{:S(2)}) copy-start(f32[24,768]{1,0:T(8,128)} %param.27) | copy-start | bytes 221188
  944.8 102.5 %copy-start.65 = (f32[24,768]{1,0:T(8,128)S(1)}, f32[24,768]{1,0:T(8,128)}, u32[]{:S(2)}) copy-start(f32[24,768]{1,0:T(8,128)} %param.32) | copy-start | bytes 221188
  944.8 102.5 %copy-start.66 = (f32[24,768]{1,0:T(8,128)S(1)}, f32[24,768]{1,0:T(8,128)}, u32[]{:S(2)}) copy-start(f32[24,768]{1,0:T(8,128)} %param.33) | copy-start | bytes 221188
  944.8 104.1 %copy-start.40 = (f32[216,384]{1,0:T(8,128)S(1)}, f32[216,384]{1,0:T(8,128)}, u32[]{:S(2)}) copy-start(f32[216,384]{1,0:T(8,128)} %param.28) | copy-start | bytes 995332
  944.8 104.1 %copy-start.44 = (f32[216,384]{1,0:T(8,128)S(1)}, f32[216,384]{1,0:T(8,128)}, u32[]{:S(2)}) copy-start(f32[216,384]{1,0:T(8,128)} %param.34) | copy-start | bytes 995332
  944.8 104.1 %copy-start.45 = (f32[216,384]{1,0:T(8,128)S(1)}, f32[216,384]{1,0:T(8,128)}, u32[]{:S(2)}) copy-start(f32[216,384]{1,0:T(8,128)} %param.35) | copy-start | bytes 995332
  (83 other events, 1301.8 us)
Sparse Core Ops, SparseCore 0:
  11.5 56.8 all-gather.7
  71.8 66.1 all-gather.5
  741.7 103.2 reduce-scatter.9
  851.9 144.3 reduce-scatter.11
where the time goes:
time: 1070 us; the launch traced here: 1060 us
  blocking collectives  435 us (41%)
  matrix products  244 us (23%)
  local copies, waits for them, and re-layouts  110 us (10%)
  waiting for transfers between devices  92.6 us (9%)
  other arithmetic  78.7 us (7%)
  starting transfers between devices  76.4 us (7%)
  between operations  21.8 us (2%)
    unnamed x2, blocking collectives  123 us
    dot_general x36, matrix products, conv_apply(): jnp.einsum(einsum_form, window, conv_taps[tap_index], preferred_element_t...  118 us
    psum x1, blocking collectives, body(): divisor = lax.psum(count_local, ('dp', 'head'))  85.9 us
    all_gather x1, blocking collectives, body(): lax.all_gather(out_master.astype(jnp.bfloat16), ('dp', 'head'), axis=0, t...  60.6 us
    all_to_all x1, waiting for transfers between devices, body(): lax.all_to_all(grad_grouped, 'head', split_axis=1, concat_axis=2, tiled=T...  54.2 us
    all_gather x1, blocking collectives, body(): lax.all_gather(qkv_master.astype(jnp.bfloat16), ('dp', 'head'), axis=0, t...  45.2 us
    all_gather x1, blocking collectives, body(): lax.all_gather(gains.astype(jnp.bfloat16), ('dp', 'head'), axis=0, tiled=...  43.4 us
    psum x1, blocking collectives, body(): square_total, loss_total = lax.psum((squares, loss_local), ('dp', 'head'))  40.3 us
  transfers between devices with their start and end apart: 32, of which 4 were waited for; matrix products, arithmetic and copies ran while one was open for 19% of the time, Pallas kernels for 0%

commit v1 on v0

v1 whole, which is shorter than its diff:
```python
import math

import jax
import jax.numpy as jnp
from jax import lax
from jax.sharding import PartitionSpec as P

HEADS = 4
GROUPS = 32
STEP = 10
TSTEPS = 4000


EPS_NORM = 1e-05
VLB_WEIGHT = 0.001
BETA_ONE = 0.9
BETA_TWO = 0.999
ADAM_EPS = 1e-08
DECAY = 0.01
RATE_MATRIX = 0.05
RATE_GAIN = 0.4
THRESHOLD = 0.002
OFFSET = 0.008


def plan(step_ids):
    moment = step_ids.astype(jnp.float32)

    def angle(values):
        return (values / TSTEPS + OFFSET) / (1.0 + OFFSET) * (0.5 * math.pi)

    start = angle(jnp.zeros_like(moment))
    before = angle(moment - 1.0)
    later_angle = angle(moment)
    beta_now = jnp.sin(later_angle - before) * jnp.sin(later_angle + before) / jnp.cos(before) ** 2
    fade_now = jnp.sin(later_angle - start) * jnp.sin(later_angle + start) / jnp.cos(start) ** 2
    fade_prev = jnp.sin(before - start) * jnp.sin(before + start) / jnp.cos(start) ** 2
    log_beta = jnp.log(beta_now)
    log_tilde = jnp.log(beta_now * fade_prev / fade_now)
    factor = beta_now * beta_now / ((1.0 - beta_now) * fade_now)
    return (log_beta, log_tilde, factor)


def embed(step_ids, width):
    half_width = width // 2
    frequency = jnp.exp(-math.log(10000.0) * jnp.arange(half_width, dtype=jnp.float32) / half_width)
    phases = step_ids.astype(jnp.float32)[:, None] * frequency[None, :]
    return jnp.concatenate([jnp.cos(phases), jnp.sin(phases)], axis=1)


def silu_slope(values):
    sigmoid_vals = jax.nn.sigmoid(values)
    return sigmoid_vals * (1.0 + values * (1.0 - sigmoid_vals))


def bit_count(axis):
    size = lax.axis_size(axis)
    count = size.bit_length() - 1
    assert size == 1 << count
    return count


def flip(values, axis, bit):
    size = lax.axis_size(axis)
    return lax.ppermute(values, axis, [(i, i ^ (1 << bit)) for i in range(size)])


def my_bit(axis, bit):
    return (lax.axis_index(axis) >> bit) & 1


def all_bits():
    return [(axis, bit) for axis in ("dp", "head") for bit in reversed(range(bit_count(axis)))]


def gather_bits(block, order):
    rank = {name: place for place, name in enumerate(all_bits())}
    shape = block.shape
    held = []
    for name in order:
        other = flip(block, *name)
        place = sum(rank[have] < rank[name] for have in held)
        bit = my_bit(*name) == 0
        block = jnp.stack([jnp.where(bit, block, other), jnp.where(bit, other, block)], axis=place)
        held.append(name)
    return block.reshape((-1,) + shape)


def scatter_bits(blocks, order, wire):
    names = sorted(order, key=all_bits().index)
    total = blocks.reshape((2,) * len(names) + blocks.shape[1:])
    for name in order:
        place = names.index(name)
        bit = my_bit(*name)
        keep = lax.dynamic_index_in_dim(total, bit, place, keepdims=False)
        send = lax.dynamic_index_in_dim(total, 1 - bit, place, keepdims=False).astype(wire)
        total = keep + flip(send, *name).astype(keep.dtype)
        names.remove(name)
    return total


def sum_bits(values, order):
    for name in order:
        values = values + flip(values, *name)
    return values


def rows_to_samples(strips):
    parts = lax.axis_size("head")
    rest = strips.shape[1:]
    held = strips.reshape((1, strips.shape[0]) + rest)
    for bit in reversed(range(bit_count("head"))):
        sources, samples = held.shape[:2]
        halves = held.reshape((sources, 2, samples // 2) + rest)
        mine = my_bit("head", bit)
        keep = lax.dynamic_index_in_dim(halves, mine, 1, keepdims=False)
        got = flip(lax.dynamic_index_in_dim(halves, 1 - mine, 1, keepdims=False), "head", bit)
        low = mine == 0
        held = jnp.stack([jnp.where(low, keep, got), jnp.where(low, got, keep)], axis=1)
        held = held.reshape((sources * 2, samples // 2) + rest)
    held = jnp.moveaxis(held, 0, 1)
    return held.reshape((held.shape[0], parts * rest[0]) + rest[1:])


def group_norm(values, gain_row, shift_row):
    samples, pixels, channels = values.shape
    grouped_vals = values.reshape(samples, pixels, GROUPS, channels // GROUPS)
    group_mean = jnp.mean(grouped_vals, axis=(1, 3))
    square_mean = jnp.mean(grouped_vals * grouped_vals, axis=(1, 3))
    inverse_std = lax.rsqrt(square_mean - group_mean * group_mean + EPS_NORM)
    normed = (
        (grouped_vals - group_mean[:, None, :, None]) * inverse_std[:, None, :, None]
    ).reshape(values.shape)
    return (normed * gain_row + shift_row, normed, inverse_std)


def group_norm_back(grad_out, normed, inverse_std, gain_row):
    samples, pixels, channels = grad_out.shape
    scaled = (grad_out * gain_row).reshape(samples, pixels, GROUPS, channels // GROUPS)
    flat_normed = normed.reshape(scaled.shape)
    back_values = (
        scaled
        - jnp.mean(scaled, axis=(1, 3))[:, None, :, None]
        - flat_normed * jnp.mean(scaled * flat_normed, axis=(1, 3))[:, None, :, None]
    ) * inverse_std[:, None, :, None]
    return (
        back_values.reshape(grad_out.shape),
        jnp.sum(grad_out * normed, axis=(0, 1)),
        jnp.sum(grad_out, axis=(0, 1)),
    )


def conv(hidden, taps, flipped):
    channels = taps.shape[-1]
    kernel = taps.reshape(3, 3, channels, channels)
    if flipped:
        kernel = jnp.flip(kernel, (0, 1))
    spec = ("NHWC", "HWOI" if flipped else "HWIO", "NHWC")
    return lax.conv_general_dilated(
        hidden, kernel, (1, 1), "SAME", dimension_numbers=spec, preferred_element_type=jnp.float32
    )


def conv_weights(hidden, grad_b):
    channels = hidden.shape[-1]
    spec = ("CHWN", "IHWO", "HWNC")
    return lax.conv_general_dilated(
        hidden, grad_b, (1, 1), ((1, 1), (1, 1)), dimension_numbers=spec, preferred_element_type=jnp.float32
    ).reshape(9 * channels, channels)


def adamw(master, gradient, first, second, step_rate, decay_rate, clip_factor):
    gradient = gradient * clip_factor
    first_new = BETA_ONE * first + (1.0 - BETA_ONE) * gradient
    second_new = BETA_TWO * second + (1.0 - BETA_TWO) * gradient * gradient
    ratio = (
        first_new
        / (1.0 - BETA_ONE**STEP)
        / (jnp.sqrt(second_new / (1.0 - BETA_TWO**STEP)) + ADAM_EPS)
    )
    return (master - step_rate * (ratio + decay_rate * master), first_new, second_new)


def body(
    images,
    noise,
    timesteps,
    extents,
    film_master,
    conv_master,
    qkv_master,
    out_master,
    gains,
    film_first,
    film_second,
    conv_first,
    conv_second,
    qkv_first,
    qkv_second,
    out_first,
    out_second,
    gain_first,
    gain_second,
):
    devices = lax.axis_size("dp") * lax.axis_size("head")
    device = lax.axis_index("dp") * lax.axis_size("head") + lax.axis_index("head")
    bits = all_bits()
    high, low_bits = bits[0], bits[1:]
    channels = images.shape[-1]
    wide = film_master.shape[1]
    half_width = channels // 2
    head_size = channels // HEADS
    factor_att = head_size ** (-0.5)
    conv_rows = conv_master.shape[0]
    film_rows = film_master.shape[0]
    out_rows = out_master.shape[0]

    local_samples = timesteps.shape[0]
    small = jnp.concatenate(
        [
            gains.reshape(-1),
            extents.astype(jnp.float32).reshape(-1),
            (timesteps // 64).astype(jnp.float32),
            (timesteps % 64).astype(jnp.float32),
        ]
    )
    small = jnp.pad(small, (0, 8 * channels - small.shape[0])).reshape(8, channels)
    block = jnp.concatenate(
        [
            conv_master,
            film_master.reshape(-1, channels),
            qkv_master.reshape(-1, channels),
            out_master,
            small,
        ]
    ).astype(jnp.bfloat16)
    every = gather_bits(block, bits)
    ends = [0]
    for length in (conv_rows, film_rows * wide // channels, 3 * out_rows, out_rows, 8):
        ends.append(ends[-1] + length)
    conv_w, film_w, qkv_w, out_w, smalls = [every[:, lo:hi] for lo, hi in zip(ends, ends[1:])]
    conv_w = conv_w.reshape(-1, channels)
    film_w = film_w.reshape(-1, wide)
    qkv_w = qkv_w.reshape(channels, 3 * channels)
    out_w = out_w.reshape(channels, channels)
    smalls = smalls.reshape(devices, -1).astype(jnp.float32)
    gain_f = smalls[:, : gains.size].reshape(channels, 6)
    dp_smalls = smalls.reshape(lax.axis_size("dp"), lax.axis_size("head"), -1)[:, 0, gains.size :]
    extents_all = dp_smalls[:, : 2 * local_samples].reshape(-1, 2)
    times = dp_smalls[:, 2 * local_samples : 4 * local_samples].reshape(-1, 2, local_samples)
    times_all = (times[:, 0] * 64.0 + times[:, 1]).reshape(-1).astype(jnp.int32)
    divisor = jnp.sum(extents_all[:, 0] * extents_all[:, 1])

    pictures = rows_to_samples(images)
    target = rows_to_samples(noise)
    samples, rows, width_px, _ = pictures.shape
    pixels = rows * width_px
    first = lax.axis_index("head") * samples
    own_times = lax.dynamic_slice_in_dim(timesteps, first, samples)
    own_extents = lax.dynamic_slice_in_dim(extents, first, samples)

    taps_one = conv_w[: 9 * channels]
    taps_two = conv_w[9 * channels :]
    log_beta, log_tilde, factor = plan(own_times)
    embedded_all = jax.nn.silu(embed(times_all, wide)).astype(jnp.bfloat16)
    embedded = jax.nn.silu(embed(own_times, wide)).astype(jnp.bfloat16)
    film_out = lax.dot_general(
        embedded, film_w, (((1,), (1,)), ((), ())), preferred_element_type=jnp.float32
    )
    scale_part = film_out[:, None, :channels]
    shift_part = film_out[:, None, channels:]
    source = pictures.reshape(samples, pixels, channels).astype(jnp.float32)
    first_out, first_normed, first_std = group_norm(source, gain_f[:, 0], gain_f[:, 1])
    hidden_one = jax.nn.silu(first_out).astype(jnp.bfloat16).reshape(pictures.shape)
    inner = conv(hidden_one, taps_one, False).reshape(source.shape)
    second_out, second_normed, second_std = group_norm(inner, gain_f[:, 2], gain_f[:, 3])
    lifted = second_out * (1.0 + scale_part) + shift_part
    hidden_two = jax.nn.silu(lifted).astype(jnp.bfloat16).reshape(pictures.shape)
    middle = source + conv(hidden_two, taps_two, False).reshape(source.shape)
    third_out, third_normed, third_std = group_norm(middle, gain_f[:, 4], gain_f[:, 5])
    normed_b = third_out.astype(jnp.bfloat16)
    packed = jnp.einsum("spc,cf->spf", normed_b, qkv_w, preferred_element_type=jnp.float32)
    packed = packed.astype(jnp.bfloat16).reshape(samples, pixels, HEADS, 3 * head_size)
    packed = jnp.moveaxis(packed, 2, 1).reshape(samples * HEADS, pixels, 3 * head_size)

    def attend(block):
        queries = block[:, :head_size]
        key_part = block[:, head_size : 2 * head_size]
        value_part = block[:, 2 * head_size :]
        scores = (
            jnp.einsum("qd,kd->qk", queries, key_part, preferred_element_type=jnp.float32)
            * factor_att
        )
        row_max = jnp.max(scores, axis=-1, keepdims=True)
        log_total = jnp.log(jnp.sum(jnp.exp(scores - row_max), axis=-1, keepdims=True)) + row_max
        weights_soft = jnp.exp(scores - log_total).astype(jnp.bfloat16)
        mixed = jnp.einsum("qk,kd->qd", weights_soft, value_part, preferred_element_type=jnp.float32)
        return (mixed.astype(jnp.bfloat16), log_total)

    mixed_all, log_totals = lax.map(attend, packed)
    attn_cat = jnp.moveaxis(mixed_all.reshape(samples, HEADS, pixels, head_size), 1, 2)
    attn_cat = attn_cat.reshape(samples, pixels, channels)
    result = middle + jnp.einsum("spc,cd->spd", attn_cat, out_w, preferred_element_type=jnp.float32)
    row_ids = jnp.arange(rows, dtype=jnp.int32)
    col_ids = jnp.arange(width_px, dtype=jnp.int32)
    valid = (
        (
            (row_ids[None, :, None] >= rows - own_extents[:, 0][:, None, None])
            & (col_ids[None, None, :] < own_extents[:, 1][:, None, None])
        )
        .astype(jnp.float32)
        .reshape(samples, pixels)
    )
    residue = result[..., :half_width] - target.reshape(samples, pixels, half_width).astype(jnp.float32)
    weight = jax.nn.sigmoid(result[..., half_width:])
    beta_log = log_beta[:, None, None]
    tilde_log = log_tilde[:, None, None]
    blended = weight * beta_log + (1.0 - weight) * tilde_log
    spread = jnp.exp(tilde_log - blended)
    damped = factor[:, None, None] * residue * residue * jnp.exp(-blended)
    diverge = 0.5 * (-1.0 + blended - tilde_log + spread + damped)
    loss_local = jnp.sum(
        valid * (jnp.mean(residue * residue, axis=-1) + VLB_WEIGHT * jnp.mean(diverge, axis=-1))
    )
    grad_guess = valid[..., None] * 2.0 * residue / (half_width * divisor)
    grad_blend = (
        valid[..., None] * (VLB_WEIGHT / half_width) * 0.5 * (1.0 - spread - damped) / divisor
    )
    grad_raw = grad_blend * (beta_log - tilde_log) * weight * (1.0 - weight)
    grad_result = jnp.concatenate([grad_guess, grad_raw], axis=-1)
    down_b = grad_result.astype(jnp.bfloat16)
    out_grad = jnp.einsum("spc,spd->cd", attn_cat, down_b, preferred_element_type=jnp.float32)
    back_mixed = jnp.einsum(
        "spd,cd->spc", down_b, out_w, preferred_element_type=jnp.float32
    ).astype(jnp.bfloat16)
    back_grouped = jnp.moveaxis(back_mixed.reshape(samples, pixels, HEADS, head_size), 2, 1)
    back_grouped = back_grouped.reshape(samples * HEADS, pixels, head_size)

    def attend_back(parts):
        block, log_total, upstream = parts
        queries = block[:, :head_size]
        key_part = block[:, head_size : 2 * head_size]
        value_part = block[:, 2 * head_size :]
        scores = (
            jnp.einsum("qd,kd->qk", queries, key_part, preferred_element_type=jnp.float32)
            * factor_att
        )
        weights_soft = jnp.exp(scores - log_total)
        grad_value = jnp.einsum(
            "qk,qd->kd", weights_soft.astype(jnp.bfloat16), upstream, preferred_element_type=jnp.float32
        )
        grad_soft = jnp.einsum("qd,kd->qk", upstream, value_part, preferred_element_type=jnp.float32)
        grad_scores = (
            weights_soft * (grad_soft - jnp.sum(weights_soft * grad_soft, axis=-1, keepdims=True))
        ).astype(jnp.bfloat16)
        grad_query = (
            jnp.einsum("qk,kd->qd", grad_scores, key_part, preferred_element_type=jnp.float32)
            * factor_att
        )
        grad_key = (
            jnp.einsum("qk,qd->kd", grad_scores, queries, preferred_element_type=jnp.float32)
            * factor_att
        )
        return jnp.concatenate([grad_query, grad_key, grad_value], axis=-1).astype(jnp.bfloat16)

    grad_grouped = lax.map(attend_back, (packed, log_totals, back_grouped))
    grad_local = jnp.moveaxis(grad_grouped.reshape(samples, HEADS, pixels, 3 * head_size), 1, 2)
    grad_local = grad_local.reshape(samples, pixels, 3 * channels)
    qkv_grad = jnp.einsum("spc,spf->cf", normed_b, grad_local, preferred_element_type=jnp.float32)
    grad_normed = jnp.einsum("spf,cf->spc", grad_local, qkv_w, preferred_element_type=jnp.float32)
    back_middle, gain_three, bias_three = group_norm_back(
        grad_normed, third_normed, third_std, gain_f[:, 4]
    )
    grad_middle = grad_result + back_middle
    grad_two_b = grad_middle.astype(jnp.bfloat16).reshape(pictures.shape)
    conv_two_grad = conv_weights(hidden_two, grad_two_b)
    grad_hidden_two = conv(grad_two_b, taps_two, True).reshape(source.shape)
    grad_lifted = grad_hidden_two * silu_slope(lifted)
    grad_scale = jnp.sum(grad_lifted * second_out, axis=1)
    grad_shift = jnp.sum(grad_lifted, axis=1)
    grad_second = grad_lifted * (1.0 + scale_part)
    back_inner, gain_two, bias_two = group_norm_back(
        grad_second, second_normed, second_std, gain_f[:, 2]
    )
    grad_one_b = back_inner.astype(jnp.bfloat16).reshape(pictures.shape)
    conv_one_grad = conv_weights(hidden_one, grad_one_b)
    grad_hidden_one = conv(grad_one_b, taps_one, True).reshape(source.shape)
    grad_first = grad_hidden_one * silu_slope(first_out)
    gain_one = jnp.sum(grad_first * first_normed, axis=(0, 1))
    bias_one = jnp.sum(grad_first, axis=(0, 1))
    film_grad_b = jnp.concatenate([grad_scale, grad_shift], axis=1).astype(jnp.bfloat16)

    back_order = tuple(reversed(bits))
    early = jnp.concatenate(
        [qkv_grad.reshape(devices, -1, channels), out_grad.reshape(devices, -1, channels)], axis=1
    )
    early = scatter_bits(early, back_order, jnp.bfloat16)
    qkv_g = early[: 3 * out_rows].reshape(qkv_master.shape)
    out_g = early[3 * out_rows :]
    back_low = tuple(reversed(low_bits))
    shares = []
    for part in (conv_two_grad, conv_one_grad):
        shares.append(scatter_bits(part.reshape(-1, conv_rows, channels), back_low, jnp.bfloat16))
    size = lax.axis_size(high[0])
    top = my_bit(*high) == 1
    sent = jnp.where(top, shares[1], shares[0]).astype(jnp.bfloat16)
    conv_g = jnp.where(top, shares[0], shares[1]) + flip(sent, *high).astype(jnp.float32)

    film_all = gather_bits(film_grad_b, bits).reshape(-1, film_grad_b.shape[1])
    film_own = lax.dynamic_slice_in_dim(film_all, device * film_rows, film_rows, axis=1)
    film_g = jnp.einsum("sf,se->fe", film_own, embedded_all, preferred_element_type=jnp.float32)
    gain_grad = jnp.stack([gain_one, bias_one, gain_two, bias_two, gain_three, bias_three], axis=1)
    gain_g = sum_bits(gain_grad, bits).reshape(devices, -1, 6)
    gain_g = lax.dynamic_index_in_dim(gain_g, device, 0, keepdims=False)
    reduced = (film_g, conv_g, qkv_g, out_g, gain_g)
    squares = jnp.zeros((), jnp.float32)
    for gradient in reduced:
        squares = squares + jnp.sum(gradient * gradient)
    totals = sum_bits(jnp.stack([squares, loss_local]), bits)
    grad_norm = jnp.sqrt(totals[0])
    clip_factor = jnp.minimum(1.0, THRESHOLD / (grad_norm + 1e-06))
    film_res = adamw(film_master, film_g, film_first, film_second, RATE_MATRIX, DECAY, clip_factor)
    conv_res = adamw(conv_master, conv_g, conv_first, conv_second, RATE_MATRIX, DECAY, clip_factor)
    qkv_res = adamw(qkv_master, qkv_g, qkv_first, qkv_second, RATE_MATRIX, DECAY, clip_factor)
    out_res = adamw(out_master, out_g, out_first, out_second, RATE_MATRIX, DECAY, clip_factor)
    gain_res = adamw(gains, gain_g, gain_first, gain_second, RATE_GAIN, 0.0, clip_factor)
    loss_parts = jnp.stack([totals[1], divisor])
    return (
        loss_parts,
        grad_norm,
        film_res[0],
        film_res[1],
        film_res[2],
        conv_res[0],
        conv_res[1],
        conv_res[2],
        qkv_res[0],
        qkv_res[1],
        qkv_res[2],
        out_res[0],
        out_res[1],
        out_res[2],
        gain_res[0],
        gain_res[1],
        gain_res[2],
    )


def solution(mesh):
    in_specs = (
        P("dp", "head", None, None),
        P("dp", "head", None, None),
        P("dp"),
        P("dp", None),
        P(("dp", "head"), None),
        P(("dp", "head"), None),
        P(("dp", "head"), None),
        P(("dp", "head"), None),
        P(("dp", "head"), None),
        P(("dp", "head"), None),
        P(("dp", "head"), None),
        P(("dp", "head"), None),
        P(("dp", "head"), None),
        P(("dp", "head"), None),
        P(("dp", "head"), None),
        P(("dp", "head"), None),
        P(("dp", "head"), None),
        P(("dp", "head"), None),
        P(("dp", "head"), None),
    )
    out_specs = (
        P(),
        P(),
        P(("dp", "head"), None),
        P(("dp", "head"), None),
        P(("dp", "head"), None),
        P(("dp", "head"), None),
        P(("dp", "head"), None),
        P(("dp", "head"), None),
        P(("dp", "head"), None),
        P(("dp", "head"), None),
        P(("dp", "head"), None),
        P(("dp", "head"), None),
        P(("dp", "head"), None),
        P(("dp", "head"), None),
        P(("dp", "head"), None),
        P(("dp", "head"), None),
        P(("dp", "head"), None),
    )
    return jax.shard_map(body, mesh=mesh, in_specs=in_specs, out_specs=out_specs, check_vma=False)
```

time: 1070 us -> 674 us (0.63)
  blocking collectives: 435 us -> 0 us
  matrix products: 244 us -> 164 us
  waiting for transfers between devices: 92.6 us -> 164 us
  other arithmetic: 78.7 us -> 134 us
  local copies, waits for them, and re-layouts: 110 us -> 149 us
  starting transfers between devices: 76.4 us -> 43.7 us
  between operations: 21.8 us -> 8.53 us
    ppermute x8 -> x38, waiting for transfers between devices: 0.72 us -> 164 us  [flip(): return lax.ppermute(values, axis, [(i, i ^ 1 << bit) for i in range(size)])]
    psum x7 -> x0, blocking collectives: 163 us -> none  [the longest x1 85.9 us: body(): divisor = lax.psum(count_local, ('dp', 'head'))]
    dot_general x111 -> x57, matrix products: 218 us -> 67.5 us  [the longest x8 16 us: attend_back(): jnp.einsum('qd,kd->qk', upstream, value_part, preferred_element_type=jnp....]
    all_gather x3 -> x0, blocking collectives: 149 us -> none  [the longest x1 60.6 us: body(): lax.all_gather(out_master.astype(jnp.bfloat16), ('dp', 'head'), axis=0, t...]
    unnamed x2 -> x0, blocking collectives: 123 us -> none
    all_to_all x4 -> x0, waiting for transfers between devices: 74.3 us -> none  [the longest x1 54.2 us: body(): lax.all_to_all(grad_grouped, 'head', split_axis=1, concat_axis=2, tiled=T...]
    conv_general_dilated x0 -> x6, matrix products: none -> 72.9 us  [the longest x4 53.7 us: conv(): lax.conv_general_dilated(hidden, kernel, (1, 1), 'SAME', dimension_number...]
    unnamed x17 -> x0, starting transfers between devices: 39.8 us -> none
  transfers between devices with their start and end apart: 32 -> 38, of which waited for: 4 -> 21; matrix products, arithmetic and copies ran while one was open for 19% -> 11% of each run, Pallas kernels for 0% -> 0%
where the time goes in v1:
time: 674 us; the launch traced here: 665 us
  waiting for transfers between devices  164 us (24%)
  matrix products  164 us (24%)
  local copies, waits for them, and re-layouts  149 us (22%)
  other arithmetic  134 us (20%)
  starting transfers between devices  43.7 us (6%)
  between operations  8.53 us (1%)
    ppermute x38, waiting for transfers between devices, flip(): return lax.ppermute(values, axis, [(i, i ^ 1 << bit) for i in range(size)])  164 us
    conv_general_dilated x4, matrix products, conv(): lax.conv_general_dilated(hidden, kernel, (1, 1), 'SAME', dimension_number...  53.7 us
    ppermute x38, starting transfers between devices, flip(): return lax.ppermute(values, axis, [(i, i ^ 1 << bit) for i in range(size)])  43.7 us
    unnamed x207, local copies, waits for them, and re-layouts  25.7 us
    squeeze x16, local copies, waits for them, and re-layouts, body(): mixed_all, log_totals = lax.map(attend, packed)  19.6 us
    another operation x20, other arithmetic, gather_bits(): jnp.stack([jnp.where(bit, block, other), jnp.where(bit, other, block)], a...  19.6 us
    conv_general_dilated x2, matrix products, conv_weights(): lax.conv_general_dilated(hidden, grad_b, (1, 1), ((1, 1), (1, 1)), dimens...  19.2 us
    dot_general x8, matrix products, attend_back(): jnp.einsum('qd,kd->qk', upstream, value_part, preferred_element_type=jnp....  16 us
  transfers between devices with their start and end apart: 38, of which 21 were waited for; matrix products, arithmetic and copies ran while one was open for 11% of the time, Pallas kernels for 0%

profile of v1, /device:TPU:0, one launch (start us, length us, event | category | flops | bytes accessed | tf_op | source)
XLA Modules:
  0.0 664.9 jit_solution(5955699834353155916)
XLA Ops:
  7.3 4.1 collective-permute-start.2
  11.4 11.2 %collective-permute-done.2 = bf16[320,384]{1,0:T(8,128)(2,1)S(1)} collective-permute-done((bf16[320,384]{1,0:T(8,128)(2,1)S(1)}, bf16[320,384]{1,0:T(8,128)(2,1)S(1)}, u32[]{:S(2)}, u32[]{:S(2)}) %collective-permute-start.2) | collective-permute-done | bytes 245792 | tf_op jit(solution)/shard_map/ppermute | solution.py:65
  23.5 11.7 %collective-permute-done.3 = bf16[2,320,384]{2,1,0:T(8,128)(2,1)S(1)} collective-permute-done((bf16[2,320,384]{2,1,0:T(8,128)(2,1)S(1)}, bf16[2,320,384]{2,1,0:T(8,128)(2,1)S(1)}, u32[]{:S(2)}, u32[]{:S(2)}) %collective-permute-start.3) | collective-permute-done | bytes 491552 | tf_op jit(solution)/shard_map/ppermute | solution.py:65
  36.7 20.9 %collective-permute-done.4 = bf16[2,2,320,384]{3,2,1,0:T(8,128)(2,1)} collective-permute-done((bf16[2,2,320,384]{3,2,1,0:T(8,128)(2,1)S(1)}, bf16[2,2,320,384]{3,2,1,0:T(8,128)(2,1)}, u32[]{:S(2)}, u32[]{:S(2)}) %collective-permute-start.4) | collective-permute-done | bytes 983072 | tf_op jit(solution)/shard_map/ppermute | solution.py:65
  63.9 42.8 %collective-permute-done.5 = bf16[2,2,2,320,384]{4,3,2,1,0:T(8,128)(2,1)} collective-permute-done((bf16[2,2,2,320,384]{4,3,2,1,0:T(8,128)(2,1)}, bf16[2,2,2,320,384]{4,3,2,1,0:T(8,128)(2,1)}, u32[]{:S(2)}, u32[]{:S(2)}) %collective-permute-start.5) | collective-permute-done | bytes 1966112 | tf_op jit(solution)/shard_map/ppermute | solution.py:65
  115.3 15.9 %collective-permute-done.7 = bf16[1,4,8,32,192]{4,3,2,1,0:T(8,128)(2,1)} collective-permute-done((bf16[1,4,8,32,192]{4,3,2,1,0:T(8,128)(2,1)}, bf16[1,4,8,32,192]{4,3,2,1,0:T(8,128)(2,1)}, u32[]{:S(2)}, u32[]{:S(2)}) %collective-permute-start.7) | collective-permute-done | bytes 393248 | tf_op jit(solution)/shard_map/ppermute | solution.py:65
  145.0 2.6 copy.268
  147.7 5.2 select_bitcast_fusion.1
  152.9 6.1 pad_maximum_fusion
  160.0 5.5 fusion.202
  176.5 11.9 %fusion.215 = (f32[32,16,5,384]{3,1,2,0:T(8,128)}, f32[32,16,5,384]{3,1,2,0:T(8,128)S(1)}) fusion(bf16[3,3,384,384]{3,2,1,0:T(8,128)(2,1)S(1)} %bitcast.427, bf16[32,2,8,7,384]{4,0,3,2,1:T(8,128)(2,1)S(1)} %fusion.66, pred[16,5]{0,1:T(8,128)(4,1)S(1)} %copy-done.89), kind=kOutput, calls=%fused_computation.434 | convolution fusion | flops 6655180800 | bytes 13271120 | tf_op jit(solution)/shard_map/conv_general_dilated | solution.py:159
  190.9 3.4 copy.262
  195.1 3.0 reshape.567
  202.8 3.0 copy-done.20
  205.7 11.2 %fusion.94 = (bf16[32,16,5,384]{3,1,2,0:T(8,128)(2,1)S(1)}, f32[32,16,5,384]{3,1,2,0:T(8,128)}, f32[32,16,5,384]{3,1,2,0:T(8,128)}) fusion(pred[16,5]{0,1:T(8,128)(4,1)S(1)} %copy-done.89, f32[32,16,5,384]{3,0,2,1:T(8,128)S(1)} %bitcast.388, f32[32,16,5,384]{3,0,2,1:T(8,128)S(1)} %bitcast.385, f32[384]{0:T(512)S(1)} %get-tuple-element.105, ...), kind=kLoop, calls=%fused_computation.165 | loop fusion | flops 11796480 | bytes 29494352 | tf_op jit(solution)/shard_map/convert_element_type | solution.py:278
  219.7 10.1 %fusion.72 = f32[32,16,5,384]{3,1,2,0:T(8,128)S(1)} fusion(bf16[3,3,384,384]{3,2,1,0:T(8,128)(2,1)S(1)} %bitcast.429, bf16[32,2,8,1,384]{4,2,1,3,0:T(8,128)(2,1)S(1)} %pad.9, bf16[32,2,8,5,384]{4,2,1,3,0:T(8,128)(2,1)S(1)} %bitcast.382, bf16[32,2,8,1,384]{4,2,1,3,0:T(8,128)(2,1)S(1)} %pad.8), kind=kOutput, calls=%fused_computation.129 | convolution fusion | flops 6661472256 | bytes 9338880 | tf_op jit(solution)/shard_map/conv_general_dilated | solution.py:159
  231.3 2.8 fusion.191
  234.1 3.4 copy.328
  245.8 3.9 add_convert_fusion.2
  249.8 2.9 convolution_convert_fusion
  252.7 2.8 fusion.203
  255.5 3.6 pad_maximum_fusion.1
  259.2 40.1 %while.22 = (s32[]{:T(128)}, bf16[8,1024,96]{1,2,0:T(8,128)(2,1)}, f32[8,1024,1]{1,2,0:T(1,128)}, bf16[8,1024,288]{2,1,0:T(8,128)(2,1)}, s32[]{:T(128)}) while((s32[]{:T(128)}, bf16[8,1024,96]{1,2,0:T(8,128)(2,1)}, f32[8,1024,1]{1,2,0:T(1,128)}, bf16[8,1024,288]{2,1,0:T(8,128)(2,1)}, s32[]{:T(128)}) %tuple.133), condition=%wide.region_15.16_spmd, body=%wide.region_12.15_spmd.sunk | while | flops 411139072 | bytes 14783553 | solution.py:300
  303.2 3.5 add.510
  310.8 3.2 multiply_reduce_fusion.9
  316.3 3.8 copy.323
  320.2 79.6 %while.23 = (s32[]{:T(128)}, bf16[8,1024,288]{1,2,0:T(8,128)(2,1)}, bf16[8,1024,288]{2,1,0:T(8,128)(2,1)}, f32[8,1024,1]{1,2,0:T(1,128)}, bf16[8,1024,96]{2,1,0:T(8,128)(2,1)}, /*index=5*/s32[]{:T(128)}) while((s32[]{:T(128)}, bf16[8,1024,288]{1,2,0:T(8,128)(2,1)}, bf16[8,1024,288]{2,1,0:T(8,128)(2,1)}, f32[8,1024,1]{1,2,0:T(1,128)}, ...), condition=%wide.region_19.20_spmd, body=%wide.region_17.19_spmd.sunk | while | flops 1021475840 | bytes 36271692 | solution.py:366
  399.8 7.2 %fusion.216 = (f32[384]{0:T(512)S(1)}, f32[2,1024,384]{2,1,0:T(8,128)}) fusion(bf16[2,1024,1152]{1,2,0:T(8,128)(2,1)} %bitcast.77, bf16[384,1152,1]{1,0,2:T(8,128)(2,1)} %reshape.680), kind=kOutput, calls=%fused_computation.435 | convolution fusion | flops 1812725376 | bytes 8750592 | tf_op jit(solution)/shard_map/spf,cf->spc/dot_general | solution.py:370
  407.0 6.2 convolution_bitcast_fusion
  418.3 3.7 copy.279
  422.0 3.1 multiply_reduce_fusion.2
  425.9 4.2 add_convert_fusion.1
  436.8 19.2 %select_reduce_fusion.1 = (f32[384]{0:T(512)S(1)}, f32[384]{0:T(512)S(1)}, f32[32,16,5,384]{3,1,2,0:T(8,128)}, f32[32,16,5,384]{3,1,2,0:T(8,128)S(1)}, f32[32,16...) fusion(pred[16,5]{0,1:T(8,128)(4,1)S(1)} %copy-done.90, f32[32,16,5,384]{3,0,2,1:T(8,128)S(1)} %bitcast.386, ...), kind=kOutput, calls=%fused_computation.80 | convolution fusion | flops 6672874496 | bytes 32938064 | tf_op jit(solution)/shard_map/conv_general_dilated | solution.py:159
  458.6 3.4 copy.302
  468.8 11.5 %fusion.91 = bf16[32,16,5,384]{3,1,2,0:T(8,128)(2,1)S(1)} fusion(f32[32,16,5,384]{3,0,2,1:T(8,128)S(1)} %bitcast.370, f32[32,16,5,384]{3,1,2,0:T(8,128)S(1)} %copy-done.16, f32[32,16,5,384]{3,0,2,1:T(8,128)} %bitcast.390, f32[32,16,5,384]{3,1,2,0:T(8,128)} %copy-done.21, f32[32,16,5,384]{3,0,2,1:T(8,128)} %bitcast.389, pred[16,5]{0,1:T(8,128)(4,1)S(1)} %copy-done.90), kind=kLoop, calls=%fused_computation.153 | loop fusion | flops 5898240 | bytes 21626960 | tf_op jit(solution)/shard_map/convert_element_type | solution.py:385
  480.5 12.5 %fusion.62 = f32[32,16,5,384]{3,1,2,0:T(8,128)S(1)} fusion(bf16[3,3,384,384]{3,2,1,0:T(8,128)(2,1)} %bitcast.426, bf16[32,2,7,1,384]{4,2,1,3,0:T(8,128)(2,1)S(1)} %get-tuple-element.179, bf16[32,2,7,1,384]{4,2,1,3,0:T(8,128)(2,1)S(1)} %get-tuple-element.178, bf16[32,2,8,5,384]{4,2,1,3,0:T(8,128)(2,1)S(1)} %bitcast.419), kind=kOutput, calls=%fused_computation.120 | convolution fusion | flops 6666977280 | bytes 9240576 | tf_op jit(solution)/shard_map/conv_general_dilated | solution.py:159
  499.4 5.4 collective-permute-start.28
  504.8 3.0 copy.309
  517.7 9.5 %fusion.40 = f32[3,3,384,384,1]{3,2,1,4,0:T(8,128)S(1)} fusion(bf16[32,16,5,384,1]{3,1,4,2,0:T(8,128)(2,1)S(1)} %bitcast.430, bf16[32,16,5,384,1]{3,1,4,2,0:T(8,128)(2,1)S(1)} %copy.298, bf16[32,16,5,384,1]{3,1,4,2,0:T(8,128)(2,1)S(1)} %bitcast.431, bf16[32,16,5,384]{3,1,2,0:T(8,128)(2,1)S(1)} %copy-done.36), kind=kOutput, calls=%fused_computation.52 | convolution fusion | flops 6670909440 | bytes 13172736 | tf_op jit(solution)/shard_map/conv_general_dilated | solution.py:167
  536.9 9.6 %fusion.46 = f32[3,3,384,384,1]{3,2,1,4,0:T(8,128)S(1)} fusion(bf16[32,16,5,384,1]{3,0,2,1,4:T(8,128)(2,1)S(1)} %bitcast.432, bf16[32,16,5,384,1]{3,1,2,0,4:T(8,128)(2,1)S(1)} %get-tuple-element.250, bf16[32,16,5,384,1]{3,1,2,0,4:T(8,128)(2,1)S(1)} %bitcast.384, bf16[32,16,5,384,1]{3,1,2,0,4:T(8,128)(2,1)S(1)} %get-tuple-element.249), kind=kOutput, calls=%fused_computation.58 | convolution fusion | flops 6659112960 | bytes 13172736 | tf_op jit(solution)/shard_map/conv_general_dilated | solution.py:167
  568.0 6.0 collective-permute-done.24
  588.2 12.8 %collective-permute-done.19 = bf16[2,2,216,384]{3,2,0,1:T(8,128)(2,1)S(1)} collective-permute-done((bf16[2,2,216,384]{3,2,0,1:T(8,128)(2,1)S(1)}, bf16[2,2,216,384]{3,2,0,1:T(8,128)(2,1)S(1)}, u32[]{:S(2)}, u32[]{:S(2)}) %collective-permute-start.19) | collective-permute-done | bytes 663584 | tf_op jit(solution)/shard_map/ppermute | solution.py:65
  602.7 9.2 %collective-permute-done.15 = bf16[2,2,216,384]{3,2,0,1:T(8,128)(2,1)S(1)} collective-permute-done((bf16[2,2,216,384]{3,2,0,1:T(8,128)(2,1)S(1)}, bf16[2,2,216,384]{3,2,0,1:T(8,128)(2,1)S(1)}, u32[]{:S(2)}, u32[]{:S(2)}) %collective-permute-start.15) | collective-permute-done | bytes 663584 | tf_op jit(solution)/shard_map/ppermute | solution.py:65
  615.0 4.4 collective-permute-done.16
  620.9 4.6 collective-permute-done.17
  627.8 5.8 collective-permute-done.22
  638.4 4.4 collective-permute-done.33
  643.5 3.5 collective-permute-done.34
  (629 shorter events, 307.5 us)
Async XLA Ops:
  7.3 15.3 %collective-permute-start.2 = (bf16[320,384]{1,0:T(8,128)(2,1)S(1)}, bf16[320,384]{1,0:T(8,128)(2,1)S(1)}, u32[]{:S(2)}, u32[]{:S(2)}) collective-permute-start(bf16[320,384]{1,0:T(8,128)(2,1)S(1)} %concatenate.53), channel_id=1, source_target_pairs={{0,16},{4,20},{8,24},{12,28},{16,0},{20,4},{24,8},{28,12},{1,17},{... | collective-permute-start | bytes 737288 | tf_op jit(solution)/shard_map/ppermute | solution.py:65
  22.7 12.5 %collective-permute-start.3 = (bf16[2,320,384]{2,1,0:T(8,128)(2,1)S(1)}, bf16[2,320,384]{2,1,0:T(8,128)(2,1)S(1)}, u32[]{:S(2)}, u32[]{:S(2)}) collective-permute-start(bf16[2,320,384]{2,1,0:T(8,128)(2,1)S(1)} %pad_maximum_fusion.8), channel_id=1, source_target_pairs={{0,8},{4,12},{8,0},{12,4},{16,24},{20,28},{24,16},{28,20},{1,9},{5... | collective-permute-start | bytes 1474568 | tf_op jit(solution)/shard_map/ppermute | solution.py:65
  35.4 22.2 %collective-permute-start.4 = (bf16[2,2,320,384]{3,2,1,0:T(8,128)(2,1)S(1)}, bf16[2,2,320,384]{3,2,1,0:T(8,128)(2,1)}, u32[]{:S(2)}, u32[]{:S(2)}) collective-permute-start(bf16[2,2,320,384]{3,2,1,0:T(8,128)(2,1)S(1)} %pad_maximum_fusion.7), channel_id=1, source_target_pairs={{0,4},{4,0},{8,12},{12,8},{16,20},{20,16},{24,28},{28,24},{1,5},{5... | collective-permute-start | bytes 2949128 | tf_op jit(solution)/shard_map/ppermute | solution.py:65
  60.6 46.1 %collective-permute-start.5 = (bf16[2,2,2,320,384]{4,3,2,1,0:T(8,128)(2,1)}, bf16[2,2,2,320,384]{4,3,2,1,0:T(8,128)(2,1)}, u32[]{:S(2)}, u32[]{:S(2)}) collective-permute-start(bf16[2,2,2,320,384]{4,3,2,1,0:T(8,128)(2,1)} %pad_maximum_fusion.5), channel_id=1, source_target_pairs={{0,2},{1,3},{2,0},{3,1},{4,6},{5,7},{6,4},{7,5},{8,10},{9,11},{10,... | collective-permute-start | bytes 5898248 | tf_op jit(solution)/shard_map/ppermute | solution.py:65
  63.1 69.4 %collective-permute-start = (bf16[1,4,8,32,384]{4,3,2,1,0:T(8,128)(2,1)S(1)}, bf16[1,4,8,32,384]{4,3,2,1,0:T(8,128)(2,1)}, u32[]{:S(2)}, u32[]{:S(2)}) collective-permute-start(bf16[1,4,8,32,384]{4,3,2,1,0:T(8,128)(2,1)S(1)} %dynamic-slice_bitcast_fusion.2), channel_id=1, source_target_pairs={{0,2},{1,3},{2,0},{3,1},{4,6},{5,7},{6,4},{7,5},{8,10},{9,11},{10,... | collective-permute-start | bytes 2359304 | tf_op jit(solution)/shard_map/ppermute | solution.py:65
  111.9 35.8 %collective-permute-start.6 = (bf16[2,2,2,2,320,384]{5,4,3,2,1,0:T(8,128)(2,1)}, bf16[2,2,2,2,320,384]{5,4,3,2,1,0:T(8,128)(2,1)}, u32[]{:S(2)}, u32[]{:S(2)}) collective-permute-start(bf16[2,2,2,2,320,384]{5,4,3,2,1,0:T(8,128)(2,1)} %pad_maximum_fusion.3), channel_id=1, source_target_pairs={{0,1},{1,0},{2,3},{3,2},{4,5},{5,4},{6,7},{7,6},{8,9},{9,8},{10,11... | collective-permute-start | bytes 11796488 | tf_op jit(solution)/shard_map/ppermute | solution.py:65
  112.7 18.4 %collective-permute-start.7 = (bf16[1,4,8,32,192]{4,3,2,1,0:T(8,128)(2,1)}, bf16[1,4,8,32,192]{4,3,2,1,0:T(8,128)(2,1)}, u32[]{:S(2)}, u32[]{:S(2)}) collective-permute-start(bf16[1,4,8,32,192]{4,3,2,1,0:T(8,128)(2,1)} %dynamic-slice_bitcast_fusion.3), channel_id=1, source_target_pairs={{0,2},{1,3},{2,0},{3,1},{4,6},{5,7},{6,4},{7,5},{8,10},{9,11},{10,... | collective-permute-start | bytes 1179656 | tf_op jit(solution)/shard_map/ppermute | solution.py:65
  132.4 4.2 collective-permute-start.8
  134.9 4.2 collective-permute-start.1
  145.0 100.8 %copy-start = (f32[2,4,8,32,384]{4,3,2,1,0:T(8,128)}, f32[2,4,8,32,384]{4,3,2,1,0:T(8,128)S(1)}, u32[]{:S(2)}) copy-start(f32[2,4,8,32,384]{4,3,2,1,0:T(8,128)S(1)} %copy.250) | copy-start | bytes 9437188
  499.4 51.5 %collective-permute-start.28 = (f32[384,6]{0,1:T(8,128)}, f32[384,6]{0,1:T(8,128)}, u32[]{:S(2)}, u32[]{:S(2)}) collective-permute-start(f32[384,6]{0,1:T(8,128)} %stack.210), channel_id=1, source_target_pairs={{0,16},{4,20},{8,24},{12,28},{16,0},{20,4},{24,8},{28,12},{1,17},{... | collective-permute-start | bytes 27656 | tf_op jit(solution)/shard_map/ppermute | solution.py:65
  514.3 49.3 %collective-permute-start.23 = (bf16[2,2,2,2,48,384]{5,4,3,2,1,0:T(8,128)(2,1)}, bf16[2,2,2,2,48,384]{5,4,3,2,1,0:T(8,128)(2,1)}, u32[]{:S(2)}, u32[]{:S(2)}) collective-permute-start(bf16[2,2,2,2,48,384]{5,4,3,2,1,0:T(8,128)(2,1)} %fusion.126), channel_id=1, source_target_pairs={{0,1},{1,0},{2,3},{3,2},{4,5},{5,4},{6,7},{7,6},{8,9},{9,8},{10,11... | collective-permute-start | bytes 1769480 | tf_op jit(solution)/shard_map/ppermute | solution.py:65
  528.6 52.0 %collective-permute-start.18 = (bf16[2,2,2,216,384]{4,3,0,1,2:T(8,128)(2,1)}, bf16[2,2,2,216,384]{4,3,0,1,2:T(8,128)(2,1)}, u32[]{:S(2)}, u32[]{:S(2)}) collective-permute-start(bf16[2,2,2,216,384]{4,3,0,1,2:T(8,128)(2,1)} %fusion.109), channel_id=1, source_target_pairs={{0,1},{1,0},{2,3},{3,2},{4,5},{5,4},{6,7},{7,6},{8,9},{9,8},{10,11... | collective-permute-start | bytes 3981320 | tf_op jit(solution)/shard_map/ppermute | solution.py:65
  533.1 13.4 %collective-permute-start.9 = (bf16[2,768]{1,0:T(2,128)(2,1)S(1)}, bf16[2,768]{1,0:T(2,128)(2,1)S(1)}, u32[]{:S(2)}, u32[]{:S(2)}) collective-permute-start(bf16[2,768]{1,0:T(2,128)(2,1)S(1)} %pad_maximum_fusion.16), channel_id=1, source_target_pairs={{0,16},{4,20},{8,24},{12,28},{16,0},{20,4},{24,8},{28,12},{1,17},{... | collective-permute-start | bytes 9224 | tf_op jit(solution)/shard_map/ppermute | solution.py:65
  546.6 6.3 collective-permute-start.10
  550.2 34.4 %collective-permute-start.14 = (bf16[2,2,2,216,384]{4,3,0,1,2:T(8,128)(2,1)}, bf16[2,2,2,216,384]{4,3,0,1,2:T(8,128)(2,1)}, u32[]{:S(2)}, u32[]{:S(2)}) collective-permute-start(bf16[2,2,2,216,384]{4,3,0,1,2:T(8,128)(2,1)} %fusion.108), channel_id=1, source_target_pairs={{0,1},{1,0},{2,3},{3,2},{4,5},{5,4},{6,7},{7,6},{8,9},{9,8},{10,11... | collective-permute-start | bytes 3981320 | tf_op jit(solution)/shard_map/ppermute | solution.py:65
  551.6 3.9 collective-permute-start.29
  552.9 4.0 collective-permute-start.11
  555.5 3.7 collective-permute-start.30
  557.0 5.9 collective-permute-start.12
  559.2 3.7 collective-permute-start.31
  562.9 4.3 collective-permute-start.32
  563.0 4.9 collective-permute-start.13
  565.0 9.1 %collective-permute-start.24 = (bf16[2,2,2,48,384]{4,3,2,1,0:T(8,128)(2,1)S(1)}, bf16[2,2,2,48,384]{4,3,2,1,0:T(8,128)(2,1)S(1)}, u32[]{:S(2)}, u32[]{:S(2)}) collective-permute-start(bf16[2,2,2,48,384]{4,3,2,1,0:T(8,128)(2,1)S(1)} %fusion.134), channel_id=1, source_target_pairs={{0,2},{1,3},{2,0},{3,1},{4,6},{5,7},{6,4},{7,5},{8,10},{9,11},{10,... | collective-permute-start | bytes 884744 | tf_op jit(solution)/shard_map/ppermute | solution.py:65
  574.1 5.2 collective-permute-start.25
  579.4 7.5 %collective-permute-start.26 = (bf16[2,48,384]{2,1,0:T(8,128)(2,1)S(1)}, bf16[2,48,384]{2,1,0:T(8,128)(2,1)S(1)}, u32[]{:S(2)}, u32[]{:S(2)}) collective-permute-start(bf16[2,48,384]{2,1,0:T(8,128)(2,1)S(1)} %fusion.144), channel_id=1, source_target_pairs={{0,8},{4,12},{8,0},{12,4},{16,24},{20,28},{24,16},{28,20},{1,9},{5... | collective-permute-start | bytes 221192 | tf_op jit(solution)/shard_map/ppermute | solution.py:65
  583.0 17.9 %collective-permute-start.19 = (bf16[2,2,216,384]{3,2,0,1:T(8,128)(2,1)S(1)}, bf16[2,2,216,384]{3,2,0,1:T(8,128)(2,1)S(1)}, u32[]{:S(2)}, u32[]{:S(2)}) collective-permute-start(bf16[2,2,216,384]{3,2,0,1:T(8,128)(2,1)S(1)} %fusion.125), channel_id=1, source_target_pairs={{0,2},{1,3},{2,0},{3,1},{4,6},{5,7},{6,4},{7,5},{8,10},{9,11},{10,... | collective-permute-start | bytes 1990664 | tf_op jit(solution)/shard_map/ppermute | solution.py:65
  586.4 25.6 %collective-permute-start.15 = (bf16[2,2,216,384]{3,2,0,1:T(8,128)(2,1)S(1)}, bf16[2,2,216,384]{3,2,0,1:T(8,128)(2,1)S(1)}, u32[]{:S(2)}, u32[]{:S(2)}) collective-permute-start(bf16[2,2,216,384]{3,2,0,1:T(8,128)(2,1)S(1)} %fusion.124), channel_id=1, source_target_pairs={{0,2},{1,3},{2,0},{3,1},{4,6},{5,7},{6,4},{7,5},{8,10},{9,11},{10,... | collective-permute-start | bytes 1990664 | tf_op jit(solution)/shard_map/ppermute | solution.py:65
  587.0 33.5 %collective-permute-start.27 = (bf16[48,384]{1,0:T(8,128)(2,1)S(1)}, bf16[48,384]{1,0:T(8,128)(2,1)S(1)}, u32[]{:S(2)}, u32[]{:S(2)}) collective-permute-start(bf16[48,384]{1,0:T(8,128)(2,1)S(1)} %fusion.147), channel_id=1, source_target_pairs={{0,16},{4,20},{8,24},{12,28},{16,0},{20,4},{24,8},{28,12},{1,17},{... | collective-permute-start | bytes 110600 | tf_op jit(solution)/shard_map/ppermute | solution.py:65
  601.2 12.5 %collective-permute-start.20 = (bf16[2,216,384]{2,1,0:T(8,128)(2,1)S(1)}, bf16[2,216,384]{2,1,0:T(8,128)(2,1)S(1)}, u32[]{:S(2)}, u32[]{:S(2)}) collective-permute-start(bf16[2,216,384]{2,1,0:T(8,128)(2,1)S(1)} %fusion.133), channel_id=1, source_target_pairs={{0,4},{4,0},{8,12},{12,8},{16,20},{20,16},{24,28},{28,24},{1,5},{5... | collective-permute-start | bytes 995336 | tf_op jit(solution)/shard_map/ppermute | solution.py:65
  612.2 7.2 %collective-permute-start.16 = (bf16[2,216,384]{2,1,0:T(8,128)(2,1)S(1)}, bf16[2,216,384]{2,1,0:T(8,128)(2,1)S(1)}, u32[]{:S(2)}, u32[]{:S(2)}) collective-permute-start(bf16[2,216,384]{2,1,0:T(8,128)(2,1)S(1)} %fusion.132), channel_id=1, source_target_pairs={{0,4},{4,0},{8,12},{12,8},{16,20},{20,16},{24,28},{28,24},{1,5},{5... | collective-permute-start | bytes 995336 | tf_op jit(solution)/shard_map/ppermute | solution.py:65
  613.8 46.5 %copy-start.82 = (f32[12,6]{0,1:T(8,128)S(1)}, f32[12,6]{0,1:T(8,128)}, u32[]{:S(2)}) copy-start(f32[12,6]{0,1:T(8,128)} %param.31) | copy-start | bytes 868
  613.8 46.5 %copy-start.91 = (f32[12,6]{0,1:T(8,128)S(1)}, f32[12,6]{0,1:T(8,128)}, u32[]{:S(2)}) copy-start(f32[12,6]{0,1:T(8,128)} %param.40) | copy-start | bytes 868
  613.9 46.5 %copy-start.92 = (f32[12,6]{0,1:T(8,128)S(1)}, f32[12,6]{0,1:T(8,128)}, u32[]{:S(2)}) copy-start(f32[12,6]{0,1:T(8,128)} %param.41) | copy-start | bytes 868
  613.9 47.1 %copy-start.59 = (f32[12,1152]{1,0:T(8,128)S(1)}, f32[12,1152]{1,0:T(8,128)}, u32[]{:S(2)}) copy-start(f32[12,1152]{1,0:T(8,128)} %param.29) | copy-start | bytes 165892
  613.9 47.1 %copy-start.63 = (f32[12,1152]{1,0:T(8,128)S(1)}, f32[12,1152]{1,0:T(8,128)}, u32[]{:S(2)}) copy-start(f32[12,1152]{1,0:T(8,128)} %param.36) | copy-start | bytes 165892
  613.9 47.1 %copy-start.64 = (f32[12,1152]{1,0:T(8,128)S(1)}, f32[12,1152]{1,0:T(8,128)}, u32[]{:S(2)}) copy-start(f32[12,1152]{1,0:T(8,128)} %param.37) | copy-start | bytes 165892
  613.9 47.8 %copy-start.50 = (f32[216,384]{1,0:T(8,128)S(1)}, f32[216,384]{1,0:T(8,128)}, u32[]{:S(2)}) copy-start(f32[216,384]{1,0:T(8,128)} %param.28) | copy-start | bytes 995332
  613.9 47.8 %copy-start.56 = (f32[216,384]{1,0:T(8,128)S(1)}, f32[216,384]{1,0:T(8,128)}, u32[]{:S(2)}) copy-start(f32[216,384]{1,0:T(8,128)} %param.34) | copy-start | bytes 995332
  613.9 47.8 %copy-start.57 = (f32[216,384]{1,0:T(8,128)S(1)}, f32[216,384]{1,0:T(8,128)}, u32[]{:S(2)}) copy-start(f32[216,384]{1,0:T(8,128)} %param.35) | copy-start | bytes 995332
  614.0 6.9 %collective-permute-start.21 = (bf16[216,384]{1,0:T(8,128)(2,1)S(1)}, bf16[216,384]{1,0:T(8,128)(2,1)S(1)}, u32[]{:S(2)}, u32[]{:S(2)}) collective-permute-start(bf16[216,384]{1,0:T(8,128)(2,1)S(1)} %fusion.139), channel_id=1, source_target_pairs={{0,8},{4,12},{8,0},{12,4},{16,24},{20,28},{24,16},{28,20},{1,9},{5... | collective-permute-start | bytes 497672 | tf_op jit(solution)/shard_map/ppermute | solution.py:65
  619.5 6.0 collective-permute-start.17
  625.6 8.1 %collective-permute-start.22 = (bf16[216,384]{1,0:T(8,128)(2,1)S(1)}, bf16[216,384]{1,0:T(8,128)(2,1)S(1)}, u32[]{:S(2)}, u32[]{:S(2)}) collective-permute-start(bf16[216,384]{1,0:T(8,128)(2,1)S(1)} %select_convert_fusion), channel_id=1, source_target_pairs={{0,16},{4,20},{8,24},{12,28},{16,0},{20,4},{24,8},{28,12},{1,17},{... | collective-permute-start | bytes 497672 | tf_op jit(solution)/shard_map/ppermute | solution.py:65
  638.3 4.4 collective-permute-start.33
  643.5 3.5 collective-permute-start.34
  647.8 4.0 collective-permute-start.35
  651.7 3.5 collective-permute-start.36
  655.3 1.1 collective-permute-start.37
  (91 other events, 850.3 us)

commit v2 on v1

v2 whole, which is shorter than its diff:
```python
import math

import jax
import jax.numpy as jnp
import numpy as np
from jax import lax
from jax.experimental import pallas as pl
from jax.experimental.pallas import tpu as pltpu
from jax.sharding import PartitionSpec as P

HEADS = 4
GROUPS = 32
STEP = 10
TSTEPS = 4000


EPS_NORM = 1e-05
VLB_WEIGHT = 0.001
BETA_ONE = 0.9
BETA_TWO = 0.999
ADAM_EPS = 1e-08
DECAY = 0.01
RATE_MATRIX = 0.05
RATE_GAIN = 0.4
THRESHOLD = 0.002
OFFSET = 0.008
LOG2E = math.log2(math.e)
VMEM_LIMIT = 56 << 20


def plan(step_ids):
    moment = step_ids.astype(jnp.float32)

    def angle(values):
        return (values / TSTEPS + OFFSET) / (1.0 + OFFSET) * (0.5 * math.pi)

    start = angle(jnp.zeros_like(moment))
    before = angle(moment - 1.0)
    later_angle = angle(moment)
    beta_now = jnp.sin(later_angle - before) * jnp.sin(later_angle + before) / jnp.cos(before) ** 2
    fade_now = jnp.sin(later_angle - start) * jnp.sin(later_angle + start) / jnp.cos(start) ** 2
    fade_prev = jnp.sin(before - start) * jnp.sin(before + start) / jnp.cos(start) ** 2
    log_beta = jnp.log(beta_now)
    log_tilde = jnp.log(beta_now * fade_prev / fade_now)
    factor = beta_now * beta_now / ((1.0 - beta_now) * fade_now)
    return (log_beta, log_tilde, factor)


def embed(step_ids, width):
    half_width = width // 2
    frequency = jnp.exp(-math.log(10000.0) * jnp.arange(half_width, dtype=jnp.float32) / half_width)
    phases = step_ids.astype(jnp.float32)[:, None] * frequency[None, :]
    return jnp.concatenate([jnp.cos(phases), jnp.sin(phases)], axis=1)


def bit_count(axis):
    size = lax.axis_size(axis)
    count = size.bit_length() - 1
    assert size == 1 << count
    return count


def flip(values, axis, bit):
    size = lax.axis_size(axis)
    return lax.ppermute(values, axis, [(i, i ^ (1 << bit)) for i in range(size)])


def my_bit(axis, bit):
    return (lax.axis_index(axis) >> bit) & 1


def all_bits():
    return [(axis, bit) for axis in ("dp", "head") for bit in reversed(range(bit_count(axis)))]


def paths():
    bits = all_bits()
    top, near = bits[0], ("head", 0)
    far = [("dp", bit) for bit in reversed(range(1, bit_count("dp") - 1))]
    across = [("head", bit) for bit in reversed(range(1, bit_count("head")))]
    side_bit = [("dp", 0)]
    return top, far + across + side_bit, side_bit + across + far[::-1], near


def pair_up(block, other, name, place):
    low = my_bit(*name) == 0
    return jnp.stack([jnp.where(low, block, other), jnp.where(low, other, block)], axis=place)


def gather_bits(block, order):
    rank = {name: place for place, name in enumerate(all_bits())}
    shape = block.shape
    held = []
    for name in order:
        place = sum(rank[have] < rank[name] for have in held)
        block = pair_up(block, flip(block, *name), name, place)
        held.append(name)
    return block.reshape((-1,) + shape)


def gather_two(block, cut):
    _, path_a, path_b, near = paths()
    halves = [gather_bits(block[:cut], path_a), gather_bits(block[cut:], path_b)]
    both = jnp.concatenate(halves, axis=1)
    both = pair_up(both, flip(both, *near), near, 1)
    return both.reshape((-1,) + both.shape[2:])


def scatter_bits(blocks, order):
    names = sorted(order, key=all_bits().index)
    total = blocks.reshape((2,) * len(names) + blocks.shape[1:])
    for name in order:
        place = names.index(name)
        bit = my_bit(*name)
        keep = lax.dynamic_index_in_dim(total, bit, place, keepdims=False)
        send = lax.dynamic_index_in_dim(total, 1 - bit, place, keepdims=False)
        got = flip(send.astype(jnp.bfloat16), *name)
        total = keep.astype(jnp.float32) + got.astype(jnp.float32)
        names.remove(name)
    return total


def scatter_two(blocks, cut):
    _, path_a, path_b, near = paths()
    halved = blocks.reshape((-1, 2) + blocks.shape[1:])
    bit = my_bit(*near)
    keep = lax.dynamic_index_in_dim(halved, bit, 1, keepdims=False)
    got = flip(lax.dynamic_index_in_dim(halved, 1 - bit, 1, keepdims=False), *near)
    total = keep.astype(jnp.float32) + got.astype(jnp.float32)
    first = scatter_bits(total[:, :cut], path_a[::-1])
    second = scatter_bits(total[:, cut:], path_b[::-1])
    return jnp.concatenate([first, second], axis=0)


def sum_bits(values, order):
    for name in order:
        values = values + flip(values, *name)
    return values


def strips_of(values):
    parts = lax.axis_size("head")
    count = values.shape[0] // parts
    mine = lax.axis_index("head")
    strips = []
    for far in range(parts):
        strip = lax.dynamic_slice_in_dim(values, (mine ^ far) * count, count, axis=0)
        if far:
            strip = lax.ppermute(strip, "head", [(i, i ^ far) for i in range(parts)])
        strips.append(strip)
    return strips


def join_strips(strips):
    mine = lax.axis_index("head")
    shape = strips[0].shape
    whole_shape = (shape[0], len(strips)) + shape[1:]
    joined = jnp.zeros(whole_shape, strips[0].dtype)
    for far, strip in enumerate(strips):
        joined = lax.dynamic_update_slice_in_dim(joined, strip[:, None], mine ^ far, axis=1)
    return joined.reshape((shape[0], len(strips) * shape[1]) + shape[2:])


NN = (((1,), (0,)), ((), ()))
NT = (((1,), (1,)), ((), ()))
TN = (((0,), (0,)), ((), ()))


def mm(left, right, form=NN):
    return lax.dot_general(left, right, form, preferred_element_type=jnp.float32)


def group_total(rows, member):
    high = rows.astype(jnp.bfloat16).astype(jnp.float32)
    rest = rows - high
    mid = rest.astype(jnp.bfloat16).astype(jnp.float32)
    parts = jnp.concatenate([high, mid, rest - mid, jnp.zeros_like(rows)], axis=0)
    sums = mm(parts.astype(jnp.bfloat16), member)
    return sums[0:8] + sums[8:16] + sums[16:24]


def fold(values):
    rows, width = values.shape
    return jnp.sum(values.reshape(rows // 8, 8, width), axis=0)


def two_rows(first, second):
    first = jnp.sum(first, axis=0, keepdims=True)
    second = jnp.sum(second, axis=0, keepdims=True)
    row = lax.broadcasted_iota(jnp.int32, (8, first.shape[1]), 0)
    return jnp.where(row == 0, first, jnp.where(row == 1, second, 0.0))


def chunks(total, size, step, init):
    return lax.fori_loop(0, total // size, lambda m, c: step(pl.multiple_of(m * size, size), c), init)


def norm_sums(load, pixels, channels, member):
    def step(at, carry):
        values = load(at)
        return (carry[0] + fold(values), carry[1] + fold(values * values))

    zero = jnp.zeros((8, channels), jnp.float32)
    first, second = chunks(pixels, CHUNK, step, (zero, zero))
    count = pixels * (channels // GROUPS)
    sums = group_total(two_rows(first, second), member) / count
    mean = sums[0:1]
    inverse = lax.rsqrt(sums[1:2] - mean * mean + EPS_NORM)
    return mean, inverse


CHUNK = 128


def attention_kernel(
    scalars,
    middle,
    noise,
    gains,
    member,
    qkv_w,
    out_w,
    down_out,
    qkv_grad,
    out_grad,
    sums_out,
    loss_out,
    qkv_wt,
    normed,
    qkv_t,
    probs,
    totals,
    mixed_t,
    attn_t,
    result,
    grad_b,
    back_t,
    dqkv_t,
    gn_t,
    qkv_acc,
    out_acc,
):
    sample = pl.program_id(0)
    _, pixels, channels = middle.shape
    half = channels // 2
    size = channels // HEADS
    factor = size ** (-0.5)
    width = int(round(pixels**0.5))

    @pl.when(sample == 0)
    def _():
        qkv_wt[...] = qkv_w[...].T
        qkv_acc[...] = jnp.zeros_like(qkv_acc)
        out_acc[...] = jnp.zeros_like(out_acc)

    load = lambda at: middle[0, pl.ds(at, CHUNK), :]
    mean, inverse = norm_sums(load, pixels, channels, member[...])
    gain, shift = gains[4:5], gains[5:6]

    def normalize(at, carry):
        hat = (load(at) - mean) * inverse
        normed[pl.ds(at, CHUNK), :] = (hat * gain + shift).astype(jnp.bfloat16)
        return carry

    chunks(pixels, CHUNK, normalize, 0)

    block = 256

    def attend(head, carry):
        base = pl.multiple_of(head * 3 * size, 32)
        qkv_t[pl.ds(base, 3 * size), :] = mm(
            qkv_wt[pl.ds(base, 3 * size), :], normed[...], NT
        ).astype(jnp.bfloat16)
        keys = qkv_t[pl.ds(base + size, size), :].T
        values_t = qkv_t[pl.ds(base + 2 * size, size), :]
        for q in range(0, pixels, block):
            queries_t = qkv_t[pl.ds(base, size), q : q + block]
            scores = mm(keys, queries_t) * (factor * LOG2E)
            top = jnp.max(scores, axis=0, keepdims=True)
            powers = jnp.exp2(scores - top)
            inv = 1.0 / jnp.sum(powers, axis=0, keepdims=True)
            powers_b = powers.astype(jnp.bfloat16)
            probs[head, :, q : q + block] = powers_b
            totals[head, :, q : q + block] = jnp.broadcast_to(inv, (8, block))
            mixed = mm(values_t, powers_b) * inv
            at = pl.multiple_of(head * size, 32)
            mixed_t[pl.ds(at, size), q : q + block] = mixed
            attn_t[pl.ds(at, size), q : q + block] = mixed.astype(jnp.bfloat16)
        return carry

    lax.fori_loop(0, HEADS, attend, 0)

    result[...] = mm(attn_t[...].T, out_w[...])
    beta_log, tilde_log, coef = scalars[sample, 0], scalars[sample, 1], scalars[sample, 2]
    divisor, high, wide = scalars[sample, 3], scalars[sample, 4], scalars[sample, 5]

    def losses(at, carry):
        total = load(at) + result[pl.ds(at, CHUNK), :]
        pixel = at + lax.broadcasted_iota(jnp.int32, (CHUNK, half), 0)
        row = (pixel // width).astype(jnp.float32)
        col = (pixel % width).astype(jnp.float32)
        valid = jnp.where((row >= width - high) & (col < wide), 1.0, 0.0)
        residue = total[:, :half] - noise[0, pl.ds(at, CHUNK), :].astype(jnp.float32)
        weight = jax.nn.sigmoid(total[:, half:])
        blended = weight * beta_log + (1.0 - weight) * tilde_log
        spread = jnp.exp(tilde_log - blended)
        damped = coef * residue * residue * jnp.exp(-blended)
        diverge = 0.5 * (-1.0 + blended - tilde_log + spread + damped)
        pixel_loss = valid * (residue * residue + VLB_WEIGHT * diverge)
        scale = valid / (half * divisor)
        grad_guess = 2.0 * residue * scale
        grad_raw = (
            scale * (0.5 * VLB_WEIGHT) * (1.0 - spread - damped)
            * (beta_log - tilde_log) * weight * (1.0 - weight)
        )
        grad = jnp.concatenate([grad_guess, grad_raw], axis=-1)
        result[pl.ds(at, CHUNK), :] = grad
        grad_b[pl.ds(at, CHUNK), :] = grad.astype(jnp.bfloat16)
        return carry + fold(pixel_loss)

    loss = chunks(pixels, CHUNK, losses, jnp.zeros((8, half), jnp.float32))
    loss_out[0] = loss * (1.0 / half)

    out_acc[...] += mm(attn_t[...], grad_b[...])
    back_t[...] = mm(out_w[...], grad_b[...], NT).astype(jnp.bfloat16)

    def attend_back(head, carry):
        base = pl.multiple_of(head * 3 * size, 32)
        at = pl.multiple_of(head * size, 32)
        keys_t = qkv_t[pl.ds(base + size, size), :]
        values = qkv_t[pl.ds(base + 2 * size, size), :].T
        grad_key = jnp.zeros((size, pixels), jnp.float32)
        grad_value = jnp.zeros((size, pixels), jnp.float32)
        for q in range(0, pixels, block):
            queries_t = qkv_t[pl.ds(base, size), q : q + block]
            upstream = back_t[pl.ds(at, size), q : q + block]
            inner = jnp.sum(
                upstream.astype(jnp.float32) * mixed_t[pl.ds(at, size), q : q + block],
                axis=0,
                keepdims=True,
            )
            soft = probs[head, :, q : q + block].astype(jnp.float32) * totals[head, 0:1, q : q + block]
            grad_soft = mm(values, upstream)
            grad_scores = (soft * (grad_soft - inner)).astype(jnp.bfloat16)
            dqkv_t[pl.ds(base, size), q : q + block] = (mm(keys_t, grad_scores) * factor).astype(jnp.bfloat16)
            grad_key += mm(queries_t, grad_scores, NT)
            grad_value += mm(upstream, soft.astype(jnp.bfloat16), NT)
        dqkv_t[pl.ds(base + size, size), :] = (grad_key * factor).astype(jnp.bfloat16)
        dqkv_t[pl.ds(base + 2 * size, size), :] = grad_value.astype(jnp.bfloat16)
        return carry

    lax.fori_loop(0, HEADS, attend_back, 0)

    qkv_acc[...] += mm(normed[...].T, dqkv_t[...], NT)
    gn_t[...] = mm(qkv_w[...], dqkv_t[...])

    def back_sums(at, carry):
        hat = (load(at) - mean) * inverse
        grad = gn_t[:, pl.ds(at, CHUNK)].T
        return (carry[0] + fold(grad * hat), carry[1] + fold(grad))

    zero = jnp.zeros((8, channels), jnp.float32)
    both = chunks(pixels, CHUNK, back_sums, (zero, zero))
    rows = two_rows(*both)
    sums_out[0] = rows
    means = group_total(rows * gain, member[...]) / (pixels * (channels // GROUPS))

    def back_norm(at, carry):
        hat = (load(at) - mean) * inverse
        grad = gn_t[:, pl.ds(at, CHUNK)].T * gain
        back = (grad - means[1:2] - hat * means[0:1]) * inverse
        down_out[0, pl.ds(at, CHUNK), :] = (result[pl.ds(at, CHUNK), :] + back).astype(jnp.bfloat16)
        return carry

    chunks(pixels, CHUNK, back_norm, 0)

    @pl.when(sample == pl.num_programs(0) - 1)
    def _():
        qkv_grad[...] = qkv_acc[...].astype(jnp.bfloat16)
        out_grad[...] = out_acc[...].astype(jnp.bfloat16)


def attention_block(scalars, middle, noise, gains, member, qkv_w, out_w):
    samples, pixels, channels = middle.shape
    half = channels // 2
    bf, f32 = jnp.bfloat16, jnp.float32
    whole = lambda *shape: pl.BlockSpec(shape, lambda s: (0,) * len(shape))
    each = lambda *shape: pl.BlockSpec((1,) + shape, lambda s: (s, 0, 0))
    return pl.pallas_call(
        attention_kernel,
        grid=(samples,),
        in_specs=[
            pl.BlockSpec(memory_space=pltpu.SMEM),
            each(pixels, channels),
            each(pixels, half),
            whole(8, channels),
            whole(channels, channels),
            whole(channels, 3 * channels),
            whole(channels, channels),
        ],
        out_specs=[
            each(pixels, channels),
            whole(channels, 3 * channels),
            whole(channels, channels),
            each(8, channels),
            each(8, half),
        ],
        out_shape=[
            jax.ShapeDtypeStruct((samples, pixels, channels), bf),
            jax.ShapeDtypeStruct((channels, 3 * channels), bf),
            jax.ShapeDtypeStruct((channels, channels), bf),
            jax.ShapeDtypeStruct((samples, 8, channels), f32),
            jax.ShapeDtypeStruct((samples, 8, half), f32),
        ],
        scratch_shapes=[
            pltpu.VMEM((3 * channels, channels), bf),
            pltpu.VMEM((pixels, channels), bf),
            pltpu.VMEM((3 * channels, pixels), bf),
            pltpu.VMEM((HEADS, pixels, pixels), bf),
            pltpu.VMEM((HEADS, 8, pixels), f32),
            pltpu.VMEM((channels, pixels), f32),
            pltpu.VMEM((channels, pixels), bf),
            pltpu.VMEM((pixels, channels), f32),
            pltpu.VMEM((pixels, channels), bf),
            pltpu.VMEM((channels, pixels), bf),
            pltpu.VMEM((3 * channels, pixels), bf),
            pltpu.VMEM((channels, pixels), f32),
            pltpu.VMEM((channels, 3 * channels), f32),
            pltpu.VMEM((channels, channels), f32),
        ],
        compiler_params=pltpu.CompilerParams(vmem_limit_bytes=VMEM_LIMIT),
        cost_estimate=pl.CostEstimate(
            flops=30 * samples * pixels * pixels * channels,
            bytes_accessed=8 * samples * pixels * channels,
            transcendentals=samples * HEADS * pixels * pixels,
        ),
    )(scalars, middle, noise, gains, member, qkv_w, out_w)


def fill(padded, at, values, width):
    rows, channels = values.shape
    col = lax.broadcasted_iota(jnp.int32, values.shape, 0) % width
    there = pl.ds(at + width, rows)
    left = jnp.where(col == 0, 0.0, pltpu.roll(values, 1, 0))
    right = jnp.where(col == width - 1, 0.0, pltpu.roll(values, rows - 1, 0))
    padded[there, 0:channels] = left.astype(jnp.bfloat16)
    padded[there, channels : 2 * channels] = values.astype(jnp.bfloat16)
    padded[there, 2 * channels :] = right.astype(jnp.bfloat16)


def clear_edges(padded, width):
    rows, wide = padded.shape
    padded[0:width, :] = jnp.zeros((width, wide), jnp.bfloat16)
    padded[rows - width :, :] = jnp.zeros((width, wide), jnp.bfloat16)


def side(pixels):
    return int(round(pixels**0.5))


def taps_product(padded, weight, pixels, width):
    wide = padded.shape[1]
    total = mm(padded[0:pixels, :], weight(0))
    for i in (1, 2):
        total += mm(padded[i * width : i * width + pixels, :], weight(i))
    return total


def rows_of(*rows):
    index = lax.broadcasted_iota(jnp.int32, (8, rows[0].shape[1]), 0)
    total = jnp.zeros(index.shape, jnp.float32)
    for place, row in enumerate(rows):
        total = jnp.where(index == place, row, total)
    return total


def first_kernel(images, gains, member, weight, inner, hidden, stats, padded):
    _, pixels, channels = images.shape
    width = side(pixels)
    wide = 3 * channels
    load = lambda at: images[0, pl.ds(at, CHUNK), :].astype(jnp.float32)
    mean, inverse = norm_sums(load, pixels, channels, member[...])
    gain, shift = gains[0:1], gains[1:2]
    clear_edges(padded, width)

    def activate(at, carry):
        out = (load(at) - mean) * inverse * gain + shift
        value = out * jax.nn.sigmoid(out)
        hidden[0, pl.ds(at, CHUNK), :] = value.astype(jnp.bfloat16)
        fill(padded, at, value, width)
        return carry

    chunks(pixels, CHUNK, activate, 0)
    inner[0] = taps_product(padded, lambda i: weight[i * wide : (i + 1) * wide, :], pixels, width)
    mean_two, inverse_two = norm_sums(
        lambda at: inner[0, pl.ds(at, CHUNK), :], pixels, channels, member[...]
    )
    stats[0] = rows_of(mean, inverse, mean_two, inverse_two)


def second_kernel(inner, images, stats, film, gains, weight, middle, hidden, padded):
    _, pixels, channels = inner.shape
    width = side(pixels)
    wide = 3 * channels
    mean, inverse = stats[0, 2:3], stats[0, 3:4]
    scale, lift = 1.0 + film[0, 0:1], film[0, 1:2]
    gain, shift = gains[2:3], gains[3:4]
    clear_edges(padded, width)

    def activate(at, carry):
        out = (inner[0, pl.ds(at, CHUNK), :] - mean) * inverse * gain + shift
        lifted = out * scale + lift
        value = lifted * jax.nn.sigmoid(lifted)
        hidden[0, pl.ds(at, CHUNK), :] = value.astype(jnp.bfloat16)
        fill(padded, at, value, width)
        return carry

    chunks(pixels, CHUNK, activate, 0)
    middle[0] = images[0].astype(jnp.float32) + taps_product(
        padded, lambda i: weight[i * wide : (i + 1) * wide, :], pixels, width
    )


def weights_kernel(hidden, grad, out, padded, total):
    sample = pl.program_id(0)
    _, pixels, channels = hidden.shape
    width = side(pixels)
    wide = 3 * channels
    clear_edges(padded, width)

    def spread(at, carry):
        fill(padded, at, hidden[0, pl.ds(at, CHUNK), :].astype(jnp.float32), width)
        return carry

    chunks(pixels, CHUNK, spread, 0)

    @pl.when(sample == 0)
    def _():
        total[...] = jnp.zeros_like(total)

    for i in range(3):
        total[i * wide : (i + 1) * wide, :] += mm(
            padded[i * width : i * width + pixels, :], grad[0], TN
        )

    @pl.when(sample == pl.num_programs(0) - 1)
    def _():
        out[...] = total[...].astype(jnp.bfloat16)


def turn_taps(weight, turned):
    channels = weight.shape[1]
    for i in range(3):
        for j in range(3):
            tap = 3 * (2 - i) + 2 - j
            turned[i, :, j * channels : (j + 1) * channels] = weight[
                tap * channels : (tap + 1) * channels, :
            ]


def input_grad(grad, weight, padded, turned, down):
    _, pixels, channels = grad.shape
    width = side(pixels)

    @pl.when(pl.program_id(0) == 0)
    def _():
        turn_taps(weight, turned)

    clear_edges(padded, width)

    def spread(at, carry):
        fill(padded, at, grad[0, pl.ds(at, CHUNK), :].astype(jnp.float32), width)
        return carry

    chunks(pixels, CHUNK, spread, 0)
    total = mm(padded[0:pixels, :], turned[0], NT)
    for i in (1, 2):
        total += mm(padded[i * width : i * width + pixels, :], turned[i], NT)
    down[...] = total


def slope_of(values):
    sig = jax.nn.sigmoid(values)
    return sig * (1.0 + values * (1.0 - sig))


def second_back_kernel(
    grad, inner, stats, film, gains, member, weight, grad_out, sums_out, padded, turned, down
):
    _, pixels, channels = grad.shape
    input_grad(grad, weight, padded, turned, down)
    mean, inverse = stats[0, 2:3], stats[0, 3:4]
    scale, lift = 1.0 + film[0, 0:1], film[0, 1:2]
    gain, shift = gains[2:3], gains[3:4]

    def slopes(at, carry):
        hat = (inner[0, pl.ds(at, CHUNK), :] - mean) * inverse
        lifted = (hat * gain + shift) * scale + lift
        lifted_grad = down[pl.ds(at, CHUNK), :] * slope_of(lifted)
        down[pl.ds(at, CHUNK), :] = lifted_grad
        return (carry[0] + fold(lifted_grad * hat), carry[1] + fold(lifted_grad))

    zero = jnp.zeros((8, channels), jnp.float32)
    rows = two_rows(*chunks(pixels, CHUNK, slopes, (zero, zero)))
    sums_out[0] = rows
    factor = scale * gain
    means = group_total(rows * factor, member[...]) / (pixels * (channels // GROUPS))

    def back_norm(at, carry):
        hat = (inner[0, pl.ds(at, CHUNK), :] - mean) * inverse
        back = (down[pl.ds(at, CHUNK), :] * factor - means[1:2] - hat * means[0:1]) * inverse
        grad_out[0, pl.ds(at, CHUNK), :] = back.astype(jnp.bfloat16)
        return carry

    chunks(pixels, CHUNK, back_norm, 0)


def first_back_kernel(grad, images, stats, gains, weight, sums_out, padded, turned, down):
    _, pixels, channels = grad.shape
    input_grad(grad, weight, padded, turned, down)
    mean, inverse = stats[0, 0:1], stats[0, 1:2]
    gain, shift = gains[0:1], gains[1:2]

    def slopes(at, carry):
        hat = (images[0, pl.ds(at, CHUNK), :].astype(jnp.float32) - mean) * inverse
        grad_first = down[pl.ds(at, CHUNK), :] * slope_of(hat * gain + shift)
        return (carry[0] + fold(grad_first * hat), carry[1] + fold(grad_first))

    zero = jnp.zeros((8, channels), jnp.float32)
    sums_out[0] = two_rows(*chunks(pixels, CHUNK, slopes, (zero, zero)))


def whole(*shape):
    return pl.BlockSpec(shape, lambda s: (0,) * len(shape))


def each(*shape):
    return pl.BlockSpec((1,) + shape, lambda s: (s,) + (0,) * len(shape))


def per_sample(kernel, samples, in_specs, outs, scratch, flops, *operands):
    return pl.pallas_call(
        kernel,
        grid=(samples,),
        in_specs=in_specs,
        out_specs=[spec for spec, _ in outs],
        out_shape=[shape for _, shape in outs],
        scratch_shapes=scratch,
        compiler_params=pltpu.CompilerParams(vmem_limit_bytes=VMEM_LIMIT),
        cost_estimate=pl.CostEstimate(flops=flops, bytes_accessed=flops // 1000, transcendentals=0),
    )(*operands)


def sized(dtype, *shape):
    return jax.ShapeDtypeStruct(shape, dtype)


def block_calls(samples, pixels, channels):
    width = side(pixels)
    act = each(pixels, channels)
    few = each(8, channels)
    gain_spec, member_spec = whole(8, channels), whole(channels, channels)
    weight_spec = whole(9 * channels, channels)
    bf, f32 = jnp.bfloat16, jnp.float32
    padded = pltpu.VMEM((pixels + 2 * width, 3 * channels), bf)
    turned = pltpu.VMEM((3, channels, 3 * channels), bf)
    down = pltpu.VMEM((pixels, channels), f32)
    act_b = sized(bf, samples, pixels, channels)
    act_f = sized(f32, samples, pixels, channels)
    few_f = sized(f32, samples, 8, channels)
    flops = 18 * samples * pixels * channels * channels

    def first(images, gains, member, weight):
        return per_sample(
            first_kernel, samples, [act, gain_spec, member_spec, weight_spec],
            [(act, act_f), (act, act_b), (few, few_f)], [padded], flops,
            images, gains, member, weight,
        )

    def second(inner, images, stats, film, gains, weight):
        return per_sample(
            second_kernel, samples, [act, act, few, few, gain_spec, weight_spec],
            [(act, act_f), (act, act_b)], [padded], flops,
            inner, images, stats, film, gains, weight,
        )

    def weights(hidden, grad):
        return per_sample(
            weights_kernel, samples, [act, act],
            [(weight_spec, sized(bf, 9 * channels, channels))],
            [padded, pltpu.VMEM((9 * channels, channels), f32)], flops, hidden, grad,
        )[0]

    def second_back(grad, inner, stats, film, gains, member, weight):
        return per_sample(
            second_back_kernel, samples,
            [act, act, few, few, gain_spec, member_spec, weight_spec],
            [(act, act_b), (few, few_f)], [padded, turned, down], flops,
            grad, inner, stats, film, gains, member, weight,
        )

    def first_back(grad, images, stats, gains, weight):
        return per_sample(
            first_back_kernel, samples, [act, act, few, gain_spec, weight_spec],
            [(few, few_f)], [padded, turned, down], flops,
            grad, images, stats, gains, weight,
        )[0]

    return first, second, weights, second_back, first_back


def adamw(master, gradient, first, second, step_rate, decay_rate, clip_factor):
    gradient = gradient * clip_factor
    first_new = BETA_ONE * first + (1.0 - BETA_ONE) * gradient
    second_new = BETA_TWO * second + (1.0 - BETA_TWO) * gradient * gradient
    ratio = (
        first_new
        / (1.0 - BETA_ONE**STEP)
        / (jnp.sqrt(second_new / (1.0 - BETA_TWO**STEP)) + ADAM_EPS)
    )
    return (master - step_rate * (ratio + decay_rate * master), first_new, second_new)


def body(
    images,
    noise,
    timesteps,
    extents,
    film_master,
    conv_master,
    qkv_master,
    out_master,
    gains,
    film_first,
    film_second,
    conv_first,
    conv_second,
    qkv_first,
    qkv_second,
    out_first,
    out_second,
    gain_first,
    gain_second,
):
    devices = lax.axis_size("dp") * lax.axis_size("head")
    device = lax.axis_index("dp") * lax.axis_size("head") + lax.axis_index("head")
    bits = all_bits()
    channels = images.shape[-1]
    wide = film_master.shape[1]
    half_width = channels // 2
    conv_rows = conv_master.shape[0]
    film_rows = film_master.shape[0]
    out_rows = out_master.shape[0]

    local_samples = timesteps.shape[0]
    small = jnp.concatenate(
        [
            gains.reshape(-1),
            extents.astype(jnp.float32).reshape(-1),
            (timesteps // 64).astype(jnp.float32),
            (timesteps % 64).astype(jnp.float32),
        ]
    )
    small = jnp.pad(small, (0, 8 * channels - small.shape[0])).reshape(8, channels)
    top, _, _, _ = paths()
    is_top = my_bit(*top) == 1
    ours = jnp.concatenate([conv_master, small]).astype(jnp.bfloat16)
    theirs = flip(ours, *top)
    rest = jnp.concatenate(
        [film_master.reshape(-1, channels), qkv_master.reshape(-1, channels), out_master]
    ).astype(jnp.bfloat16)
    rest_two = pair_up(rest, flip(rest, *top), top, 0)
    one = jnp.where(is_top, theirs, ours)
    two = jnp.where(is_top, ours, theirs)
    small_two = jnp.stack([one[conv_rows:], two[conv_rows:]]).reshape(-1, channels)
    cut = conv_rows // 16 * 8
    group_one = gather_two(jnp.concatenate([one[:conv_rows], small_two]), cut)
    strips = strips_of(images)
    held_rows = rest.shape[0]
    group_two = gather_two(
        jnp.concatenate([two[:conv_rows], rest_two.reshape(-1, channels)]),
        (conv_rows + 2 * held_rows) // 16 * 8,
    )
    taps_one = group_one[:, :conv_rows].reshape(-1, channels)
    taps_two = group_two[:, :conv_rows].reshape(-1, channels)
    smalls = jnp.moveaxis(group_one[:, conv_rows:].reshape(-1, 2, 8 * channels), 0, 1)
    others = jnp.moveaxis(group_two[:, conv_rows:].reshape(-1, 2, held_rows, channels), 0, 1)
    others = others.reshape(devices, held_rows, channels)
    film_own_rows = film_rows * wide // channels
    film_w = others[:, :film_own_rows].reshape(-1, wide)
    qkv_w = others[:, film_own_rows : film_own_rows + 3 * out_rows].reshape(channels, 3 * channels)
    out_w = others[:, film_own_rows + 3 * out_rows :].reshape(channels, channels)
    smalls = smalls.reshape(devices, -1).astype(jnp.float32)
    gain_f = smalls[:, : gains.size].reshape(channels, 6)
    dp_smalls = smalls.reshape(lax.axis_size("dp"), lax.axis_size("head"), -1)[:, 0, gains.size :]
    extents_all = dp_smalls[:, : 2 * local_samples].reshape(-1, 2)
    times = dp_smalls[:, 2 * local_samples : 4 * local_samples].reshape(-1, 2, local_samples)
    times_all = (times[:, 0] * 64.0 + times[:, 1]).reshape(-1).astype(jnp.int32)
    divisor = jnp.sum(extents_all[:, 0] * extents_all[:, 1])

    pictures = join_strips(strips)
    target = join_strips(strips_of(noise))
    samples, rows, width_px, _ = pictures.shape
    pixels = rows * width_px
    first = lax.axis_index("head") * samples
    own_times = lax.dynamic_slice_in_dim(timesteps, first, samples)
    own_extents = lax.dynamic_slice_in_dim(extents, first, samples)

    log_beta, log_tilde, factor = plan(own_times)
    embedded_all = jax.nn.silu(embed(times_all, wide)).astype(jnp.bfloat16)
    embedded = jax.nn.silu(embed(own_times, wide)).astype(jnp.bfloat16)
    film_out = lax.dot_general(
        embedded, film_w, (((1,), (1,)), ((), ())), preferred_element_type=jnp.float32
    )
    film = jnp.pad(film_out.reshape(samples, 2, channels), ((0, 0), (0, 6), (0, 0)))
    scale = 1.0 + film_out[:, :channels]
    source = pictures.reshape(samples, pixels, channels)
    gains_t = jnp.pad(gain_f.T, ((0, 2), (0, 0)))
    member = jnp.asarray(np.kron(np.eye(GROUPS), np.ones((channels // GROUPS,) * 2)), jnp.bfloat16)
    scalars = jnp.stack(
        [log_beta, log_tilde, factor, jnp.broadcast_to(divisor, factor.shape)]
        + [own_extents[:, 0].astype(jnp.float32), own_extents[:, 1].astype(jnp.float32)],
        axis=1,
    )
    first_call, second_call, weights, second_back, first_back = block_calls(samples, pixels, channels)
    inner, hidden_one, stats = first_call(source, gains_t, member, taps_one)
    middle, hidden_two = second_call(inner, source, stats, film, gains_t, taps_two)
    grad_two_b, qkv_grad, out_grad, sums_three, losses = attention_block(
        scalars, middle, target.reshape(samples, pixels, half_width), gains_t, member, qkv_w, out_w
    )
    loss_local = jnp.sum(losses)
    conv_two_grad = weights(hidden_two, grad_two_b)
    grad_one_b, sums_two = second_back(grad_two_b, inner, stats, film, gains_t, member, taps_two)
    conv_one_grad = weights(hidden_one, grad_one_b)
    sums_one = first_back(grad_one_b, source, stats, gains_t, taps_one)
    gain_one, bias_one = jnp.sum(sums_one[:, 0], axis=0), jnp.sum(sums_one[:, 1], axis=0)
    gain_two, bias_two = jnp.sum(sums_two[:, 0] * scale, axis=0), jnp.sum(sums_two[:, 1] * scale, axis=0)
    gain_three, bias_three = jnp.sum(sums_three[:, 0], axis=0), jnp.sum(sums_three[:, 1], axis=0)
    grad_scale = sums_two[:, 0] * gains_t[2] + sums_two[:, 1] * gains_t[3]
    film_grad_b = jnp.concatenate([grad_scale, sums_two[:, 1]], axis=1).astype(jnp.bfloat16)

    both_grads = jnp.concatenate(
        [qkv_grad.reshape(2, -1, 3 * out_rows, channels), out_grad.reshape(2, -1, out_rows, channels)],
        axis=2,
    )
    both_grads = jnp.moveaxis(both_grads, 0, 1).reshape(devices // 2, 8 * out_rows, channels)
    two_grads = jnp.concatenate(
        [conv_two_grad.reshape(-1, conv_rows, channels), both_grads], axis=1
    )
    share_two = scatter_two(two_grads, (conv_rows + 8 * out_rows) // 16 * 8)
    share_one = scatter_two(conv_one_grad.reshape(-1, conv_rows, channels), cut)
    small_shares = share_two[conv_rows:].reshape(2, 4 * out_rows, channels)
    mine = jnp.concatenate(
        [
            jnp.where(is_top, share_two[:conv_rows], share_one),
            jnp.where(is_top, small_shares[1], small_shares[0]),
        ]
    )
    sent = jnp.concatenate(
        [
            jnp.where(is_top, share_one, share_two[:conv_rows]),
            jnp.where(is_top, small_shares[0], small_shares[1]),
        ]
    )
    summed = mine + flip(sent.astype(jnp.bfloat16), *top).astype(jnp.float32)
    conv_g = summed[:conv_rows]
    qkv_g = summed[conv_rows : conv_rows + 3 * out_rows].reshape(qkv_master.shape)
    out_g = summed[conv_rows + 3 * out_rows :]

    film_all = gather_bits(film_grad_b, bits).reshape(-1, film_grad_b.shape[1])
    film_own = lax.dynamic_slice_in_dim(film_all, device * film_rows, film_rows, axis=1)
    film_g = jnp.einsum("sf,se->fe", film_own, embedded_all, preferred_element_type=jnp.float32)
    gain_grad = jnp.stack([gain_one, bias_one, gain_two, bias_two, gain_three, bias_three], axis=1)
    gain_g = sum_bits(gain_grad, bits).reshape(devices, -1, 6)
    gain_g = lax.dynamic_index_in_dim(gain_g, device, 0, keepdims=False)
    reduced = (film_g, conv_g, qkv_g, out_g, gain_g)
    squares = jnp.zeros((), jnp.float32)
    for gradient in reduced:
        squares = squares + jnp.sum(gradient * gradient)
    totals = sum_bits(jnp.stack([squares, loss_local]), bits)
    grad_norm = jnp.sqrt(totals[0])
    clip_factor = jnp.minimum(1.0, THRESHOLD / (grad_norm + 1e-06))
    film_res = adamw(film_master, film_g, film_first, film_second, RATE_MATRIX, DECAY, clip_factor)
    conv_res = adamw(conv_master, conv_g, conv_first, conv_second, RATE_MATRIX, DECAY, clip_factor)
    qkv_res = adamw(qkv_master, qkv_g, qkv_first, qkv_second, RATE_MATRIX, DECAY, clip_factor)
    out_res = adamw(out_master, out_g, out_first, out_second, RATE_MATRIX, DECAY, clip_factor)
    gain_res = adamw(gains, gain_g, gain_first, gain_second, RATE_GAIN, 0.0, clip_factor)
    loss_parts = jnp.stack([totals[1], divisor])
    return (
        loss_parts,
        grad_norm,
        film_res[0],
        film_res[1],
        film_res[2],
        conv_res[0],
        conv_res[1],
        conv_res[2],
        qkv_res[0],
        qkv_res[1],
        qkv_res[2],
        out_res[0],
        out_res[1],
        out_res[2],
        gain_res[0],
        gain_res[1],
        gain_res[2],
    )


def solution(mesh):
    in_specs = (
        P("dp", "head", None, None),
        P("dp", "head", None, None),
        P("dp"),
        P("dp", None),
        P(("dp", "head"), None),
        P(("dp", "head"), None),
        P(("dp", "head"), None),
        P(("dp", "head"), None),
        P(("dp", "head"), None),
        P(("dp", "head"), None),
        P(("dp", "head"), None),
        P(("dp", "head"), None),
        P(("dp", "head"), None),
        P(("dp", "head"), None),
        P(("dp", "head"), None),
        P(("dp", "head"), None),
        P(("dp", "head"), None),
        P(("dp", "head"), None),
        P(("dp", "head"), None),
    )
    out_specs = (
        P(),
        P(),
        P(("dp", "head"), None),
        P(("dp", "head"), None),
        P(("dp", "head"), None),
        P(("dp", "head"), None),
        P(("dp", "head"), None),
        P(("dp", "head"), None),
        P(("dp", "head"), None),
        P(("dp", "head"), None),
        P(("dp", "head"), None),
        P(("dp", "head"), None),
        P(("dp", "head"), None),
        P(("dp", "head"), None),
        P(("dp", "head"), None),
        P(("dp", "head"), None),
        P(("dp", "head"), None),
    )
    return jax.shard_map(body, mesh=mesh, in_specs=in_specs, out_specs=out_specs, check_vma=False)
```

time: 674 us -> 404 us (0.60)
  matrix products: 164 us -> 2.04 us
  Pallas kernels: 0 us -> 160 us
  local copies, waits for them, and re-layouts: 149 us -> 33.8 us
  other arithmetic: 134 us -> 38 us
  waiting for transfers between devices: 164 us -> 92.8 us
  starting transfers between devices: 43.7 us -> 62.2 us
    pallas_call x0 -> x7, Pallas kernels: none -> 160 us  [the longest x6 84.7 us: per_sample(): pl.pallas_call(kernel, grid=(samples,), in_specs=in_specs, out_specs=[spe...]
    ppermute x38 -> x46, waiting for transfers between devices: 164 us -> 74.8 us  [flip(): return lax.ppermute(values, axis, [(i, i ^ 1 << bit) for i in range(size)])]
    dot_general x62 -> x0, matrix products: 88.7 us -> none  [the longest x8 16 us: attend_back(): jnp.einsum('qd,kd->qk', upstream, value_part, preferred_element_type=jnp....]
    conv_general_dilated x6 -> x0, matrix products: 72.9 us -> none  [the longest x4 53.7 us: conv(): lax.conv_general_dilated(hidden, kernel, (1, 1), 'SAME', dimension_number...]
    convert_element_type x19 -> x2, other arithmetic: 45.5 us -> 0.01 us  [the longest x1 0.01 us: body(): own_extents[:, 0].astype(jnp.float32)]
    unnamed x207 -> x66, local copies, waits for them, and re-layouts: 25.7 us -> 1.94 us
    convert_element_type x30 -> x12, local copies, waits for them, and re-layouts: 21.2 us -> 0.44 us  [scatter_bits(): got = flip(send.astype(jnp.bfloat16), *name)]
    squeeze x18 -> x1, local copies, waits for them, and re-layouts: 21.7 us -> 1.46 us  [scatter_two(): lax.dynamic_index_in_dim(halved, 1 - bit, 1, keepdims=False)]
  transfers between devices with their start and end apart: 38 -> 52, of which waited for: 21 -> 26; matrix products, arithmetic and copies ran while one was open for 11% -> 11% of each run, Pallas kernels for 0% -> 10%
where the time goes in v2:
time: 404 us; the launch traced here: 396 us
  Pallas kernels  160 us (40%)
  waiting for transfers between devices  92.8 us (23%)
  starting transfers between devices  62.2 us (15%)
  other arithmetic  38 us (9%)
  local copies, waits for them, and re-layouts  33.8 us (8%)
  between operations  7.39 us (2%)
    pallas_call x6, Pallas kernels, per_sample(): pl.pallas_call(kernel, grid=(samples,), in_specs=in_specs, out_specs=[spe...  84.7 us
    pallas_call x1, Pallas kernels, attention_block(): pl.pallas_call(attention_kernel, grid=(samples,), in_specs=[pl.BlockSpec(...  75 us
    ppermute x46, waiting for transfers between devices, flip(): return lax.ppermute(values, axis, [(i, i ^ 1 << bit) for i in range(size)])  74.8 us
    ppermute x46, starting transfers between devices, flip(): return lax.ppermute(values, axis, [(i, i ^ 1 << bit) for i in range(size)])  58 us
    ppermute x6, waiting for transfers between devices, strips_of(): strip = lax.ppermute(strip, 'head', [(i, i ^ far) for i in range(parts)])  18 us
  transfers between devices with their start and end apart: 52, of which 26 were waited for; matrix products, arithmetic and copies ran while one was open for 11% of the time, Pallas kernels for 10%

profile of v2, /device:TPU:0, one launch (start us, length us, event | category | flops | bytes accessed | tf_op | source)
XLA Modules:
  0.0 396.0 jit_solution(11321222019679490761)
XLA Ops:
  5.0 4.0 %collective-permute-start = (bf16[224,384]{1,0:T(8,128)(2,1)}, bf16[224,384]{1,0:T(8,128)(2,1)}, u32[]{:S(2)}, u32[]{:S(2)}) collective-permute-start(bf16[224,384]{1,0:T(8,128)(2,1)} %pad_maximum_fusion.19), channel_id=1, source_target_pairs={{0,16},{4,20},{8,24},{12,28},{16,0},{20,4},{24,8},{28,12},{1,17},{... | collective-permute-start | bytes 516104 | tf_op jit(solution)/shard_map/ppermute | solution.py:65
  12.3 2.3 constant_dynamic-slice_fusion.7
  14.6 1.9 collective-permute-start.9
  22.7 1.9 collective-permute-start.20
  25.9 14.9 %collective-permute-done.20 = bf16[2,8,32,192]{3,2,1,0:T(8,128)(2,1)S(1)} collective-permute-done((bf16[2,8,32,192]{3,2,1,0:T(8,128)(2,1)S(1)}, bf16[2,8,32,192]{3,2,1,0:T(8,128)(2,1)S(1)}, u32[]{:S(2)}, u32[]{:S(2)}) %collective-permute-start.20) | collective-permute-done | bytes 196640 | tf_op jit(solution)/shard_map/ppermute | solution.py:149
  40.7 1.9 collective-permute-start.11
  42.7 3.1 collective-permute-done.21
  47.5 3.0 collective-permute-done.1
  52.3 2.9 collective-permute-done.4
  58.6 1.9 collective-permute-done.15
  63.7 1.8 collective-permute-start.16
  68.4 1.8 collective-permute-start.6
  70.2 4.7 %collective-permute-done.12 = bf16[2,200,384]{2,1,0:T(8,128)(2,1)S(1)} collective-permute-done((bf16[2,200,384]{2,1,0:T(8,128)(2,1)S(1)}, bf16[2,200,384]{2,1,0:T(8,128)(2,1)S(1)}, u32[]{:S(2)}, u32[]{:S(2)}) %collective-permute-start.12) | collective-permute-done | bytes 307232 | tf_op jit(solution)/shard_map/ppermute | solution.py:65
  75.0 1.7 collective-permute-start.13
  77.5 2.3 collective-permute-done.16
  79.9 1.8 collective-permute-start.17
  82.8 4.3 %collective-permute-done.13 = bf16[2,2,200,384]{3,2,0,1:T(8,128)(2,1)S(1)} collective-permute-done((bf16[2,2,200,384]{3,2,0,1:T(8,128)(2,1)S(1)}, bf16[2,2,200,384]{3,2,0,1:T(8,128)(2,1)S(1)}, u32[]{:S(2)}, u32[]{:S(2)}) %collective-permute-start.13) | collective-permute-done | bytes 614432 | tf_op jit(solution)/shard_map/ppermute | solution.py:65
  87.5 7.0 %collective-permute-done.17 = bf16[2,2,208,384]{3,2,0,1:T(8,128)(2,1)S(1)} collective-permute-done((bf16[2,2,208,384]{3,2,0,1:T(8,128)(2,1)S(1)}, bf16[2,2,208,384]{3,2,0,1:T(8,128)(2,1)S(1)}, u32[]{:S(2)}, u32[]{:S(2)}) %collective-permute-start.17) | collective-permute-done | bytes 639008 | tf_op jit(solution)/shard_map/ppermute | solution.py:65
  95.0 1.8 pad_maximum_fusion.2
  97.9 1.8 slice.211
  104.4 15.0 %shard_map.323 = (f32[2,1024,384]{2,1,0:T(8,128)}, bf16[2,1024,384]{2,1,0:T(8,128)(2,1)}, f32[2,8,384]{2,1,0:T(8,128)}) custom-call(bf16[2,1024,384]{2,1,0:T(8,128)(2,1)} %bitcast.285, f32[8,384]{1,0:T(8,128)} %pad.14.gains, bf16[384,384]{1,0:T(8,128)(2,1)} %constant.261.clone.member, bf16[3456,384]{1,0:T(8,128)(2,1)} %bitcast.279), custom_call_target="tpu_custom_call" | custom-call | flops 5435817984 | bytes 5435817 | tf_op jit(solution)/shard_map/pallas_call | solution.py:642
  119.4 2.7 select_bitcast_fusion.1
  123.5 1.7 slice.216
  130.3 13.8 %shard_map.324 = (f32[2,1024,384]{2,1,0:T(8,128)}, bf16[2,1024,384]{2,1,0:T(8,128)(2,1)}) custom-call(f32[2,1024,384]{2,1,0:T(8,128)} %get-tuple-element.29.inner, bf16[2,1024,384]{2,1,0:T(8,128)(2,1)} %bitcast.286, f32[2,8,384]{2,1,0:T(8,128)} %get-tuple-element.30.stats, f32[2,8,384]{2,1,0:T(8,128)} %pad.15.film, f32[8,384]{1,0:T(8,128)} %pad.14.gains, ...), custom_call_target="tpu_custom_call" | custom-call | flops 5435817984 | bytes 5435817 | tf_op jit(solution)/shard_map/pallas_call | solution.py:642
  144.2 75.0 %shard_map.325 = (bf16[2,1024,384]{2,1,0:T(8,128)(2,1)}, bf16[384,1152]{1,0:T(8,128)(2,1)}, bf16[384,384]{1,0:T(8,128)(2,1)}, f32[2,8,384]{2,1,0:T(8,128)}, f32[2,8,192]{2,1,0:T(8,128)}) custom-call(f32[2,6]{1,0:T(2,128)} %stack.266.scalars, f32[2,1024,384]{2,1,0:T(8,128)} %get-tuple-element.31.middle, bf16[2,1024,192]{2,1,0:T(8,128)(2,1)} %bitcast.288, ...), custom_call_target="tpu_custom_call" | custom-call | flops 24159191040 | bytes 6291456 | tf_op jit(solution)/shard_map/pallas_call | solution.py:389
  219.2 16.9 %shard_map.326 = (bf16[2,1024,384]{2,1,0:T(8,128)(2,1)}, f32[2,8,384]{2,1,0:T(8,128)}) custom-call(bf16[2,1024,384]{2,1,0:T(8,128)(2,1)} %get-tuple-element.32.grad, f32[2,1024,384]{2,1,0:T(8,128)} %get-tuple-element.29.inner, f32[2,8,384]{2,1,0:T(8,128)} %get-tuple-element.30.stats, f32[2,8,384]{2,1,0:T(8,128)} %pad.15.film, f32[8,384]{1,0:T(8,128)} %pad.14.gains, ...), custom_call_target="tpu_custom_call" | custom-call | flops 5435817984 | bytes 5435817 | tf_op jit(solution)/shard_map/pallas_call | solution.py:642
  237.6 14.3 %shard_map.329 = f32[2,8,384]{2,1,0:T(8,128)} custom-call(bf16[2,1024,384]{2,1,0:T(8,128)(2,1)} %get-tuple-element.38.grad, bf16[2,1024,384]{2,1,0:T(8,128)(2,1)} %bitcast.287, f32[2,8,384]{2,1,0:T(8,128)} %get-tuple-element.30.stats, f32[8,384]{1,0:T(8,128)} %pad.14.gains, bf16[3456,384]{1,0:T(8,128)(2,1)} %bitcast.280), custom_call_target="tpu_custom_call" | custom-call | flops 5435817984 | bytes 5435817 | tf_op jit(solution)/shard_map/pallas_call | solution.py:642
  253.7 2.7 collective-permute-start.42
  256.7 12.5 %shard_map.328 = bf16[3456,384]{1,0:T(8,128)(2,1)} custom-call(bf16[2,1024,384]{2,1,0:T(8,128)(2,1)} %get-tuple-element.37.hidden, bf16[2,1024,384]{2,1,0:T(8,128)(2,1)} %get-tuple-element.38.grad), custom_call_target="tpu_custom_call" | custom-call | flops 5435817984 | bytes 5435817 | tf_op jit(solution)/shard_map/pallas_call | solution.py:642
  274.0 12.2 %shard_map.327 = bf16[3456,384]{1,0:T(8,128)(2,1)} custom-call(bf16[2,1024,384]{2,1,0:T(8,128)(2,1)} %get-tuple-element.34.hidden, bf16[2,1024,384]{2,1,0:T(8,128)(2,1)} %get-tuple-element.32.grad), custom_call_target="tpu_custom_call" | custom-call | flops 5435817984 | bytes 5435817 | tf_op jit(solution)/shard_map/pallas_call | solution.py:642
  286.2 1.8 reshape.231
  293.8 1.9 collective-permute-done.45
  299.4 2.0 convert_add_fusion.1
  309.9 3.2 collective-permute-done.35
  314.7 3.7 collective-permute-done.38
  321.9 2.4 collective-permute-done.39
  325.4 1.9 convert_add_fusion
  330.5 8.4 %collective-permute-done.28 = bf16[2,2,152,384]{3,2,1,0:T(8,128)(2,1)S(1)} collective-permute-done((bf16[2,2,152,384]{3,2,1,0:T(8,128)(2,1)S(1)}, bf16[2,2,152,384]{3,2,1,0:T(8,128)(2,1)S(1)}, u32[]{:S(2)}, u32[]{:S(2)}) %collective-permute-start.28) | collective-permute-done | bytes 466976 | tf_op jit(solution)/shard_map/ppermute | solution.py:65
  341.8 5.4 %collective-permute-done.29 = bf16[2,152,384]{2,1,0:T(8,128)(2,1)S(1)} collective-permute-done((bf16[2,152,384]{2,1,0:T(8,128)(2,1)S(1)}, bf16[2,152,384]{2,1,0:T(8,128)(2,1)S(1)}, u32[]{:S(2)}, u32[]{:S(2)}) %collective-permute-start.29) | collective-permute-done | bytes 233504 | tf_op jit(solution)/shard_map/ppermute | solution.py:65
  347.2 1.7 collective-permute-start.30
  352.1 2.7 collective-permute-done.33
  355.1 2.7 collective-permute-start.41
  357.9 6.1 %collective-permute-done.41 = bf16[264,384]{1,0:T(8,128)(2,1)S(1)} collective-permute-done((bf16[264,384]{1,0:T(8,128)(2,1)S(1)}, bf16[264,384]{1,0:T(8,128)(2,1)S(1)}, u32[]{:S(2)}, u32[]{:S(2)}) %collective-permute-start.41) | collective-permute-done | bytes 202784 | tf_op jit(solution)/shard_map/ppermute | solution.py:65
  370.5 3.9 collective-permute-done.47
  376.3 2.3 collective-permute-done.48
  380.2 2.7 collective-permute-done.49
  384.5 1.9 collective-permute-done.50
  390.7 1.9 pad_maximum_fusion.33
  (342 shorter events, 98.7 us)
Async XLA Ops:
  5.0 17.6 %collective-permute-start = (bf16[224,384]{1,0:T(8,128)(2,1)}, bf16[224,384]{1,0:T(8,128)(2,1)}, u32[]{:S(2)}, u32[]{:S(2)}) collective-permute-start(bf16[224,384]{1,0:T(8,128)(2,1)} %pad_maximum_fusion.19), channel_id=1, source_target_pairs={{0,16},{4,20},{8,24},{12,28},{16,0},{20,4},{24,8},{28,12},{1,17},{... | collective-permute-start | bytes 516104 | tf_op jit(solution)/shard_map/ppermute | solution.py:65
  12.3 9.2 %collective-permute-start.14 = (bf16[96,384]{1,0:T(8,128)(2,1)}, bf16[96,384]{1,0:T(8,128)(2,1)}, u32[]{:S(2)}, u32[]{:S(2)}) collective-permute-start(bf16[96,384]{1,0:T(8,128)(2,1)} %pad_maximum_fusion.25), channel_id=1, source_target_pairs={{0,16},{4,20},{8,24},{12,28},{16,0},{20,4},{24,8},{28,12},{1,17},{... | collective-permute-start | bytes 221192 | tf_op jit(solution)/shard_map/ppermute | solution.py:65
  14.6 47.7 %collective-permute-start.8 = (bf16[2,8,32,384]{3,2,1,0:T(8,128)(2,1)}, bf16[2,8,32,384]{3,2,1,0:T(8,128)(2,1)}, u32[]{:S(2)}, u32[]{:S(2)}) collective-permute-start(bf16[2,8,32,384]{3,2,1,0:T(8,128)(2,1)} %get-tuple-element.73), channel_id=1, source_target_pairs={{0,1},{1,0},{2,3},{3,2},{4,5},{5,4},{6,7},{7,6},{8,9},{9,8},{10,11... | collective-permute-start | bytes 1179656 | tf_op jit(solution)/shard_map/ppermute | solution.py:149
  14.6 49.1 %collective-permute-start.9 = (bf16[2,8,32,384]{3,2,1,0:T(8,128)(2,1)}, bf16[2,8,32,384]{3,2,1,0:T(8,128)(2,1)}, u32[]{:S(2)}, u32[]{:S(2)}) collective-permute-start(bf16[2,8,32,384]{3,2,1,0:T(8,128)(2,1)} %get-tuple-element.74), channel_id=1, source_target_pairs={{0,2},{1,3},{2,0},{3,1},{4,6},{5,7},{6,4},{7,5},{8,10},{9,11},{10,... | collective-permute-start | bytes 1179656 | tf_op jit(solution)/shard_map/ppermute | solution.py:149
  16.4 65.3 %collective-permute-start.10 = (bf16[2,8,32,384]{3,2,1,0:T(8,128)(2,1)S(1)}, bf16[2,8,32,384]{3,2,1,0:T(8,128)(2,1)}, u32[]{:S(2)}, u32[]{:S(2)}) collective-permute-start(bf16[2,8,32,384]{3,2,1,0:T(8,128)(2,1)S(1)} %get-tuple-element.72), channel_id=1, source_target_pairs={{0,3},{1,2},{2,1},{3,0},{4,7},{5,6},{6,5},{7,4},{8,11},{9,10},{10,... | collective-permute-start | bytes 1179656 | tf_op jit(solution)/shard_map/ppermute | solution.py:149
  21.5 4.3 %collective-permute-start.19 = (bf16[2,8,32,192]{3,2,1,0:T(8,128)(2,1)}, bf16[2,8,32,192]{3,2,1,0:T(8,128)(2,1)S(1)}, u32[]{:S(2)}, u32[]{:S(2)}) collective-permute-start(bf16[2,8,32,192]{3,2,1,0:T(8,128)(2,1)} %get-tuple-element.80), channel_id=1, source_target_pairs={{0,1},{1,0},{2,3},{3,2},{4,5},{5,4},{6,7},{7,6},{8,9},{9,8},{10,11... | collective-permute-start | bytes 589832 | tf_op jit(solution)/shard_map/ppermute | solution.py:149
  22.7 18.1 %collective-permute-start.20 = (bf16[2,8,32,192]{3,2,1,0:T(8,128)(2,1)S(1)}, bf16[2,8,32,192]{3,2,1,0:T(8,128)(2,1)S(1)}, u32[]{:S(2)}, u32[]{:S(2)}) collective-permute-start(bf16[2,8,32,192]{3,2,1,0:T(8,128)(2,1)S(1)} %copy-done.13), channel_id=1, source_target_pairs={{0,2},{1,3},{2,0},{3,1},{4,6},{5,7},{6,4},{7,5},{8,10},{9,11},{10,... | collective-permute-start | bytes 589832 | tf_op jit(solution)/shard_map/ppermute | solution.py:149
  25.8 20.1 %collective-permute-start.21 = (bf16[2,8,32,192]{3,2,1,0:T(8,128)(2,1)S(1)}, bf16[2,8,32,192]{3,2,1,0:T(8,128)(2,1)S(1)}, u32[]{:S(2)}, u32[]{:S(2)}) collective-permute-start(bf16[2,8,32,192]{3,2,1,0:T(8,128)(2,1)S(1)} %get-tuple-element.79), channel_id=1, source_target_pairs={{0,3},{1,2},{2,1},{3,0},{4,7},{5,6},{6,5},{7,4},{8,11},{9,10},{10,... | collective-permute-start | bytes 589832 | tf_op jit(solution)/shard_map/ppermute | solution.py:149
  40.7 16.2 %collective-permute-start.11 = (bf16[200,384]{1,0:T(8,128)(2,1)S(1)}, bf16[200,384]{1,0:T(8,128)(2,1)S(1)}, u32[]{:S(2)}, u32[]{:S(2)}) collective-permute-start(bf16[200,384]{1,0:T(8,128)(2,1)S(1)} %slice.212), channel_id=1, source_target_pairs={{0,8},{4,12},{8,0},{12,4},{16,24},{20,28},{24,16},{28,20},{1,9},{5... | collective-permute-start | bytes 460808 | tf_op jit(solution)/shard_map/ppermute | solution.py:65
  45.8 4.7 %collective-permute-start.1 = (bf16[104,384]{1,0:T(8,128)(2,1)S(1)}, bf16[104,384]{1,0:T(8,128)(2,1)S(1)}, u32[]{:S(2)}, u32[]{:S(2)}) collective-permute-start(bf16[104,384]{1,0:T(8,128)(2,1)S(1)} %slice.201), channel_id=1, source_target_pairs={{0,8},{4,12},{8,0},{12,4},{16,24},{20,28},{24,16},{28,20},{1,9},{5... | collective-permute-start | bytes 239624 | tf_op jit(solution)/shard_map/ppermute | solution.py:65
  50.6 4.6 %collective-permute-start.4 = (bf16[128,384]{1,0:T(8,128)(2,1)S(1)}, bf16[128,384]{1,0:T(8,128)(2,1)S(1)}, u32[]{:S(2)}, u32[]{:S(2)}) collective-permute-start(bf16[128,384]{1,0:T(8,128)(2,1)S(1)} %pad_maximum_fusion.23), channel_id=1, source_target_pairs={{0,4},{4,0},{8,12},{12,8},{16,20},{20,16},{24,28},{28,24},{1,5},{5... | collective-permute-start | bytes 294920 | tf_op jit(solution)/shard_map/ppermute | solution.py:65
  55.2 5.3 %collective-permute-start.15 = (bf16[208,384]{1,0:T(8,128)(2,1)S(1)}, bf16[208,384]{1,0:T(8,128)(2,1)S(1)}, u32[]{:S(2)}, u32[]{:S(2)}) collective-permute-start(bf16[208,384]{1,0:T(8,128)(2,1)S(1)} %pad_maximum_fusion.20), channel_id=1, source_target_pairs={{0,4},{4,0},{8,12},{12,8},{16,20},{20,16},{24,28},{28,24},{1,5},{5... | collective-permute-start | bytes 479240 | tf_op jit(solution)/shard_map/ppermute | solution.py:65
  56.9 9.6 %collective-permute-start.2 = (bf16[2,104,384]{2,1,0:T(8,128)(2,1)S(1)}, bf16[2,104,384]{2,1,0:T(8,128)(2,1)S(1)}, u32[]{:S(2)}, u32[]{:S(2)}) collective-permute-start(bf16[2,104,384]{2,1,0:T(8,128)(2,1)S(1)} %pad_maximum_fusion.21), channel_id=1, source_target_pairs={{0,2},{1,3},{2,0},{3,1},{4,6},{5,7},{6,4},{7,5},{8,10},{9,11},{10,... | collective-permute-start | bytes 479240 | tf_op jit(solution)/shard_map/ppermute | solution.py:65
  60.5 7.8 %collective-permute-start.5 = (bf16[2,128,384]{2,1,0:T(8,128)(2,1)S(1)}, bf16[2,128,384]{2,1,0:T(8,128)(2,1)S(1)}, u32[]{:S(2)}, u32[]{:S(2)}) collective-permute-start(bf16[2,128,384]{2,1,0:T(8,128)(2,1)S(1)} %pad_maximum_fusion.17), channel_id=1, source_target_pairs={{0,2},{1,3},{2,0},{3,1},{4,6},{5,7},{6,4},{7,5},{8,10},{9,11},{10,... | collective-permute-start | bytes 589832 | tf_op jit(solution)/shard_map/ppermute | solution.py:65
  62.2 12.6 %collective-permute-start.12 = (bf16[2,200,384]{2,1,0:T(8,128)(2,1)S(1)}, bf16[2,200,384]{2,1,0:T(8,128)(2,1)S(1)}, u32[]{:S(2)}, u32[]{:S(2)}) collective-permute-start(bf16[2,200,384]{2,1,0:T(8,128)(2,1)S(1)} %pad_maximum_fusion.15), channel_id=1, source_target_pairs={{0,2},{1,3},{2,0},{3,1},{4,6},{5,7},{6,4},{7,5},{8,10},{9,11},{10,... | collective-permute-start | bytes 921608 | tf_op jit(solution)/shard_map/ppermute | solution.py:65
  63.7 16.0 %collective-permute-start.16 = (bf16[2,208,384]{2,1,0:T(8,128)(2,1)S(1)}, bf16[2,208,384]{2,1,0:T(8,128)(2,1)S(1)}, u32[]{:S(2)}, u32[]{:S(2)}) collective-permute-start(bf16[2,208,384]{2,1,0:T(8,128)(2,1)S(1)} %pad_maximum_fusion.14), channel_id=1, source_target_pairs={{0,2},{1,3},{2,0},{3,1},{4,6},{5,7},{6,4},{7,5},{8,10},{9,11},{10,... | collective-permute-start | bytes 958472 | tf_op jit(solution)/shard_map/ppermute | solution.py:65
  66.7 10.1 %collective-permute-start.3 = (bf16[2,2,104,384]{3,2,1,0:T(8,128)(2,1)S(1)}, bf16[2,2,104,384]{3,2,1,0:T(8,128)(2,1)S(1)}, u32[]{:S(2)}, u32[]{:S(2)}) collective-permute-start(bf16[2,2,104,384]{3,2,1,0:T(8,128)(2,1)S(1)} %pad_maximum_fusion.13), channel_id=1, source_target_pairs={{0,4},{4,0},{8,12},{12,8},{16,20},{20,16},{24,28},{28,24},{1,5},{5... | collective-permute-start | bytes 958472 | tf_op jit(solution)/shard_map/ppermute | solution.py:65
  68.4 8.5 %collective-permute-start.6 = (bf16[2,2,128,384]{3,2,0,1:T(8,128)(2,1)S(1)}, bf16[2,2,128,384]{3,2,0,1:T(8,128)(2,1)S(1)}, u32[]{:S(2)}, u32[]{:S(2)}) collective-permute-start(bf16[2,2,128,384]{3,2,0,1:T(8,128)(2,1)S(1)} %pad_maximum_fusion.10), channel_id=1, source_target_pairs={{0,8},{4,12},{8,0},{12,4},{16,24},{20,28},{24,16},{28,20},{1,9},{5... | collective-permute-start | bytes 1179656 | tf_op jit(solution)/shard_map/ppermute | solution.py:65
  75.0 12.0 %collective-permute-start.13 = (bf16[2,2,200,384]{3,2,0,1:T(8,128)(2,1)S(1)}, bf16[2,2,200,384]{3,2,0,1:T(8,128)(2,1)S(1)}, u32[]{:S(2)}, u32[]{:S(2)}) collective-permute-start(bf16[2,2,200,384]{3,2,0,1:T(8,128)(2,1)S(1)} %pad_maximum_fusion.9), channel_id=1, source_target_pairs={{0,4},{4,0},{8,12},{12,8},{16,20},{20,16},{24,28},{28,24},{1,5},{5... | collective-permute-start | bytes 1843208 | tf_op jit(solution)/shard_map/ppermute | solution.py:65
  77.4 19.4 %collective-permute-start.7 = (bf16[8,232,384]{2,1,0:T(8,128)(2,1)S(1)}, bf16[8,232,384]{2,1,0:T(8,128)(2,1)S(1)}, u32[]{:S(2)}, u32[]{:S(2)}) collective-permute-start(bf16[8,232,384]{2,1,0:T(8,128)(2,1)S(1)} %pad_maximum_fusion.3), channel_id=1, source_target_pairs={{0,1},{1,0},{2,3},{3,2},{4,5},{5,4},{6,7},{7,6},{8,9},{9,8},{10,11... | collective-permute-start | bytes 4276232 | tf_op jit(solution)/shard_map/ppermute | solution.py:65
  79.9 14.6 %collective-permute-start.17 = (bf16[2,2,208,384]{3,2,0,1:T(8,128)(2,1)S(1)}, bf16[2,2,208,384]{3,2,0,1:T(8,128)(2,1)S(1)}, u32[]{:S(2)}, u32[]{:S(2)}) collective-permute-start(bf16[2,2,208,384]{3,2,0,1:T(8,128)(2,1)S(1)} %pad_maximum_fusion.8), channel_id=1, source_target_pairs={{0,8},{4,12},{8,0},{12,4},{16,24},{20,28},{24,16},{28,20},{1,9},{5... | collective-permute-start | bytes 1916936 | tf_op jit(solution)/shard_map/ppermute | solution.py:65
  96.8 22.6 %collective-permute-start.18 = (bf16[8,408,384]{2,1,0:T(8,128)(2,1)}, bf16[8,408,384]{2,1,0:T(8,128)(2,1)}, u32[]{:S(2)}, u32[]{:S(2)}) collective-permute-start(bf16[8,408,384]{2,1,0:T(8,128)(2,1)} %pad_maximum_fusion.2), channel_id=1, source_target_pairs={{0,1},{1,0},{2,3},{3,2},{4,5},{5,4},{6,7},{7,6},{8,9},{9,8},{10,11... | collective-permute-start | bytes 7520264 | tf_op jit(solution)/shard_map/ppermute | solution.py:65
  253.7 18.7 %collective-permute-start.42 = (f32[384,6]{0,1:T(8,128)S(1)}, f32[384,6]{0,1:T(8,128)S(1)}, u32[]{:S(2)}, u32[]{:S(2)}) collective-permute-start(f32[384,6]{0,1:T(8,128)S(1)} %stack.312), channel_id=1, source_target_pairs={{0,16},{4,20},{8,24},{12,28},{16,0},{20,4},{24,8},{28,12},{1,17},{... | collective-permute-start | bytes 27656 | tf_op jit(solution)/shard_map/ppermute | solution.py:65
  256.4 12.8 %collective-permute-start.22 = (bf16[2,768]{1,0:T(2,128)(2,1)S(1)}, bf16[2,768]{1,0:T(2,128)(2,1)S(1)}, u32[]{:S(2)}, u32[]{:S(2)}) collective-permute-start(bf16[2,768]{1,0:T(2,128)(2,1)S(1)} %pad_maximum_fusion.31), channel_id=1, source_target_pairs={{0,16},{4,20},{8,24},{12,28},{16,0},{20,4},{24,8},{28,12},{1,17},{... | collective-permute-start | bytes 9224 | tf_op jit(solution)/shard_map/ppermute | solution.py:65
  269.2 3.7 collective-permute-start.23
  272.4 27.0 %collective-permute-start.34 = (bf16[8,216,384]{2,1,0:T(8,128)(2,1)S(1)}, bf16[8,216,384]{2,1,0:T(8,128)(2,1)}, u32[]{:S(2)}, u32[]{:S(2)}) collective-permute-start(bf16[8,216,384]{2,1,0:T(8,128)(2,1)S(1)} %dynamic-slice_bitcast_fusion), channel_id=1, source_target_pairs={{0,1},{1,0},{2,3},{3,2},{4,5},{5,4},{6,7},{7,6},{8,9},{9,8},{10,11... | collective-permute-start | bytes 3981320 | tf_op jit(solution)/shard_map/ppermute | solution.py:65
  272.5 15.7 %collective-permute-start.43 = (f32[384,6]{0,1:T(8,128)S(1)}, f32[384,6]{0,1:T(8,128)S(1)}, u32[]{:S(2)}, u32[]{:S(2)}) collective-permute-start(f32[384,6]{0,1:T(8,128)S(1)} %add.376), channel_id=1, source_target_pairs={{0,8},{4,12},{8,0},{12,4},{16,24},{20,28},{24,16},{28,20},{1,9},{5... | collective-permute-start | bytes 27656 | tf_op jit(solution)/shard_map/ppermute | solution.py:65
  273.0 16.3 %collective-permute-start.24 = (bf16[2,2,2,768]{3,2,0,1:T(2,128)(2,1)S(1)}, bf16[2,2,2,768]{3,2,0,1:T(2,128)(2,1)S(1)}, u32[]{:S(2)}, u32[]{:S(2)}) collective-permute-start(bf16[2,2,2,768]{3,2,0,1:T(2,128)(2,1)S(1)} %pad_maximum_fusion.28), channel_id=1, source_target_pairs={{0,4},{4,0},{8,12},{12,8},{16,20},{20,16},{24,28},{28,24},{1,5},{5... | collective-permute-start | bytes 36872 | tf_op jit(solution)/shard_map/ppermute | solution.py:65
  288.2 3.8 collective-permute-start.44
  289.4 6.3 %collective-permute-start.25 = (bf16[2,2,2,2,768]{4,3,0,1,2:T(2,128)(2,1)S(1)}, bf16[2,2,2,2,768]{4,3,0,1,2:T(2,128)(2,1)S(1)}, u32[]{:S(2)}, u32[]{:S(2)}) collective-permute-start(bf16[2,2,2,2,768]{4,3,0,1,2:T(2,128)(2,1)S(1)} %pad_maximum_fusion.27), channel_id=1, source_target_pairs={{0,2},{1,3},{2,0},{3,1},{4,6},{5,7},{6,4},{7,5},{8,10},{9,11},{10,... | collective-permute-start | bytes 73736 | tf_op jit(solution)/shard_map/ppermute | solution.py:65
  291.9 3.7 collective-permute-start.45
  297.8 27.5 %collective-permute-start.27 = (bf16[8,312,384]{2,1,0:T(8,128)(2,1)}, bf16[8,312,384]{2,1,0:T(8,128)(2,1)}, u32[]{:S(2)}, u32[]{:S(2)}) collective-permute-start(bf16[8,312,384]{2,1,0:T(8,128)(2,1)} %fusion.1), channel_id=1, source_target_pairs={{0,1},{1,0},{2,3},{3,2},{4,5},{5,4},{6,7},{7,6},{8,9},{9,8},{10,11... | collective-permute-start | bytes 5750792 | tf_op jit(solution)/shard_map/ppermute | solution.py:65
  303.1 10.0 %collective-permute-start.35 = (bf16[2,2,104,384]{3,2,0,1:T(8,128)(2,1)S(1)}, bf16[2,2,104,384]{3,2,0,1:T(8,128)(2,1)S(1)}, u32[]{:S(2)}, u32[]{:S(2)}) collective-permute-start(bf16[2,2,104,384]{3,2,0,1:T(8,128)(2,1)S(1)} %fusion.8), channel_id=1, source_target_pairs={{0,4},{4,0},{8,12},{12,8},{16,20},{20,16},{24,28},{28,24},{1,5},{5... | collective-permute-start | bytes 958472 | tf_op jit(solution)/shard_map/ppermute | solution.py:65
  308.2 10.2 %collective-permute-start.38 = (bf16[2,2,112,384]{3,2,0,1:T(8,128)(2,1)S(1)}, bf16[2,2,112,384]{3,2,0,1:T(8,128)(2,1)S(1)}, u32[]{:S(2)}, u32[]{:S(2)}) collective-permute-start(bf16[2,2,112,384]{3,2,0,1:T(8,128)(2,1)S(1)} %fusion.6), channel_id=1, source_target_pairs={{0,8},{4,12},{8,0},{12,4},{16,24},{20,28},{24,16},{28,20},{1,9},{5... | collective-permute-start | bytes 1032200 | tf_op jit(solution)/shard_map/ppermute | solution.py:65
  313.2 7.0 %collective-permute-start.36 = (bf16[2,104,384]{2,1,0:T(8,128)(2,1)S(1)}, bf16[2,104,384]{2,1,0:T(8,128)(2,1)S(1)}, u32[]{:S(2)}, u32[]{:S(2)}) collective-permute-start(bf16[2,104,384]{2,1,0:T(8,128)(2,1)S(1)} %fusion.13), channel_id=1, source_target_pairs={{0,2},{1,3},{2,0},{3,1},{4,6},{5,7},{6,4},{7,5},{8,10},{9,11},{10,... | collective-permute-start | bytes 479240 | tf_op jit(solution)/shard_map/ppermute | solution.py:65
  318.5 5.7 %collective-permute-start.39 = (bf16[2,112,384]{2,1,0:T(8,128)(2,1)S(1)}, bf16[2,112,384]{2,1,0:T(8,128)(2,1)S(1)}, u32[]{:S(2)}, u32[]{:S(2)}) collective-permute-start(bf16[2,112,384]{2,1,0:T(8,128)(2,1)S(1)} %fusion.12), channel_id=1, source_target_pairs={{0,2},{1,3},{2,0},{3,1},{4,6},{5,7},{6,4},{7,5},{8,10},{9,11},{10,... | collective-permute-start | bytes 516104 | tf_op jit(solution)/shard_map/ppermute | solution.py:65
  320.2 8.4 %collective-permute-start.37 = (bf16[104,384]{1,0:T(8,128)(2,1)S(1)}, bf16[104,384]{1,0:T(8,128)(2,1)S(1)}, u32[]{:S(2)}, u32[]{:S(2)}) collective-permute-start(bf16[104,384]{1,0:T(8,128)(2,1)S(1)} %fusion.18), channel_id=1, source_target_pairs={{0,8},{4,12},{8,0},{12,4},{16,24},{20,28},{24,16},{28,20},{1,9},{5... | collective-permute-start | bytes 239624 | tf_op jit(solution)/shard_map/ppermute | solution.py:65
  324.3 6.2 %collective-permute-start.40 = (bf16[112,384]{1,0:T(8,128)(2,1)S(1)}, bf16[112,384]{1,0:T(8,128)(2,1)S(1)}, u32[]{:S(2)}, u32[]{:S(2)}) collective-permute-start(bf16[112,384]{1,0:T(8,128)(2,1)S(1)} %fusion.17), channel_id=1, source_target_pairs={{0,4},{4,0},{8,12},{12,8},{16,20},{20,16},{24,28},{28,24},{1,5},{5... | collective-permute-start | bytes 258056 | tf_op jit(solution)/shard_map/ppermute | solution.py:65
  327.5 11.4 %collective-permute-start.28 = (bf16[2,2,152,384]{3,2,1,0:T(8,128)(2,1)S(1)}, bf16[2,2,152,384]{3,2,1,0:T(8,128)(2,1)S(1)}, u32[]{:S(2)}, u32[]{:S(2)}) collective-permute-start(bf16[2,2,152,384]{3,2,1,0:T(8,128)(2,1)S(1)} %fusion.5), channel_id=1, source_target_pairs={{0,4},{4,0},{8,12},{12,8},{16,20},{20,16},{24,28},{28,24},{1,5},{5... | collective-permute-start | bytes 1400840 | tf_op jit(solution)/shard_map/ppermute | solution.py:65
  328.8 11.8 %collective-permute-start.31 = (bf16[2,2,160,384]{3,2,1,0:T(8,128)(2,1)S(1)}, bf16[2,2,160,384]{3,2,1,0:T(8,128)(2,1)S(1)}, u32[]{:S(2)}, u32[]{:S(2)}) collective-permute-start(bf16[2,2,160,384]{3,2,1,0:T(8,128)(2,1)S(1)} %fusion.4), channel_id=1, source_target_pairs={{0,8},{4,12},{8,0},{12,4},{16,24},{20,28},{24,16},{28,20},{1,9},{5... | collective-permute-start | bytes 1474568 | tf_op jit(solution)/shard_map/ppermute | solution.py:65
  339.0 8.1 %collective-permute-start.29 = (bf16[2,152,384]{2,1,0:T(8,128)(2,1)S(1)}, bf16[2,152,384]{2,1,0:T(8,128)(2,1)S(1)}, u32[]{:S(2)}, u32[]{:S(2)}) collective-permute-start(bf16[2,152,384]{2,1,0:T(8,128)(2,1)S(1)} %fusion.11), channel_id=1, source_target_pairs={{0,2},{1,3},{2,0},{3,1},{4,6},{5,7},{6,4},{7,5},{8,10},{9,11},{10,... | collective-permute-start | bytes 700424 | tf_op jit(solution)/shard_map/ppermute | solution.py:65
  340.8 9.0 %collective-permute-start.32 = (bf16[2,160,384]{2,1,0:T(8,128)(2,1)S(1)}, bf16[2,160,384]{2,1,0:T(8,128)(2,1)S(1)}, u32[]{:S(2)}, u32[]{:S(2)}) collective-permute-start(bf16[2,160,384]{2,1,0:T(8,128)(2,1)S(1)} %fusion.10), channel_id=1, source_target_pairs={{0,2},{1,3},{2,0},{3,1},{4,6},{5,7},{6,4},{7,5},{8,10},{9,11},{10,... | collective-permute-start | bytes 737288 | tf_op jit(solution)/shard_map/ppermute | solution.py:65
  347.2 4.9 %collective-permute-start.30 = (bf16[152,384]{1,0:T(8,128)(2,1)S(1)}, bf16[152,384]{1,0:T(8,128)(2,1)S(1)}, u32[]{:S(2)}, u32[]{:S(2)}) collective-permute-start(bf16[152,384]{1,0:T(8,128)(2,1)S(1)} %fusion.15), channel_id=1, source_target_pairs={{0,8},{4,12},{8,0},{12,4},{16,24},{20,28},{24,16},{28,20},{1,9},{5... | collective-permute-start | bytes 350216 | tf_op jit(solution)/shard_map/ppermute | solution.py:65
  349.9 4.9 %collective-permute-start.33 = (bf16[160,384]{1,0:T(8,128)(2,1)S(1)}, bf16[160,384]{1,0:T(8,128)(2,1)S(1)}, u32[]{:S(2)}, u32[]{:S(2)}) collective-permute-start(bf16[160,384]{1,0:T(8,128)(2,1)S(1)} %fusion.14), channel_id=1, source_target_pairs={{0,4},{4,0},{8,12},{12,8},{16,20},{20,16},{24,28},{28,24},{1,5},{5... | collective-permute-start | bytes 368648 | tf_op jit(solution)/shard_map/ppermute | solution.py:65
  355.1 8.9 %collective-permute-start.41 = (bf16[264,384]{1,0:T(8,128)(2,1)S(1)}, bf16[264,384]{1,0:T(8,128)(2,1)S(1)}, u32[]{:S(2)}, u32[]{:S(2)}) collective-permute-start(bf16[264,384]{1,0:T(8,128)(2,1)S(1)} %pad_maximum_fusion.16), channel_id=1, source_target_pairs={{0,16},{4,20},{8,24},{12,28},{16,0},{20,4},{24,8},{28,12},{1,17},{... | collective-permute-start | bytes 608264 | tf_op jit(solution)/shard_map/ppermute | solution.py:65
  369.9 4.4 %collective-permute-start.47 = (f32[2]{0:T(128)S(1)}, f32[2]{0:T(128)S(1)}, u32[]{:S(2)}, u32[]{:S(2)}) collective-permute-start(f32[2]{0:T(128)S(1)} %pad_maximum_fusion.32), channel_id=1, source_target_pairs={{0,16},{4,20},{8,24},{12,28},{16,0},{20,4},{24,8},{28,12},{1,17},{... | collective-permute-start | bytes 32 | tf_op jit(solution)/shard_map/ppermute | solution.py:65
  375.1 3.5 collective-permute-start.48
  379.3 3.5 collective-permute-start.49
  (35 other events, 627.4 us)

commit v3 on v2

--- a/solution.py
+++ b/solution.py
@@ -1,3 +1,4 @@
+import functools
 import math
 
 import jax
@@ -53,89 +54,54 @@
     return jnp.concatenate([jnp.cos(phases), jnp.sin(phases)], axis=1)
 
 
-def bit_count(axis):
-    size = lax.axis_size(axis)
-    count = size.bit_length() - 1
-    assert size == 1 << count
-    return count
-
-
-def flip(values, axis, bit):
-    size = lax.axis_size(axis)
-    return lax.ppermute(values, axis, [(i, i ^ (1 << bit)) for i in range(size)])
-
-
-def my_bit(axis, bit):
-    return (lax.axis_index(axis) >> bit) & 1
-
-
-def all_bits():
-    return [(axis, bit) for axis in ("dp", "head") for bit in reversed(range(bit_count(axis)))]
-
-
-def paths():
-    bits = all_bits()
-    top, near = bits[0], ("head", 0)
-    far = [("dp", bit) for bit in reversed(range(1, bit_count("dp") - 1))]
-    across = [("head", bit) for bit in reversed(range(1, bit_count("head")))]
-    side_bit = [("dp", 0)]
-    return top, far + across + side_bit, side_bit + across + far[::-1], near
-
-
-def pair_up(block, other, name, place):
-    low = my_bit(*name) == 0
+def behind(values, *others):
+    return lax.optimization_barrier((values,) + others)[0]
+
+
+def pair_up(block, other, low, place):
     return jnp.stack([jnp.where(low, block, other), jnp.where(low, other, block)], axis=place)
 
 
-def gather_bits(block, order):
-    rank = {name: place for place, name in enumerate(all_bits())}
-    shape = block.shape
-    held = []
-    for name in order:
-        place = sum(rank[have] < rank[name] for have in held)
-        block = pair_up(block, flip(block, *name), name, place)
-        held.append(name)
-    return block.reshape((-1,) + shape)
-
-
-def gather_two(block, cut):
-    _, path_a, path_b, near = paths()
-    halves = [gather_bits(block[:cut], path_a), gather_bits(block[cut:], path_b)]
-    both = jnp.concatenate(halves, axis=1)
-    both = pair_up(both, flip(both, *near), near, 1)
-    return both.reshape((-1,) + both.shape[2:])
-
-
-def scatter_bits(blocks, order):
-    names = sorted(order, key=all_bits().index)
-    total = blocks.reshape((2,) * len(names) + blocks.shape[1:])
-    for name in order:
-        place = names.index(name)
-        bit = my_bit(*name)
-        keep = lax.dynamic_index_in_dim(total, bit, place, keepdims=False)
-        send = lax.dynamic_index_in_dim(total, 1 - bit, place, keepdims=False)
-        got = flip(send.astype(jnp.bfloat16), *name)
-        total = keep.astype(jnp.float32) + got.astype(jnp.float32)
-        names.remove(name)
-    return total
-
-
-def scatter_two(blocks, cut):
-    _, path_a, path_b, near = paths()
-    halved = blocks.reshape((-1, 2) + blocks.shape[1:])
-    bit = my_bit(*near)
-    keep = lax.dynamic_index_in_dim(halved, bit, 1, keepdims=False)
-    got = flip(lax.dynamic_index_in_dim(halved, 1 - bit, 1, keepdims=False), *near)
-    total = keep.astype(jnp.float32) + got.astype(jnp.float32)
-    first = scatter_bits(total[:, :cut], path_a[::-1])
-    second = scatter_bits(total[:, cut:], path_b[::-1])
-    return jnp.concatenate([first, second], axis=0)
-
-
-def sum_bits(values, order):
-    for name in order:
-        values = values + flip(values, *name)
-    return values
+def class_count():
+    return lax.axis_size("dp") * lax.axis_size("head") // 4
+
+
+def last_bit():
+    return lax.axis_index("head") % 2
+
+
+def exchange(values, mask):
+    size = lax.axis_size("dp") * lax.axis_size("head")
+    return lax.ppermute(values, ("dp", "head"), [(i, i ^ mask) for i in range(size)])
+
+
+def across_classes(blocks):
+    count = class_count()
+    groups = [
+        [(high * count + k) * 2 + last for k in range(count)] for high in range(2) for last in range(2)
+    ]
+    return lax.all_to_all(
+        blocks, ("dp", "head"), split_axis=0, concat_axis=0, axis_index_groups=groups, tiled=True
+    )
+
+
+def gather_classes(block):
+    return across_classes(jnp.broadcast_to(block[None], (class_count(),) + block.shape))
+
+
+def finish_gather(both, parts):
+    other = exchange(both, 1)
+    low = last_bit() == 0
+    joined, at = [], 0
+    for rows in parts:
+        piece = pair_up(both[:, at : at + rows], other[:, at : at + rows], low, 1)
+        joined.append(piece.reshape((-1,) + piece.shape[2:]))
+        at += rows
+    return joined
+
+
+def to_all(blocks):
+    return lax.all_to_all(blocks, ("dp", "head"), split_axis=0, concat_axis=0, tiled=True)
 
 
 def strips_of(values):
@@ -151,16 +117,6 @@
     return strips
 
 
-def join_strips(strips):
-    mine = lax.axis_index("head")
-    shape = strips[0].shape
-    whole_shape = (shape[0], len(strips)) + shape[1:]
-    joined = jnp.zeros(whole_shape, strips[0].dtype)
-    for far, strip in enumerate(strips):
-        joined = lax.dynamic_update_slice_in_dim(joined, strip[:, None], mine ^ far, axis=1)
-    return joined.reshape((shape[0], len(strips) * shape[1]) + shape[2:])
-
-
 NN = (((1,), (0,)), ((), ()))
 NT = (((1,), (1,)), ((), ()))
 TN = (((0,), (0,)), ((), ()))
@@ -212,19 +168,25 @@
 CHUNK = 128
 
 
-def attention_kernel(
+def attention_kernel(parts, places, scalars, middle, *refs):
+    attention_body(places, scalars, middle, refs[:parts], *refs[parts:])
+
+
+def attention_body(
+    places,
     scalars,
     middle,
-    noise,
+    strips,
     gains,
     member,
     qkv_w,
     out_w,
+    order,
     down_out,
-    qkv_grad,
-    out_grad,
+    shares,
     sums_out,
     loss_out,
+    noise,
     qkv_wt,
     normed,
     qkv_t,
@@ -253,6 +215,7 @@
         qkv_acc[...] = jnp.zeros_like(qkv_acc)
         out_acc[...] = jnp.zeros_like(out_acc)
 
+    join_strips(places, strips, noise)
     load = lambda at: middle[0, pl.ds(at, CHUNK), :]
     mean, inverse = norm_sums(load, pixels, channels, member[...])
     gain, shift = gains[4:5], gains[5:6]
@@ -300,7 +263,7 @@
         row = (pixel // width).astype(jnp.float32)
         col = (pixel % width).astype(jnp.float32)
         valid = jnp.where((row >= width - high) & (col < wide), 1.0, 0.0)
-        residue = total[:, :half] - noise[0, pl.ds(at, CHUNK), :].astype(jnp.float32)
+        residue = total[:, :half] - noise[pl.ds(at, CHUNK), :].astype(jnp.float32)
         weight = jax.nn.sigmoid(total[:, half:])
         blended = weight * beta_log + (1.0 - weight) * tilde_log
         spread = jnp.exp(tilde_log - blended)
@@ -376,43 +339,44 @@
 
     @pl.when(sample == pl.num_programs(0) - 1)
     def _():
-        qkv_grad[...] = qkv_acc[...].astype(jnp.bfloat16)
-        out_grad[...] = out_acc[...].astype(jnp.bfloat16)
-
-
-def attention_block(scalars, middle, noise, gains, member, qkv_w, out_w):
+        wide = 3 * channels
+        shares[:, 0:wide] = mm(order[...], qkv_acc[...].astype(jnp.bfloat16)).astype(jnp.bfloat16)
+        shares[:, wide:] = mm(order[...], out_acc[...].astype(jnp.bfloat16)).astype(jnp.bfloat16)
+
+
+def attention_block(places, scalars, middle, strips, gains, member, qkv_w, out_w, order):
+    parts = len(strips)
     samples, pixels, channels = middle.shape
     half = channels // 2
     bf, f32 = jnp.bfloat16, jnp.float32
-    whole = lambda *shape: pl.BlockSpec(shape, lambda s: (0,) * len(shape))
-    each = lambda *shape: pl.BlockSpec((1,) + shape, lambda s: (s, 0, 0))
     return pl.pallas_call(
-        attention_kernel,
+        functools.partial(attention_kernel, parts),
         grid=(samples,),
         in_specs=[
             pl.BlockSpec(memory_space=pltpu.SMEM),
+            pl.BlockSpec(memory_space=pltpu.SMEM),
             each(pixels, channels),
-            each(pixels, half),
+            *[each(pixels // parts, half)] * parts,
             whole(8, channels),
             whole(channels, channels),
             whole(channels, 3 * channels),
             whole(channels, channels),
+            whole(channels, channels),
         ],
         out_specs=[
             each(pixels, channels),
-            whole(channels, 3 * channels),
-            whole(channels, channels),
+            whole(channels, 4 * channels),
             each(8, channels),
             each(8, half),
         ],
         out_shape=[
             jax.ShapeDtypeStruct((samples, pixels, channels), bf),
-            jax.ShapeDtypeStruct((channels, 3 * channels), bf),
-            jax.ShapeDtypeStruct((channels, channels), bf),
+            jax.ShapeDtypeStruct((channels, 4 * channels), bf),
             jax.ShapeDtypeStruct((samples, 8, channels), f32),
             jax.ShapeDtypeStruct((samples, 8, half), f32),
         ],
         scratch_shapes=[
+            pltpu.VMEM((pixels, half), bf),
             pltpu.VMEM((3 * channels, channels), bf),
             pltpu.VMEM((pixels, channels), bf),
             pltpu.VMEM((3 * channels, pixels), bf),
@@ -434,7 +398,7 @@
             bytes_accessed=8 * samples * pixels * channels,
             transcendentals=samples * HEADS * pixels * pixels,
         ),
-    )(scalars, middle, noise, gains, member, qkv_w, out_w)
+    )(places, scalars, middle, *strips, gains, member, qkv_w, out_w, order)
 
 
 def fill(padded, at, values, width):
@@ -474,8 +438,16 @@
     return total
 
 
-def first_kernel(images, gains, member, weight, inner, hidden, stats, padded):
+def join_strips(places, strips, joined):
+    rows = strips[0].shape[1]
+    for far, strip in enumerate(strips):
+        joined[pl.ds(pl.multiple_of(places[far] * rows, rows), rows), :] = strip[0]
+
+
+def first_kernel(parts, places, *refs):
+    strips, (gains, member, weight, inner, hidden, stats, images, padded) = refs[:parts], refs[parts:]
     _, pixels, channels = images.shape
+    join_strips(places, strips, images.at[0])
     width = side(pixels)
     wide = 3 * channels
     load = lambda at: images[0, pl.ds(at, CHUNK), :].astype(jnp.float32)
@@ -521,8 +493,7 @@
     )
 
 
-def weights_kernel(hidden, grad, out, padded, total):
-    sample = pl.program_id(0)
+def weights_sums(hidden, grad, padded, total):
     _, pixels, channels = hidden.shape
     width = side(pixels)
     wide = 3 * channels
@@ -534,7 +505,7 @@
 
     chunks(pixels, CHUNK, spread, 0)
 
-    @pl.when(sample == 0)
+    @pl.when(pl.program_id(0) == 0)
     def _():
         total[...] = jnp.zeros_like(total)
 
@@ -543,9 +514,35 @@
             padded[i * width : i * width + pixels, :], grad[0], TN
         )
 
-    @pl.when(sample == pl.num_programs(0) - 1)
+
+def weights_kernel(hidden, grad, out, padded, total):
+    weights_sums(hidden, grad, padded, total)
+
+    @pl.when(pl.program_id(0) == pl.num_programs(0) - 1)
     def _():
         out[...] = total[...].astype(jnp.bfloat16)
+
+
+def shares_kernel(extra, place, hidden, grad, *refs):
+    others, (mine, theirs, padded, total) = refs[:extra], refs[extra:]
+    weights_sums(hidden, grad, padded, total)
+    classes = mine.shape[0]
+    channels = total.shape[1]
+    rows = total.shape[0] // (2 * classes)
+
+    @pl.when(pl.program_id(0) == pl.num_programs(0) - 1)
+    def _():
+        for far in range(classes):
+            for last, out in enumerate((mine, theirs)):
+                owner = far * 2 + (place[0] ^ last)
+                parts = [total[pl.ds(pl.multiple_of(owner * rows, 8), rows), :]]
+                for other in others:
+                    lines = other.shape[0] // (2 * classes)
+                    at = (last * classes + far) * lines
+                    for k in range(other.shape[1] // channels):
+                        piece = other[at : at + lines, k * channels : (k + 1) * channels]
+                        parts.append(piece.astype(jnp.float32))
+                out[far] = jnp.concatenate(parts, axis=0).astype(jnp.bfloat16)
 
 
 def turn_taps(weight, turned):
@@ -670,11 +667,14 @@
     few_f = sized(f32, samples, 8, channels)
     flops = 18 * samples * pixels * channels * channels
 
-    def first(images, gains, member, weight):
+    def first(places, strips, gains, member, weight):
+        parts = len(strips)
         return per_sample(
-            first_kernel, samples, [act, gain_spec, member_spec, weight_spec],
-            [(act, act_f), (act, act_b), (few, few_f)], [padded], flops,
-            images, gains, member, weight,
+            functools.partial(first_kernel, parts), samples,
+            [pl.BlockSpec(memory_space=pltpu.SMEM)] + [each(pixels // parts, channels)] * parts
+            + [gain_spec, member_spec, weight_spec],
+            [(act, act_f), (act, act_b), (few, few_f), (act, act_b)], [padded], flops,
+            places, *strips, gains, member, weight,
         )
 
     def second(inner, images, stats, film, gains, weight):
@@ -684,12 +684,33 @@
             inner, images, stats, film, gains, weight,
         )
 
-    def weights(hidden, grad):
+    def weights(hidden, grad, place, classes, others=()):
+        scratch = [padded, pltpu.VMEM((9 * channels, channels), f32)]
+        conv_rows = 9 * channels // (2 * classes)
+        more = [other.shape[0] * other.shape[1] // (2 * classes * channels) for other in others]
+        if conv_rows % 8:
+            (whole_grad,) = per_sample(
+                weights_kernel, samples, [act, act],
+                [(weight_spec, sized(bf, 9 * channels, channels))], scratch, flops, hidden, grad,
+            )
+            blocks = whole_grad.reshape(2 * classes, conv_rows, channels)
+            both = []
+            for last in range(2):
+                owner = place[0] ^ last
+                cut = blocks.reshape(classes, 2, conv_rows, channels)
+                parts = [lax.dynamic_index_in_dim(cut, owner, 1, keepdims=False)]
+                for other in others:
+                    cut = other.reshape(2, classes, -1, other.shape[1] // channels, channels)[last]
+                    parts.append(jnp.moveaxis(cut, 2, 1).reshape(classes, -1, channels))
+                both.append(jnp.concatenate(parts, axis=1))
+            return both
+        shape = (classes, conv_rows + sum(more), channels)
+        out = (whole(*shape), sized(bf, *shape))
         return per_sample(
-            weights_kernel, samples, [act, act],
-            [(weight_spec, sized(bf, 9 * channels, channels))],
-            [padded, pltpu.VMEM((9 * channels, channels), f32)], flops, hidden, grad,
-        )[0]
+            functools.partial(shares_kernel, len(others)), samples,
+            [pl.BlockSpec(memory_space=pltpu.SMEM), act, act] + [whole(*o.shape) for o in others],
+            [out, out], scratch, flops, place, hidden, grad, *others,
+        )
 
     def second_back(grad, inner, stats, film, gains, member, weight):
         return per_sample(
@@ -744,7 +765,6 @@
 ):
     devices = lax.axis_size("dp") * lax.axis_size("head")
     device = lax.axis_index("dp") * lax.axis_size("head") + lax.axis_index("head")
-    bits = all_bits()
     channels = images.shape[-1]
     wide = film_master.shape[1]
     half_width = channels // 2
@@ -762,34 +782,29 @@
         ]
     )
     small = jnp.pad(small, (0, 8 * channels - small.shape[0])).reshape(8, channels)
-    top, _, _, _ = paths()
-    is_top = my_bit(*top) == 1
-    ours = jnp.concatenate([conv_master, small]).astype(jnp.bfloat16)
-    theirs = flip(ours, *top)
-    rest = jnp.concatenate(
-        [film_master.reshape(-1, channels), qkv_master.reshape(-1, channels), out_master]
-    ).astype(jnp.bfloat16)
-    rest_two = pair_up(rest, flip(rest, *top), top, 0)
-    one = jnp.where(is_top, theirs, ours)
-    two = jnp.where(is_top, ours, theirs)
-    small_two = jnp.stack([one[conv_rows:], two[conv_rows:]]).reshape(-1, channels)
-    cut = conv_rows // 16 * 8
-    group_one = gather_two(jnp.concatenate([one[:conv_rows], small_two]), cut)
+    classes = class_count()
+    top_mask = devices // 2
+    is_top = device >= top_mask
+    film_cut = film_rows * wide // channels
+    ours = jnp.concatenate([conv_master, small, film_master.reshape(-1, channels)])
+    ours = ours.astype(jnp.bfloat16)
+    theirs = exchange(ours, top_mask)
     strips = strips_of(images)
-    held_rows = rest.shape[0]
-    group_two = gather_two(
-        jnp.concatenate([two[:conv_rows], rest_two.reshape(-1, channels)]),
-        (conv_rows + 2 * held_rows) // 16 * 8,
-    )
-    taps_one = group_one[:, :conv_rows].reshape(-1, channels)
-    taps_two = group_two[:, :conv_rows].reshape(-1, channels)
-    smalls = jnp.moveaxis(group_one[:, conv_rows:].reshape(-1, 2, 8 * channels), 0, 1)
-    others = jnp.moveaxis(group_two[:, conv_rows:].reshape(-1, 2, held_rows, channels), 0, 1)
-    others = others.reshape(devices, held_rows, channels)
-    film_own_rows = film_rows * wide // channels
-    film_w = others[:, :film_own_rows].reshape(-1, wide)
-    qkv_w = others[:, film_own_rows : film_own_rows + 3 * out_rows].reshape(channels, 3 * channels)
-    out_w = others[:, film_own_rows + 3 * out_rows :].reshape(channels, channels)
+    low, high = jnp.where(is_top, theirs, ours), jnp.where(is_top, ours, theirs)
+    small_two = [part[conv_rows : conv_rows + 8] for part in (low, high)]
+    film_two = [part[conv_rows + 8 :] for part in (low, high)]
+    every_one = gather_classes(jnp.concatenate([low[:conv_rows]] + small_two + film_two))
+    rest = jnp.concatenate([qkv_master.reshape(-1, channels), out_master]).astype(jnp.bfloat16)
+    rest = behind(rest, theirs)
+    rest_two = pair_up(rest, exchange(rest, top_mask), jnp.logical_not(is_top), 0)
+    every_two = gather_classes(
+        behind(jnp.concatenate([high[:conv_rows], rest_two.reshape(-1, channels)]), every_one)
+    )
+    taps_one, smalls, film_w = finish_gather(
+        behind(every_one, *strips), [conv_rows, 16, 2 * film_cut]
+    )
+    taps_one = taps_one.reshape(-1, channels)
+    smalls = jnp.moveaxis(smalls.reshape(-1, 2, 8 * channels), 0, 1)
     smalls = smalls.reshape(devices, -1).astype(jnp.float32)
     gain_f = smalls[:, : gains.size].reshape(channels, 6)
     dp_smalls = smalls.reshape(lax.axis_size("dp"), lax.axis_size("head"), -1)[:, 0, gains.size :]
@@ -798,9 +813,10 @@
     times_all = (times[:, 0] * 64.0 + times[:, 1]).reshape(-1).astype(jnp.int32)
     divisor = jnp.sum(extents_all[:, 0] * extents_all[:, 1])
 
-    pictures = join_strips(strips)
-    target = join_strips(strips_of(noise))
-    samples, rows, width_px, _ = pictures.shape
+    parts = lax.axis_size("head")
+    samples, strip_rows, width_px, _ = strips[0].shape
+    places = lax.axis_index("head") ^ jnp.arange(parts, dtype=jnp.int32)
+    rows = strip_rows * parts
     pixels = rows * width_px
     first = lax.axis_index("head") * samples
     own_times = lax.dynamic_slice_in_dim(timesteps, first, samples)
@@ -809,12 +825,6 @@
     log_beta, log_tilde, factor = plan(own_times)
     embedded_all = jax.nn.silu(embed(times_all, wide)).astype(jnp.bfloat16)
     embedded = jax.nn.silu(embed(own_times, wide)).astype(jnp.bfloat16)
-    film_out = lax.dot_general(
-        embedded, film_w, (((1,), (1,)), ((), ())), preferred_element_type=jnp.float32
-    )
-    film = jnp.pad(film_out.reshape(samples, 2, channels), ((0, 0), (0, 6), (0, 0)))
-    scale = 1.0 + film_out[:, :channels]
-    source = pictures.reshape(samples, pixels, channels)
     gains_t = jnp.pad(gain_f.T, ((0, 2), (0, 0)))
     member = jnp.asarray(np.kron(np.eye(GROUPS), np.ones((channels // GROUPS,) * 2)), jnp.bfloat16)
     scalars = jnp.stack(
@@ -823,15 +833,43 @@
         axis=1,
     )
     first_call, second_call, weights, second_back, first_back = block_calls(samples, pixels, channels)
-    inner, hidden_one, stats = first_call(source, gains_t, member, taps_one)
+    flat = lambda values: [v.reshape(samples, strip_rows * width_px, -1) for v in values]
+    inner, hidden_one, stats, source = first_call(places, flat(strips), gains_t, member, taps_one)
+    taps_two, others = finish_gather(behind(every_two, inner), [conv_rows, 8 * out_rows])
+    taps_two = taps_two.reshape(-1, channels)
+    film_w = jnp.moveaxis(film_w.reshape(-1, 2, film_cut, channels), 0, 1).reshape(-1, wide)
+    others = jnp.moveaxis(others.reshape(-1, 2, 4 * out_rows, channels), 0, 1)
+    others = others.reshape(devices, 4 * out_rows, channels)
+    qkv_w = others[:, : 3 * out_rows].reshape(channels, 3 * channels)
+    out_w = others[:, 3 * out_rows :].reshape(channels, channels)
+    noise_strips = strips_of(behind(noise, inner))
+    film_out = lax.dot_general(
+        embedded, film_w, (((1,), (1,)), ((), ())), preferred_element_type=jnp.float32
+    )
+    film = jnp.pad(film_out.reshape(samples, 2, channels), ((0, 0), (0, 6), (0, 0)))
+    scale = 1.0 + film_out[:, :channels]
     middle, hidden_two = second_call(inner, source, stats, film, gains_t, taps_two)
-    grad_two_b, qkv_grad, out_grad, sums_three, losses = attention_block(
-        scalars, middle, target.reshape(samples, pixels, half_width), gains_t, member, qkv_w, out_w
+    my_last = last_bit()
+    place = my_last.reshape(1).astype(jnp.int32)
+    line = jnp.arange(channels, dtype=jnp.int32)
+    owner, spot = line // out_rows, line % out_rows
+    source_device = (
+        (owner % 2) * 2 * classes + (owner // 2 % classes) * 2 + (my_last ^ (owner // (2 * classes)))
+    )
+    order = (line[None, :] == (source_device * out_rows + spot)[:, None]).astype(jnp.bfloat16)
+    grad_two_b, shares, sums_three, losses = attention_block(
+        places, scalars, middle, flat(noise_strips), gains_t, member, qkv_w, out_w, order
     )
     loss_local = jnp.sum(losses)
-    conv_two_grad = weights(hidden_two, grad_two_b)
+    two_shares = weights(hidden_two, grad_two_b, place, classes, (shares,))
+    grad_two_b = behind(grad_two_b, *two_shares)
     grad_one_b, sums_two = second_back(grad_two_b, inner, stats, film, gains_t, member, taps_two)
-    conv_one_grad = weights(hidden_one, grad_one_b)
+    two_sent = (two_shares[0].astype(jnp.float32) + exchange(two_shares[1], 1).astype(jnp.float32)).astype(jnp.bfloat16)
+    share_two = jnp.sum(across_classes(two_sent).astype(jnp.float32), axis=0)
+    one_shares = weights(behind(hidden_one, two_sent), grad_one_b, place, classes)
+    one_sent = (one_shares[0].astype(jnp.float32) + exchange(one_shares[1], 1).astype(jnp.float32)).astype(jnp.bfloat16)
+    share_one = jnp.sum(across_classes(one_sent).astype(jnp.float32), axis=0)
+    grad_one_b = behind(grad_one_b, share_two, one_sent)
     sums_one = first_back(grad_one_b, source, stats, gains_t, taps_one)
     gain_one, bias_one = jnp.sum(sums_one[:, 0], axis=0), jnp.sum(sums_one[:, 1], axis=0)
     gain_two, bias_two = jnp.sum(sums_two[:, 0] * scale, axis=0), jnp.sum(sums_two[:, 1] * scale, axis=0)
@@ -839,53 +877,48 @@
     grad_scale = sums_two[:, 0] * gains_t[2] + sums_two[:, 1] * gains_t[3]
     film_grad_b = jnp.concatenate([grad_scale, sums_two[:, 1]], axis=1).astype(jnp.bfloat16)
 
-    both_grads = jnp.concatenate(
-        [qkv_grad.reshape(2, -1, 3 * out_rows, channels), out_grad.reshape(2, -1, out_rows, channels)],
-        axis=2,
-    )
-    both_grads = jnp.moveaxis(both_grads, 0, 1).reshape(devices // 2, 8 * out_rows, channels)
-    two_grads = jnp.concatenate(
-        [conv_two_grad.reshape(-1, conv_rows, channels), both_grads], axis=1
-    )
-    share_two = scatter_two(two_grads, (conv_rows + 8 * out_rows) // 16 * 8)
-    share_one = scatter_two(conv_one_grad.reshape(-1, conv_rows, channels), cut)
-    small_shares = share_two[conv_rows:].reshape(2, 4 * out_rows, channels)
-    mine = jnp.concatenate(
+    small_shares = share_two[conv_rows:].reshape(4, 2, out_rows, channels)
+    keep_two = jnp.where(is_top, small_shares[:, 1], small_shares[:, 0])
+    send_two = jnp.where(is_top, small_shares[:, 0], small_shares[:, 1])
+    send_two = jnp.concatenate([share_two[:conv_rows], send_two.reshape(-1, channels)])
+    got_two = exchange(send_two.astype(jnp.bfloat16), top_mask).astype(jnp.float32)
+    got_one = exchange(share_one.astype(jnp.bfloat16), top_mask).astype(jnp.float32)
+    conv_g = jnp.where(is_top, share_two[:conv_rows] + got_two[:conv_rows], share_one + got_one)
+    small_g = keep_two + got_two[conv_rows:].reshape(keep_two.shape)
+    qkv_g = jnp.concatenate([small_g[0], small_g[1], small_g[2]], axis=1)
+    out_g = small_g[3]
+
+    gain_grad = jnp.stack([gain_one, bias_one, gain_two, bias_two, gain_three, bias_three], axis=1)
+    common = jnp.concatenate([film_grad_b.astype(jnp.float32).reshape(-1), loss_local[None]])
+    parcel = jnp.concatenate(
         [
-            jnp.where(is_top, share_two[:conv_rows], share_one),
-            jnp.where(is_top, small_shares[1], small_shares[0]),
-        ]
-    )
-    sent = jnp.concatenate(
-        [
-            jnp.where(is_top, share_one, share_two[:conv_rows]),
-            jnp.where(is_top, small_shares[0], small_shares[1]),
-        ]
-    )
-    summed = mine + flip(sent.astype(jnp.bfloat16), *top).astype(jnp.float32)
-    conv_g = summed[:conv_rows]
-    qkv_g = summed[conv_rows : conv_rows + 3 * out_rows].reshape(qkv_master.shape)
-    out_g = summed[conv_rows + 3 * out_rows :]
-
-    film_all = gather_bits(film_grad_b, bits).reshape(-1, film_grad_b.shape[1])
+            behind(gain_grad, share_one).reshape(devices, -1),
+            jnp.broadcast_to(common[None], (devices, common.shape[0])),
+        ],
+        axis=1,
+    )
+    length = parcel.shape[1]
+    parcel = jnp.pad(parcel, ((0, 0), (0, -length % 1024))).reshape(devices, -1, 128)
+    parcels = to_all(parcel).reshape(devices, -1)
+    gain_g = jnp.sum(parcels[:, : gains.size], axis=0).reshape(gains.shape)
+    film_all = parcels[:, gains.size : length - 1].reshape(-1, film_grad_b.shape[1])
+    loss_total = jnp.sum(parcels[:, length - 1])
     film_own = lax.dynamic_slice_in_dim(film_all, device * film_rows, film_rows, axis=1)
-    film_g = jnp.einsum("sf,se->fe", film_own, embedded_all, preferred_element_type=jnp.float32)
-    gain_grad = jnp.stack([gain_one, bias_one, gain_two, bias_two, gain_three, bias_three], axis=1)
-    gain_g = sum_bits(gain_grad, bits).reshape(devices, -1, 6)
-    gain_g = lax.dynamic_index_in_dim(gain_g, device, 0, keepdims=False)
+    film_g = jnp.einsum(
+        "sf,se->fe", film_own.astype(jnp.bfloat16), embedded_all, preferred_element_type=jnp.float32
+    )
     reduced = (film_g, conv_g, qkv_g, out_g, gain_g)
     squares = jnp.zeros((), jnp.float32)
     for gradient in reduced:
         squares = squares + jnp.sum(gradient * gradient)
-    totals = sum_bits(jnp.stack([squares, loss_local]), bits)
-    grad_norm = jnp.sqrt(totals[0])
+    grad_norm = jnp.sqrt(jnp.sum(to_all(jnp.broadcast_to(squares, (devices, 8, 128)))[:, 0, 0]))
     clip_factor = jnp.minimum(1.0, THRESHOLD / (grad_norm + 1e-06))
     film_res = adamw(film_master, film_g, film_first, film_second, RATE_MATRIX, DECAY, clip_factor)
     conv_res = adamw(conv_master, conv_g, conv_first, conv_second, RATE_MATRIX, DECAY, clip_factor)
     qkv_res = adamw(qkv_master, qkv_g, qkv_first, qkv_second, RATE_MATRIX, DECAY, clip_factor)
     out_res = adamw(out_master, out_g, out_first, out_second, RATE_MATRIX, DECAY, clip_factor)
     gain_res = adamw(gains, gain_g, gain_first, gain_second, RATE_GAIN, 0.0, clip_factor)
-    loss_parts = jnp.stack([totals[1], divisor])
+    loss_parts = jnp.stack([loss_total, divisor])
     return (
         loss_parts,
         grad_norm,

time: 404 us -> 352 us (0.87)
  waiting for transfers between devices: 92.8 us -> 65.7 us
  starting transfers between devices: 62.2 us -> 43.6 us
  Pallas kernels: 160 us -> 172 us
  local copies, waits for them, and re-layouts: 33.8 us -> 22.6 us
    ppermute x46 -> x8, waiting for transfers between devices: 74.8 us -> 17.5 us  [exchange(): lax.ppermute(values, ('dp', 'head'), [(i, i ^ mask) for i in range(size)])]
    ppermute x46 -> x8, starting transfers between devices: 58 us -> 13.1 us  [exchange(): lax.ppermute(values, ('dp', 'head'), [(i, i ^ mask) for i in range(size)])]
    all_to_all x0 -> x6, starting transfers between devices: none -> 26.4 us  [the longest x4 17.3 us: across_classes(): lax.all_to_all(blocks, ('dp', 'head'), split_axis=0, concat_axis=0, axis_...]
    all_to_all x0 -> x6, waiting for transfers between devices: none -> 16.4 us  [the longest x2 12.9 us: to_all(): lax.all_to_all(blocks, ('dp', 'head'), split_axis=0, concat_axis=0, tiled...]
    ppermute x6, waiting for transfers between devices: 18 us -> 31.8 us  [strips_of(): strip = lax.ppermute(strip, 'head', [(i, i ^ far) for i in range(parts)])]
    pallas_call x6, Pallas kernels: 84.7 us -> 95.9 us  [per_sample(): pl.pallas_call(kernel, grid=(samples,), in_specs=in_specs, out_specs=[spe...]
    convert_element_type x0 -> x6, other arithmetic: none -> 6.99 us  [the longest x1 3.35 us: body(): (two_shares[0].astype(jnp.float32) + exchange(two_shares[1], 1).astype(jn...]
    slice x16 -> x12, local copies, waits for them, and re-layouts: 7.38 us -> 0.4 us  [the longest x1 0.11 us: body(): out_w = others[:, 3 * out_rows:].reshape(channels, channels)]
  transfers between devices with their start and end apart: 52 -> 20, of which waited for: 26 -> 9; matrix products, arithmetic and copies ran while one was open for 11% -> 12% of each run, Pallas kernels for 10% -> 21%
where the time goes in v3:
time: 352 us; the launch traced here: 347 us
  Pallas kernels  172 us (49%)
  waiting for transfers between devices  65.7 us (19%)
  starting transfers between devices  43.6 us (12%)
  other arithmetic  35.1 us (10%)
  local copies, waits for them, and re-layouts  22.6 us (6%)
  between operations  6.8 us (2%)
    pallas_call x6, Pallas kernels, per_sample(): pl.pallas_call(kernel, grid=(samples,), in_specs=in_specs, out_specs=[spe...  95.9 us
    pallas_call x1, Pallas kernels, attention_block(): pl.pallas_call(functools.partial(attention_kernel, parts), grid=(samples,...  75.8 us
    ppermute x6, waiting for transfers between devices, strips_of(): strip = lax.ppermute(strip, 'head', [(i, i ^ far) for i in range(parts)])  31.8 us
    ppermute x8, waiting for transfers between devices, exchange(): lax.ppermute(values, ('dp', 'head'), [(i, i ^ mask) for i in range(size)])  17.5 us
    all_to_all x4, starting transfers between devices, across_classes(): lax.all_to_all(blocks, ('dp', 'head'), split_axis=0, concat_axis=0, axis_...  17.3 us
    ppermute x8, starting transfers between devices, exchange(): lax.ppermute(values, ('dp', 'head'), [(i, i ^ mask) for i in range(size)])  13.1 us
    all_to_all x2, waiting for transfers between devices, to_all(): lax.all_to_all(blocks, ('dp', 'head'), split_axis=0, concat_axis=0, tiled...  12.9 us
    all_to_all x2, starting transfers between devices, to_all(): lax.all_to_all(blocks, ('dp', 'head'), split_axis=0, concat_axis=0, tiled...  9.09 us
  transfers between devices with their start and end apart: 20, of which 9 were waited for; matrix products, arithmetic and copies ran while one was open for 12% of the time, Pallas kernels for 21%

profile of v3, /device:TPU:0, one launch (start us, length us, event | category | flops | bytes accessed | tf_op | source)
XLA Modules:
  0.0 346.8 jit_solution(10546299302716014675)
XLA Ops:
  3.2 1.0 convert.57
  4.2 0.9 convert.62
  5.1 4.1 %collective-permute-start = (bf16[272,384]{1,0:T(8,128)(2,1)S(1)}, bf16[272,384]{1,0:T(8,128)(2,1)S(1)}, u32[]{:S(2)}, u32[]{:S(2)}) collective-permute-start(bf16[272,384]{1,0:T(8,128)(2,1)S(1)} %pad_maximum_fusion.7), channel_id=1, source_target_pairs={{0,16},{1,17},{2,18},{3,19},{4,20},{5,21},{6,22},{7,23},{8,24},{9,... | collective-permute-start | bytes 626696 | tf_op jit(solution)/shard_map/ppermute | solution.py:75
  9.2 9.6 %collective-permute-done = bf16[272,384]{1,0:T(8,128)(2,1)S(1)} collective-permute-done((bf16[272,384]{1,0:T(8,128)(2,1)S(1)}, bf16[272,384]{1,0:T(8,128)(2,1)S(1)}, u32[]{:S(2)}, u32[]{:S(2)}) %collective-permute-start) | collective-permute-done | bytes 208928 | tf_op jit(solution)/shard_map/ppermute | solution.py:75
  19.1 1.5 broadcast_in_dim.10
  20.6 3.9 %all-to-all-start = ((bf16[8,328,384]{2,1,0:T(8,128)(2,1)}), bf16[8,328,384]{2,1,0:T(8,128)(2,1)S(1)}, u32[]{:S(2)}, u32[]{:S(2)}) async-start(bf16[8,328,384]{2,1,0:T(8,128)(2,1)} %broadcast_in_dim.10), calls=%async_computation | async-start | bytes 4030464 | tf_op jit(solution)/shard_map/all_to_all | solution.py:83
  24.5 2.5 constant_dynamic-slice_fusion.5
  26.9 2.0 collective-permute-start.2
  29.2 3.4 collective-permute-start.5
  32.7 25.5 %collective-permute-done.2 = bf16[2,8,32,384]{3,2,1,0:T(8,128)(2,1)} collective-permute-done((bf16[2,8,32,384]{3,2,1,0:T(8,128)(2,1)S(1)}, bf16[2,8,32,384]{3,2,1,0:T(8,128)(2,1)}, u32[]{:S(2)}, u32[]{:S(2)}) %collective-permute-start.2) | collective-permute-done | bytes 393248 | tf_op jit(solution)/shard_map/ppermute | solution.py:115
  58.1 6.4 %collective-permute-done.3 = bf16[2,8,32,384]{3,2,1,0:T(8,128)(2,1)} collective-permute-done((bf16[2,8,32,384]{3,2,1,0:T(8,128)(2,1)S(1)}, bf16[2,8,32,384]{3,2,1,0:T(8,128)(2,1)}, u32[]{:S(2)}, u32[]{:S(2)}) %collective-permute-start.3) | collective-permute-done | bytes 393248 | tf_op jit(solution)/shard_map/ppermute | solution.py:115
  64.5 0.9 collective-permute-start.4
  65.4 1.4 broadcast_in_dim.11
  66.8 4.5 %all-to-all-start.1 = ((bf16[8,312,384]{2,1,0:T(8,128)(2,1)}), bf16[8,312,384]{2,1,0:T(8,128)(2,1)}, u32[]{:S(2)}, u32[]{:S(2)}) async-start(bf16[8,312,384]{2,1,0:T(8,128)(2,1)} %broadcast_in_dim.11), calls=%async_computation.1 | async-start | bytes 3833856 | tf_op jit(solution)/shard_map/all_to_all | solution.py:83
  72.3 0.8 fusion.refs_8_
  73.2 1.6 select_bitcast_fusion.3
  75.0 1.8 copy.165
  76.9 0.9 select_bitcast_fusion.9
  78.8 15.5 %shard_map.323 = (f32[2,1024,384]{2,1,0:T(8,128)}, bf16[2,1024,384]{2,1,0:T(8,128)(2,1)}, f32[2,8,384]{2,1,0:T(8,128)}, bf16[2,1024,384]{2,1,0:T(8,128)(2,1)}) custom-call(s32[4]{0:T(128)} %iota_xor_fusion.places, bf16[2,256,384]{2,1,0:T(8,128)(2,1)} %bitcast.118, bf16[2,256,384]{2,1,0:T(8,128)(2,1)} %bitcast.7.refs_1_, ...), custom_call_target="tpu_custom_call" | custom-call | flops 5435817984 | bytes 5435817 | tf_op jit(solution)/shard_map/pallas_call | solution.py:639
  94.2 3.4 all-to-all-done.1
  99.5 1.2 select_bitcast_fusion.7
  103.8 1.4 collective-permute-start.9
  107.5 2.0 select_bitcast_fusion.1
  109.8 1.8 copy.168
  111.5 14.1 %shard_map.324 = (f32[2,1024,384]{2,1,0:T(8,128)}, bf16[2,1024,384]{2,1,0:T(8,128)(2,1)}) custom-call(f32[2,1024,384]{2,1,0:T(8,128)} %get-tuple-element.43.inner, bf16[2,1024,384]{2,1,0:T(8,128)(2,1)} %get-tuple-element.44.images, f32[2,8,384]{2,1,0:T(8,128)} %get-tuple-element.45.stats, f32[2,8,384]{2,1,0:T(8,128)} %pad.19.film, ...), custom_call_target="tpu_custom_call" | custom-call | flops 5435817984 | bytes 5435817 | tf_op jit(solution)/shard_map/pallas_call | solution.py:639
  125.6 1.4 select_bitcast_fusion.5
  127.7 1.4 reshape.277.refs_6_
  130.8 75.8 %shard_map.325 = (bf16[2,1024,384]{2,1,0:T(8,128)(2,1)}, bf16[384,1536]{1,0:T(8,128)(2,1)}, f32[2,8,384]{2,1,0:T(8,128)}, f32[2,8,192]{2,1,0:T(8,128)}) custom-call(s32[4]{0:T(128)} %iota_xor_fusion.places, f32[2,6]{1,0:T(2,128)} %stack.104.scalars, f32[2,1024,384]{2,1,0:T(8,128)} %get-tuple-element.49.middle, bf16[2,256,192]{2,1,0:T(8,128)(2,1)} %bitcast.120, ...), custom_call_target="tpu_custom_call" | custom-call | flops 24159191040 | bytes 6291456 | tf_op jit(solution)/shard_map/pallas_call | solution.py:352
  206.7 23.3 %shard_map.326 = (bf16[8,312,384]{2,1,0:T(8,128)(2,1)}, bf16[8,312,384]{2,1,0:T(8,128)(2,1)}) custom-call(s32[1]{0:T(128)} %bitcast.35.place, bf16[2,1024,384]{2,1,0:T(8,128)(2,1)} %get-tuple-element.52.hidden, bf16[2,1024,384]{2,1,0:T(8,128)(2,1)} %get-tuple-element.56.grad, bf16[384,1536]{1,0:T(8,128)(2,1)} %get-tuple-element.53.refs_0_), custom_call_target="tpu_custom_call" | custom-call | flops 5435817984 | bytes 5435817 | tf_op jit(solution)/shard_map/pallas_call | solution.py:639
  230.7 3.7 %collective-permute-done.10 = bf16[8,312,384]{2,1,0:T(8,128)(2,1)S(1)} collective-permute-done((bf16[8,312,384]{2,1,0:T(8,128)(2,1)}, bf16[8,312,384]{2,1,0:T(8,128)(2,1)S(1)}, u32[]{:S(2)}, u32[]{:S(2)}) %collective-permute-start.10) | collective-permute-done | bytes 1916960 | tf_op jit(solution)/shard_map/ppermute | solution.py:75
  234.5 3.3 add_convert_fusion
  237.8 3.6 %all-to-all-start.2 = ((bf16[8,312,384]{2,1,0:T(8,128)(2,1)}), bf16[8,312,384]{2,1,0:T(8,128)(2,1)S(1)}, u32[]{:S(2)}, u32[]{:S(2)}) async-start(bf16[8,312,384]{2,1,0:T(8,128)(2,1)} %add_convert_fusion), calls=%async_computation.2 | async-start | bytes 3833856 | tf_op jit(solution)/shard_map/all_to_all | solution.py:83
  241.4 16.6 %shard_map.327 = (bf16[2,1024,384]{2,1,0:T(8,128)(2,1)}, f32[2,8,384]{2,1,0:T(8,128)}) custom-call(bf16[2,1024,384]{2,1,0:T(8,128)(2,1)} %get-tuple-element.56.grad, f32[2,1024,384]{2,1,0:T(8,128)} %get-tuple-element.43.inner, f32[2,8,384]{2,1,0:T(8,128)} %get-tuple-element.45.stats, f32[2,8,384]{2,1,0:T(8,128)} %pad.19.film, f32[8,384]{1,0:T(8,128)} %pad.18.refs_4_.gains, ...), custom_call_target="tpu_custom_call" | custom-call | flops 5435817984 | bytes 5435817 | tf_op jit(solution)/shard_map/pallas_call | solution.py:639
  258.0 12.2 %shard_map.328 = (bf16[8,216,384]{2,1,0:T(8,128)(2,1)}, bf16[8,216,384]{2,1,0:T(8,128)(2,1)}) custom-call(s32[1]{0:T(128)} %bitcast.35.place, bf16[2,1024,384]{2,1,0:T(8,128)(2,1)} %get-tuple-element.59.hidden, bf16[2,1024,384]{2,1,0:T(8,128)(2,1)} %get-tuple-element.62.grad), custom_call_target="tpu_custom_call" | custom-call | flops 5435817984 | bytes 5435817 | tf_op jit(solution)/shard_map/pallas_call | solution.py:639
  270.6 2.9 collective-permute-done.11
  273.5 2.8 add_convert_fusion.1
  276.2 5.4 %all-to-all-start.3 = ((bf16[8,216,384]{2,1,0:T(8,128)(2,1)}), bf16[8,216,384]{2,1,0:T(8,128)(2,1)S(1)}, u32[]{:S(2)}, u32[]{:S(2)}) async-start(bf16[8,216,384]{2,1,0:T(8,128)(2,1)} %add_convert_fusion.1), calls=%async_computation.3 | async-start | bytes 2654208 | tf_op jit(solution)/shard_map/all_to_all | solution.py:83
  281.9 1.1 multiply_cosine_fusion
  286.4 3.4 collective-permute-start.12
  289.9 14.3 %shard_map.329 = f32[2,8,384]{2,1,0:T(8,128)} custom-call(bf16[2,1024,384]{2,1,0:T(8,128)(2,1)} %get-tuple-element.62.grad, bf16[2,1024,384]{2,1,0:T(8,128)(2,1)} %get-tuple-element.44.images, f32[2,8,384]{2,1,0:T(8,128)} %get-tuple-element.45.stats, f32[8,384]{1,0:T(8,128)} %pad.18.refs_4_.gains, bf16[3456,384]{1,0:T(8,128)(2,1)} %bitcast.109), custom_call_target="tpu_custom_call" | custom-call | flops 5435817984 | bytes 5435817 | tf_op jit(solution)/shard_map/pallas_call | solution.py:639
  306.4 6.5 %all-to-all-start.4 = ((f32[32,16,128]{2,1,0:T(8,128)}), f32[32,16,128]{2,1,0:T(8,128)S(1)}, u32[]{:S(2)}, u32[]{:S(2)}) async-start(f32[32,16,128]{2,1,0:T(8,128)} %bitcast.53), calls=%async_computation.4 | async-start | bytes 524288 | tf_op jit(solution)/shard_map/all_to_all | solution.py:104
  314.3 1.2 collective-permute-done.13
  316.3 7.3 %all-to-all-done.4 = f32[32,16,128]{2,1,0:T(8,128)S(1)} async-done(((f32[32,16,128]{2,1,0:T(8,128)}), f32[32,16,128]{2,1,0:T(8,128)S(1)}, u32[]{:S(2)}, u32[]{:S(2)}) %all-to-all-start.4) | async-done | bytes 262176 | tf_op jit(solution)/shard_map/all_to_all | solution.py:104
  324.4 0.9 multiply_reduce_fusion.2
  329.2 2.6 all-to-all-start.5
  332.5 1.9 pad_maximum_fusion.16
  334.4 5.6 %all-to-all-done.5 = f32[32,8,128]{2,1,0:T(8,128)S(1)} async-done(((f32[32,8,128]{2,1,0:T(8,128)}), f32[32,8,128]{2,1,0:T(8,128)S(1)}, u32[]{:S(2)}, u32[]{:S(2)}) %all-to-all-start.5) | async-done | bytes 131104 | tf_op jit(solution)/shard_map/all_to_all | solution.py:104
  343.6 1.1 multiply_subtract_fusion
  (203 shorter events, 29.8 us)
Async XLA Ops:
  5.1 13.7 %collective-permute-start = (bf16[272,384]{1,0:T(8,128)(2,1)S(1)}, bf16[272,384]{1,0:T(8,128)(2,1)S(1)}, u32[]{:S(2)}, u32[]{:S(2)}) collective-permute-start(bf16[272,384]{1,0:T(8,128)(2,1)S(1)} %pad_maximum_fusion.7), channel_id=1, source_target_pairs={{0,16},{1,17},{2,18},{3,19},{4,20},{5,21},{6,22},{7,23},{8,24},{9,... | collective-permute-start | bytes 626696 | tf_op jit(solution)/shard_map/ppermute | solution.py:75
  20.6 43.9 %all-to-all-start = ((bf16[8,328,384]{2,1,0:T(8,128)(2,1)}), bf16[8,328,384]{2,1,0:T(8,128)(2,1)S(1)}, u32[]{:S(2)}, u32[]{:S(2)}) async-start(bf16[8,328,384]{2,1,0:T(8,128)(2,1)} %broadcast_in_dim.10), calls=%async_computation | async-start | bytes 4030464 | tf_op jit(solution)/shard_map/all_to_all | solution.py:83
  24.4 4.7 %copy-start.7 = (f32[12,1152]{1,0:T(8,128)S(1)}, f32[12,1152]{1,0:T(8,128)}, u32[]{:S(2)}) copy-start(f32[12,1152]{1,0:T(8,128)} %param.26) | copy-start | bytes 165892
  24.4 4.7 %copy-start.10 = (f32[12,384]{1,0:T(8,128)S(1)}, f32[12,384]{1,0:T(8,128)}, u32[]{:S(2)}) copy-start(f32[12,384]{1,0:T(8,128)} %param.27) | copy-start | bytes 55300
  26.9 5.7 %collective-permute-start.1 = (bf16[2,8,32,384]{3,2,1,0:T(8,128)(2,1)}, bf16[2,8,32,384]{3,2,1,0:T(8,128)(2,1)}, u32[]{:S(2)}, u32[]{:S(2)}) collective-permute-start(bf16[2,8,32,384]{3,2,1,0:T(8,128)(2,1)} %get-tuple-element.192), channel_id=1, source_target_pairs={{0,1},{1,0},{2,3},{3,2},{4,5},{5,4},{6,7},{7,6},{8,9},{9,8},{10,11... | collective-permute-start | bytes 1179656 | tf_op jit(solution)/shard_map/ppermute | solution.py:115
  26.9 31.2 %collective-permute-start.2 = (bf16[2,8,32,384]{3,2,1,0:T(8,128)(2,1)S(1)}, bf16[2,8,32,384]{3,2,1,0:T(8,128)(2,1)}, u32[]{:S(2)}, u32[]{:S(2)}) collective-permute-start(bf16[2,8,32,384]{3,2,1,0:T(8,128)(2,1)S(1)} %get-tuple-element.194), channel_id=1, source_target_pairs={{0,2},{1,3},{2,0},{3,1},{4,6},{5,7},{6,4},{7,5},{8,10},{9,11},{10,... | collective-permute-start | bytes 1179656 | tf_op jit(solution)/shard_map/ppermute | solution.py:115
  28.9 35.5 %collective-permute-start.3 = (bf16[2,8,32,384]{3,2,1,0:T(8,128)(2,1)S(1)}, bf16[2,8,32,384]{3,2,1,0:T(8,128)(2,1)}, u32[]{:S(2)}, u32[]{:S(2)}) collective-permute-start(bf16[2,8,32,384]{3,2,1,0:T(8,128)(2,1)S(1)} %get-tuple-element.191), channel_id=1, source_target_pairs={{0,3},{1,2},{2,1},{3,0},{4,7},{5,6},{6,5},{7,4},{8,11},{9,10},{10,... | collective-permute-start | bytes 1179656 | tf_op jit(solution)/shard_map/ppermute | solution.py:115
  29.2 36.2 %collective-permute-start.5 = (bf16[48,384]{1,0:T(8,128)(2,1)S(1)}, bf16[48,384]{1,0:T(8,128)(2,1)S(1)}, u32[]{:S(2)}, u32[]{:S(2)}) collective-permute-start(bf16[48,384]{1,0:T(8,128)(2,1)S(1)} %pad_maximum_fusion.13), channel_id=1, source_target_pairs={{0,16},{1,17},{2,18},{3,19},{4,20},{5,21},{6,22},{7,23},{8,24},{9,... | collective-permute-start | bytes 110600 | tf_op jit(solution)/shard_map/ppermute | solution.py:75
  64.5 8.7 %collective-permute-start.4 = (bf16[8,328,384]{2,1,0:T(8,128)(2,1)S(1)}, bf16[8,328,384]{2,1,0:T(8,128)(2,1)}, u32[]{:S(2)}, u32[]{:S(2)}) collective-permute-start(bf16[8,328,384]{2,1,0:T(8,128)(2,1)S(1)} %all-to-all-done), channel_id=1, source_target_pairs={{0,1},{1,0},{2,3},{3,2},{4,5},{5,4},{6,7},{7,6},{8,9},{9,8},{10,11... | collective-permute-start | bytes 6045704 | tf_op jit(solution)/shard_map/ppermute | solution.py:75
  66.8 5.0 %copy-start.24 = (s32[8]{0:T(128)S(1)}, s32[8]{0:T(128)}, u32[]{:S(2)}) copy-start(s32[8]{0:T(128)} %param.22) | copy-start | bytes 100
  66.8 5.2 %copy-start.23 = (s32[8,2]{0,1:T(2,128)S(1)}, s32[8,2]{0,1:T(2,128)}, u32[]{:S(2)}) copy-start(s32[8,2]{0,1:T(2,128)} %param.23) | copy-start | bytes 196
  66.8 30.8 %all-to-all-start.1 = ((bf16[8,312,384]{2,1,0:T(8,128)(2,1)}), bf16[8,312,384]{2,1,0:T(8,128)(2,1)}, u32[]{:S(2)}, u32[]{:S(2)}) async-start(bf16[8,312,384]{2,1,0:T(8,128)(2,1)} %broadcast_in_dim.11), calls=%async_computation.1 | async-start | bytes 3833856 | tf_op jit(solution)/shard_map/all_to_all | solution.py:83
  97.7 9.8 %collective-permute-start.6 = (bf16[8,312,384]{2,1,0:T(8,128)(2,1)}, bf16[8,312,384]{2,1,0:T(8,128)(2,1)}, u32[]{:S(2)}, u32[]{:S(2)}) collective-permute-start(bf16[8,312,384]{2,1,0:T(8,128)(2,1)} %all-to-all-done.1), channel_id=1, source_target_pairs={{0,1},{1,0},{2,3},{3,2},{4,5},{5,4},{6,7},{7,6},{8,9},{9,8},{10,11... | collective-permute-start | bytes 5750792 | tf_op jit(solution)/shard_map/ppermute | solution.py:75
  100.9 1.6 copy-start.3
  101.4 3.8 %copy-start.4 = (bf16[8,4,3072]{2,1,0:T(4,128)(2,1)S(1)}, bf16[8,4,3072]{2,1,0:T(4,128)(2,1)}, u32[]{:S(2)}) copy-start(bf16[8,4,3072]{2,1,0:T(4,128)(2,1)} %convert_element_type.127) | copy-start | bytes 589828
  101.8 5.0 %copy-start.22 = (f32[2,1]{1,0:T(2,128)S(1)}, f32[2,1]{1,0:T(2,128)}, u32[]{:S(2)}) copy-start(f32[2,1]{1,0:T(2,128)} %copy.162) | copy-start | bytes 28
  103.3 26.6 %collective-permute-start.7 = (bf16[2,8,32,192]{3,2,1,0:T(8,128)(2,1)S(1)}, bf16[2,8,32,192]{3,2,1,0:T(8,128)(2,1)S(1)}, u32[]{:S(2)}, u32[]{:S(2)}) collective-permute-start(bf16[2,8,32,192]{3,2,1,0:T(8,128)(2,1)S(1)} %get-tuple-element.197), channel_id=1, source_target_pairs={{0,1},{1,0},{2,3},{3,2},{4,5},{5,4},{6,7},{7,6},{8,9},{9,8},{10,11... | collective-permute-start | bytes 589832 | tf_op jit(solution)/shard_map/ppermute | solution.py:115
  103.8 26.1 %collective-permute-start.8 = (bf16[2,8,32,192]{3,2,1,0:T(8,128)(2,1)S(1)}, bf16[2,8,32,192]{3,2,1,0:T(8,128)(2,1)S(1)}, u32[]{:S(2)}, u32[]{:S(2)}) collective-permute-start(bf16[2,8,32,192]{3,2,1,0:T(8,128)(2,1)S(1)} %get-tuple-element.196), channel_id=1, source_target_pairs={{0,2},{1,3},{2,0},{3,1},{4,6},{5,7},{6,4},{7,5},{8,10},{9,11},{10,... | collective-permute-start | bytes 589832 | tf_op jit(solution)/shard_map/ppermute | solution.py:115
  103.8 26.1 %collective-permute-start.9 = (bf16[2,8,32,192]{3,2,1,0:T(8,128)(2,1)S(1)}, bf16[2,8,32,192]{3,2,1,0:T(8,128)(2,1)S(1)}, u32[]{:S(2)}, u32[]{:S(2)}) collective-permute-start(bf16[2,8,32,192]{3,2,1,0:T(8,128)(2,1)S(1)} %get-tuple-element.195), channel_id=1, source_target_pairs={{0,3},{1,2},{2,1},{3,0},{4,7},{5,6},{6,5},{7,4},{8,11},{9,10},{10,... | collective-permute-start | bytes 589832 | tf_op jit(solution)/shard_map/ppermute | solution.py:115
  129.9 0.7 copy-start.25
  129.9 0.8 copy-start.26
  129.9 0.9 copy-start.27
  229.9 4.5 %collective-permute-start.10 = (bf16[8,312,384]{2,1,0:T(8,128)(2,1)}, bf16[8,312,384]{2,1,0:T(8,128)(2,1)S(1)}, u32[]{:S(2)}, u32[]{:S(2)}) collective-permute-start(bf16[8,312,384]{2,1,0:T(8,128)(2,1)} %get-tuple-element.55), channel_id=1, source_target_pairs={{0,1},{1,0},{2,3},{3,2},{4,5},{5,4},{6,7},{7,6},{8,9},{9,8},{10,11... | collective-permute-start | bytes 5750792 | tf_op jit(solution)/shard_map/ppermute | solution.py:75
  237.8 38.4 %all-to-all-start.2 = ((bf16[8,312,384]{2,1,0:T(8,128)(2,1)}), bf16[8,312,384]{2,1,0:T(8,128)(2,1)S(1)}, u32[]{:S(2)}, u32[]{:S(2)}) async-start(bf16[8,312,384]{2,1,0:T(8,128)(2,1)} %add_convert_fusion), calls=%async_computation.2 | async-start | bytes 3833856 | tf_op jit(solution)/shard_map/all_to_all | solution.py:83
  270.2 3.3 collective-permute-start.11
  276.2 6.7 %copy-start.15 = (f32[2,8,384]{2,1,0:T(8,128)S(1)}, f32[2,8,384]{2,1,0:T(8,128)}, u32[]{:S(2)}) copy-start(f32[2,8,384]{2,1,0:T(8,128)} %get-tuple-element.63) | copy-start | bytes 73732
  276.2 6.8 %copy-start.19 = (f32[2,8,192]{2,1,0:T(8,128)S(1)}, f32[2,8,192]{2,1,0:T(8,128)}, u32[]{:S(2)}) copy-start(f32[2,8,192]{2,1,0:T(8,128)} %get-tuple-element.66) | copy-start | bytes 36868
  276.2 28.8 %all-to-all-start.3 = ((bf16[8,216,384]{2,1,0:T(8,128)(2,1)}), bf16[8,216,384]{2,1,0:T(8,128)(2,1)S(1)}, u32[]{:S(2)}, u32[]{:S(2)}) async-start(bf16[8,216,384]{2,1,0:T(8,128)(2,1)} %add_convert_fusion.1), calls=%async_computation.3 | async-start | bytes 2654208 | tf_op jit(solution)/shard_map/all_to_all | solution.py:83
  285.5 0.8 copy-start
  286.4 18.6 %collective-permute-start.12 = (bf16[264,384]{1,0:T(8,128)(2,1)S(1)}, bf16[264,384]{1,0:T(8,128)(2,1)S(1)}, u32[]{:S(2)}, u32[]{:S(2)}) collective-permute-start(bf16[264,384]{1,0:T(8,128)(2,1)S(1)} %pad_maximum_fusion.8), channel_id=1, source_target_pairs={{0,16},{1,17},{2,18},{3,19},{4,20},{5,21},{6,22},{7,23},{8,24},{9,... | collective-permute-start | bytes 608264 | tf_op jit(solution)/shard_map/ppermute | solution.py:75
  305.3 10.2 %collective-permute-start.13 = (bf16[216,384]{1,0:T(8,128)(2,1)S(1)}, bf16[216,384]{1,0:T(8,128)(2,1)S(1)}, u32[]{:S(2)}, u32[]{:S(2)}) collective-permute-start(bf16[216,384]{1,0:T(8,128)(2,1)S(1)} %convert_element_type.149), channel_id=1, source_target_pairs={{0,16},{1,17},{2,18},{3,19},{4,20},{5,21},{6,22},{7,23},{8,24},{9,... | collective-permute-start | bytes 497672 | tf_op jit(solution)/shard_map/ppermute | solution.py:75
  305.5 10.0 %copy-start.1 = (f32[312,384]{1,0:T(8,128)S(1)}, f32[312,384]{1,0:T(8,128)}, u32[]{:S(2)}) copy-start(f32[312,384]{1,0:T(8,128)} %copy-done) | copy-start | bytes 1437700
  306.4 17.1 %all-to-all-start.4 = ((f32[32,16,128]{2,1,0:T(8,128)}), f32[32,16,128]{2,1,0:T(8,128)S(1)}, u32[]{:S(2)}, u32[]{:S(2)}) async-start(f32[32,16,128]{2,1,0:T(8,128)} %bitcast.53), calls=%async_computation.4 | async-start | bytes 524288 | tf_op jit(solution)/shard_map/all_to_all | solution.py:104
  313.0 11.4 %copy-start.9 = (f32[64,384]{1,0:T(8,128)S(1)}, f32[64,384]{1,0:T(8,128)}, u32[]{:S(2)}) copy-start(f32[64,384]{1,0:T(8,128)} %get-tuple-element.211) | copy-start | bytes 294916
  316.2 25.3 %copy-start.16 = (f32[12,384]{1,0:T(8,128)S(1)}, f32[12,384]{1,0:T(8,128)}, u32[]{:S(2)}) copy-start(f32[12,384]{1,0:T(8,128)} %param.35) | copy-start | bytes 55300
  316.2 25.3 %copy-start.17 = (f32[12,384]{1,0:T(8,128)S(1)}, f32[12,384]{1,0:T(8,128)}, u32[]{:S(2)}) copy-start(f32[12,384]{1,0:T(8,128)} %param.36) | copy-start | bytes 55300
  316.2 26.0 %copy-start.11 = (f32[12,1152]{1,0:T(8,128)S(1)}, f32[12,1152]{1,0:T(8,128)}, u32[]{:S(2)}) copy-start(f32[12,1152]{1,0:T(8,128)} %param.33) | copy-start | bytes 165892
  316.2 26.0 %copy-start.12 = (f32[12,1152]{1,0:T(8,128)S(1)}, f32[12,1152]{1,0:T(8,128)}, u32[]{:S(2)}) copy-start(f32[12,1152]{1,0:T(8,128)} %param.34) | copy-start | bytes 165892
  316.2 26.7 %copy-start.18 = (f32[12,6]{0,1:T(8,128)S(1)}, f32[12,6]{0,1:T(8,128)}, u32[]{:S(2)}) copy-start(f32[12,6]{0,1:T(8,128)} %param.28) | copy-start | bytes 868
  316.2 26.7 %copy-start.20 = (f32[12,6]{0,1:T(8,128)S(1)}, f32[12,6]{0,1:T(8,128)}, u32[]{:S(2)}) copy-start(f32[12,6]{0,1:T(8,128)} %param.37) | copy-start | bytes 868
  316.3 26.7 %copy-start.21 = (f32[12,6]{0,1:T(8,128)S(1)}, f32[12,6]{0,1:T(8,128)}, u32[]{:S(2)}) copy-start(f32[12,6]{0,1:T(8,128)} %param.38) | copy-start | bytes 868
  323.6 20.0 %copy-start.2 = (f32[216,384]{1,0:T(8,128)S(1)}, f32[216,384]{1,0:T(8,128)}, u32[]{:S(2)}) copy-start(f32[216,384]{1,0:T(8,128)} %param.25) | copy-start | bytes 995332
  323.6 20.0 %copy-start.5 = (f32[216,384]{1,0:T(8,128)S(1)}, f32[216,384]{1,0:T(8,128)}, u32[]{:S(2)}) copy-start(f32[216,384]{1,0:T(8,128)} %param.31) | copy-start | bytes 995332
  323.6 20.0 %copy-start.6 = (f32[216,384]{1,0:T(8,128)S(1)}, f32[216,384]{1,0:T(8,128)}, u32[]{:S(2)}) copy-start(f32[216,384]{1,0:T(8,128)} %param.32) | copy-start | bytes 995332
  329.2 10.8 %all-to-all-start.5 = ((f32[32,8,128]{2,1,0:T(8,128)}), f32[32,8,128]{2,1,0:T(8,128)S(1)}, u32[]{:S(2)}, u32[]{:S(2)}) async-start(f32[32,8,128]{2,1,0:T(8,128)} %broadcast_in_dim.14), calls=%async_computation.5 | async-start | bytes 262144 | tf_op jit(solution)/shard_map/all_to_all | solution.py:104
  331.8 12.9 %copy-start.8 = (f32[24,768]{1,0:T(8,128)S(1)}, f32[24,768]{1,0:T(8,128)}, u32[]{:S(2)}) copy-start(f32[24,768]{1,0:T(8,128)} %param.24) | copy-start | bytes 221188
  331.8 12.9 %copy-start.13 = (f32[24,768]{1,0:T(8,128)S(1)}, f32[24,768]{1,0:T(8,128)}, u32[]{:S(2)}) copy-start(f32[24,768]{1,0:T(8,128)} %param.29) | copy-start | bytes 221188
  331.8 12.9 %copy-start.14 = (f32[24,768]{1,0:T(8,128)S(1)}, f32[24,768]{1,0:T(8,128)}, u32[]{:S(2)}) copy-start(f32[24,768]{1,0:T(8,128)} %param.30) | copy-start | bytes 221188

commit v4 on v3

--- a/solution.py
+++ b/solution.py
@@ -59,7 +59,9 @@
 
 
 def pair_up(block, other, low, place):
-    return jnp.stack([jnp.where(low, block, other), jnp.where(low, other, block)], axis=place)
+    shape = [2 if dim == place else 1 for dim in range(block.ndim + 1)]
+    first = jnp.arange(2, dtype=jnp.int32).reshape(shape) == 0
+    return jnp.where(first == low, jnp.expand_dims(block, place), jnp.expand_dims(other, place))
 
 
 def class_count():
@@ -165,7 +167,7 @@
     return mean, inverse
 
 
-CHUNK = 128
+CHUNK = 256
 
 
 def attention_kernel(parts, places, scalars, middle, *refs):
@@ -229,29 +231,30 @@
 
     block = 256
 
-    def attend(head, carry):
-        base = pl.multiple_of(head * 3 * size, 32)
-        qkv_t[pl.ds(base, 3 * size), :] = mm(
-            qkv_wt[pl.ds(base, 3 * size), :], normed[...], NT
-        ).astype(jnp.bfloat16)
-        keys = qkv_t[pl.ds(base + size, size), :].T
-        values_t = qkv_t[pl.ds(base + 2 * size, size), :]
-        for q in range(0, pixels, block):
-            queries_t = qkv_t[pl.ds(base, size), q : q + block]
-            scores = mm(keys, queries_t) * (factor * LOG2E)
-            top = jnp.max(scores, axis=0, keepdims=True)
-            powers = jnp.exp2(scores - top)
-            inv = 1.0 / jnp.sum(powers, axis=0, keepdims=True)
-            powers_b = powers.astype(jnp.bfloat16)
-            probs[head, :, q : q + block] = powers_b
-            totals[head, :, q : q + block] = jnp.broadcast_to(inv, (8, block))
-            mixed = mm(values_t, powers_b) * inv
-            at = pl.multiple_of(head * size, 32)
-            mixed_t[pl.ds(at, size), q : q + block] = mixed
-            attn_t[pl.ds(at, size), q : q + block] = mixed.astype(jnp.bfloat16)
-        return carry
-
-    lax.fori_loop(0, HEADS, attend, 0)
+    qkv_t[...] = mm(qkv_wt[...], normed[...], NT).astype(jnp.bfloat16)
+
+    def rows_of_head(head, part):
+        at = (3 * head + part) * size
+        return slice(at, at + size)
+
+    def scores_of(head):
+        return mm(qkv_t[rows_of_head(head, 1), :].T, qkv_t[rows_of_head(head, 0), :])
+
+    following = scores_of(0)
+    for head in range(HEADS):
+        scores = following
+        if head + 1 < HEADS:
+            following = scores_of(head + 1)
+        top = jnp.max(scores, axis=0, keepdims=True)
+        powers = jnp.exp2((scores - top) * (factor * LOG2E))
+        inv = 1.0 / jnp.sum(powers, axis=0, keepdims=True)
+        powers_b = powers.astype(jnp.bfloat16)
+        probs[head] = powers_b
+        totals[head] = jnp.broadcast_to(inv, (8, pixels))
+        mixed = mm(qkv_t[rows_of_head(head, 2), :], powers_b) * inv
+        at = slice(head * size, (head + 1) * size)
+        mixed_t[at, :] = mixed
+        attn_t[at, :] = mixed.astype(jnp.bfloat16)
 
     result[...] = mm(attn_t[...].T, out_w[...])
     beta_log, tilde_log, coef = scalars[sample, 0], scalars[sample, 1], scalars[sample, 2]
@@ -287,39 +290,36 @@
     out_acc[...] += mm(attn_t[...], grad_b[...])
     back_t[...] = mm(out_w[...], grad_b[...], NT).astype(jnp.bfloat16)
 
-    def attend_back(head, carry):
-        base = pl.multiple_of(head * 3 * size, 32)
-        at = pl.multiple_of(head * size, 32)
-        keys_t = qkv_t[pl.ds(base + size, size), :]
-        values = qkv_t[pl.ds(base + 2 * size, size), :].T
-        grad_key = jnp.zeros((size, pixels), jnp.float32)
-        grad_value = jnp.zeros((size, pixels), jnp.float32)
-        for q in range(0, pixels, block):
-            queries_t = qkv_t[pl.ds(base, size), q : q + block]
-            upstream = back_t[pl.ds(at, size), q : q + block]
-            inner = jnp.sum(
-                upstream.astype(jnp.float32) * mixed_t[pl.ds(at, size), q : q + block],
-                axis=0,
-                keepdims=True,
-            )
-            soft = probs[head, :, q : q + block].astype(jnp.float32) * totals[head, 0:1, q : q + block]
-            grad_soft = mm(values, upstream)
-            grad_scores = (soft * (grad_soft - inner)).astype(jnp.bfloat16)
-            dqkv_t[pl.ds(base, size), q : q + block] = (mm(keys_t, grad_scores) * factor).astype(jnp.bfloat16)
-            grad_key += mm(queries_t, grad_scores, NT)
-            grad_value += mm(upstream, soft.astype(jnp.bfloat16), NT)
-        dqkv_t[pl.ds(base + size, size), :] = (grad_key * factor).astype(jnp.bfloat16)
-        dqkv_t[pl.ds(base + 2 * size, size), :] = grad_value.astype(jnp.bfloat16)
-        return carry
-
-    lax.fori_loop(0, HEADS, attend_back, 0)
+    def upstream_of(head):
+        return back_t[head * size : (head + 1) * size, :]
+
+    def soft_grad(head):
+        return mm(qkv_t[rows_of_head(head, 2), :].T, upstream_of(head))
+
+    following = soft_grad(0)
+    for head in range(HEADS):
+        grad_soft = following
+        if head + 1 < HEADS:
+            following = soft_grad(head + 1)
+        upstream = upstream_of(head)
+        inner = jnp.sum(
+            upstream.astype(jnp.float32) * mixed_t[head * size : (head + 1) * size, :],
+            axis=0,
+            keepdims=True,
+        )
+        soft = probs[head].astype(jnp.float32) * totals[head, 0:1]
+        grad_scores = (soft * (grad_soft - inner)).astype(jnp.bfloat16)
+        queries_t, keys_t = qkv_t[rows_of_head(head, 0), :], qkv_t[rows_of_head(head, 1), :]
+        dqkv_t[rows_of_head(head, 0), :] = (mm(keys_t, grad_scores) * factor).astype(jnp.bfloat16)
+        dqkv_t[rows_of_head(head, 1), :] = (mm(queries_t, grad_scores, NT) * factor).astype(jnp.bfloat16)
+        dqkv_t[rows_of_head(head, 2), :] = mm(upstream, soft.astype(jnp.bfloat16), NT).astype(jnp.bfloat16)
 
     qkv_acc[...] += mm(normed[...].T, dqkv_t[...], NT)
-    gn_t[...] = mm(qkv_w[...], dqkv_t[...])
+    gn_t[...] = mm(qkv_w[...], dqkv_t[...]).T
 
     def back_sums(at, carry):
         hat = (load(at) - mean) * inverse
-        grad = gn_t[:, pl.ds(at, CHUNK)].T
+        grad = gn_t[pl.ds(at, CHUNK), :]
         return (carry[0] + fold(grad * hat), carry[1] + fold(grad))
 
     zero = jnp.zeros((8, channels), jnp.float32)
@@ -330,7 +330,7 @@
 
     def back_norm(at, carry):
         hat = (load(at) - mean) * inverse
-        grad = gn_t[:, pl.ds(at, CHUNK)].T * gain
+        grad = gn_t[pl.ds(at, CHUNK), :] * gain
         back = (grad - means[1:2] - hat * means[0:1]) * inverse
         down_out[0, pl.ds(at, CHUNK), :] = (result[pl.ds(at, CHUNK), :] + back).astype(jnp.bfloat16)
         return carry
@@ -388,7 +388,7 @@
             pltpu.VMEM((pixels, channels), bf),
             pltpu.VMEM((channels, pixels), bf),
             pltpu.VMEM((3 * channels, pixels), bf),
-            pltpu.VMEM((channels, pixels), f32),
+            pltpu.VMEM((pixels, channels), f32),
             pltpu.VMEM((channels, 3 * channels), f32),
             pltpu.VMEM((channels, channels), f32),
         ],
@@ -775,42 +775,25 @@
     local_samples = timesteps.shape[0]
     small = jnp.concatenate(
         [
-            gains.reshape(-1),
+            lax.reduce_precision(gains.reshape(-1), 8, 7),
             extents.astype(jnp.float32).reshape(-1),
-            (timesteps // 64).astype(jnp.float32),
-            (timesteps % 64).astype(jnp.float32),
+            timesteps.astype(jnp.float32),
         ]
     )
-    small = jnp.pad(small, (0, 8 * channels - small.shape[0])).reshape(8, channels)
+    small = jnp.pad(small, (0, -small.shape[0] % 128))
+    smalls = to_all(jnp.broadcast_to(small[None, None], (devices, 1, small.shape[0])))
     classes = class_count()
     top_mask = devices // 2
     is_top = device >= top_mask
-    film_cut = film_rows * wide // channels
-    ours = jnp.concatenate([conv_master, small, film_master.reshape(-1, channels)])
-    ours = ours.astype(jnp.bfloat16)
+    ours = conv_master.astype(jnp.bfloat16)
     theirs = exchange(ours, top_mask)
     strips = strips_of(images)
     low, high = jnp.where(is_top, theirs, ours), jnp.where(is_top, ours, theirs)
-    small_two = [part[conv_rows : conv_rows + 8] for part in (low, high)]
-    film_two = [part[conv_rows + 8 :] for part in (low, high)]
-    every_one = gather_classes(jnp.concatenate([low[:conv_rows]] + small_two + film_two))
-    rest = jnp.concatenate([qkv_master.reshape(-1, channels), out_master]).astype(jnp.bfloat16)
-    rest = behind(rest, theirs)
-    rest_two = pair_up(rest, exchange(rest, top_mask), jnp.logical_not(is_top), 0)
-    every_two = gather_classes(
-        behind(jnp.concatenate([high[:conv_rows], rest_two.reshape(-1, channels)]), every_one)
-    )
-    taps_one, smalls, film_w = finish_gather(
-        behind(every_one, *strips), [conv_rows, 16, 2 * film_cut]
-    )
-    taps_one = taps_one.reshape(-1, channels)
-    smalls = jnp.moveaxis(smalls.reshape(-1, 2, 8 * channels), 0, 1)
-    smalls = smalls.reshape(devices, -1).astype(jnp.float32)
+    smalls = smalls.reshape(devices, -1)
     gain_f = smalls[:, : gains.size].reshape(channels, 6)
     dp_smalls = smalls.reshape(lax.axis_size("dp"), lax.axis_size("head"), -1)[:, 0, gains.size :]
     extents_all = dp_smalls[:, : 2 * local_samples].reshape(-1, 2)
-    times = dp_smalls[:, 2 * local_samples : 4 * local_samples].reshape(-1, 2, local_samples)
-    times_all = (times[:, 0] * 64.0 + times[:, 1]).reshape(-1).astype(jnp.int32)
+    times_all = dp_smalls[:, 2 * local_samples : 3 * local_samples].reshape(-1).astype(jnp.int32)
     divisor = jnp.sum(extents_all[:, 0] * extents_all[:, 1])
 
     parts = lax.axis_size("head")
@@ -824,7 +807,24 @@
 
     log_beta, log_tilde, factor = plan(own_times)
     embedded_all = jax.nn.silu(embed(times_all, wide)).astype(jnp.bfloat16)
-    embedded = jax.nn.silu(embed(own_times, wide)).astype(jnp.bfloat16)
+    film_rows_out = lax.dot_general(
+        film_master.astype(jnp.bfloat16),
+        embedded_all,
+        (((1,), (1,)), ((), ())),
+        preferred_element_type=jnp.float32,
+    )
+    film_blocks = film_rows_out.T.reshape(devices, -1)
+    film_blocks = jnp.pad(film_blocks, ((0, 0), (0, -film_blocks.shape[1] % 128)))
+    film_blocks = to_all(film_blocks[:, None]).reshape(devices, -1)
+    film_blocks = film_blocks[:, : samples * film_rows].reshape(devices, samples, film_rows)
+    film_out = jnp.moveaxis(film_blocks, 1, 0).reshape(samples, devices * film_rows)
+    every_one = gather_classes(behind(low, film_out, *strips))
+    rest = jnp.concatenate([qkv_master.reshape(-1, channels), out_master]).astype(jnp.bfloat16)
+    rest = behind(rest, theirs)
+    rest_two = pair_up(rest, exchange(rest, top_mask), jnp.logical_not(is_top), 0)
+    every_two = gather_classes(
+        behind(jnp.concatenate([high, rest_two.reshape(-1, channels)]), every_one)
+    )
     gains_t = jnp.pad(gain_f.T, ((0, 2), (0, 0)))
     member = jnp.asarray(np.kron(np.eye(GROUPS), np.ones((channels // GROUPS,) * 2)), jnp.bfloat16)
     scalars = jnp.stack(
@@ -834,18 +834,16 @@
     )
     first_call, second_call, weights, second_back, first_back = block_calls(samples, pixels, channels)
     flat = lambda values: [v.reshape(samples, strip_rows * width_px, -1) for v in values]
+    (taps_one,) = finish_gather(every_one, [conv_rows])
+    taps_one = taps_one.reshape(-1, channels)
     inner, hidden_one, stats, source = first_call(places, flat(strips), gains_t, member, taps_one)
     taps_two, others = finish_gather(behind(every_two, inner), [conv_rows, 8 * out_rows])
     taps_two = taps_two.reshape(-1, channels)
-    film_w = jnp.moveaxis(film_w.reshape(-1, 2, film_cut, channels), 0, 1).reshape(-1, wide)
     others = jnp.moveaxis(others.reshape(-1, 2, 4 * out_rows, channels), 0, 1)
     others = others.reshape(devices, 4 * out_rows, channels)
     qkv_w = others[:, : 3 * out_rows].reshape(channels, 3 * channels)
     out_w = others[:, 3 * out_rows :].reshape(channels, channels)
-    noise_strips = strips_of(behind(noise, inner))
-    film_out = lax.dot_general(
-        embedded, film_w, (((1,), (1,)), ((), ())), preferred_element_type=jnp.float32
-    )
+    noise_strips = strips_of(behind(noise, taps_two))
     film = jnp.pad(film_out.reshape(samples, 2, channels), ((0, 0), (0, 6), (0, 0)))
     scale = 1.0 + film_out[:, :channels]
     middle, hidden_two = second_call(inner, source, stats, film, gains_t, taps_two)

time: 352 us -> 317 us (0.901); the launches traced: 347 us -> 320 us
  Pallas kernels: 172 us -> 155 us
  waiting for transfers between devices: 65.7 us -> 56.6 us
    ppermute x6, waiting for transfers between devices: 31.8 us -> 0.02 us  [strips_of(): strip = lax.ppermute(strip, 'head', [(i, i ^ far) for i in range(parts)])]
    another operation x20 -> x3, other arithmetic: 11.9 us -> 0.03 us  [the longest x12 7.93 us: pair_up(): jnp.stack([jnp.where(low, block, other), jnp.where(low, other, block)], a...]
    all_to_all x2 -> x4, waiting for transfers between devices: 12.9 us -> 24 us  [to_all(): lax.all_to_all(blocks, ('dp', 'head'), split_axis=0, concat_axis=0, tiled...]
    pallas_call x6, Pallas kernels: 95.9 us -> 85.8 us  [per_sample(): pl.pallas_call(kernel, grid=(samples,), in_specs=in_specs, out_specs=[spe...]
    all_to_all x2 -> x4, starting transfers between devices: 9.09 us -> 17.5 us  [to_all(): lax.all_to_all(blocks, ('dp', 'head'), split_axis=0, concat_axis=0, tiled...]
    ppermute x8, waiting for transfers between devices: 17.5 us -> 25.4 us  [exchange(): lax.ppermute(values, ('dp', 'head'), [(i, i ^ mask) for i in range(size)])]
    ppermute x8, starting transfers between devices: 13.1 us -> 6.13 us  [exchange(): lax.ppermute(values, ('dp', 'head'), [(i, i ^ mask) for i in range(size)])]
    pallas_call x1, Pallas kernels: 75.8 us -> 68.9 us  [attention_block(): pl.pallas_call(functools.partial(attention_kernel, parts), grid=(samples,...]
  transfers between devices with their start and end apart: 20 -> 22, of which waited for: 9 -> 12; matrix products, arithmetic and copies ran while one was open for 12% -> 10% of each run, Pallas kernels for 21% -> 23%
where the time goes in v4:
time: 317 us; the launch traced here: 320 us
  Pallas kernels  155 us (49%)
  waiting for transfers between devices  56.6 us (18%)
  starting transfers between devices  45.5 us (14%)
  other arithmetic  31.7 us (10%)
  local copies, waits for them, and re-layouts  23.5 us (7%)
  between operations  6.75 us (2%)
    pallas_call x6, Pallas kernels, per_sample(): pl.pallas_call(kernel, grid=(samples,), in_specs=in_specs, out_specs=[spe...  85.8 us
    pallas_call x1, Pallas kernels, attention_block(): pl.pallas_call(functools.partial(attention_kernel, parts), grid=(samples,...  68.9 us
    ppermute x8, waiting for transfers between devices, exchange(): lax.ppermute(values, ('dp', 'head'), [(i, i ^ mask) for i in range(size)])  25.4 us
    all_to_all x4, waiting for transfers between devices, to_all(): lax.all_to_all(blocks, ('dp', 'head'), split_axis=0, concat_axis=0, tiled...  24 us
    all_to_all x4, starting transfers between devices, across_classes(): lax.all_to_all(blocks, ('dp', 'head'), split_axis=0, concat_axis=0, axis_...  17.6 us
    all_to_all x4, starting transfers between devices, to_all(): lax.all_to_all(blocks, ('dp', 'head'), split_axis=0, concat_axis=0, tiled...  17.5 us
    all_to_all x4, waiting for transfers between devices, across_classes(): lax.all_to_all(blocks, ('dp', 'head'), split_axis=0, concat_axis=0, axis_...  7.28 us
  transfers between devices with their start and end apart: 22, of which 12 were waited for; matrix products, arithmetic and copies ran while one was open for 10% of the time, Pallas kernels for 23%

profile of v4, /device:TPU:0, one launch (start us, length us, event | category | flops | bytes accessed | tf_op | source)
XLA Modules:
  0.0 319.8 jit_solution(14941589194975956667)
XLA Ops:
  3.7 7.3 %all-to-all-start = ((f32[32,1,128]{2,1,0:T(1,128)}), f32[32,1,128]{2,1,0:T(1,128)S(1)}, u32[]{:S(2)}, u32[]{:S(2)}) async-start(f32[32,1,128]{2,1,0:T(1,128)} %broadcast_in_dim.158), calls=%async_computation | async-start | bytes 32768 | tf_op jit(solution)/shard_map/all_to_all | solution.py:106
  11.0 1.0 convert_element_type.110
  12.0 2.7 collective-permute-start.3
  14.8 2.4 constant_dynamic-slice_fusion.4
  17.2 0.9 collective-permute-start.2
  21.5 3.7 %all-to-all-start.1 = ((f32[32,1,128]{2,1,0:T(1,128)}), f32[32,1,128]{2,1,0:T(1,128)S(1)}, u32[]{:S(2)}, u32[]{:S(2)}) async-start(f32[32,1,128]{2,1,0:T(1,128)} %bitcast.12), calls=%async_computation.1 | async-start | bytes 32768 | tf_op jit(solution)/shard_map/all_to_all | solution.py:106
  25.2 12.0 %all-to-all-done.1 = f32[32,1,128]{2,1,0:T(1,128)S(1)} async-done(((f32[32,1,128]{2,1,0:T(1,128)}), f32[32,1,128]{2,1,0:T(1,128)S(1)}, u32[]{:S(2)}, u32[]{:S(2)}) %all-to-all-start.1) | async-done | bytes 16416 | tf_op jit(solution)/shard_map/all_to_all | solution.py:106
  38.2 1.3 broadcast_in_dim.163
  39.7 4.6 %all-to-all-start.2 = ((bf16[8,216,384]{2,1,0:T(8,128)(2,1)}), bf16[8,216,384]{2,1,0:T(8,128)(2,1)S(1)}, u32[]{:S(2)}, u32[]{:S(2)}) async-start(bf16[8,216,384]{2,1,0:T(8,128)(2,1)} %broadcast_in_dim.163), calls=%async_computation.2 | async-start | bytes 2654208 | tf_op jit(solution)/shard_map/all_to_all | solution.py:85
  45.1 15.0 %collective-permute-done.5 = bf16[48,384]{1,0:T(8,128)(2,1)S(1)} collective-permute-done((bf16[48,384]{1,0:T(8,128)(2,1)S(1)}, bf16[48,384]{1,0:T(8,128)(2,1)S(1)}, u32[]{:S(2)}, u32[]{:S(2)}) %collective-permute-start.5) | collective-permute-done | bytes 36896 | tf_op jit(solution)/shard_map/ppermute | solution.py:77
  60.2 1.9 all-to-all-done.2
  62.2 1.5 broadcast_in_dim.175
  63.6 4.0 %all-to-all-start.3 = ((bf16[8,312,384]{2,1,0:T(8,128)(2,1)}), bf16[8,312,384]{2,1,0:T(8,128)(2,1)S(1)}, u32[]{:S(2)}, u32[]{:S(2)}) async-start(bf16[8,312,384]{2,1,0:T(8,128)(2,1)} %broadcast_in_dim.175), calls=%async_computation.3 | async-start | bytes 3833856 | tf_op jit(solution)/shard_map/all_to_all | solution.py:85
  69.9 1.0 collective-permute-done.4
  70.9 3.7 %bitcast_select_fusion.1.refs_6_.weight = bf16[3456,384]{1,0:T(8,128)(2,1)} fusion(pred[3456]{0:T(1024)(128)(4,1)} %broadcast_in_dim.160, bf16[8,216,384]{2,1,0:T(8,128)(2,1)} %collective-permute-done.4, bf16[8,216,384]{2,1,0:T(8,128)(2,1)S(1)} %all-to-all-done.2), kind=kLoop, calls=%fused_computation.3 | loop fusion | flops 1327104 | bytes 5311872 | tf_op jit(solution)/shard_map/jit(_where)/select_n | solution.py:64
  74.6 15.5 %shard_map.323 = (f32[2,1024,384]{2,1,0:T(8,128)}, bf16[2,1024,384]{2,1,0:T(8,128)(2,1)}, f32[2,8,384]{2,1,0:T(8,128)}, bf16[2,1024,384]{2,1,0:T(8,128)(2,1)}) custom-call(s32[4]{0:T(128)} %iota_xor_fusion.places, bf16[2,256,384]{2,1,0:T(8,128)(2,1)} %bitcast.97, bf16[2,256,384]{2,1,0:T(8,128)(2,1)} %bitcast.109, bf16[2,256,384]{2,1,0:T(8,128)(2,1)} %bitcast.110, ...), custom_call_target="tpu_custom_call" | custom-call | flops 5435817984 | bytes 5435817 | tf_op jit(solution)/shard_map/pallas_call | solution.py:639
  90.0 3.7 %all-to-all-done.3 = bf16[8,312,384]{2,1,0:T(8,128)(2,1)S(1)} async-done(((bf16[8,312,384]{2,1,0:T(8,128)(2,1)}), bf16[8,312,384]{2,1,0:T(8,128)(2,1)S(1)}, u32[]{:S(2)}, u32[]{:S(2)}) %all-to-all-start.3) | async-done | bytes 1916960 | tf_op jit(solution)/shard_map/all_to_all | solution.py:85
  94.8 0.8 fusion.refs_8_
  98.6 1.5 slice.165
  100.1 2.3 bitcast_select_fusion.weight
  103.2 2.1 collective-permute-start.8
  105.3 13.8 %shard_map.324 = (f32[2,1024,384]{2,1,0:T(8,128)}, bf16[2,1024,384]{2,1,0:T(8,128)(2,1)}) custom-call(f32[2,1024,384]{2,1,0:T(8,128)} %get-tuple-element.43.inner, bf16[2,1024,384]{2,1,0:T(8,128)(2,1)} %get-tuple-element.44.images, f32[2,8,384]{2,1,0:T(8,128)} %get-tuple-element.45.stats, f32[2,8,384]{2,1,0:T(8,128)} %pad.23.film, ...), custom_call_target="tpu_custom_call" | custom-call | flops 5435817984 | bytes 5435817 | tf_op jit(solution)/shard_map/pallas_call | solution.py:639
  119.2 1.1 slice.166
  121.1 1.4 reshape.286.refs_6_
  122.5 0.8 reshape.287.refs_7_
  124.3 68.9 %shard_map.325 = (bf16[2,1024,384]{2,1,0:T(8,128)(2,1)}, bf16[384,1536]{1,0:T(8,128)(2,1)}, f32[2,8,384]{2,1,0:T(8,128)}, f32[2,8,192]{2,1,0:T(8,128)}) custom-call(s32[4]{0:T(128)} %iota_xor_fusion.places, f32[2,6]{1,0:T(2,128)} %stack.47.scalars, f32[2,1024,384]{2,1,0:T(8,128)} %get-tuple-element.49.middle, bf16[2,256,192]{2,1,0:T(8,128)(2,1)} %bitcast.98, ...), custom_call_target="tpu_custom_call" | custom-call | flops 24159191040 | bytes 6291456 | tf_op jit(solution)/shard_map/pallas_call | solution.py:352
  193.2 13.2 %shard_map.326 = (bf16[8,312,384]{2,1,0:T(8,128)(2,1)}, bf16[8,312,384]{2,1,0:T(8,128)(2,1)}) custom-call(s32[1]{0:T(128)} %bitcast.31.place, bf16[2,1024,384]{2,1,0:T(8,128)(2,1)} %get-tuple-element.52.hidden, bf16[2,1024,384]{2,1,0:T(8,128)(2,1)} %get-tuple-element.56.grad, bf16[384,1536]{1,0:T(8,128)(2,1)} %get-tuple-element.53.refs_0_), custom_call_target="tpu_custom_call" | custom-call | flops 5435817984 | bytes 5435817 | tf_op jit(solution)/shard_map/pallas_call | solution.py:639
  206.8 3.7 %collective-permute-done.10 = bf16[8,312,384]{2,1,0:T(8,128)(2,1)S(1)} collective-permute-done((bf16[8,312,384]{2,1,0:T(8,128)(2,1)}, bf16[8,312,384]{2,1,0:T(8,128)(2,1)S(1)}, u32[]{:S(2)}, u32[]{:S(2)}) %collective-permute-start.10) | collective-permute-done | bytes 1916960 | tf_op jit(solution)/shard_map/ppermute | solution.py:77
  210.6 3.4 %add_convert_fusion = bf16[8,312,384]{2,1,0:T(8,128)(2,1)} fusion(bf16[8,312,384]{2,1,0:T(8,128)(2,1)S(1)} %collective-permute-done.10, bf16[8,312,384]{2,1,0:T(8,128)(2,1)} %get-tuple-element.54), kind=kLoop, calls=%fused_computation.1 | loop fusion | flops 3833856 | bytes 5750784 | tf_op jit(solution)/shard_map/convert_element_type | solution.py:865
  213.9 3.6 %all-to-all-start.4 = ((bf16[8,312,384]{2,1,0:T(8,128)(2,1)}), bf16[8,312,384]{2,1,0:T(8,128)(2,1)S(1)}, u32[]{:S(2)}, u32[]{:S(2)}) async-start(bf16[8,312,384]{2,1,0:T(8,128)(2,1)} %add_convert_fusion), calls=%async_computation.4 | async-start | bytes 3833856 | tf_op jit(solution)/shard_map/all_to_all | solution.py:85
  217.5 16.4 %shard_map.327 = (bf16[2,1024,384]{2,1,0:T(8,128)(2,1)}, f32[2,8,384]{2,1,0:T(8,128)}) custom-call(bf16[2,1024,384]{2,1,0:T(8,128)(2,1)} %get-tuple-element.56.grad, f32[2,1024,384]{2,1,0:T(8,128)} %get-tuple-element.43.inner, f32[2,8,384]{2,1,0:T(8,128)} %get-tuple-element.45.stats, f32[2,8,384]{2,1,0:T(8,128)} %pad.23.film, f32[8,384]{1,0:T(8,128)} %pad.21.refs_4_.gains, ...), custom_call_target="tpu_custom_call" | custom-call | flops 5435817984 | bytes 5435817 | tf_op jit(solution)/shard_map/pallas_call | solution.py:639
  233.9 12.3 %shard_map.328 = (bf16[8,216,384]{2,1,0:T(8,128)(2,1)}, bf16[8,216,384]{2,1,0:T(8,128)(2,1)}) custom-call(s32[1]{0:T(128)} %bitcast.31.place, bf16[2,1024,384]{2,1,0:T(8,128)(2,1)} %get-tuple-element.59.hidden, bf16[2,1024,384]{2,1,0:T(8,128)(2,1)} %get-tuple-element.62.grad), custom_call_target="tpu_custom_call" | custom-call | flops 5435817984 | bytes 5435817 | tf_op jit(solution)/shard_map/pallas_call | solution.py:639
  246.6 2.9 collective-permute-done.11
  249.5 2.8 add_convert_fusion.1
  252.3 5.4 %all-to-all-start.5 = ((bf16[8,216,384]{2,1,0:T(8,128)(2,1)}), bf16[8,216,384]{2,1,0:T(8,128)(2,1)S(1)}, u32[]{:S(2)}, u32[]{:S(2)}) async-start(bf16[8,216,384]{2,1,0:T(8,128)(2,1)} %add_convert_fusion.1), calls=%async_computation.5 | async-start | bytes 2654208 | tf_op jit(solution)/shard_map/all_to_all | solution.py:85
  258.3 0.8 slice_reduce_fusion.5
  261.3 14.7 %shard_map.329 = f32[2,8,384]{2,1,0:T(8,128)} custom-call(bf16[2,1024,384]{2,1,0:T(8,128)(2,1)} %get-tuple-element.62.grad, bf16[2,1024,384]{2,1,0:T(8,128)(2,1)} %get-tuple-element.44.images, f32[2,8,384]{2,1,0:T(8,128)} %get-tuple-element.45.stats, f32[8,384]{1,0:T(8,128)} %pad.21.refs_4_.gains, bf16[3456,384]{1,0:T(8,128)(2,1)} %bitcast_select_fusion.1.refs_6_.weight), custom_call_target="tpu_custom_call" | custom-call | flops 5435817984 | bytes 5435817 | tf_op jit(solution)/shard_map/pallas_call | solution.py:639
  275.9 0.8 slice_reduce_fusion.3
  277.3 1.6 all-to-all-done.5
  279.2 1.9 collective-permute-start.13
  282.1 3.2 %all-to-all-start.6 = ((f32[32,16,128]{2,1,0:T(8,128)}), f32[32,16,128]{2,1,0:T(8,128)S(1)}, u32[]{:S(2)}, u32[]{:S(2)}) async-start(f32[32,16,128]{2,1,0:T(8,128)} %bitcast.44), calls=%async_computation.6 | async-start | bytes 524288 | tf_op jit(solution)/shard_map/all_to_all | solution.py:106
  286.7 2.2 collective-permute-done.13
  289.6 6.3 %all-to-all-done.6 = f32[32,16,128]{2,1,0:T(8,128)S(1)} async-done(((f32[32,16,128]{2,1,0:T(8,128)}), f32[32,16,128]{2,1,0:T(8,128)S(1)}, u32[]{:S(2)}, u32[]{:S(2)}) %all-to-all-start.6) | async-done | bytes 262176 | tf_op jit(solution)/shard_map/all_to_all | solution.py:106
  296.8 0.9 multiply_reduce_fusion.2
  301.6 3.3 %all-to-all-start.7 = ((f32[32,8,128]{2,1,0:T(8,128)}), f32[32,8,128]{2,1,0:T(8,128)S(1)}, u32[]{:S(2)}, u32[]{:S(2)}) async-start(f32[32,8,128]{2,1,0:T(8,128)} %broadcast_in_dim.189), calls=%async_computation.7 | async-start | bytes 262144 | tf_op jit(solution)/shard_map/all_to_all | solution.py:106
  305.5 1.9 pad_maximum_fusion.7
  307.4 5.7 %all-to-all-done.7 = f32[32,8,128]{2,1,0:T(8,128)S(1)} async-done(((f32[32,8,128]{2,1,0:T(8,128)}), f32[32,8,128]{2,1,0:T(8,128)S(1)}, u32[]{:S(2)}, u32[]{:S(2)}) %all-to-all-start.7) | async-done | bytes 131104 | tf_op jit(solution)/shard_map/all_to_all | solution.py:106
  317.4 1.1 multiply_subtract_fusion
  (220 shorter events, 30.1 us)
Async XLA Ops:
  3.7 15.6 %all-to-all-start = ((f32[32,1,128]{2,1,0:T(1,128)}), f32[32,1,128]{2,1,0:T(1,128)S(1)}, u32[]{:S(2)}, u32[]{:S(2)}) async-start(f32[32,1,128]{2,1,0:T(1,128)} %broadcast_in_dim.158), calls=%async_computation | async-start | bytes 32768 | tf_op jit(solution)/shard_map/all_to_all | solution.py:106
  12.0 26.1 %collective-permute-start.3 = (bf16[216,384]{1,0:T(8,128)(2,1)S(1)}, bf16[216,384]{1,0:T(8,128)(2,1)S(1)}, u32[]{:S(2)}, u32[]{:S(2)}) collective-permute-start(bf16[216,384]{1,0:T(8,128)(2,1)S(1)} %convert_element_type.110), channel_id=1, source_target_pairs={{0,16},{1,17},{2,18},{3,19},{4,20},{5,21},{6,22},{7,23},{8,24},{9,... | collective-permute-start | bytes 497672 | tf_op jit(solution)/shard_map/ppermute | solution.py:77
  14.8 5.9 %copy-start.7 = (f32[24,768]{1,0:T(8,128)S(1)}, f32[24,768]{1,0:T(8,128)}, u32[]{:S(2)}) copy-start(f32[24,768]{1,0:T(8,128)} %param.24) | copy-start | bytes 221188
  14.8 23.3 %copy-start = (f32[216,384]{1,0:T(8,128)S(1)}, f32[216,384]{1,0:T(8,128)}, u32[]{:S(2)}) copy-start(f32[216,384]{1,0:T(8,128)} %param.25) | copy-start | bytes 995332
  17.2 21.0 %collective-permute-start.2 = (bf16[2,8,32,384]{3,2,1,0:T(8,128)(2,1)S(1)}, bf16[2,8,32,384]{3,2,1,0:T(8,128)(2,1)S(1)}, u32[]{:S(2)}, u32[]{:S(2)}) collective-permute-start(bf16[2,8,32,384]{3,2,1,0:T(8,128)(2,1)S(1)} %get-tuple-element.197), channel_id=1, source_target_pairs={{0,3},{1,2},{2,1},{3,0},{4,7},{5,6},{6,5},{7,4},{8,11},{9,10},{10,... | collective-permute-start | bytes 1179656 | tf_op jit(solution)/shard_map/ppermute | solution.py:117
  18.1 20.1 %collective-permute-start = (bf16[2,8,32,384]{3,2,1,0:T(8,128)(2,1)S(1)}, bf16[2,8,32,384]{3,2,1,0:T(8,128)(2,1)S(1)}, u32[]{:S(2)}, u32[]{:S(2)}) collective-permute-start(bf16[2,8,32,384]{3,2,1,0:T(8,128)(2,1)S(1)} %get-tuple-element.198), channel_id=1, source_target_pairs={{0,1},{1,0},{2,3},{3,2},{4,5},{5,4},{6,7},{7,6},{8,9},{9,8},{10,11... | collective-permute-start | bytes 1179656 | tf_op jit(solution)/shard_map/ppermute | solution.py:117
  18.7 19.5 %collective-permute-start.1 = (bf16[2,8,32,384]{3,2,1,0:T(8,128)(2,1)S(1)}, bf16[2,8,32,384]{3,2,1,0:T(8,128)(2,1)S(1)}, u32[]{:S(2)}, u32[]{:S(2)}) collective-permute-start(bf16[2,8,32,384]{3,2,1,0:T(8,128)(2,1)S(1)} %get-tuple-element.200), channel_id=1, source_target_pairs={{0,2},{1,3},{2,0},{3,1},{4,6},{5,7},{6,4},{7,5},{8,10},{9,11},{10,... | collective-permute-start | bytes 1179656 | tf_op jit(solution)/shard_map/ppermute | solution.py:117
  21.5 15.7 %all-to-all-start.1 = ((f32[32,1,128]{2,1,0:T(1,128)}), f32[32,1,128]{2,1,0:T(1,128)S(1)}, u32[]{:S(2)}, u32[]{:S(2)}) async-start(f32[32,1,128]{2,1,0:T(1,128)} %bitcast.12), calls=%async_computation.1 | async-start | bytes 32768 | tf_op jit(solution)/shard_map/all_to_all | solution.py:106
  39.7 22.5 %all-to-all-start.2 = ((bf16[8,216,384]{2,1,0:T(8,128)(2,1)}), bf16[8,216,384]{2,1,0:T(8,128)(2,1)S(1)}, u32[]{:S(2)}, u32[]{:S(2)}) async-start(bf16[8,216,384]{2,1,0:T(8,128)(2,1)} %broadcast_in_dim.163), calls=%async_computation.2 | async-start | bytes 2654208 | tf_op jit(solution)/shard_map/all_to_all | solution.py:85
  44.4 15.7 %collective-permute-start.5 = (bf16[48,384]{1,0:T(8,128)(2,1)S(1)}, bf16[48,384]{1,0:T(8,128)(2,1)S(1)}, u32[]{:S(2)}, u32[]{:S(2)}) collective-permute-start(bf16[48,384]{1,0:T(8,128)(2,1)S(1)} %pad_maximum_fusion.5), channel_id=1, source_target_pairs={{0,16},{1,17},{2,18},{3,19},{4,20},{5,21},{6,22},{7,23},{8,24},{9,... | collective-permute-start | bytes 110600 | tf_op jit(solution)/shard_map/ppermute | solution.py:77
  44.9 22.8 %copy-start.32 = (pred[2]{0:T(512)(128)(4,1)}, pred[2]{0:T(512)(128)(4,1)S(1)}, u32[]{:S(2)}) copy-start(pred[2]{0:T(512)(128)(4,1)S(1)} %get-tuple-element.221) | copy-start | bytes 10
  63.6 30.1 %all-to-all-start.3 = ((bf16[8,312,384]{2,1,0:T(8,128)(2,1)}), bf16[8,312,384]{2,1,0:T(8,128)(2,1)S(1)}, u32[]{:S(2)}, u32[]{:S(2)}) async-start(bf16[8,312,384]{2,1,0:T(8,128)(2,1)} %broadcast_in_dim.175), calls=%async_computation.3 | async-start | bytes 3833856 | tf_op jit(solution)/shard_map/all_to_all | solution.py:85
  67.6 3.3 %collective-permute-start.4 = (bf16[8,216,384]{2,1,0:T(8,128)(2,1)S(1)}, bf16[8,216,384]{2,1,0:T(8,128)(2,1)}, u32[]{:S(2)}, u32[]{:S(2)}) collective-permute-start(bf16[8,216,384]{2,1,0:T(8,128)(2,1)S(1)} %all-to-all-done.2), channel_id=1, source_target_pairs={{0,1},{1,0},{2,3},{3,2},{4,5},{5,4},{6,7},{7,6},{8,9},{9,8},{10,11... | collective-permute-start | bytes 3981320 | tf_op jit(solution)/shard_map/ppermute | solution.py:77
  74.6 19.2 %copy-start.33 = (pred[2]{0:T(512)(128)(4,1)S(1)}, pred[2]{0:T(512)(128)(4,1)}, u32[]{:S(2)}) copy-start(pred[2]{0:T(512)(128)(4,1)} %copy-done.32) | copy-start | bytes 10
  74.6 19.3 %copy-start.30 = (s32[8,2]{0,1:T(2,128)S(1)}, s32[8,2]{0,1:T(2,128)}, u32[]{:S(2)}) copy-start(s32[8,2]{0,1:T(2,128)} %param.23) | copy-start | bytes 196
  74.6 19.6 %copy-start.31 = (s32[8]{0:T(128)S(1)}, s32[8]{0:T(128)}, u32[]{:S(2)}) copy-start(s32[8]{0:T(128)} %param.22) | copy-start | bytes 100
  74.6 21.1 %copy-start.21 = (f32[8,1,56]{2,1,0:T(1,128)S(1)}, f32[8,1,56]{2,1,0:T(1,128)}, u32[]{:S(2)}) copy-start(f32[8,1,56]{2,1,0:T(1,128)} %copy-done.20) | copy-start | bytes 5380
  74.6 23.1 %copy-start.12 = (f32[2,32,24]{2,1,0:T(8,128)S(1)}, f32[2,32,24]{2,1,0:T(8,128)}, u32[]{:S(2)}) copy-start(f32[2,32,24]{2,1,0:T(8,128)} %copy-done.11) | copy-start | bytes 18436
  93.8 4.9 %collective-permute-start.6 = (bf16[8,312,384]{2,1,0:T(8,128)(2,1)S(1)}, bf16[8,312,384]{2,1,0:T(8,128)(2,1)}, u32[]{:S(2)}, u32[]{:S(2)}) collective-permute-start(bf16[8,312,384]{2,1,0:T(8,128)(2,1)S(1)} %all-to-all-done.3), channel_id=1, source_target_pairs={{0,1},{1,0},{2,3},{3,2},{4,5},{5,4},{6,7},{7,6},{8,9},{9,8},{10,11... | collective-permute-start | bytes 5750792 | tf_op jit(solution)/shard_map/ppermute | solution.py:77
  103.2 20.1 %collective-permute-start.9 = (bf16[2,8,32,192]{3,2,1,0:T(8,128)(2,1)S(1)}, bf16[2,8,32,192]{3,2,1,0:T(8,128)(2,1)S(1)}, u32[]{:S(2)}, u32[]{:S(2)}) collective-permute-start(bf16[2,8,32,192]{3,2,1,0:T(8,128)(2,1)S(1)} %get-tuple-element.201), channel_id=1, source_target_pairs={{0,3},{1,2},{2,1},{3,0},{4,7},{5,6},{6,5},{7,4},{8,11},{9,10},{10,... | collective-permute-start | bytes 589832 | tf_op jit(solution)/shard_map/ppermute | solution.py:117
  103.2 20.1 %collective-permute-start.8 = (bf16[2,8,32,192]{3,2,1,0:T(8,128)(2,1)S(1)}, bf16[2,8,32,192]{3,2,1,0:T(8,128)(2,1)S(1)}, u32[]{:S(2)}, u32[]{:S(2)}) collective-permute-start(bf16[2,8,32,192]{3,2,1,0:T(8,128)(2,1)S(1)} %get-tuple-element.202), channel_id=1, source_target_pairs={{0,2},{1,3},{2,0},{3,1},{4,6},{5,7},{6,4},{7,5},{8,10},{9,11},{10,... | collective-permute-start | bytes 589832 | tf_op jit(solution)/shard_map/ppermute | solution.py:117
  105.3 18.0 %collective-permute-start.7 = (bf16[2,8,32,192]{3,2,1,0:T(8,128)(2,1)S(1)}, bf16[2,8,32,192]{3,2,1,0:T(8,128)(2,1)S(1)}, u32[]{:S(2)}, u32[]{:S(2)}) collective-permute-start(bf16[2,8,32,192]{3,2,1,0:T(8,128)(2,1)S(1)} %get-tuple-element.203), channel_id=1, source_target_pairs={{0,1},{1,0},{2,3},{3,2},{4,5},{5,4},{6,7},{7,6},{8,9},{9,8},{10,11... | collective-permute-start | bytes 589832 | tf_op jit(solution)/shard_map/ppermute | solution.py:117
  206.3 4.2 %collective-permute-start.10 = (bf16[8,312,384]{2,1,0:T(8,128)(2,1)}, bf16[8,312,384]{2,1,0:T(8,128)(2,1)S(1)}, u32[]{:S(2)}, u32[]{:S(2)}) collective-permute-start(bf16[8,312,384]{2,1,0:T(8,128)(2,1)} %get-tuple-element.55), channel_id=1, source_target_pairs={{0,1},{1,0},{2,3},{3,2},{4,5},{5,4},{6,7},{7,6},{8,9},{9,8},{10,11... | collective-permute-start | bytes 5750792 | tf_op jit(solution)/shard_map/ppermute | solution.py:77
  213.9 38.3 %all-to-all-start.4 = ((bf16[8,312,384]{2,1,0:T(8,128)(2,1)}), bf16[8,312,384]{2,1,0:T(8,128)(2,1)S(1)}, u32[]{:S(2)}, u32[]{:S(2)}) async-start(bf16[8,312,384]{2,1,0:T(8,128)(2,1)} %add_convert_fusion), calls=%async_computation.4 | async-start | bytes 3833856 | tf_op jit(solution)/shard_map/all_to_all | solution.py:85
  246.2 3.3 %collective-permute-start.11 = (bf16[8,216,384]{2,1,0:T(8,128)(2,1)}, bf16[8,216,384]{2,1,0:T(8,128)(2,1)S(1)}, u32[]{:S(2)}, u32[]{:S(2)}) collective-permute-start(bf16[8,216,384]{2,1,0:T(8,128)(2,1)} %get-tuple-element.61), channel_id=1, source_target_pairs={{0,1},{1,0},{2,3},{3,2},{4,5},{5,4},{6,7},{7,6},{8,9},{9,8},{10,11... | collective-permute-start | bytes 3981320 | tf_op jit(solution)/shard_map/ppermute | solution.py:77
  252.3 5.5 %copy-start.26 = (f32[2,8,192]{2,1,0:T(8,128)S(1)}, f32[2,8,192]{2,1,0:T(8,128)}, u32[]{:S(2)}) copy-start(f32[2,8,192]{2,1,0:T(8,128)} %get-tuple-element.66) | copy-start | bytes 36868
  252.3 7.0 %copy-start.27 = (f32[2,768]{1,0:T(2,128)S(1)}, f32[2,768]{1,0:T(2,128)}, u32[]{:S(2)}) copy-start(f32[2,768]{1,0:T(2,128)} %reshape.279) | copy-start | bytes 18436
  252.3 26.7 %all-to-all-start.5 = ((bf16[8,216,384]{2,1,0:T(8,128)(2,1)}), bf16[8,216,384]{2,1,0:T(8,128)(2,1)S(1)}, u32[]{:S(2)}, u32[]{:S(2)}) async-start(bf16[8,216,384]{2,1,0:T(8,128)(2,1)} %add_convert_fusion.1), calls=%async_computation.5 | async-start | bytes 2654208 | tf_op jit(solution)/shard_map/all_to_all | solution.py:85
  261.2 16.1 %collective-permute-start.12 = (bf16[264,384]{1,0:T(8,128)(2,1)S(1)}, bf16[264,384]{1,0:T(8,128)(2,1)S(1)}, u32[]{:S(2)}, u32[]{:S(2)}) collective-permute-start(bf16[264,384]{1,0:T(8,128)(2,1)S(1)} %pad_maximum_fusion.2), channel_id=1, source_target_pairs={{0,16},{1,17},{2,18},{3,19},{4,20},{5,21},{6,22},{7,23},{8,24},{9,... | collective-permute-start | bytes 608264 | tf_op jit(solution)/shard_map/ppermute | solution.py:77
  279.2 9.7 %collective-permute-start.13 = (bf16[216,384]{1,0:T(8,128)(2,1)S(1)}, bf16[216,384]{1,0:T(8,128)(2,1)S(1)}, u32[]{:S(2)}, u32[]{:S(2)}) collective-permute-start(bf16[216,384]{1,0:T(8,128)(2,1)S(1)} %convert_element_type.129), channel_id=1, source_target_pairs={{0,16},{1,17},{2,18},{3,19},{4,20},{5,21},{6,22},{7,23},{8,24},{9,... | collective-permute-start | bytes 497672 | tf_op jit(solution)/shard_map/ppermute | solution.py:77
  281.2 7.7 %copy-start.3 = (f32[312,384]{1,0:T(8,128)S(1)}, f32[312,384]{1,0:T(8,128)}, u32[]{:S(2)}) copy-start(f32[312,384]{1,0:T(8,128)} %copy-done.2) | copy-start | bytes 1437700
  282.1 13.8 %all-to-all-start.6 = ((f32[32,16,128]{2,1,0:T(8,128)}), f32[32,16,128]{2,1,0:T(8,128)S(1)}, u32[]{:S(2)}, u32[]{:S(2)}) async-start(f32[32,16,128]{2,1,0:T(8,128)} %bitcast.44), calls=%async_computation.6 | async-start | bytes 524288 | tf_op jit(solution)/shard_map/all_to_all | solution.py:106
  286.0 28.6 %copy-start.14 = (f32[12,384]{1,0:T(8,128)S(1)}, f32[12,384]{1,0:T(8,128)}, u32[]{:S(2)}) copy-start(f32[12,384]{1,0:T(8,128)} %param.27) | copy-start | bytes 55300
  286.0 28.6 %copy-start.23 = (f32[12,384]{1,0:T(8,128)S(1)}, f32[12,384]{1,0:T(8,128)}, u32[]{:S(2)}) copy-start(f32[12,384]{1,0:T(8,128)} %param.35) | copy-start | bytes 55300
  286.0 28.6 %copy-start.24 = (f32[12,384]{1,0:T(8,128)S(1)}, f32[12,384]{1,0:T(8,128)}, u32[]{:S(2)}) copy-start(f32[12,384]{1,0:T(8,128)} %param.36) | copy-start | bytes 55300
  286.6 28.6 %copy-start.10 = (f32[12,1152]{1,0:T(8,128)S(1)}, f32[12,1152]{1,0:T(8,128)}, u32[]{:S(2)}) copy-start(f32[12,1152]{1,0:T(8,128)} %param.26) | copy-start | bytes 165892
  286.6 28.6 %copy-start.15 = (f32[12,1152]{1,0:T(8,128)S(1)}, f32[12,1152]{1,0:T(8,128)}, u32[]{:S(2)}) copy-start(f32[12,1152]{1,0:T(8,128)} %param.33) | copy-start | bytes 165892
  286.6 28.6 %copy-start.16 = (f32[12,1152]{1,0:T(8,128)S(1)}, f32[12,1152]{1,0:T(8,128)}, u32[]{:S(2)}) copy-start(f32[12,1152]{1,0:T(8,128)} %param.34) | copy-start | bytes 165892
  286.6 29.4 %copy-start.25 = (f32[12,6]{0,1:T(8,128)S(1)}, f32[12,6]{0,1:T(8,128)}, u32[]{:S(2)}) copy-start(f32[12,6]{0,1:T(8,128)} %param.28) | copy-start | bytes 868
  286.6 29.4 %copy-start.28 = (f32[12,6]{0,1:T(8,128)S(1)}, f32[12,6]{0,1:T(8,128)}, u32[]{:S(2)}) copy-start(f32[12,6]{0,1:T(8,128)} %param.37) | copy-start | bytes 868
  286.6 29.4 %copy-start.29 = (f32[12,6]{0,1:T(8,128)S(1)}, f32[12,6]{0,1:T(8,128)}, u32[]{:S(2)}) copy-start(f32[12,6]{0,1:T(8,128)} %param.38) | copy-start | bytes 868
  286.7 30.0 %copy-start.8 = (f32[24,768]{1,0:T(8,128)S(1)}, f32[24,768]{1,0:T(8,128)}, u32[]{:S(2)}) copy-start(f32[24,768]{1,0:T(8,128)} %param.24) | copy-start | bytes 221188
  286.7 30.0 %copy-start.17 = (f32[24,768]{1,0:T(8,128)S(1)}, f32[24,768]{1,0:T(8,128)}, u32[]{:S(2)}) copy-start(f32[24,768]{1,0:T(8,128)} %param.29) | copy-start | bytes 221188
  286.7 29.9 %copy-start.18 = (f32[24,768]{1,0:T(8,128)S(1)}, f32[24,768]{1,0:T(8,128)}, u32[]{:S(2)}) copy-start(f32[24,768]{1,0:T(8,128)} %param.30) | copy-start | bytes 221188
  289.6 27.8 %copy-start.1 = (f32[216,384]{1,0:T(8,128)S(1)}, f32[216,384]{1,0:T(8,128)}, u32[]{:S(2)}) copy-start(f32[216,384]{1,0:T(8,128)} %param.25) | copy-start | bytes 995332
  289.6 27.8 %copy-start.5 = (f32[216,384]{1,0:T(8,128)S(1)}, f32[216,384]{1,0:T(8,128)}, u32[]{:S(2)}) copy-start(f32[216,384]{1,0:T(8,128)} %param.31) | copy-start | bytes 995332
  289.6 27.8 %copy-start.6 = (f32[216,384]{1,0:T(8,128)S(1)}, f32[216,384]{1,0:T(8,128)}, u32[]{:S(2)}) copy-start(f32[216,384]{1,0:T(8,128)} %param.32) | copy-start | bytes 995332
  301.6 11.5 %all-to-all-start.7 = ((f32[32,8,128]{2,1,0:T(8,128)}), f32[32,8,128]{2,1,0:T(8,128)S(1)}, u32[]{:S(2)}, u32[]{:S(2)}) async-start(f32[32,8,128]{2,1,0:T(8,128)} %broadcast_in_dim.189), calls=%async_computation.7 | async-start | bytes 262144 | tf_op jit(solution)/shard_map/all_to_all | solution.py:106
  (14 other events, 27.4 us)

commit v5 on v4

--- a/solution.py
+++ b/solution.py
@@ -91,15 +91,11 @@
     return across_classes(jnp.broadcast_to(block[None], (class_count(),) + block.shape))
 
 
-def finish_gather(both, parts):
-    other = exchange(both, 1)
-    low = last_bit() == 0
-    joined, at = [], 0
-    for rows in parts:
-        piece = pair_up(both[:, at : at + rows], other[:, at : at + rows], low, 1)
-        joined.append(piece.reshape((-1,) + piece.shape[2:]))
-        at += rows
-    return joined
+def conv_pieces(both, other, rows):
+    if rows % 8 == 0:
+        return [both, other]
+    joined = pair_up(both[:, :rows], other[:, :rows], last_bit() == 0, 1)
+    return [joined.reshape(-1, both.shape[-1])]
 
 
 def to_all(blocks):
@@ -153,13 +149,13 @@
     return lax.fori_loop(0, total // size, lambda m, c: step(pl.multiple_of(m * size, size), c), init)
 
 
-def norm_sums(load, pixels, channels, member):
+def norm_sums(load, pixels, channels, member, size):
     def step(at, carry):
         values = load(at)
         return (carry[0] + fold(values), carry[1] + fold(values * values))
 
     zero = jnp.zeros((8, channels), jnp.float32)
-    first, second = chunks(pixels, CHUNK, step, (zero, zero))
+    first, second = chunks(pixels, size, step, (zero, zero))
     count = pixels * (channels // GROUPS)
     sums = group_total(two_rows(first, second), member) / count
     mean = sums[0:1]
@@ -167,7 +163,8 @@
     return mean, inverse
 
 
-CHUNK = 256
+CHUNK = 1024
+PART = 256
 
 
 def attention_kernel(parts, places, scalars, middle, *refs):
@@ -218,16 +215,16 @@
         out_acc[...] = jnp.zeros_like(out_acc)
 
     join_strips(places, strips, noise)
-    load = lambda at: middle[0, pl.ds(at, CHUNK), :]
-    mean, inverse = norm_sums(load, pixels, channels, member[...])
+    load = lambda at: middle[0, pl.ds(at, PART), :]
+    mean, inverse = norm_sums(load, pixels, channels, member[...], PART)
     gain, shift = gains[4:5], gains[5:6]
 
     def normalize(at, carry):
         hat = (load(at) - mean) * inverse
-        normed[pl.ds(at, CHUNK), :] = (hat * gain + shift).astype(jnp.bfloat16)
+        normed[pl.ds(at, PART), :] = (hat * gain + shift).astype(jnp.bfloat16)
         return carry
 
-    chunks(pixels, CHUNK, normalize, 0)
+    chunks(pixels, PART, normalize, 0)
 
     block = 256
 
@@ -261,12 +258,12 @@
     divisor, high, wide = scalars[sample, 3], scalars[sample, 4], scalars[sample, 5]
 
     def losses(at, carry):
-        total = load(at) + result[pl.ds(at, CHUNK), :]
-        pixel = at + lax.broadcasted_iota(jnp.int32, (CHUNK, half), 0)
+        total = load(at) + result[pl.ds(at, PART), :]
+        pixel = at + lax.broadcasted_iota(jnp.int32, (PART, half), 0)
         row = (pixel // width).astype(jnp.float32)
         col = (pixel % width).astype(jnp.float32)
         valid = jnp.where((row >= width - high) & (col < wide), 1.0, 0.0)
-        residue = total[:, :half] - noise[pl.ds(at, CHUNK), :].astype(jnp.float32)
+        residue = total[:, :half] - noise[pl.ds(at, PART), :].astype(jnp.float32)
         weight = jax.nn.sigmoid(total[:, half:])
         blended = weight * beta_log + (1.0 - weight) * tilde_log
         spread = jnp.exp(tilde_log - blended)
@@ -280,11 +277,11 @@
             * (beta_log - tilde_log) * weight * (1.0 - weight)
         )
         grad = jnp.concatenate([grad_guess, grad_raw], axis=-1)
-        result[pl.ds(at, CHUNK), :] = grad
-        grad_b[pl.ds(at, CHUNK), :] = grad.astype(jnp.bfloat16)
+        result[pl.ds(at, PART), :] = grad
+        grad_b[pl.ds(at, PART), :] = grad.astype(jnp.bfloat16)
         return carry + fold(pixel_loss)
 
-    loss = chunks(pixels, CHUNK, losses, jnp.zeros((8, half), jnp.float32))
+    loss = chunks(pixels, PART, losses, jnp.zeros((8, half), jnp.float32))
     loss_out[0] = loss * (1.0 / half)
 
     out_acc[...] += mm(attn_t[...], grad_b[...])
@@ -319,23 +316,23 @@
 
     def back_sums(at, carry):
         hat = (load(at) - mean) * inverse
-        grad = gn_t[pl.ds(at, CHUNK), :]
+        grad = gn_t[pl.ds(at, PART), :]
         return (carry[0] + fold(grad * hat), carry[1] + fold(grad))
 
     zero = jnp.zeros((8, channels), jnp.float32)
-    both = chunks(pixels, CHUNK, back_sums, (zero, zero))
+    both = chunks(pixels, PART, back_sums, (zero, zero))
     rows = two_rows(*both)
     sums_out[0] = rows
     means = group_total(rows * gain, member[...]) / (pixels * (channels // GROUPS))
 
     def back_norm(at, carry):
         hat = (load(at) - mean) * inverse
-        grad = gn_t[pl.ds(at, CHUNK), :] * gain
+        grad = gn_t[pl.ds(at, PART), :] * gain
         back = (grad - means[1:2] - hat * means[0:1]) * inverse
-        down_out[0, pl.ds(at, CHUNK), :] = (result[pl.ds(at, CHUNK), :] + back).astype(jnp.bfloat16)
+        down_out[0, pl.ds(at, PART), :] = (result[pl.ds(at, PART), :] + back).astype(jnp.bfloat16)
         return carry
 
-    chunks(pixels, CHUNK, back_norm, 0)
+    chunks(pixels, PART, back_norm, 0)
 
     @pl.when(sample == pl.num_programs(0) - 1)
     def _():
@@ -444,14 +441,35 @@
         joined[pl.ds(pl.multiple_of(places[far] * rows, rows), rows), :] = strip[0]
 
 
-def first_kernel(parts, places, *refs):
-    strips, (gains, member, weight, inner, hidden, stats, images, padded) = refs[:parts], refs[parts:]
+def join_weights(last, pieces, weight):
+    if len(pieces) == 1:
+        weight[...] = pieces[0][...]
+        return
+    rows = weight.shape[0] // (2 * pieces[0].shape[0])
+    for low in range(2):
+
+        @pl.when(last[0] == low)
+        def _():
+            for k in range(pieces[0].shape[0]):
+                both = [pieces[low ^ half][k, 0:rows, :].astype(jnp.float32) for half in range(2)]
+                pair = jnp.concatenate(both, axis=0).astype(jnp.bfloat16)
+                weight[2 * rows * k : 2 * rows * (k + 1), :] = pair
+
+
+def first_kernel(parts, count, places, last, *refs):
+    strips, pieces, refs = refs[:parts], refs[parts : parts + count], refs[parts + count :]
+    gains, member, inner, hidden, stats, images, weight, padded = refs
     _, pixels, channels = images.shape
+
+    @pl.when(pl.program_id(0) == 0)
+    def _():
+        join_weights(last, pieces, weight)
+
     join_strips(places, strips, images.at[0])
     width = side(pixels)
     wide = 3 * channels
     load = lambda at: images[0, pl.ds(at, CHUNK), :].astype(jnp.float32)
-    mean, inverse = norm_sums(load, pixels, channels, member[...])
+    mean, inverse = norm_sums(load, pixels, channels, member[...], CHUNK)
     gain, shift = gains[0:1], gains[1:2]
     clear_edges(padded, width)
 
@@ -465,13 +483,20 @@
     chunks(pixels, CHUNK, activate, 0)
     inner[0] = taps_product(padded, lambda i: weight[i * wide : (i + 1) * wide, :], pixels, width)
     mean_two, inverse_two = norm_sums(
-        lambda at: inner[0, pl.ds(at, CHUNK), :], pixels, channels, member[...]
+        lambda at: inner[0, pl.ds(at, CHUNK), :], pixels, channels, member[...], CHUNK
     )
     stats[0] = rows_of(mean, inverse, mean_two, inverse_two)
 
 
-def second_kernel(inner, images, stats, film, gains, weight, middle, hidden, padded):
+def second_kernel(count, last, *refs):
+    pieces, refs = refs[:count], refs[count:]
+    inner, images, stats, film, gains, middle, hidden, weight, padded = refs
     _, pixels, channels = inner.shape
+
+    @pl.when(pl.program_id(0) == 0)
+    def _():
+        join_weights(last, pieces, weight)
+
     width = side(pixels)
     wide = 3 * channels
     mean, inverse = stats[0, 2:3], stats[0, 3:4]
@@ -667,21 +692,25 @@
     few_f = sized(f32, samples, 8, channels)
     flops = 18 * samples * pixels * channels * channels
 
-    def first(places, strips, gains, member, weight):
-        parts = len(strips)
+    weight_out = (weight_spec, sized(bf, 9 * channels, channels))
+    smem = pl.BlockSpec(memory_space=pltpu.SMEM)
+
+    def first(places, last, strips, pieces, gains, member):
+        parts, count = len(strips), len(pieces)
         return per_sample(
-            functools.partial(first_kernel, parts), samples,
-            [pl.BlockSpec(memory_space=pltpu.SMEM)] + [each(pixels // parts, channels)] * parts
-            + [gain_spec, member_spec, weight_spec],
-            [(act, act_f), (act, act_b), (few, few_f), (act, act_b)], [padded], flops,
-            places, *strips, gains, member, weight,
+            functools.partial(first_kernel, parts, count), samples,
+            [smem, smem] + [each(pixels // parts, channels)] * parts
+            + [whole(*piece.shape) for piece in pieces] + [gain_spec, member_spec],
+            [(act, act_f), (act, act_b), (few, few_f), (act, act_b), weight_out], [padded], flops,
+            places, last, *strips, *pieces, gains, member,
         )
 
-    def second(inner, images, stats, film, gains, weight):
+    def second(last, pieces, inner, images, stats, film, gains):
         return per_sample(
-            second_kernel, samples, [act, act, few, few, gain_spec, weight_spec],
-            [(act, act_f), (act, act_b)], [padded], flops,
-            inner, images, stats, film, gains, weight,
+            functools.partial(second_kernel, len(pieces)), samples,
+            [smem] + [whole(*piece.shape) for piece in pieces] + [act, act, few, few, gain_spec],
+            [(act, act_f), (act, act_b), weight_out], [padded], flops,
+            last, *pieces, inner, images, stats, film, gains,
         )
 
     def weights(hidden, grad, place, classes, others=()):
@@ -789,6 +818,10 @@
     theirs = exchange(ours, top_mask)
     strips = strips_of(images)
     low, high = jnp.where(is_top, theirs, ours), jnp.where(is_top, ours, theirs)
+    every_one = gather_classes(behind(low, smalls, *strips))
+    rest = jnp.concatenate([qkv_master.reshape(-1, channels), out_master]).astype(jnp.bfloat16)
+    rest = behind(rest, theirs)
+    rest_two = pair_up(rest, exchange(rest, top_mask), jnp.logical_not(is_top), 0)
     smalls = smalls.reshape(devices, -1)
     gain_f = smalls[:, : gains.size].reshape(channels, 6)
     dp_smalls = smalls.reshape(lax.axis_size("dp"), lax.axis_size("head"), -1)[:, 0, gains.size :]
@@ -813,19 +846,17 @@
         (((1,), (1,)), ((), ())),
         preferred_element_type=jnp.float32,
     )
-    film_blocks = film_rows_out.T.reshape(devices, -1)
-    film_blocks = jnp.pad(film_blocks, ((0, 0), (0, -film_blocks.shape[1] % 128)))
-    film_blocks = to_all(film_blocks[:, None]).reshape(devices, -1)
-    film_blocks = film_blocks[:, : samples * film_rows].reshape(devices, samples, film_rows)
-    film_out = jnp.moveaxis(film_blocks, 1, 0).reshape(samples, devices * film_rows)
-    every_one = gather_classes(behind(low, film_out, *strips))
-    rest = jnp.concatenate([qkv_master.reshape(-1, channels), out_master]).astype(jnp.bfloat16)
-    rest = behind(rest, theirs)
-    rest_two = pair_up(rest, exchange(rest, top_mask), jnp.logical_not(is_top), 0)
-    every_two = gather_classes(
-        behind(jnp.concatenate([high, rest_two.reshape(-1, channels)]), every_one)
-    )
-    gains_t = jnp.pad(gain_f.T, ((0, 2), (0, 0)))
+    film_flat = film_rows_out.T.reshape(-1, channels)
+    film_high = lax.reduce_precision(film_flat, 8, 7)
+    film_parts = jnp.concatenate([film_high, film_flat - film_high]).astype(jnp.bfloat16)
+    film_lines = film_flat.shape[0]
+    film_two = pair_up(film_parts, exchange(film_parts, top_mask), jnp.logical_not(is_top), 0)
+    two_block = jnp.concatenate(
+        [high, rest_two.reshape(-1, channels), film_two.reshape(-1, channels)]
+    )
+    every_two = gather_classes(behind(two_block, every_one))
+    gain_gate = two_block
+    gains_t = behind(jnp.pad(gain_f.T, ((0, 2), (0, 0))), gain_gate)
     member = jnp.asarray(np.kron(np.eye(GROUPS), np.ones((channels // GROUPS,) * 2)), jnp.bfloat16)
     scalars = jnp.stack(
         [log_beta, log_tilde, factor, jnp.broadcast_to(divisor, factor.shape)]
@@ -834,21 +865,36 @@
     )
     first_call, second_call, weights, second_back, first_back = block_calls(samples, pixels, channels)
     flat = lambda values: [v.reshape(samples, strip_rows * width_px, -1) for v in values]
-    (taps_one,) = finish_gather(every_one, [conv_rows])
-    taps_one = taps_one.reshape(-1, channels)
-    inner, hidden_one, stats, source = first_call(places, flat(strips), gains_t, member, taps_one)
-    taps_two, others = finish_gather(behind(every_two, inner), [conv_rows, 8 * out_rows])
-    taps_two = taps_two.reshape(-1, channels)
+    place = last_bit().reshape(1).astype(jnp.int32)
+    pieces_one = conv_pieces(every_one, exchange(every_one, 1), conv_rows)
+    inner, hidden_one, stats, source, taps_one = first_call(
+        places, place, flat(strips), pieces_one, gains_t, member
+    )
+    every_two = behind(every_two, inner)
+    other_two = exchange(every_two, 1)
+    pieces_two = conv_pieces(every_two, other_two, conv_rows)
+    film_at = conv_rows + 8 * out_rows
+    first_own = lax.axis_index("dp") * local_samples + first
+    line, spot = first_own * film_rows // channels, first_own * film_rows % channels
+    film_got = pair_up(every_two[:, film_at:], other_two[:, film_at:], last_bit() == 0, 1)
+    film_got = film_got.reshape(classes, 2, 2, 2, film_lines, channels)
+    film_got = lax.dynamic_slice(
+        film_got, (0, 0, 0, 0, line, spot), film_got.shape[:4] + (1, samples * film_rows)
+    ).astype(jnp.float32)
+    film_got = jnp.sum(film_got, axis=(3, 4)).reshape(classes, 2, 2, samples, film_rows)
+    film_out = film_got.transpose(3, 2, 0, 1, 4).reshape(samples, devices * film_rows)
+    noise_strips = strips_of(behind(noise, other_two))
+    film = jnp.pad(film_out.reshape(samples, 2, channels), ((0, 0), (0, 6), (0, 0)))
+    scale = 1.0 + film_out[:, :channels]
+    middle, hidden_two, taps_two = second_call(
+        place, pieces_two, inner, source, stats, film, gains_t
+    )
+    others = pair_up(every_two[:, conv_rows:film_at], other_two[:, conv_rows:film_at], last_bit() == 0, 1)
     others = jnp.moveaxis(others.reshape(-1, 2, 4 * out_rows, channels), 0, 1)
     others = others.reshape(devices, 4 * out_rows, channels)
     qkv_w = others[:, : 3 * out_rows].reshape(channels, 3 * channels)
     out_w = others[:, 3 * out_rows :].reshape(channels, channels)
-    noise_strips = strips_of(behind(noise, taps_two))
-    film = jnp.pad(film_out.reshape(samples, 2, channels), ((0, 0), (0, 6), (0, 0)))
-    scale = 1.0 + film_out[:, :channels]
-    middle, hidden_two = second_call(inner, source, stats, film, gains_t, taps_two)
     my_last = last_bit()
-    place = my_last.reshape(1).astype(jnp.int32)
     line = jnp.arange(channels, dtype=jnp.int32)
     owner, spot = line // out_rows, line % out_rows
     source_device = (

time: 317 us -> 297 us (0.937); the launches traced: 320 us -> 293 us
  Pallas kernels: 155 us -> 136 us
  other arithmetic: 31.7 us -> 24.3 us
  starting transfers between devices: 45.5 us -> 41.5 us
    pallas_call x1, Pallas kernels: 68.9 us -> 54.7 us  [attention_block(): pl.pallas_call(functools.partial(attention_kernel, parts), grid=(samples,...]
    all_to_all x4 -> x3, starting transfers between devices: 17.5 us -> 9.63 us  [to_all(): lax.all_to_all(blocks, ('dp', 'head'), split_axis=0, concat_axis=0, tiled...]
    select_n x3 -> x2, other arithmetic: 6.03 us -> 0.16 us  [pair_up(): jnp.where(first == low, jnp.expand_dims(block, place), jnp.expand_dims(ot...]
    all_to_all x4, waiting for transfers between devices: 7.28 us -> 12.1 us  [across_classes(): lax.all_to_all(blocks, ('dp', 'head'), split_axis=0, concat_axis=0, axis_...]
    ppermute x8 -> x9, waiting for transfers between devices: 25.4 us -> 20.8 us  [exchange(): lax.ppermute(values, ('dp', 'head'), [(i, i ^ mask) for i in range(size)])]
    ppermute x8 -> x9, starting transfers between devices: 6.13 us -> 10.3 us  [exchange(): lax.ppermute(values, ('dp', 'head'), [(i, i ^ mask) for i in range(size)])]
    pallas_call x6, Pallas kernels: 85.8 us -> 81.7 us  [per_sample(): pl.pallas_call(kernel, grid=(samples,), in_specs=in_specs, out_specs=[spe...]
    all_to_all x4 -> x3, waiting for transfers between devices: 24 us -> 26 us  [to_all(): lax.all_to_all(blocks, ('dp', 'head'), split_axis=0, concat_axis=0, tiled...]
  transfers between devices with their start and end apart: 22 -> 22, of which waited for: 12 -> 13; matrix products, arithmetic and copies ran while one was open for 10% -> 10% of each run, Pallas kernels for 23% -> 23%
where the time goes in v5:
time: 297 us; the launch traced here: 293 us
  Pallas kernels  136 us (46%)
  waiting for transfers between devices  58.9 us (20%)
  starting transfers between devices  41.5 us (14%)
  other arithmetic  24.3 us (8%)
  local copies, waits for them, and re-layouts  24.2 us (8%)
  between operations  6.84 us (2%)
    pallas_call x6, Pallas kernels, per_sample(): pl.pallas_call(kernel, grid=(samples,), in_specs=in_specs, out_specs=[spe...  81.7 us
    pallas_call x1, Pallas kernels, attention_block(): pl.pallas_call(functools.partial(attention_kernel, parts), grid=(samples,...  54.7 us
    all_to_all x3, waiting for transfers between devices, to_all(): lax.all_to_all(blocks, ('dp', 'head'), split_axis=0, concat_axis=0, tiled...  26 us
    ppermute x9, waiting for transfers between devices, exchange(): lax.ppermute(values, ('dp', 'head'), [(i, i ^ mask) for i in range(size)])  20.8 us
    all_to_all x4, starting transfers between devices, across_classes(): lax.all_to_all(blocks, ('dp', 'head'), split_axis=0, concat_axis=0, axis_...  17.8 us
    all_to_all x4, waiting for transfers between devices, across_classes(): lax.all_to_all(blocks, ('dp', 'head'), split_axis=0, concat_axis=0, axis_...  12.1 us
    ppermute x9, starting transfers between devices, exchange(): lax.ppermute(values, ('dp', 'head'), [(i, i ^ mask) for i in range(size)])  10.3 us
    all_to_all x3, starting transfers between devices, to_all(): lax.all_to_all(blocks, ('dp', 'head'), split_axis=0, concat_axis=0, tiled...  9.63 us
  transfers between devices with their start and end apart: 22, of which 13 were waited for; matrix products, arithmetic and copies ran while one was open for 10% of the time, Pallas kernels for 23%

profile of v5, /device:TPU:0, one launch (start us, length us, event | category | flops | bytes accessed | tf_op | source)
XLA Modules:
  0.0 293.3 jit_solution(16175495067421940745)
XLA Ops:
  0.7 1.0 convert_element_type.116
  1.7 4.1 %collective-permute-start = (bf16[216,384]{1,0:T(8,128)(2,1)S(1)}, bf16[216,384]{1,0:T(8,128)(2,1)S(1)}, u32[]{:S(2)}, u32[]{:S(2)}) collective-permute-start(bf16[216,384]{1,0:T(8,128)(2,1)S(1)} %convert_element_type.116), channel_id=1, source_target_pairs={{0,16},{1,17},{2,18},{3,19},{4,20},{5,21},{6,22},{7,23},{8,24},{9,... | collective-permute-start | bytes 497672 | tf_op jit(solution)/shard_map/ppermute | solution.py:77
  5.8 2.3 constant_dynamic-slice_fusion.6
  8.1 1.5 collective-permute-start.4
  11.0 3.8 %all-to-all-start = ((f32[32,1,128]{2,1,0:T(1,128)}), f32[32,1,128]{2,1,0:T(1,128)S(1)}, u32[]{:S(2)}, u32[]{:S(2)}) async-start(f32[32,1,128]{2,1,0:T(1,128)} %broadcast_in_dim.166), calls=%async_computation | async-start | bytes 32768 | tf_op jit(solution)/shard_map/all_to_all | solution.py:102
  15.0 13.2 %all-to-all-done = f32[32,1,128]{2,1,0:T(1,128)S(1)} async-done(((f32[32,1,128]{2,1,0:T(1,128)}), f32[32,1,128]{2,1,0:T(1,128)S(1)}, u32[]{:S(2)}, u32[]{:S(2)}) %all-to-all-start) | async-done | bytes 16416 | tf_op jit(solution)/shard_map/all_to_all | solution.py:102
  28.2 1.3 broadcast_in_dim.181
  29.7 4.7 %all-to-all-start.1 = ((bf16[8,216,384]{2,1,0:T(8,128)(2,1)}), bf16[8,216,384]{2,1,0:T(8,128)(2,1)S(1)}, u32[]{:S(2)}, u32[]{:S(2)}) async-start(bf16[8,216,384]{2,1,0:T(8,128)(2,1)} %broadcast_in_dim.181), calls=%async_computation.1 | async-start | bytes 2654208 | tf_op jit(solution)/shard_map/all_to_all | solution.py:85
  36.8 2.6 collective-permute-start.1
  39.4 10.4 %collective-permute-done.2 = bf16[8,384]{1,0:T(8,128)(2,1)S(1)} collective-permute-done((bf16[8,384]{1,0:T(8,128)(2,1)S(1)}, bf16[8,384]{1,0:T(8,128)(2,1)S(1)}, u32[]{:S(2)}, u32[]{:S(2)}) %collective-permute-start.2) | collective-permute-done | bytes 6176 | tf_op jit(solution)/shard_map/ppermute | solution.py:77
  50.3 1.9 all-to-all-done.1.refs_4_
  52.2 1.7 broadcast_in_dim.182
  53.8 3.8 %all-to-all-start.2 = ((bf16[8,328,384]{2,1,0:T(8,128)(2,1)}), bf16[8,328,384]{2,1,0:T(8,128)(2,1)S(1)}, u32[]{:S(2)}, u32[]{:S(2)}) async-start(bf16[8,328,384]{2,1,0:T(8,128)(2,1)} %broadcast_in_dim.182), calls=%async_computation.2 | async-start | bytes 4030464 | tf_op jit(solution)/shard_map/all_to_all | solution.py:85
  59.0 1.0 copy.164
  60.9 15.0 %shard_map.323 = (f32[2,1024,384]{2,1,0:T(8,128)}, bf16[2,1024,384]{2,1,0:T(8,128)(2,1)}, f32[2,8,384]{2,1,0:T(8,128)}, bf16[2,1024,384]{2,1,0:T(8,128)(2,1)}, bf16[3456,384]{1,0:T(8,128)(2,1)}) custom-call(s32[4]{0:T(128)} %iota_xor_fusion.places, s32[1]{0:T(128)} %bitcast.5.last.place, bf16[2,256,384]{2,1,0:T(8,128)(2,1)} %bitcast.93, ...), custom_call_target="tpu_custom_call" | custom-call | flops 5435817984 | bytes 5435817 | tf_op jit(solution)/shard_map/pallas_call | solution.py:664
  75.9 8.7 %all-to-all-done.2.refs_0_ = bf16[8,328,384]{2,1,0:T(8,128)(2,1)S(1)} async-done(((bf16[8,328,384]{2,1,0:T(8,128)(2,1)}), bf16[8,328,384]{2,1,0:T(8,128)(2,1)S(1)}, u32[]{:S(2)}, u32[]{:S(2)}) %all-to-all-start.2) | async-done | bytes 2015264 | tf_op jit(solution)/shard_map/all_to_all | solution.py:85
  85.7 0.8 fusion.refs_8_
  88.8 0.9 slice.158
  90.8 2.1 constant_dynamic-slice_fusion.1
  93.3 1.4 collective-permute-start.10
  94.7 1.1 slice.159
  95.8 13.7 %shard_map.324 = (f32[2,1024,384]{2,1,0:T(8,128)}, bf16[2,1024,384]{2,1,0:T(8,128)(2,1)}, bf16[3456,384]{1,0:T(8,128)(2,1)}) custom-call(s32[1]{0:T(128)} %bitcast.5.last.place, bf16[8,328,384]{2,1,0:T(8,128)(2,1)} %copy-done, bf16[8,328,384]{2,1,0:T(8,128)(2,1)} %collective-permute-done.7.refs_1_, f32[2,1024,384]{2,1,0:T(8,128)} %get-tuple-element.49.refs_2_.inner, ...), custom_call_target="tpu_custom_call" | custom-call | flops 5435817984 | bytes 5435817 | tf_op jit(solution)/shard_map/pallas_call | solution.py:664
  110.3 1.4 reshape.300.refs_6_
  113.4 54.7 %shard_map.325 = (bf16[2,1024,384]{2,1,0:T(8,128)(2,1)}, bf16[384,1536]{1,0:T(8,128)(2,1)}, f32[2,8,384]{2,1,0:T(8,128)}, f32[2,8,192]{2,1,0:T(8,128)}) custom-call(s32[4]{0:T(128)} %iota_xor_fusion.places, f32[2,6]{1,0:T(2,128)} %stack.47.scalars, f32[2,1024,384]{2,1,0:T(8,128)} %get-tuple-element.53.middle, bf16[2,256,192]{2,1,0:T(8,128)(2,1)} %bitcast.94, ...), custom_call_target="tpu_custom_call" | custom-call | flops 24159191040 | bytes 6291456 | tf_op jit(solution)/shard_map/pallas_call | solution.py:349
  168.1 13.1 %shard_map.326 = (bf16[8,312,384]{2,1,0:T(8,128)(2,1)}, bf16[8,312,384]{2,1,0:T(8,128)(2,1)}) custom-call(s32[1]{0:T(128)} %bitcast.5.last.place, bf16[2,1024,384]{2,1,0:T(8,128)(2,1)} %get-tuple-element.56.hidden, bf16[2,1024,384]{2,1,0:T(8,128)(2,1)} %get-tuple-element.60.grad, bf16[384,1536]{1,0:T(8,128)(2,1)} %get-tuple-element.57.refs_0_), custom_call_target="tpu_custom_call" | custom-call | flops 5435817984 | bytes 5435817 | tf_op jit(solution)/shard_map/pallas_call | solution.py:664
  182.0 3.7 %collective-permute-done.11 = bf16[8,312,384]{2,1,0:T(8,128)(2,1)S(1)} collective-permute-done((bf16[8,312,384]{2,1,0:T(8,128)(2,1)}, bf16[8,312,384]{2,1,0:T(8,128)(2,1)S(1)}, u32[]{:S(2)}, u32[]{:S(2)}) %collective-permute-start.11) | collective-permute-done | bytes 1916960 | tf_op jit(solution)/shard_map/ppermute | solution.py:77
  185.7 3.3 %add_convert_fusion = bf16[8,312,384]{2,1,0:T(8,128)(2,1)} fusion(bf16[8,312,384]{2,1,0:T(8,128)(2,1)S(1)} %collective-permute-done.11, bf16[8,312,384]{2,1,0:T(8,128)(2,1)} %get-tuple-element.58), kind=kLoop, calls=%fused_computation.1 | loop fusion | flops 3833856 | bytes 5750784 | tf_op jit(solution)/shard_map/convert_element_type | solution.py:911
  189.0 3.8 %all-to-all-start.3 = ((bf16[8,312,384]{2,1,0:T(8,128)(2,1)}), bf16[8,312,384]{2,1,0:T(8,128)(2,1)S(1)}, u32[]{:S(2)}, u32[]{:S(2)}) async-start(bf16[8,312,384]{2,1,0:T(8,128)(2,1)} %add_convert_fusion), calls=%async_computation.3 | async-start | bytes 3833856 | tf_op jit(solution)/shard_map/all_to_all | solution.py:85
  192.9 15.2 %shard_map.327 = (bf16[2,1024,384]{2,1,0:T(8,128)(2,1)}, f32[2,8,384]{2,1,0:T(8,128)}) custom-call(bf16[2,1024,384]{2,1,0:T(8,128)(2,1)} %get-tuple-element.60.grad, f32[2,1024,384]{2,1,0:T(8,128)} %get-tuple-element.49.refs_2_.inner, f32[2,8,384]{2,1,0:T(8,128)} %get-tuple-element.52.refs_4_.stats, f32[2,8,384]{2,1,0:T(8,128)} %pad.18.refs_5_.film, ...), custom_call_target="tpu_custom_call" | custom-call | flops 5435817984 | bytes 5435817 | tf_op jit(solution)/shard_map/pallas_call | solution.py:664
  208.0 12.2 %shard_map.328 = (bf16[8,216,384]{2,1,0:T(8,128)(2,1)}, bf16[8,216,384]{2,1,0:T(8,128)(2,1)}) custom-call(s32[1]{0:T(128)} %bitcast.5.last.place, bf16[2,1024,384]{2,1,0:T(8,128)(2,1)} %get-tuple-element.64.hidden, bf16[2,1024,384]{2,1,0:T(8,128)(2,1)} %get-tuple-element.67.grad), custom_call_target="tpu_custom_call" | custom-call | flops 5435817984 | bytes 5435817 | tf_op jit(solution)/shard_map/pallas_call | solution.py:664
  220.6 2.9 collective-permute-done.12
  223.5 2.7 add_convert_fusion.1
  226.2 5.5 %all-to-all-start.4 = ((bf16[8,216,384]{2,1,0:T(8,128)(2,1)}), bf16[8,216,384]{2,1,0:T(8,128)(2,1)S(1)}, u32[]{:S(2)}, u32[]{:S(2)}) async-start(bf16[8,216,384]{2,1,0:T(8,128)(2,1)} %add_convert_fusion.1), calls=%async_computation.4 | async-start | bytes 2654208 | tf_op jit(solution)/shard_map/all_to_all | solution.py:85
  231.7 0.8 slice_reduce_fusion.8
  233.4 0.8 slice_reduce_fusion.5
  236.2 12.5 %shard_map.329 = f32[2,8,384]{2,1,0:T(8,128)} custom-call(bf16[2,1024,384]{2,1,0:T(8,128)(2,1)} %get-tuple-element.67.grad, bf16[2,1024,384]{2,1,0:T(8,128)(2,1)} %get-tuple-element.51.refs_3_.images, f32[2,8,384]{2,1,0:T(8,128)} %get-tuple-element.52.refs_4_.stats, f32[8,384]{1,0:T(8,128)} %pad.17.refs_6_.refs_4_.gains, ...), custom_call_target="tpu_custom_call" | custom-call | flops 5435817984 | bytes 5435817 | tf_op jit(solution)/shard_map/pallas_call | solution.py:664
  248.7 0.8 slice_reduce_fusion.3
  249.6 1.8 collective-permute-done.13
  251.4 1.6 all-to-all-done.4
  253.2 1.9 collective-permute-start.14
  256.2 3.2 %all-to-all-start.5 = ((f32[32,16,128]{2,1,0:T(8,128)}), f32[32,16,128]{2,1,0:T(8,128)S(1)}, u32[]{:S(2)}, u32[]{:S(2)}) async-start(f32[32,16,128]{2,1,0:T(8,128)} %bitcast.40), calls=%async_computation.5 | async-start | bytes 524288 | tf_op jit(solution)/shard_map/all_to_all | solution.py:102
  260.8 1.4 collective-permute-done.14
  262.9 7.1 %all-to-all-done.5 = f32[32,16,128]{2,1,0:T(8,128)S(1)} async-done(((f32[32,16,128]{2,1,0:T(8,128)}), f32[32,16,128]{2,1,0:T(8,128)S(1)}, u32[]{:S(2)}, u32[]{:S(2)}) %all-to-all-start.5) | async-done | bytes 262176 | tf_op jit(solution)/shard_map/all_to_all | solution.py:102
  270.9 0.9 multiply_reduce_fusion.2
  275.6 2.6 all-to-all-start.6
  278.9 1.9 pad_maximum_fusion.8
  280.8 5.7 %all-to-all-done.6 = f32[32,8,128]{2,1,0:T(8,128)S(1)} async-done(((f32[32,8,128]{2,1,0:T(8,128)}), f32[32,8,128]{2,1,0:T(8,128)S(1)}, u32[]{:S(2)}, u32[]{:S(2)}) %all-to-all-start.6) | async-done | bytes 131104 | tf_op jit(solution)/shard_map/all_to_all | solution.py:102
  290.0 1.1 multiply_subtract_fusion
  (216 shorter events, 26.5 us)
Async XLA Ops:
  1.7 13.2 %collective-permute-start = (bf16[216,384]{1,0:T(8,128)(2,1)S(1)}, bf16[216,384]{1,0:T(8,128)(2,1)S(1)}, u32[]{:S(2)}, u32[]{:S(2)}) collective-permute-start(bf16[216,384]{1,0:T(8,128)(2,1)S(1)} %convert_element_type.116), channel_id=1, source_target_pairs={{0,16},{1,17},{2,18},{3,19},{4,20},{5,21},{6,22},{7,23},{8,24},{9,... | collective-permute-start | bytes 497672 | tf_op jit(solution)/shard_map/ppermute | solution.py:77
  5.8 9.1 %copy-start.1 = (f32[216,384]{1,0:T(8,128)S(1)}, f32[216,384]{1,0:T(8,128)}, u32[]{:S(2)}) copy-start(f32[216,384]{1,0:T(8,128)} %param.25) | copy-start | bytes 995332
  8.1 20.1 %collective-permute-start.3 = (bf16[2,8,32,384]{3,2,1,0:T(8,128)(2,1)S(1)}, bf16[2,8,32,384]{3,2,1,0:T(8,128)(2,1)S(1)}, u32[]{:S(2)}, u32[]{:S(2)}) collective-permute-start(bf16[2,8,32,384]{3,2,1,0:T(8,128)(2,1)S(1)} %get-tuple-element.204), channel_id=1, source_target_pairs={{0,1},{1,0},{2,3},{3,2},{4,5},{5,4},{6,7},{7,6},{8,9},{9,8},{10,11... | collective-permute-start | bytes 1179656 | tf_op jit(solution)/shard_map/ppermute | solution.py:113
  8.1 20.1 %collective-permute-start.4 = (bf16[2,8,32,384]{3,2,1,0:T(8,128)(2,1)S(1)}, bf16[2,8,32,384]{3,2,1,0:T(8,128)(2,1)S(1)}, u32[]{:S(2)}, u32[]{:S(2)}) collective-permute-start(bf16[2,8,32,384]{3,2,1,0:T(8,128)(2,1)S(1)} %get-tuple-element.206), channel_id=1, source_target_pairs={{0,2},{1,3},{2,0},{3,1},{4,6},{5,7},{6,4},{7,5},{8,10},{9,11},{10,... | collective-permute-start | bytes 1179656 | tf_op jit(solution)/shard_map/ppermute | solution.py:113
  9.6 18.6 %collective-permute-start.5 = (bf16[2,8,32,384]{3,2,1,0:T(8,128)(2,1)S(1)}, bf16[2,8,32,384]{3,2,1,0:T(8,128)(2,1)S(1)}, u32[]{:S(2)}, u32[]{:S(2)}) collective-permute-start(bf16[2,8,32,384]{3,2,1,0:T(8,128)(2,1)S(1)} %get-tuple-element.203), channel_id=1, source_target_pairs={{0,3},{1,2},{2,1},{3,0},{4,7},{5,6},{6,5},{7,4},{8,11},{9,10},{10,... | collective-permute-start | bytes 1179656 | tf_op jit(solution)/shard_map/ppermute | solution.py:113
  11.0 17.2 %all-to-all-start = ((f32[32,1,128]{2,1,0:T(1,128)}), f32[32,1,128]{2,1,0:T(1,128)S(1)}, u32[]{:S(2)}, u32[]{:S(2)}) async-start(f32[32,1,128]{2,1,0:T(1,128)} %broadcast_in_dim.166), calls=%async_computation | async-start | bytes 32768 | tf_op jit(solution)/shard_map/all_to_all | solution.py:102
  29.6 4.9 %copy-start.9 = (f32[12,1152]{1,0:T(8,128)S(1)}, f32[12,1152]{1,0:T(8,128)}, u32[]{:S(2)}) copy-start(f32[12,1152]{1,0:T(8,128)} %param.26) | copy-start | bytes 165892
  29.6 4.9 %copy-start.11 = (f32[12,384]{1,0:T(8,128)S(1)}, f32[12,384]{1,0:T(8,128)}, u32[]{:S(2)}) copy-start(f32[12,384]{1,0:T(8,128)} %param.27) | copy-start | bytes 55300
  29.6 5.7 %copy-start.8 = (f32[24,768]{1,0:T(8,128)S(1)}, f32[24,768]{1,0:T(8,128)}, u32[]{:S(2)}) copy-start(f32[24,768]{1,0:T(8,128)} %param.24) | copy-start | bytes 221188
  29.7 22.4 %all-to-all-start.1 = ((bf16[8,216,384]{2,1,0:T(8,128)(2,1)}), bf16[8,216,384]{2,1,0:T(8,128)(2,1)S(1)}, u32[]{:S(2)}, u32[]{:S(2)}) async-start(bf16[8,216,384]{2,1,0:T(8,128)(2,1)} %broadcast_in_dim.181), calls=%async_computation.1 | async-start | bytes 2654208 | tf_op jit(solution)/shard_map/all_to_all | solution.py:85
  35.6 14.2 %collective-permute-start.2 = (bf16[8,384]{1,0:T(8,128)(2,1)S(1)}, bf16[8,384]{1,0:T(8,128)(2,1)S(1)}, u32[]{:S(2)}, u32[]{:S(2)}) collective-permute-start(bf16[8,384]{1,0:T(8,128)(2,1)S(1)} %pad_maximum_fusion.7), channel_id=1, source_target_pairs={{0,16},{1,17},{2,18},{3,19},{4,20},{5,21},{6,22},{7,23},{8,24},{9,... | collective-permute-start | bytes 18440 | tf_op jit(solution)/shard_map/ppermute | solution.py:77
  36.8 13.3 %collective-permute-start.1 = (bf16[48,384]{1,0:T(8,128)(2,1)S(1)}, bf16[48,384]{1,0:T(8,128)(2,1)S(1)}, u32[]{:S(2)}, u32[]{:S(2)}) collective-permute-start(bf16[48,384]{1,0:T(8,128)(2,1)S(1)} %pad_maximum_fusion.5), channel_id=1, source_target_pairs={{0,16},{1,17},{2,18},{3,19},{4,20},{5,21},{6,22},{7,23},{8,24},{9,... | collective-permute-start | bytes 110600 | tf_op jit(solution)/shard_map/ppermute | solution.py:77
  52.2 5.5 %copy-start.5 = (bf16[8,216,384]{2,1,0:T(8,128)(2,1)}, bf16[8,216,384]{2,1,0:T(8,128)(2,1)S(1)}, u32[]{:S(2)}) copy-start(bf16[8,216,384]{2,1,0:T(8,128)(2,1)S(1)} %all-to-all-done.1.refs_4_) | copy-start | bytes 3981316
  53.8 30.8 %all-to-all-start.2 = ((bf16[8,328,384]{2,1,0:T(8,128)(2,1)}), bf16[8,328,384]{2,1,0:T(8,128)(2,1)S(1)}, u32[]{:S(2)}, u32[]{:S(2)}) async-start(bf16[8,328,384]{2,1,0:T(8,128)(2,1)} %broadcast_in_dim.182), calls=%async_computation.2 | async-start | bytes 4030464 | tf_op jit(solution)/shard_map/all_to_all | solution.py:85
  57.6 3.3 %collective-permute-start.6 = (bf16[8,216,384]{2,1,0:T(8,128)(2,1)S(1)}, bf16[8,216,384]{2,1,0:T(8,128)(2,1)}, u32[]{:S(2)}, u32[]{:S(2)}) collective-permute-start(bf16[8,216,384]{2,1,0:T(8,128)(2,1)S(1)} %all-to-all-done.1.refs_4_), channel_id=1, source_target_pairs={{0,1},{1,0},{2,3},{3,2},{4,5},{5,4},{6,7},{7,6},{8,9},{9,8},{10,11... | collective-permute-start | bytes 3981320 | tf_op jit(solution)/shard_map/ppermute | solution.py:77
  60.9 23.7 %copy-start.28 = (pred[2]{0:T(512)(128)(4,1)S(1)}, pred[2]{0:T(512)(128)(4,1)}, u32[]{:S(2)}) copy-start(pred[2]{0:T(512)(128)(4,1)} %get-tuple-element.228) | copy-start | bytes 10
  60.9 23.8 %copy-start.30 = (s32[8]{0:T(128)S(1)}, s32[8]{0:T(128)}, u32[]{:S(2)}) copy-start(s32[8]{0:T(128)} %param.22) | copy-start | bytes 100
  60.9 24.4 %copy-start.27 = (s32[8,2]{0,1:T(2,128)S(1)}, s32[8,2]{0,1:T(2,128)}, u32[]{:S(2)}) copy-start(s32[8,2]{0,1:T(2,128)} %param.23) | copy-start | bytes 196
  60.9 25.6 %copy-start.17 = (f32[8,1,56]{2,1,0:T(1,128)S(1)}, f32[8,1,56]{2,1,0:T(1,128)}, u32[]{:S(2)}) copy-start(f32[8,1,56]{2,1,0:T(1,128)} %copy-done.16) | copy-start | bytes 5380
  84.6 8.2 %copy-start = (bf16[8,328,384]{2,1,0:T(8,128)(2,1)}, bf16[8,328,384]{2,1,0:T(8,128)(2,1)S(1)}, u32[]{:S(2)}) copy-start(bf16[8,328,384]{2,1,0:T(8,128)(2,1)S(1)} %all-to-all-done.2.refs_0_) | copy-start | bytes 6045700
  84.6 4.2 %collective-permute-start.7 = (bf16[8,328,384]{2,1,0:T(8,128)(2,1)S(1)}, bf16[8,328,384]{2,1,0:T(8,128)(2,1)}, u32[]{:S(2)}, u32[]{:S(2)}) collective-permute-start(bf16[8,328,384]{2,1,0:T(8,128)(2,1)S(1)} %all-to-all-done.2.refs_0_), channel_id=1, source_target_pairs={{0,1},{1,0},{2,3},{3,2},{4,5},{5,4},{6,7},{7,6},{8,9},{9,8},{10,11... | collective-permute-start | bytes 6045704 | tf_op jit(solution)/shard_map/ppermute | solution.py:77
  92.8 19.7 %collective-permute-start.8 = (bf16[2,8,32,192]{3,2,1,0:T(8,128)(2,1)}, bf16[2,8,32,192]{3,2,1,0:T(8,128)(2,1)S(1)}, u32[]{:S(2)}, u32[]{:S(2)}) collective-permute-start(bf16[2,8,32,192]{3,2,1,0:T(8,128)(2,1)} %get-tuple-element.209), channel_id=1, source_target_pairs={{0,1},{1,0},{2,3},{3,2},{4,5},{5,4},{6,7},{7,6},{8,9},{9,8},{10,11... | collective-permute-start | bytes 589832 | tf_op jit(solution)/shard_map/ppermute | solution.py:113
  93.3 19.3 %collective-permute-start.9 = (bf16[2,8,32,192]{3,2,1,0:T(8,128)(2,1)S(1)}, bf16[2,8,32,192]{3,2,1,0:T(8,128)(2,1)S(1)}, u32[]{:S(2)}, u32[]{:S(2)}) collective-permute-start(bf16[2,8,32,192]{3,2,1,0:T(8,128)(2,1)S(1)} %get-tuple-element.208), channel_id=1, source_target_pairs={{0,2},{1,3},{2,0},{3,1},{4,6},{5,7},{6,4},{7,5},{8,10},{9,11},{10,... | collective-permute-start | bytes 589832 | tf_op jit(solution)/shard_map/ppermute | solution.py:113
  93.3 19.3 %collective-permute-start.10 = (bf16[2,8,32,192]{3,2,1,0:T(8,128)(2,1)S(1)}, bf16[2,8,32,192]{3,2,1,0:T(8,128)(2,1)}, u32[]{:S(2)}, u32[]{:S(2)}) collective-permute-start(bf16[2,8,32,192]{3,2,1,0:T(8,128)(2,1)S(1)} %get-tuple-element.207), channel_id=1, source_target_pairs={{0,3},{1,2},{2,1},{3,0},{4,7},{5,6},{6,5},{7,4},{8,11},{9,10},{10,... | collective-permute-start | bytes 589832 | tf_op jit(solution)/shard_map/ppermute | solution.py:113
  181.2 4.5 %collective-permute-start.11 = (bf16[8,312,384]{2,1,0:T(8,128)(2,1)}, bf16[8,312,384]{2,1,0:T(8,128)(2,1)S(1)}, u32[]{:S(2)}, u32[]{:S(2)}) collective-permute-start(bf16[8,312,384]{2,1,0:T(8,128)(2,1)} %get-tuple-element.59), channel_id=1, source_target_pairs={{0,1},{1,0},{2,3},{3,2},{4,5},{5,4},{6,7},{7,6},{8,9},{9,8},{10,11... | collective-permute-start | bytes 5750792 | tf_op jit(solution)/shard_map/ppermute | solution.py:77
  189.0 37.2 %all-to-all-start.3 = ((bf16[8,312,384]{2,1,0:T(8,128)(2,1)}), bf16[8,312,384]{2,1,0:T(8,128)(2,1)S(1)}, u32[]{:S(2)}, u32[]{:S(2)}) async-start(bf16[8,312,384]{2,1,0:T(8,128)(2,1)} %add_convert_fusion), calls=%async_computation.3 | async-start | bytes 3833856 | tf_op jit(solution)/shard_map/all_to_all | solution.py:85
  220.2 3.3 %collective-permute-start.12 = (bf16[8,216,384]{2,1,0:T(8,128)(2,1)}, bf16[8,216,384]{2,1,0:T(8,128)(2,1)S(1)}, u32[]{:S(2)}, u32[]{:S(2)}) collective-permute-start(bf16[8,216,384]{2,1,0:T(8,128)(2,1)} %get-tuple-element.66), channel_id=1, source_target_pairs={{0,1},{1,0},{2,3},{3,2},{4,5},{5,4},{6,7},{7,6},{8,9},{9,8},{10,11... | collective-permute-start | bytes 3981320 | tf_op jit(solution)/shard_map/ppermute | solution.py:77
  226.2 6.4 %copy-start.18 = (f32[2,8,384]{2,1,0:T(8,128)S(1)}, f32[2,8,384]{2,1,0:T(8,128)}, u32[]{:S(2)}) copy-start(f32[2,8,384]{2,1,0:T(8,128)} %get-tuple-element.69) | copy-start | bytes 73732
  226.2 6.5 %copy-start.23 = (f32[2,8,192]{2,1,0:T(8,128)S(1)}, f32[2,8,192]{2,1,0:T(8,128)}, u32[]{:S(2)}) copy-start(f32[2,8,192]{2,1,0:T(8,128)} %get-tuple-element.72) | copy-start | bytes 36868
  226.2 26.8 %all-to-all-start.4 = ((bf16[8,216,384]{2,1,0:T(8,128)(2,1)}), bf16[8,216,384]{2,1,0:T(8,128)(2,1)S(1)}, u32[]{:S(2)}, u32[]{:S(2)}) async-start(bf16[8,216,384]{2,1,0:T(8,128)(2,1)} %add_convert_fusion.1), calls=%async_computation.4 | async-start | bytes 2654208 | tf_op jit(solution)/shard_map/all_to_all | solution.py:85
  236.1 15.3 %collective-permute-start.13 = (bf16[264,384]{1,0:T(8,128)(2,1)S(1)}, bf16[264,384]{1,0:T(8,128)(2,1)S(1)}, u32[]{:S(2)}, u32[]{:S(2)}) collective-permute-start(bf16[264,384]{1,0:T(8,128)(2,1)S(1)} %pad_maximum_fusion.2), channel_id=1, source_target_pairs={{0,16},{1,17},{2,18},{3,19},{4,20},{5,21},{6,22},{7,23},{8,24},{9,... | collective-permute-start | bytes 608264 | tf_op jit(solution)/shard_map/ppermute | solution.py:77
  253.2 9.0 %collective-permute-start.14 = (bf16[216,384]{1,0:T(8,128)(2,1)S(1)}, bf16[216,384]{1,0:T(8,128)(2,1)S(1)}, u32[]{:S(2)}, u32[]{:S(2)}) collective-permute-start(bf16[216,384]{1,0:T(8,128)(2,1)S(1)} %convert_element_type.136), channel_id=1, source_target_pairs={{0,16},{1,17},{2,18},{3,19},{4,20},{5,21},{6,22},{7,23},{8,24},{9,... | collective-permute-start | bytes 497672 | tf_op jit(solution)/shard_map/ppermute | solution.py:77
  255.2 6.9 %copy-start.4 = (f32[312,384]{1,0:T(8,128)S(1)}, f32[312,384]{1,0:T(8,128)}, u32[]{:S(2)}) copy-start(f32[312,384]{1,0:T(8,128)} %copy-done.3) | copy-start | bytes 1437700
  256.2 13.8 %all-to-all-start.5 = ((f32[32,16,128]{2,1,0:T(8,128)}), f32[32,16,128]{2,1,0:T(8,128)S(1)}, u32[]{:S(2)}, u32[]{:S(2)}) async-start(f32[32,16,128]{2,1,0:T(8,128)} %bitcast.40), calls=%async_computation.5 | async-start | bytes 524288 | tf_op jit(solution)/shard_map/all_to_all | solution.py:102
  260.1 27.9 %copy-start.19 = (f32[12,384]{1,0:T(8,128)S(1)}, f32[12,384]{1,0:T(8,128)}, u32[]{:S(2)}) copy-start(f32[12,384]{1,0:T(8,128)} %param.35) | copy-start | bytes 55300
  260.1 27.9 %copy-start.20 = (f32[12,384]{1,0:T(8,128)S(1)}, f32[12,384]{1,0:T(8,128)}, u32[]{:S(2)}) copy-start(f32[12,384]{1,0:T(8,128)} %param.36) | copy-start | bytes 55300
  260.7 27.9 %copy-start.10 = (f32[12,1152]{1,0:T(8,128)S(1)}, f32[12,1152]{1,0:T(8,128)}, u32[]{:S(2)}) copy-start(f32[12,1152]{1,0:T(8,128)} %param.26) | copy-start | bytes 165892
  260.7 27.9 %copy-start.12 = (f32[12,1152]{1,0:T(8,128)S(1)}, f32[12,1152]{1,0:T(8,128)}, u32[]{:S(2)}) copy-start(f32[12,1152]{1,0:T(8,128)} %param.33) | copy-start | bytes 165892
  260.7 27.9 %copy-start.13 = (f32[12,1152]{1,0:T(8,128)S(1)}, f32[12,1152]{1,0:T(8,128)}, u32[]{:S(2)}) copy-start(f32[12,1152]{1,0:T(8,128)} %param.34) | copy-start | bytes 165892
  260.7 28.7 %copy-start.22 = (f32[12,6]{0,1:T(8,128)S(1)}, f32[12,6]{0,1:T(8,128)}, u32[]{:S(2)}) copy-start(f32[12,6]{0,1:T(8,128)} %param.28) | copy-start | bytes 868
  260.7 28.7 %copy-start.24 = (f32[12,6]{0,1:T(8,128)S(1)}, f32[12,6]{0,1:T(8,128)}, u32[]{:S(2)}) copy-start(f32[12,6]{0,1:T(8,128)} %param.37) | copy-start | bytes 868
  260.7 28.7 %copy-start.25 = (f32[12,6]{0,1:T(8,128)S(1)}, f32[12,6]{0,1:T(8,128)}, u32[]{:S(2)}) copy-start(f32[12,6]{0,1:T(8,128)} %param.38) | copy-start | bytes 868
  260.7 29.3 %copy-start.2 = (f32[216,384]{1,0:T(8,128)S(1)}, f32[216,384]{1,0:T(8,128)}, u32[]{:S(2)}) copy-start(f32[216,384]{1,0:T(8,128)} %param.25) | copy-start | bytes 995332
  260.8 29.3 %copy-start.6 = (f32[216,384]{1,0:T(8,128)S(1)}, f32[216,384]{1,0:T(8,128)}, u32[]{:S(2)}) copy-start(f32[216,384]{1,0:T(8,128)} %param.31) | copy-start | bytes 995332
  260.8 29.3 %copy-start.7 = (f32[216,384]{1,0:T(8,128)S(1)}, f32[216,384]{1,0:T(8,128)}, u32[]{:S(2)}) copy-start(f32[216,384]{1,0:T(8,128)} %param.32) | copy-start | bytes 995332
  275.6 10.8 %all-to-all-start.6 = ((f32[32,8,128]{2,1,0:T(8,128)}), f32[32,8,128]{2,1,0:T(8,128)S(1)}, u32[]{:S(2)}, u32[]{:S(2)}) async-start(f32[32,8,128]{2,1,0:T(8,128)} %broadcast_in_dim.197), calls=%async_computation.6 | async-start | bytes 262144 | tf_op jit(solution)/shard_map/all_to_all | solution.py:102
  278.2 12.9 %copy-start.14 = (f32[24,768]{1,0:T(8,128)S(1)}, f32[24,768]{1,0:T(8,128)}, u32[]{:S(2)}) copy-start(f32[24,768]{1,0:T(8,128)} %param.29) | copy-start | bytes 221188
  278.2 12.9 %copy-start.15 = (f32[24,768]{1,0:T(8,128)S(1)}, f32[24,768]{1,0:T(8,128)}, u32[]{:S(2)}) copy-start(f32[24,768]{1,0:T(8,128)} %param.30) | copy-start | bytes 221188
  (10 other events, 20.3 us)

commit v6 on v5

--- a/solution.py
+++ b/solution.py
@@ -102,13 +102,13 @@
     return lax.all_to_all(blocks, ("dp", "head"), split_axis=0, concat_axis=0, tiled=True)
 
 
-def strips_of(values):
+def strips_of(values, cuts=()):
     parts = lax.axis_size("head")
     count = values.shape[0] // parts
     mine = lax.axis_index("head")
     strips = []
     for far in range(parts):
-        strip = lax.dynamic_slice_in_dim(values, (mine ^ far) * count, count, axis=0)
+        strip = cuts[far] if cuts else lax.dynamic_slice_in_dim(values, (mine ^ far) * count, count, axis=0)
         if far:
             strip = lax.ppermute(strip, "head", [(i, i ^ far) for i in range(parts)])
         strips.append(strip)
@@ -854,7 +854,13 @@
     two_block = jnp.concatenate(
         [high, rest_two.reshape(-1, channels), film_two.reshape(-1, channels)]
     )
-    every_two = gather_classes(behind(two_block, every_one))
+    mine = lax.axis_index("head")
+    own_count = noise.shape[0] // lax.axis_size("head")
+    noise_cuts = [
+        lax.dynamic_slice_in_dim(noise, (mine ^ far) * own_count, own_count, axis=0)
+        for far in range(lax.axis_size("head"))
+    ]
+    every_two = gather_classes(behind(two_block, every_one, *noise_cuts))
     gain_gate = two_block
     gains_t = behind(jnp.pad(gain_f.T, ((0, 2), (0, 0))), gain_gate)
     member = jnp.asarray(np.kron(np.eye(GROUPS), np.ones((channels // GROUPS,) * 2)), jnp.bfloat16)
@@ -883,7 +889,7 @@
     ).astype(jnp.float32)
     film_got = jnp.sum(film_got, axis=(3, 4)).reshape(classes, 2, 2, samples, film_rows)
     film_out = film_got.transpose(3, 2, 0, 1, 4).reshape(samples, devices * film_rows)
-    noise_strips = strips_of(behind(noise, other_two))
+    noise_strips = strips_of(noise, [behind(cut, other_two) for cut in noise_cuts])
     film = jnp.pad(film_out.reshape(samples, 2, channels), ((0, 0), (0, 6), (0, 0)))
     scale = 1.0 + film_out[:, :channels]
     middle, hidden_two, taps_two = second_call(
@@ -926,7 +932,8 @@
     send_two = jnp.where(is_top, small_shares[:, 0], small_shares[:, 1])
     send_two = jnp.concatenate([share_two[:conv_rows], send_two.reshape(-1, channels)])
     got_two = exchange(send_two.astype(jnp.bfloat16), top_mask).astype(jnp.float32)
-    got_one = exchange(share_one.astype(jnp.bfloat16), top_mask).astype(jnp.float32)
+    one_low = share_one.astype(jnp.bfloat16)
+    got_one = exchange(one_low, top_mask).astype(jnp.float32)
     conv_g = jnp.where(is_top, share_two[:conv_rows] + got_two[:conv_rows], share_one + got_one)
     small_g = keep_two + got_two[conv_rows:].reshape(keep_two.shape)
     qkv_g = jnp.concatenate([small_g[0], small_g[1], small_g[2]], axis=1)
@@ -936,7 +943,7 @@
     common = jnp.concatenate([film_grad_b.astype(jnp.float32).reshape(-1), loss_local[None]])
     parcel = jnp.concatenate(
         [
-            behind(gain_grad, share_one).reshape(devices, -1),
+            behind(gain_grad, one_low).reshape(devices, -1),
             jnp.broadcast_to(common[None], (devices, common.shape[0])),
         ],
         axis=1,

time: 297 us -> 294 us (0.990)
  transfers between devices with their start and end apart: 22 -> 22, of which waited for: 13 -> 13; matrix products, arithmetic and copies ran while one was open for 10% -> 10% of each run, Pallas kernels for 23% -> 24%
where the time goes in v6:
time: 294 us; the launch traced here: 291 us
  Pallas kernels  136 us (46%)
  waiting for transfers between devices  58 us (20%)
  starting transfers between devices  41.6 us (14%)
  other arithmetic  24.3 us (8%)
  local copies, waits for them, and re-layouts  22.4 us (8%)
  between operations  6.84 us (2%)
    pallas_call x6, Pallas kernels, per_sample(): pl.pallas_call(kernel, grid=(samples,), in_specs=in_specs, out_specs=[spe...  81.7 us
    pallas_call x1, Pallas kernels, attention_block(): pl.pallas_call(functools.partial(attention_kernel, parts), grid=(samples,...  54.7 us
    all_to_all x3, waiting for transfers between devices, to_all(): lax.all_to_all(blocks, ('dp', 'head'), split_axis=0, concat_axis=0, tiled...  26 us
    ppermute x9, waiting for transfers between devices, exchange(): lax.ppermute(values, ('dp', 'head'), [(i, i ^ mask) for i in range(size)])  19.8 us
    all_to_all x4, starting transfers between devices, across_classes(): lax.all_to_all(blocks, ('dp', 'head'), split_axis=0, concat_axis=0, axis_...  18 us
    all_to_all x4, waiting for transfers between devices, across_classes(): lax.all_to_all(blocks, ('dp', 'head'), split_axis=0, concat_axis=0, axis_...  12.2 us
    ppermute x9, starting transfers between devices, exchange(): lax.ppermute(values, ('dp', 'head'), [(i, i ^ mask) for i in range(size)])  10.3 us
    all_to_all x3, starting transfers between devices, to_all(): lax.all_to_all(blocks, ('dp', 'head'), split_axis=0, concat_axis=0, tiled...  9.63 us
  transfers between devices with their start and end apart: 22, of which 13 were waited for; matrix products, arithmetic and copies ran while one was open for 10% of the time, Pallas kernels for 24%

profile of v6, /device:TPU:0, one launch (start us, length us, event | category | flops | bytes accessed | tf_op | source)
XLA Modules:
  0.0 290.6 jit_solution(12259053940012339234)
XLA Ops:
  0.7 1.0 convert_element_type.116
  1.7 4.1 %collective-permute-start = (bf16[216,384]{1,0:T(8,128)(2,1)S(1)}, bf16[216,384]{1,0:T(8,128)(2,1)S(1)}, u32[]{:S(2)}, u32[]{:S(2)}) collective-permute-start(bf16[216,384]{1,0:T(8,128)(2,1)S(1)} %convert_element_type.116), channel_id=1, source_target_pairs={{0,16},{1,17},{2,18},{3,19},{4,20},{5,21},{6,22},{7,23},{8,24},{9,... | collective-permute-start | bytes 497672 | tf_op jit(solution)/shard_map/ppermute | solution.py:77
  5.8 2.3 constant_dynamic-slice_fusion.6
  8.1 1.5 collective-permute-start.4
  11.0 3.8 %all-to-all-start = ((f32[32,1,128]{2,1,0:T(1,128)}), f32[32,1,128]{2,1,0:T(1,128)S(1)}, u32[]{:S(2)}, u32[]{:S(2)}) async-start(f32[32,1,128]{2,1,0:T(1,128)} %broadcast_in_dim.166), calls=%async_computation | async-start | bytes 32768 | tf_op jit(solution)/shard_map/all_to_all | solution.py:102
  15.0 13.2 %all-to-all-done = f32[32,1,128]{2,1,0:T(1,128)S(1)} async-done(((f32[32,1,128]{2,1,0:T(1,128)}), f32[32,1,128]{2,1,0:T(1,128)S(1)}, u32[]{:S(2)}, u32[]{:S(2)}) %all-to-all-start) | async-done | bytes 16416 | tf_op jit(solution)/shard_map/all_to_all | solution.py:102
  28.3 1.3 broadcast_in_dim.181
  29.7 4.9 %all-to-all-start.1 = ((bf16[8,216,384]{2,1,0:T(8,128)(2,1)}), bf16[8,216,384]{2,1,0:T(8,128)(2,1)S(1)}, u32[]{:S(2)}, u32[]{:S(2)}) async-start(bf16[8,216,384]{2,1,0:T(8,128)(2,1)} %broadcast_in_dim.181), calls=%async_computation.1 | async-start | bytes 2654208 | tf_op jit(solution)/shard_map/all_to_all | solution.py:85
  34.7 1.0 constant_dynamic-slice_fusion.2
  38.0 2.6 collective-permute-start.1
  40.6 9.3 %collective-permute-done.2 = bf16[8,384]{1,0:T(8,128)(2,1)S(1)} collective-permute-done((bf16[8,384]{1,0:T(8,128)(2,1)S(1)}, bf16[8,384]{1,0:T(8,128)(2,1)S(1)}, u32[]{:S(2)}, u32[]{:S(2)}) %collective-permute-start.2) | collective-permute-done | bytes 6176 | tf_op jit(solution)/shard_map/ppermute | solution.py:77
  50.4 1.9 all-to-all-done.1.refs_4_
  52.3 1.7 broadcast_in_dim.182
  54.0 3.8 %all-to-all-start.2 = ((bf16[8,328,384]{2,1,0:T(8,128)(2,1)}), bf16[8,328,384]{2,1,0:T(8,128)(2,1)S(1)}, u32[]{:S(2)}, u32[]{:S(2)}) async-start(bf16[8,328,384]{2,1,0:T(8,128)(2,1)} %broadcast_in_dim.182), calls=%async_computation.2 | async-start | bytes 4030464 | tf_op jit(solution)/shard_map/all_to_all | solution.py:85
  59.1 1.0 copy.164
  61.0 15.0 %shard_map.323 = (f32[2,1024,384]{2,1,0:T(8,128)}, bf16[2,1024,384]{2,1,0:T(8,128)(2,1)}, f32[2,8,384]{2,1,0:T(8,128)}, bf16[2,1024,384]{2,1,0:T(8,128)(2,1)}, bf16[3456,384]{1,0:T(8,128)(2,1)}) custom-call(s32[4]{0:T(128)} %iota_xor_fusion.places, s32[1]{0:T(128)} %bitcast.5.last.place, bf16[2,256,384]{2,1,0:T(8,128)(2,1)} %bitcast.93, ...), custom_call_target="tpu_custom_call" | custom-call | flops 5435817984 | bytes 5435817 | tf_op jit(solution)/shard_map/pallas_call | solution.py:664
  76.1 8.7 %all-to-all-done.2.refs_0_ = bf16[8,328,384]{2,1,0:T(8,128)(2,1)S(1)} async-done(((bf16[8,328,384]{2,1,0:T(8,128)(2,1)}), bf16[8,328,384]{2,1,0:T(8,128)(2,1)S(1)}, u32[]{:S(2)}, u32[]{:S(2)}) %all-to-all-start.2) | async-done | bytes 2015264 | tf_op jit(solution)/shard_map/all_to_all | solution.py:85
  85.8 0.8 fusion.refs_8_
  89.0 0.9 slice.158
  91.4 1.4 collective-permute-start.10
  92.8 1.1 slice.159
  93.9 13.7 %shard_map.324 = (f32[2,1024,384]{2,1,0:T(8,128)}, bf16[2,1024,384]{2,1,0:T(8,128)(2,1)}, bf16[3456,384]{1,0:T(8,128)(2,1)}) custom-call(s32[1]{0:T(128)} %bitcast.5.last.place, bf16[8,328,384]{2,1,0:T(8,128)(2,1)} %copy-done, bf16[8,328,384]{2,1,0:T(8,128)(2,1)} %collective-permute-done.7.refs_1_, f32[2,1024,384]{2,1,0:T(8,128)} %get-tuple-element.52.refs_2_.inner, ...), custom_call_target="tpu_custom_call" | custom-call | flops 5435817984 | bytes 5435817 | tf_op jit(solution)/shard_map/pallas_call | solution.py:664
  108.5 1.4 reshape.300.refs_6_
  110.7 54.7 %shard_map.325 = (bf16[2,1024,384]{2,1,0:T(8,128)(2,1)}, bf16[384,1536]{1,0:T(8,128)(2,1)}, f32[2,8,384]{2,1,0:T(8,128)}, f32[2,8,192]{2,1,0:T(8,128)}) custom-call(s32[4]{0:T(128)} %iota_xor_fusion.places, f32[2,6]{1,0:T(2,128)} %stack.47.scalars, f32[2,1024,384]{2,1,0:T(8,128)} %get-tuple-element.56.middle, bf16[2,256,192]{2,1,0:T(8,128)(2,1)} %bitcast.94, ...), custom_call_target="tpu_custom_call" | custom-call | flops 24159191040 | bytes 6291456 | tf_op jit(solution)/shard_map/pallas_call | solution.py:349
  165.4 13.1 %shard_map.326 = (bf16[8,312,384]{2,1,0:T(8,128)(2,1)}, bf16[8,312,384]{2,1,0:T(8,128)(2,1)}) custom-call(s32[1]{0:T(128)} %bitcast.5.last.place, bf16[2,1024,384]{2,1,0:T(8,128)(2,1)} %get-tuple-element.62.hidden, bf16[2,1024,384]{2,1,0:T(8,128)(2,1)} %get-tuple-element.66.grad, bf16[384,1536]{1,0:T(8,128)(2,1)} %get-tuple-element.63.refs_0_), custom_call_target="tpu_custom_call" | custom-call | flops 5435817984 | bytes 5435817 | tf_op jit(solution)/shard_map/pallas_call | solution.py:664
  179.3 3.7 %collective-permute-done.11 = bf16[8,312,384]{2,1,0:T(8,128)(2,1)S(1)} collective-permute-done((bf16[8,312,384]{2,1,0:T(8,128)(2,1)}, bf16[8,312,384]{2,1,0:T(8,128)(2,1)S(1)}, u32[]{:S(2)}, u32[]{:S(2)}) %collective-permute-start.11) | collective-permute-done | bytes 1916960 | tf_op jit(solution)/shard_map/ppermute | solution.py:77
  183.0 3.3 %add_convert_fusion = bf16[8,312,384]{2,1,0:T(8,128)(2,1)} fusion(bf16[8,312,384]{2,1,0:T(8,128)(2,1)S(1)} %collective-permute-done.11, bf16[8,312,384]{2,1,0:T(8,128)(2,1)} %get-tuple-element.64), kind=kLoop, calls=%fused_computation.1 | loop fusion | flops 3833856 | bytes 5750784 | tf_op jit(solution)/shard_map/convert_element_type | solution.py:917
  186.4 3.8 %all-to-all-start.3 = ((bf16[8,312,384]{2,1,0:T(8,128)(2,1)}), bf16[8,312,384]{2,1,0:T(8,128)(2,1)S(1)}, u32[]{:S(2)}, u32[]{:S(2)}) async-start(bf16[8,312,384]{2,1,0:T(8,128)(2,1)} %add_convert_fusion), calls=%async_computation.3 | async-start | bytes 3833856 | tf_op jit(solution)/shard_map/all_to_all | solution.py:85
  190.2 15.2 %shard_map.327 = (bf16[2,1024,384]{2,1,0:T(8,128)(2,1)}, f32[2,8,384]{2,1,0:T(8,128)}) custom-call(bf16[2,1024,384]{2,1,0:T(8,128)(2,1)} %get-tuple-element.66.grad, f32[2,1024,384]{2,1,0:T(8,128)} %get-tuple-element.52.refs_2_.inner, f32[2,8,384]{2,1,0:T(8,128)} %get-tuple-element.55.refs_4_.stats, f32[2,8,384]{2,1,0:T(8,128)} %pad.18.refs_5_.film, ...), custom_call_target="tpu_custom_call" | custom-call | flops 5435817984 | bytes 5435817 | tf_op jit(solution)/shard_map/pallas_call | solution.py:664
  205.3 12.2 %shard_map.328 = (bf16[8,216,384]{2,1,0:T(8,128)(2,1)}, bf16[8,216,384]{2,1,0:T(8,128)(2,1)}) custom-call(s32[1]{0:T(128)} %bitcast.5.last.place, bf16[2,1024,384]{2,1,0:T(8,128)(2,1)} %get-tuple-element.70.hidden, bf16[2,1024,384]{2,1,0:T(8,128)(2,1)} %get-tuple-element.73.grad), custom_call_target="tpu_custom_call" | custom-call | flops 5435817984 | bytes 5435817 | tf_op jit(solution)/shard_map/pallas_call | solution.py:664
  217.9 2.9 collective-permute-done.12
  220.8 2.7 add_convert_fusion.1
  223.6 5.5 %all-to-all-start.4 = ((bf16[8,216,384]{2,1,0:T(8,128)(2,1)}), bf16[8,216,384]{2,1,0:T(8,128)(2,1)S(1)}, u32[]{:S(2)}, u32[]{:S(2)}) async-start(bf16[8,216,384]{2,1,0:T(8,128)(2,1)} %add_convert_fusion.1), calls=%async_computation.4 | async-start | bytes 2654208 | tf_op jit(solution)/shard_map/all_to_all | solution.py:85
  229.1 0.8 slice_reduce_fusion.8
  230.1 0.8 slice_reduce_fusion.5
  233.5 12.5 %shard_map.329 = f32[2,8,384]{2,1,0:T(8,128)} custom-call(bf16[2,1024,384]{2,1,0:T(8,128)(2,1)} %get-tuple-element.73.grad, bf16[2,1024,384]{2,1,0:T(8,128)(2,1)} %get-tuple-element.54.refs_3_.images, f32[2,8,384]{2,1,0:T(8,128)} %get-tuple-element.55.refs_4_.stats, f32[8,384]{1,0:T(8,128)} %pad.17.refs_6_.refs_4_.gains, ...), custom_call_target="tpu_custom_call" | custom-call | flops 5435817984 | bytes 5435817 | tf_op jit(solution)/shard_map/pallas_call | solution.py:664
  246.0 0.8 slice_reduce_fusion.3
  246.9 1.8 collective-permute-done.13
  248.8 1.6 all-to-all-done.4
  250.5 1.9 collective-permute-start.14
  253.5 3.2 %all-to-all-start.5 = ((f32[32,16,128]{2,1,0:T(8,128)}), f32[32,16,128]{2,1,0:T(8,128)S(1)}, u32[]{:S(2)}, u32[]{:S(2)}) async-start(f32[32,16,128]{2,1,0:T(8,128)} %bitcast.40), calls=%async_computation.5 | async-start | bytes 524288 | tf_op jit(solution)/shard_map/all_to_all | solution.py:102
  258.0 1.5 collective-permute-done.14
  260.2 7.1 %all-to-all-done.5 = f32[32,16,128]{2,1,0:T(8,128)S(1)} async-done(((f32[32,16,128]{2,1,0:T(8,128)}), f32[32,16,128]{2,1,0:T(8,128)S(1)}, u32[]{:S(2)}, u32[]{:S(2)}) %all-to-all-start.5) | async-done | bytes 262176 | tf_op jit(solution)/shard_map/all_to_all | solution.py:102
  268.2 0.9 multiply_reduce_fusion.2
  273.0 2.6 all-to-all-start.6
  276.2 1.9 pad_maximum_fusion.8
  278.1 5.7 %all-to-all-done.6 = f32[32,8,128]{2,1,0:T(8,128)S(1)} async-done(((f32[32,8,128]{2,1,0:T(8,128)}), f32[32,8,128]{2,1,0:T(8,128)S(1)}, u32[]{:S(2)}, u32[]{:S(2)}) %all-to-all-start.6) | async-done | bytes 131104 | tf_op jit(solution)/shard_map/all_to_all | solution.py:102
  287.5 1.1 multiply_subtract_fusion
  (218 shorter events, 25.7 us)
Async XLA Ops:
  1.7 13.2 %collective-permute-start = (bf16[216,384]{1,0:T(8,128)(2,1)S(1)}, bf16[216,384]{1,0:T(8,128)(2,1)S(1)}, u32[]{:S(2)}, u32[]{:S(2)}) collective-permute-start(bf16[216,384]{1,0:T(8,128)(2,1)S(1)} %convert_element_type.116), channel_id=1, source_target_pairs={{0,16},{1,17},{2,18},{3,19},{4,20},{5,21},{6,22},{7,23},{8,24},{9,... | collective-permute-start | bytes 497672 | tf_op jit(solution)/shard_map/ppermute | solution.py:77
  5.8 4.4 %copy-start.24 = (f32[12,6]{0,1:T(8,128)S(1)}, f32[12,6]{0,1:T(8,128)}, u32[]{:S(2)}) copy-start(f32[12,6]{0,1:T(8,128)} %param.28) | copy-start | bytes 868
  5.8 9.1 %copy-start.1 = (f32[216,384]{1,0:T(8,128)S(1)}, f32[216,384]{1,0:T(8,128)}, u32[]{:S(2)}) copy-start(f32[216,384]{1,0:T(8,128)} %param.25) | copy-start | bytes 995332
  8.1 20.1 %collective-permute-start.3 = (bf16[2,8,32,384]{3,2,1,0:T(8,128)(2,1)S(1)}, bf16[2,8,32,384]{3,2,1,0:T(8,128)(2,1)S(1)}, u32[]{:S(2)}, u32[]{:S(2)}) collective-permute-start(bf16[2,8,32,384]{3,2,1,0:T(8,128)(2,1)S(1)} %get-tuple-element.210), channel_id=1, source_target_pairs={{0,1},{1,0},{2,3},{3,2},{4,5},{5,4},{6,7},{7,6},{8,9},{9,8},{10,11... | collective-permute-start | bytes 1179656 | tf_op jit(solution)/shard_map/ppermute | solution.py:113
  8.1 20.1 %collective-permute-start.4 = (bf16[2,8,32,384]{3,2,1,0:T(8,128)(2,1)S(1)}, bf16[2,8,32,384]{3,2,1,0:T(8,128)(2,1)S(1)}, u32[]{:S(2)}, u32[]{:S(2)}) collective-permute-start(bf16[2,8,32,384]{3,2,1,0:T(8,128)(2,1)S(1)} %get-tuple-element.212), channel_id=1, source_target_pairs={{0,2},{1,3},{2,0},{3,1},{4,6},{5,7},{6,4},{7,5},{8,10},{9,11},{10,... | collective-permute-start | bytes 1179656 | tf_op jit(solution)/shard_map/ppermute | solution.py:113
  9.6 18.6 %collective-permute-start.5 = (bf16[2,8,32,384]{3,2,1,0:T(8,128)(2,1)S(1)}, bf16[2,8,32,384]{3,2,1,0:T(8,128)(2,1)S(1)}, u32[]{:S(2)}, u32[]{:S(2)}) collective-permute-start(bf16[2,8,32,384]{3,2,1,0:T(8,128)(2,1)S(1)} %get-tuple-element.209), channel_id=1, source_target_pairs={{0,3},{1,2},{2,1},{3,0},{4,7},{5,6},{6,5},{7,4},{8,11},{9,10},{10,... | collective-permute-start | bytes 1179656 | tf_op jit(solution)/shard_map/ppermute | solution.py:113
  11.0 17.2 %all-to-all-start = ((f32[32,1,128]{2,1,0:T(1,128)}), f32[32,1,128]{2,1,0:T(1,128)S(1)}, u32[]{:S(2)}, u32[]{:S(2)}) async-start(f32[32,1,128]{2,1,0:T(1,128)} %broadcast_in_dim.166), calls=%async_computation | async-start | bytes 32768 | tf_op jit(solution)/shard_map/all_to_all | solution.py:102
  29.6 5.0 %copy-start.14 = (f32[12,384]{1,0:T(8,128)S(1)}, f32[12,384]{1,0:T(8,128)}, u32[]{:S(2)}) copy-start(f32[12,384]{1,0:T(8,128)} %param.27) | copy-start | bytes 55300
  29.6 5.0 %copy-start.10 = (f32[12,1152]{1,0:T(8,128)S(1)}, f32[12,1152]{1,0:T(8,128)}, u32[]{:S(2)}) copy-start(f32[12,1152]{1,0:T(8,128)} %param.26) | copy-start | bytes 165892
  29.6 5.1 %copy-start.6 = (bf16[8,8,32,192]{3,2,1,0:T(8,128)(2,1)S(1)}, bf16[8,8,32,192]{3,2,1,0:T(8,128)(2,1)}, u32[]{:S(2)}) copy-start(bf16[8,8,32,192]{3,2,1,0:T(8,128)(2,1)} %param.21) | copy-start | bytes 2359300
  29.7 22.6 %all-to-all-start.1 = ((bf16[8,216,384]{2,1,0:T(8,128)(2,1)}), bf16[8,216,384]{2,1,0:T(8,128)(2,1)S(1)}, u32[]{:S(2)}, u32[]{:S(2)}) async-start(bf16[8,216,384]{2,1,0:T(8,128)(2,1)} %broadcast_in_dim.181), calls=%async_computation.1 | async-start | bytes 2654208 | tf_op jit(solution)/shard_map/all_to_all | solution.py:85
  36.8 13.2 %collective-permute-start.2 = (bf16[8,384]{1,0:T(8,128)(2,1)S(1)}, bf16[8,384]{1,0:T(8,128)(2,1)S(1)}, u32[]{:S(2)}, u32[]{:S(2)}) collective-permute-start(bf16[8,384]{1,0:T(8,128)(2,1)S(1)} %pad_maximum_fusion.7), channel_id=1, source_target_pairs={{0,16},{1,17},{2,18},{3,19},{4,20},{5,21},{6,22},{7,23},{8,24},{9,... | collective-permute-start | bytes 18440 | tf_op jit(solution)/shard_map/ppermute | solution.py:77
  38.0 12.3 %collective-permute-start.1 = (bf16[48,384]{1,0:T(8,128)(2,1)S(1)}, bf16[48,384]{1,0:T(8,128)(2,1)S(1)}, u32[]{:S(2)}, u32[]{:S(2)}) collective-permute-start(bf16[48,384]{1,0:T(8,128)(2,1)S(1)} %pad_maximum_fusion.5), channel_id=1, source_target_pairs={{0,16},{1,17},{2,18},{3,19},{4,20},{5,21},{6,22},{7,23},{8,24},{9,... | collective-permute-start | bytes 110600 | tf_op jit(solution)/shard_map/ppermute | solution.py:77
  52.3 5.5 %copy-start.5 = (bf16[8,216,384]{2,1,0:T(8,128)(2,1)}, bf16[8,216,384]{2,1,0:T(8,128)(2,1)S(1)}, u32[]{:S(2)}) copy-start(bf16[8,216,384]{2,1,0:T(8,128)(2,1)S(1)} %all-to-all-done.1.refs_4_) | copy-start | bytes 3981316
  54.0 30.8 %all-to-all-start.2 = ((bf16[8,328,384]{2,1,0:T(8,128)(2,1)}), bf16[8,328,384]{2,1,0:T(8,128)(2,1)S(1)}, u32[]{:S(2)}, u32[]{:S(2)}) async-start(bf16[8,328,384]{2,1,0:T(8,128)(2,1)} %broadcast_in_dim.182), calls=%async_computation.2 | async-start | bytes 4030464 | tf_op jit(solution)/shard_map/all_to_all | solution.py:85
  57.8 3.3 %collective-permute-start.6 = (bf16[8,216,384]{2,1,0:T(8,128)(2,1)S(1)}, bf16[8,216,384]{2,1,0:T(8,128)(2,1)}, u32[]{:S(2)}, u32[]{:S(2)}) collective-permute-start(bf16[8,216,384]{2,1,0:T(8,128)(2,1)S(1)} %all-to-all-done.1.refs_4_), channel_id=1, source_target_pairs={{0,1},{1,0},{2,3},{3,2},{4,5},{5,4},{6,7},{7,6},{8,9},{9,8},{10,11... | collective-permute-start | bytes 3981320 | tf_op jit(solution)/shard_map/ppermute | solution.py:77
  61.0 23.8 %copy-start.33 = (s32[8]{0:T(128)S(1)}, s32[8]{0:T(128)}, u32[]{:S(2)}) copy-start(s32[8]{0:T(128)} %param.22) | copy-start | bytes 100
  61.0 24.4 %copy-start.30 = (s32[8,2]{0,1:T(2,128)S(1)}, s32[8,2]{0,1:T(2,128)}, u32[]{:S(2)}) copy-start(s32[8,2]{0,1:T(2,128)} %param.23) | copy-start | bytes 196
  61.0 24.7 %copy-start.31 = (pred[2]{0:T(512)(128)(4,1)S(1)}, pred[2]{0:T(512)(128)(4,1)}, u32[]{:S(2)}) copy-start(pred[2]{0:T(512)(128)(4,1)} %get-tuple-element.234) | copy-start | bytes 10
  61.0 25.6 %copy-start.20 = (f32[8,1,56]{2,1,0:T(1,128)S(1)}, f32[8,1,56]{2,1,0:T(1,128)}, u32[]{:S(2)}) copy-start(f32[8,1,56]{2,1,0:T(1,128)} %copy-done.19) | copy-start | bytes 5380
  76.1 15.4 %copy-start.13 = (bf16[2,8,32,192]{3,2,1,0:T(8,128)(2,1)S(1)}, bf16[2,8,32,192]{3,2,1,0:T(8,128)(2,1)}, u32[]{:S(2)}) copy-start(bf16[2,8,32,192]{3,2,1,0:T(8,128)(2,1)} %get-tuple-element.59) | copy-start | bytes 589828
  76.1 15.3 %copy-start.12 = (bf16[2,8,32,192]{3,2,1,0:T(8,128)(2,1)S(1)}, bf16[2,8,32,192]{3,2,1,0:T(8,128)(2,1)}, u32[]{:S(2)}) copy-start(bf16[2,8,32,192]{3,2,1,0:T(8,128)(2,1)} %get-tuple-element.60) | copy-start | bytes 589828
  84.8 9.1 %copy-start = (bf16[8,328,384]{2,1,0:T(8,128)(2,1)}, bf16[8,328,384]{2,1,0:T(8,128)(2,1)S(1)}, u32[]{:S(2)}) copy-start(bf16[8,328,384]{2,1,0:T(8,128)(2,1)S(1)} %all-to-all-done.2.refs_0_) | copy-start | bytes 6045700
  84.8 4.2 %collective-permute-start.7 = (bf16[8,328,384]{2,1,0:T(8,128)(2,1)S(1)}, bf16[8,328,384]{2,1,0:T(8,128)(2,1)}, u32[]{:S(2)}, u32[]{:S(2)}) collective-permute-start(bf16[8,328,384]{2,1,0:T(8,128)(2,1)S(1)} %all-to-all-done.2.refs_0_), channel_id=1, source_target_pairs={{0,1},{1,0},{2,3},{3,2},{4,5},{5,4},{6,7},{7,6},{8,9},{9,8},{10,11... | collective-permute-start | bytes 6045704 | tf_op jit(solution)/shard_map/ppermute | solution.py:77
  90.9 19.7 %collective-permute-start.8 = (bf16[2,8,32,192]{3,2,1,0:T(8,128)(2,1)}, bf16[2,8,32,192]{3,2,1,0:T(8,128)(2,1)}, u32[]{:S(2)}, u32[]{:S(2)}) collective-permute-start(bf16[2,8,32,192]{3,2,1,0:T(8,128)(2,1)} %get-tuple-element.58), channel_id=1, source_target_pairs={{0,1},{1,0},{2,3},{3,2},{4,5},{5,4},{6,7},{7,6},{8,9},{9,8},{10,11... | collective-permute-start | bytes 589832 | tf_op jit(solution)/shard_map/ppermute | solution.py:113
  91.4 19.3 %collective-permute-start.9 = (bf16[2,8,32,192]{3,2,1,0:T(8,128)(2,1)S(1)}, bf16[2,8,32,192]{3,2,1,0:T(8,128)(2,1)}, u32[]{:S(2)}, u32[]{:S(2)}) collective-permute-start(bf16[2,8,32,192]{3,2,1,0:T(8,128)(2,1)S(1)} %copy-done.13), channel_id=1, source_target_pairs={{0,2},{1,3},{2,0},{3,1},{4,6},{5,7},{6,4},{7,5},{8,10},{9,11},{10,... | collective-permute-start | bytes 589832 | tf_op jit(solution)/shard_map/ppermute | solution.py:113
  91.4 19.3 %collective-permute-start.10 = (bf16[2,8,32,192]{3,2,1,0:T(8,128)(2,1)S(1)}, bf16[2,8,32,192]{3,2,1,0:T(8,128)(2,1)}, u32[]{:S(2)}, u32[]{:S(2)}) collective-permute-start(bf16[2,8,32,192]{3,2,1,0:T(8,128)(2,1)S(1)} %copy-done.12), channel_id=1, source_target_pairs={{0,3},{1,2},{2,1},{3,0},{4,7},{5,6},{6,5},{7,4},{8,11},{9,10},{10,... | collective-permute-start | bytes 589832 | tf_op jit(solution)/shard_map/ppermute | solution.py:113
  178.5 4.5 %collective-permute-start.11 = (bf16[8,312,384]{2,1,0:T(8,128)(2,1)}, bf16[8,312,384]{2,1,0:T(8,128)(2,1)S(1)}, u32[]{:S(2)}, u32[]{:S(2)}) collective-permute-start(bf16[8,312,384]{2,1,0:T(8,128)(2,1)} %get-tuple-element.65), channel_id=1, source_target_pairs={{0,1},{1,0},{2,3},{3,2},{4,5},{5,4},{6,7},{7,6},{8,9},{9,8},{10,11... | collective-permute-start | bytes 5750792 | tf_op jit(solution)/shard_map/ppermute | solution.py:77
  186.4 37.2 %all-to-all-start.3 = ((bf16[8,312,384]{2,1,0:T(8,128)(2,1)}), bf16[8,312,384]{2,1,0:T(8,128)(2,1)S(1)}, u32[]{:S(2)}, u32[]{:S(2)}) async-start(bf16[8,312,384]{2,1,0:T(8,128)(2,1)} %add_convert_fusion), calls=%async_computation.3 | async-start | bytes 3833856 | tf_op jit(solution)/shard_map/all_to_all | solution.py:85
  217.5 3.3 %collective-permute-start.12 = (bf16[8,216,384]{2,1,0:T(8,128)(2,1)}, bf16[8,216,384]{2,1,0:T(8,128)(2,1)S(1)}, u32[]{:S(2)}, u32[]{:S(2)}) collective-permute-start(bf16[8,216,384]{2,1,0:T(8,128)(2,1)} %get-tuple-element.72), channel_id=1, source_target_pairs={{0,1},{1,0},{2,3},{3,2},{4,5},{5,4},{6,7},{7,6},{8,9},{9,8},{10,11... | collective-permute-start | bytes 3981320 | tf_op jit(solution)/shard_map/ppermute | solution.py:77
  223.6 6.4 %copy-start.21 = (f32[2,8,384]{2,1,0:T(8,128)S(1)}, f32[2,8,384]{2,1,0:T(8,128)}, u32[]{:S(2)}) copy-start(f32[2,8,384]{2,1,0:T(8,128)} %get-tuple-element.75) | copy-start | bytes 73732
  223.6 7.4 %copy-start.26 = (f32[2,8,192]{2,1,0:T(8,128)S(1)}, f32[2,8,192]{2,1,0:T(8,128)}, u32[]{:S(2)}) copy-start(f32[2,8,192]{2,1,0:T(8,128)} %get-tuple-element.78) | copy-start | bytes 36868
  223.6 26.8 %all-to-all-start.4 = ((bf16[8,216,384]{2,1,0:T(8,128)(2,1)}), bf16[8,216,384]{2,1,0:T(8,128)(2,1)S(1)}, u32[]{:S(2)}, u32[]{:S(2)}) async-start(bf16[8,216,384]{2,1,0:T(8,128)(2,1)} %add_convert_fusion.1), calls=%async_computation.4 | async-start | bytes 2654208 | tf_op jit(solution)/shard_map/all_to_all | solution.py:85
  233.5 15.3 %collective-permute-start.13 = (bf16[264,384]{1,0:T(8,128)(2,1)S(1)}, bf16[264,384]{1,0:T(8,128)(2,1)S(1)}, u32[]{:S(2)}, u32[]{:S(2)}) collective-permute-start(bf16[264,384]{1,0:T(8,128)(2,1)S(1)} %pad_maximum_fusion.2), channel_id=1, source_target_pairs={{0,16},{1,17},{2,18},{3,19},{4,20},{5,21},{6,22},{7,23},{8,24},{9,... | collective-permute-start | bytes 608264 | tf_op jit(solution)/shard_map/ppermute | solution.py:77
  250.5 9.0 %collective-permute-start.14 = (bf16[216,384]{1,0:T(8,128)(2,1)S(1)}, bf16[216,384]{1,0:T(8,128)(2,1)S(1)}, u32[]{:S(2)}, u32[]{:S(2)}) collective-permute-start(bf16[216,384]{1,0:T(8,128)(2,1)S(1)} %convert_element_type.132), channel_id=1, source_target_pairs={{0,16},{1,17},{2,18},{3,19},{4,20},{5,21},{6,22},{7,23},{8,24},{9,... | collective-permute-start | bytes 497672 | tf_op jit(solution)/shard_map/ppermute | solution.py:77
  252.6 6.9 %copy-start.4 = (f32[312,384]{1,0:T(8,128)S(1)}, f32[312,384]{1,0:T(8,128)}, u32[]{:S(2)}) copy-start(f32[312,384]{1,0:T(8,128)} %copy-done.3) | copy-start | bytes 1437700
  253.5 13.8 %all-to-all-start.5 = ((f32[32,16,128]{2,1,0:T(8,128)}), f32[32,16,128]{2,1,0:T(8,128)S(1)}, u32[]{:S(2)}, u32[]{:S(2)}) async-start(f32[32,16,128]{2,1,0:T(8,128)} %bitcast.40), calls=%async_computation.5 | async-start | bytes 524288 | tf_op jit(solution)/shard_map/all_to_all | solution.py:102
  257.4 27.9 %copy-start.11 = (f32[12,1152]{1,0:T(8,128)S(1)}, f32[12,1152]{1,0:T(8,128)}, u32[]{:S(2)}) copy-start(f32[12,1152]{1,0:T(8,128)} %param.26) | copy-start | bytes 165892
  257.4 27.9 %copy-start.15 = (f32[12,1152]{1,0:T(8,128)S(1)}, f32[12,1152]{1,0:T(8,128)}, u32[]{:S(2)}) copy-start(f32[12,1152]{1,0:T(8,128)} %param.33) | copy-start | bytes 165892
  257.4 27.9 %copy-start.16 = (f32[12,1152]{1,0:T(8,128)S(1)}, f32[12,1152]{1,0:T(8,128)}, u32[]{:S(2)}) copy-start(f32[12,1152]{1,0:T(8,128)} %param.34) | copy-start | bytes 165892
  258.0 28.0 %copy-start.22 = (f32[12,384]{1,0:T(8,128)S(1)}, f32[12,384]{1,0:T(8,128)}, u32[]{:S(2)}) copy-start(f32[12,384]{1,0:T(8,128)} %param.35) | copy-start | bytes 55300
  258.0 28.0 %copy-start.23 = (f32[12,384]{1,0:T(8,128)S(1)}, f32[12,384]{1,0:T(8,128)}, u32[]{:S(2)}) copy-start(f32[12,384]{1,0:T(8,128)} %param.36) | copy-start | bytes 55300
  258.0 28.7 %copy-start.17 = (f32[24,768]{1,0:T(8,128)S(1)}, f32[24,768]{1,0:T(8,128)}, u32[]{:S(2)}) copy-start(f32[24,768]{1,0:T(8,128)} %param.29) | copy-start | bytes 221188
  258.0 28.7 %copy-start.18 = (f32[24,768]{1,0:T(8,128)S(1)}, f32[24,768]{1,0:T(8,128)}, u32[]{:S(2)}) copy-start(f32[24,768]{1,0:T(8,128)} %param.30) | copy-start | bytes 221188
  260.2 27.2 %copy-start.2 = (f32[216,384]{1,0:T(8,128)S(1)}, f32[216,384]{1,0:T(8,128)}, u32[]{:S(2)}) copy-start(f32[216,384]{1,0:T(8,128)} %param.25) | copy-start | bytes 995332
  260.2 27.2 %copy-start.7 = (f32[216,384]{1,0:T(8,128)S(1)}, f32[216,384]{1,0:T(8,128)}, u32[]{:S(2)}) copy-start(f32[216,384]{1,0:T(8,128)} %param.31) | copy-start | bytes 995332
  260.2 27.2 %copy-start.8 = (f32[216,384]{1,0:T(8,128)S(1)}, f32[216,384]{1,0:T(8,128)}, u32[]{:S(2)}) copy-start(f32[216,384]{1,0:T(8,128)} %param.32) | copy-start | bytes 995332
  273.0 10.8 %all-to-all-start.6 = ((f32[32,8,128]{2,1,0:T(8,128)}), f32[32,8,128]{2,1,0:T(8,128)S(1)}, u32[]{:S(2)}, u32[]{:S(2)}) async-start(f32[32,8,128]{2,1,0:T(8,128)} %broadcast_in_dim.197), calls=%async_computation.6 | async-start | bytes 262144 | tf_op jit(solution)/shard_map/all_to_all | solution.py:102
  (11 other events, 23.5 us)

commit v7 on v6

--- a/solution.py
+++ b/solution.py
@@ -940,21 +940,22 @@
     out_g = small_g[3]
 
     gain_grad = jnp.stack([gain_one, bias_one, gain_two, bias_two, gain_three, bias_three], axis=1)
-    common = jnp.concatenate([film_grad_b.astype(jnp.float32).reshape(-1), loss_local[None]])
+    film_sent = jnp.moveaxis(film_grad_b.astype(jnp.float32).reshape(samples, devices, film_rows), 1, 0)
     parcel = jnp.concatenate(
         [
+            film_sent.reshape(devices, -1),
             behind(gain_grad, one_low).reshape(devices, -1),
-            jnp.broadcast_to(common[None], (devices, common.shape[0])),
+            jnp.broadcast_to(loss_local, (devices, 1)),
         ],
         axis=1,
     )
     length = parcel.shape[1]
-    parcel = jnp.pad(parcel, ((0, 0), (0, -length % 1024))).reshape(devices, -1, 128)
-    parcels = to_all(parcel).reshape(devices, -1)
-    gain_g = jnp.sum(parcels[:, : gains.size], axis=0).reshape(gains.shape)
-    film_all = parcels[:, gains.size : length - 1].reshape(-1, film_grad_b.shape[1])
+    parcel = jnp.pad(parcel, ((0, 0), (0, -length % 128)))
+    parcels = to_all(parcel[:, None]).reshape(devices, -1)
+    film_size = samples * film_rows
+    film_own = parcels[:, :film_size].reshape(-1, film_rows)
+    gain_g = jnp.sum(parcels[:, film_size : length - 1], axis=0).reshape(gains.shape)
     loss_total = jnp.sum(parcels[:, length - 1])
-    film_own = lax.dynamic_slice_in_dim(film_all, device * film_rows, film_rows, axis=1)
     film_g = jnp.einsum(
         "sf,se->fe", film_own.astype(jnp.bfloat16), embedded_all, preferred_element_type=jnp.float32
     )

time: 294 us -> 296 us (level)
  starting transfers between devices: 41.6 us -> 45.8 us
  waiting for transfers between devices: 58 us -> 55 us
    all_to_all x3, waiting for transfers between devices: 26 us -> 22.1 us  [to_all(): lax.all_to_all(blocks, ('dp', 'head'), split_axis=0, concat_axis=0, tiled...]
    all_to_all x3, starting transfers between devices: 9.63 us -> 13.1 us  [to_all(): lax.all_to_all(blocks, ('dp', 'head'), split_axis=0, concat_axis=0, tiled...]
  transfers between devices with their start and end apart: 22 -> 22, of which waited for: 13 -> 13; matrix products, arithmetic and copies ran while one was open for 10% -> 10% of each run, Pallas kernels for 24% -> 23%
where the time goes in v7:
time: 296 us; the launch traced here: 293 us
  Pallas kernels  136 us (46%)
  waiting for transfers between devices  55 us (19%)
  starting transfers between devices  45.8 us (15%)
  local copies, waits for them, and re-layouts  23.8 us (8%)
  other arithmetic  23.7 us (8%)
  between operations  6.85 us (2%)
    pallas_call x6, Pallas kernels, per_sample(): pl.pallas_call(kernel, grid=(samples,), in_specs=in_specs, out_specs=[spe...  81.7 us
    pallas_call x1, Pallas kernels, attention_block(): pl.pallas_call(functools.partial(attention_kernel, parts), grid=(samples,...  54.7 us
    all_to_all x3, waiting for transfers between devices, to_all(): lax.all_to_all(blocks, ('dp', 'head'), split_axis=0, concat_axis=0, tiled...  22.1 us
    ppermute x9, waiting for transfers between devices, exchange(): lax.ppermute(values, ('dp', 'head'), [(i, i ^ mask) for i in range(size)])  20.8 us
    all_to_all x4, starting transfers between devices, across_classes(): lax.all_to_all(blocks, ('dp', 'head'), split_axis=0, concat_axis=0, axis_...  17.9 us
    all_to_all x3, starting transfers between devices, to_all(): lax.all_to_all(blocks, ('dp', 'head'), split_axis=0, concat_axis=0, tiled...  13.1 us
    all_to_all x4, waiting for transfers between devices, across_classes(): lax.all_to_all(blocks, ('dp', 'head'), split_axis=0, concat_axis=0, axis_...  12.1 us
    ppermute x9, starting transfers between devices, exchange(): lax.ppermute(values, ('dp', 'head'), [(i, i ^ mask) for i in range(size)])  11 us
  transfers between devices with their start and end apart: 22, of which 13 were waited for; matrix products, arithmetic and copies ran while one was open for 10% of the time, Pallas kernels for 23%

profile of v7, /device:TPU:0, one launch (start us, length us, event | category | flops | bytes accessed | tf_op | source)
XLA Modules:
  0.0 292.7 jit_solution(11815017092270985722)
XLA Ops:
  0.7 1.0 convert_element_type.111
  1.7 4.1 %collective-permute-start = (bf16[216,384]{1,0:T(8,128)(2,1)S(1)}, bf16[216,384]{1,0:T(8,128)(2,1)S(1)}, u32[]{:S(2)}, u32[]{:S(2)}) collective-permute-start(bf16[216,384]{1,0:T(8,128)(2,1)S(1)} %convert_element_type.111), channel_id=1, source_target_pairs={{0,16},{1,17},{2,18},{3,19},{4,20},{5,21},{6,22},{7,23},{8,24},{9,... | collective-permute-start | bytes 497672 | tf_op jit(solution)/shard_map/ppermute | solution.py:77
  5.8 2.3 constant_dynamic-slice_fusion.6
  8.1 1.5 collective-permute-start.4
  11.0 3.8 %all-to-all-start = ((f32[32,1,128]{2,1,0:T(1,128)}), f32[32,1,128]{2,1,0:T(1,128)S(1)}, u32[]{:S(2)}, u32[]{:S(2)}) async-start(f32[32,1,128]{2,1,0:T(1,128)} %broadcast_in_dim.163), calls=%async_computation | async-start | bytes 32768 | tf_op jit(solution)/shard_map/all_to_all | solution.py:102
  15.0 13.2 %all-to-all-done = f32[32,1,128]{2,1,0:T(1,128)S(1)} async-done(((f32[32,1,128]{2,1,0:T(1,128)}), f32[32,1,128]{2,1,0:T(1,128)S(1)}, u32[]{:S(2)}, u32[]{:S(2)}) %all-to-all-start) | async-done | bytes 16416 | tf_op jit(solution)/shard_map/all_to_all | solution.py:102
  28.3 1.3 broadcast_in_dim.178
  29.7 4.9 %all-to-all-start.1 = ((bf16[8,216,384]{2,1,0:T(8,128)(2,1)}), bf16[8,216,384]{2,1,0:T(8,128)(2,1)S(1)}, u32[]{:S(2)}, u32[]{:S(2)}) async-start(bf16[8,216,384]{2,1,0:T(8,128)(2,1)} %broadcast_in_dim.178), calls=%async_computation.1 | async-start | bytes 2654208 | tf_op jit(solution)/shard_map/all_to_all | solution.py:85
  34.7 1.0 constant_dynamic-slice_fusion.2
  38.5 2.6 collective-permute-start.1
  41.1 8.8 %collective-permute-done.2 = bf16[8,384]{1,0:T(8,128)(2,1)S(1)} collective-permute-done((bf16[8,384]{1,0:T(8,128)(2,1)S(1)}, bf16[8,384]{1,0:T(8,128)(2,1)S(1)}, u32[]{:S(2)}, u32[]{:S(2)}) %collective-permute-start.2) | collective-permute-done | bytes 6176 | tf_op jit(solution)/shard_map/ppermute | solution.py:77
  50.4 2.0 all-to-all-done.1.refs_4_
  52.4 1.7 broadcast_in_dim.179
  54.0 3.8 %all-to-all-start.2 = ((bf16[8,328,384]{2,1,0:T(8,128)(2,1)}), bf16[8,328,384]{2,1,0:T(8,128)(2,1)S(1)}, u32[]{:S(2)}, u32[]{:S(2)}) async-start(bf16[8,328,384]{2,1,0:T(8,128)(2,1)} %broadcast_in_dim.179), calls=%async_computation.2 | async-start | bytes 4030464 | tf_op jit(solution)/shard_map/all_to_all | solution.py:85
  59.2 1.0 copy.195
  61.1 15.0 %shard_map.323 = (f32[2,1024,384]{2,1,0:T(8,128)}, bf16[2,1024,384]{2,1,0:T(8,128)(2,1)}, f32[2,8,384]{2,1,0:T(8,128)}, bf16[2,1024,384]{2,1,0:T(8,128)(2,1)}, bf16[3456,384]{1,0:T(8,128)(2,1)}) custom-call(s32[4]{0:T(128)} %iota_xor_fusion.places, s32[1]{0:T(128)} %bitcast.5.last.place, bf16[2,256,384]{2,1,0:T(8,128)(2,1)} %bitcast.83, ...), custom_call_target="tpu_custom_call" | custom-call | flops 5435817984 | bytes 5435817 | tf_op jit(solution)/shard_map/pallas_call | solution.py:664
  76.2 8.6 %all-to-all-done.2.refs_0_ = bf16[8,328,384]{2,1,0:T(8,128)(2,1)S(1)} async-done(((bf16[8,328,384]{2,1,0:T(8,128)(2,1)}), bf16[8,328,384]{2,1,0:T(8,128)(2,1)S(1)}, u32[]{:S(2)}, u32[]{:S(2)}) %all-to-all-start.2) | async-done | bytes 2015264 | tf_op jit(solution)/shard_map/all_to_all | solution.py:85
  85.8 0.8 fusion.refs_8_
  88.9 0.9 slice.159
  91.4 1.4 collective-permute-start.10
  92.8 1.1 slice.160
  93.9 13.7 %shard_map.324 = (f32[2,1024,384]{2,1,0:T(8,128)}, bf16[2,1024,384]{2,1,0:T(8,128)(2,1)}, bf16[3456,384]{1,0:T(8,128)(2,1)}) custom-call(s32[1]{0:T(128)} %bitcast.5.last.place, bf16[8,328,384]{2,1,0:T(8,128)(2,1)} %copy-done, bf16[8,328,384]{2,1,0:T(8,128)(2,1)} %collective-permute-done.7.refs_1_, f32[2,1024,384]{2,1,0:T(8,128)} %get-tuple-element.52.refs_2_.inner, ...), custom_call_target="tpu_custom_call" | custom-call | flops 5435817984 | bytes 5435817 | tf_op jit(solution)/shard_map/pallas_call | solution.py:664
  108.4 1.4 reshape.312.refs_6_
  110.6 54.7 %shard_map.325 = (bf16[2,1024,384]{2,1,0:T(8,128)(2,1)}, bf16[384,1536]{1,0:T(8,128)(2,1)}, f32[2,8,384]{2,1,0:T(8,128)}, f32[2,8,192]{2,1,0:T(8,128)}) custom-call(s32[4]{0:T(128)} %iota_xor_fusion.places, f32[2,6]{1,0:T(2,128)} %stack.47.scalars, f32[2,1024,384]{2,1,0:T(8,128)} %get-tuple-element.56.middle, bf16[2,256,192]{2,1,0:T(8,128)(2,1)} %bitcast.84, ...), custom_call_target="tpu_custom_call" | custom-call | flops 24159191040 | bytes 6291456 | tf_op jit(solution)/shard_map/pallas_call | solution.py:349
  165.4 13.1 %shard_map.326 = (bf16[8,312,384]{2,1,0:T(8,128)(2,1)}, bf16[8,312,384]{2,1,0:T(8,128)(2,1)}) custom-call(s32[1]{0:T(128)} %bitcast.5.last.place, bf16[2,1024,384]{2,1,0:T(8,128)(2,1)} %get-tuple-element.62.hidden, bf16[2,1024,384]{2,1,0:T(8,128)(2,1)} %get-tuple-element.66.grad, bf16[384,1536]{1,0:T(8,128)(2,1)} %get-tuple-element.63.refs_0_), custom_call_target="tpu_custom_call" | custom-call | flops 5435817984 | bytes 5435817 | tf_op jit(solution)/shard_map/pallas_call | solution.py:664
  179.2 3.7 %collective-permute-done.11 = bf16[8,312,384]{2,1,0:T(8,128)(2,1)S(1)} collective-permute-done((bf16[8,312,384]{2,1,0:T(8,128)(2,1)}, bf16[8,312,384]{2,1,0:T(8,128)(2,1)S(1)}, u32[]{:S(2)}, u32[]{:S(2)}) %collective-permute-start.11) | collective-permute-done | bytes 1916960 | tf_op jit(solution)/shard_map/ppermute | solution.py:77
  183.0 3.3 %add_convert_fusion = bf16[8,312,384]{2,1,0:T(8,128)(2,1)} fusion(bf16[8,312,384]{2,1,0:T(8,128)(2,1)S(1)} %collective-permute-done.11, bf16[8,312,384]{2,1,0:T(8,128)(2,1)} %get-tuple-element.64), kind=kLoop, calls=%fused_computation.1 | loop fusion | flops 3833856 | bytes 5750784 | tf_op jit(solution)/shard_map/convert_element_type | solution.py:917
  186.3 3.8 %all-to-all-start.3 = ((bf16[8,312,384]{2,1,0:T(8,128)(2,1)}), bf16[8,312,384]{2,1,0:T(8,128)(2,1)S(1)}, u32[]{:S(2)}, u32[]{:S(2)}) async-start(bf16[8,312,384]{2,1,0:T(8,128)(2,1)} %add_convert_fusion), calls=%async_computation.3 | async-start | bytes 3833856 | tf_op jit(solution)/shard_map/all_to_all | solution.py:85
  190.1 15.2 %shard_map.327 = (bf16[2,1024,384]{2,1,0:T(8,128)(2,1)}, f32[2,8,384]{2,1,0:T(8,128)}) custom-call(bf16[2,1024,384]{2,1,0:T(8,128)(2,1)} %get-tuple-element.66.grad, f32[2,1024,384]{2,1,0:T(8,128)} %get-tuple-element.52.refs_2_.inner, f32[2,8,384]{2,1,0:T(8,128)} %get-tuple-element.55.refs_4_.stats, f32[2,8,384]{2,1,0:T(8,128)} %pad.18.refs_5_.film, ...), custom_call_target="tpu_custom_call" | custom-call | flops 5435817984 | bytes 5435817 | tf_op jit(solution)/shard_map/pallas_call | solution.py:664
  205.3 12.2 %shard_map.328 = (bf16[8,216,384]{2,1,0:T(8,128)(2,1)}, bf16[8,216,384]{2,1,0:T(8,128)(2,1)}) custom-call(s32[1]{0:T(128)} %bitcast.5.last.place, bf16[2,1024,384]{2,1,0:T(8,128)(2,1)} %get-tuple-element.71.hidden, bf16[2,1024,384]{2,1,0:T(8,128)(2,1)} %get-tuple-element.74.grad), custom_call_target="tpu_custom_call" | custom-call | flops 5435817984 | bytes 5435817 | tf_op jit(solution)/shard_map/pallas_call | solution.py:664
  217.9 2.9 collective-permute-done.12
  220.8 2.7 add_convert_fusion.1
  223.5 5.5 %all-to-all-start.4 = ((bf16[8,216,384]{2,1,0:T(8,128)(2,1)}), bf16[8,216,384]{2,1,0:T(8,128)(2,1)S(1)}, u32[]{:S(2)}, u32[]{:S(2)}) async-start(bf16[8,216,384]{2,1,0:T(8,128)(2,1)} %add_convert_fusion.1), calls=%async_computation.4 | async-start | bytes 2654208 | tf_op jit(solution)/shard_map/all_to_all | solution.py:85
  229.0 0.8 slice_reduce_fusion.8
  230.2 0.8 slice_reduce_fusion.5
  234.0 12.5 %shard_map.329 = f32[2,8,384]{2,1,0:T(8,128)} custom-call(bf16[2,1024,384]{2,1,0:T(8,128)(2,1)} %get-tuple-element.74.grad, bf16[2,1024,384]{2,1,0:T(8,128)(2,1)} %get-tuple-element.54.refs_3_.images, f32[2,8,384]{2,1,0:T(8,128)} %get-tuple-element.55.refs_4_.stats, f32[8,384]{1,0:T(8,128)} %pad.17.refs_6_.refs_4_.gains, ...), custom_call_target="tpu_custom_call" | custom-call | flops 5435817984 | bytes 5435817 | tf_op jit(solution)/shard_map/pallas_call | solution.py:664
  246.5 0.8 slice_reduce_fusion.3
  247.4 1.3 collective-permute-done.13
  248.7 1.5 all-to-all-done.4
  251.4 3.7 %all-to-all-start.5 = ((f32[32,1,128]{2,1,0:T(1,128)}), f32[32,1,128]{2,1,0:T(1,128)S(1)}, u32[]{:S(2)}, u32[]{:S(2)}) async-start(f32[32,1,128]{2,1,0:T(1,128)} %bitcast.31), calls=%async_computation.5 | async-start | bytes 32768 | tf_op jit(solution)/shard_map/all_to_all | solution.py:102
  256.5 2.7 collective-permute-start.14
  259.1 3.2 %all-to-all-done.5 = f32[32,1,128]{2,1,0:T(1,128)S(1)} async-done(((f32[32,1,128]{2,1,0:T(1,128)}), f32[32,1,128]{2,1,0:T(1,128)S(1)}, u32[]{:S(2)}, u32[]{:S(2)}) %all-to-all-start.5) | async-done | bytes 16416 | tf_op jit(solution)/shard_map/all_to_all | solution.py:102
  262.4 0.8 multiply_reduce_fusion.2
  263.9 3.5 %collective-permute-done.14 = bf16[216,384]{1,0:T(8,128)(2,1)S(1)} collective-permute-done((bf16[216,384]{1,0:T(8,128)(2,1)S(1)}, bf16[216,384]{1,0:T(8,128)(2,1)S(1)}, u32[]{:S(2)}, u32[]{:S(2)}) %collective-permute-start.14) | collective-permute-done | bytes 165920 | tf_op jit(solution)/shard_map/ppermute | solution.py:77
  272.0 5.6 %all-to-all-start.6 = ((f32[32,8,128]{2,1,0:T(8,128)}), f32[32,8,128]{2,1,0:T(8,128)S(1)}, u32[]{:S(2)}, u32[]{:S(2)}) async-start(f32[32,8,128]{2,1,0:T(8,128)} %broadcast_in_dim.194), calls=%async_computation.6 | async-start | bytes 262144 | tf_op jit(solution)/shard_map/all_to_all | solution.py:102
  278.3 1.9 pad_maximum_fusion.6
  280.2 5.7 %all-to-all-done.6 = f32[32,8,128]{2,1,0:T(8,128)S(1)} async-done(((f32[32,8,128]{2,1,0:T(8,128)}), f32[32,8,128]{2,1,0:T(8,128)S(1)}, u32[]{:S(2)}, u32[]{:S(2)}) %all-to-all-start.6) | async-done | bytes 131104 | tf_op jit(solution)/shard_map/all_to_all | solution.py:102
  289.5 1.1 multiply_subtract_fusion
  (222 shorter events, 26.6 us)
Async XLA Ops:
  1.7 13.2 %collective-permute-start = (bf16[216,384]{1,0:T(8,128)(2,1)S(1)}, bf16[216,384]{1,0:T(8,128)(2,1)S(1)}, u32[]{:S(2)}, u32[]{:S(2)}) collective-permute-start(bf16[216,384]{1,0:T(8,128)(2,1)S(1)} %convert_element_type.111), channel_id=1, source_target_pairs={{0,16},{1,17},{2,18},{3,19},{4,20},{5,21},{6,22},{7,23},{8,24},{9,... | collective-permute-start | bytes 497672 | tf_op jit(solution)/shard_map/ppermute | solution.py:77
  5.8 4.4 %copy-start.24 = (f32[12,6]{0,1:T(8,128)S(1)}, f32[12,6]{0,1:T(8,128)}, u32[]{:S(2)}) copy-start(f32[12,6]{0,1:T(8,128)} %param.28) | copy-start | bytes 868
  5.8 9.1 %copy-start.1 = (f32[216,384]{1,0:T(8,128)S(1)}, f32[216,384]{1,0:T(8,128)}, u32[]{:S(2)}) copy-start(f32[216,384]{1,0:T(8,128)} %param.25) | copy-start | bytes 995332
  8.1 20.1 %collective-permute-start.3 = (bf16[2,8,32,384]{3,2,1,0:T(8,128)(2,1)S(1)}, bf16[2,8,32,384]{3,2,1,0:T(8,128)(2,1)S(1)}, u32[]{:S(2)}, u32[]{:S(2)}) collective-permute-start(bf16[2,8,32,384]{3,2,1,0:T(8,128)(2,1)S(1)} %get-tuple-element.210), channel_id=1, source_target_pairs={{0,1},{1,0},{2,3},{3,2},{4,5},{5,4},{6,7},{7,6},{8,9},{9,8},{10,11... | collective-permute-start | bytes 1179656 | tf_op jit(solution)/shard_map/ppermute | solution.py:113
  8.1 20.1 %collective-permute-start.4 = (bf16[2,8,32,384]{3,2,1,0:T(8,128)(2,1)S(1)}, bf16[2,8,32,384]{3,2,1,0:T(8,128)(2,1)S(1)}, u32[]{:S(2)}, u32[]{:S(2)}) collective-permute-start(bf16[2,8,32,384]{3,2,1,0:T(8,128)(2,1)S(1)} %get-tuple-element.212), channel_id=1, source_target_pairs={{0,2},{1,3},{2,0},{3,1},{4,6},{5,7},{6,4},{7,5},{8,10},{9,11},{10,... | collective-permute-start | bytes 1179656 | tf_op jit(solution)/shard_map/ppermute | solution.py:113
  9.6 18.6 %collective-permute-start.5 = (bf16[2,8,32,384]{3,2,1,0:T(8,128)(2,1)S(1)}, bf16[2,8,32,384]{3,2,1,0:T(8,128)(2,1)S(1)}, u32[]{:S(2)}, u32[]{:S(2)}) collective-permute-start(bf16[2,8,32,384]{3,2,1,0:T(8,128)(2,1)S(1)} %get-tuple-element.209), channel_id=1, source_target_pairs={{0,3},{1,2},{2,1},{3,0},{4,7},{5,6},{6,5},{7,4},{8,11},{9,10},{10,... | collective-permute-start | bytes 1179656 | tf_op jit(solution)/shard_map/ppermute | solution.py:113
  11.0 17.2 %all-to-all-start = ((f32[32,1,128]{2,1,0:T(1,128)}), f32[32,1,128]{2,1,0:T(1,128)S(1)}, u32[]{:S(2)}, u32[]{:S(2)}) async-start(f32[32,1,128]{2,1,0:T(1,128)} %broadcast_in_dim.163), calls=%async_computation | async-start | bytes 32768 | tf_op jit(solution)/shard_map/all_to_all | solution.py:102
  29.6 5.0 %copy-start.14 = (f32[12,384]{1,0:T(8,128)S(1)}, f32[12,384]{1,0:T(8,128)}, u32[]{:S(2)}) copy-start(f32[12,384]{1,0:T(8,128)} %param.27) | copy-start | bytes 55300
  29.6 5.0 %copy-start.10 = (f32[12,1152]{1,0:T(8,128)S(1)}, f32[12,1152]{1,0:T(8,128)}, u32[]{:S(2)}) copy-start(f32[12,1152]{1,0:T(8,128)} %param.26) | copy-start | bytes 165892
  29.6 5.1 %copy-start.6 = (bf16[8,8,32,192]{3,2,1,0:T(8,128)(2,1)S(1)}, bf16[8,8,32,192]{3,2,1,0:T(8,128)(2,1)}, u32[]{:S(2)}) copy-start(bf16[8,8,32,192]{3,2,1,0:T(8,128)(2,1)} %param.21) | copy-start | bytes 2359300
  29.7 22.6 %all-to-all-start.1 = ((bf16[8,216,384]{2,1,0:T(8,128)(2,1)}), bf16[8,216,384]{2,1,0:T(8,128)(2,1)S(1)}, u32[]{:S(2)}, u32[]{:S(2)}) async-start(bf16[8,216,384]{2,1,0:T(8,128)(2,1)} %broadcast_in_dim.178), calls=%async_computation.1 | async-start | bytes 2654208 | tf_op jit(solution)/shard_map/all_to_all | solution.py:85
  37.3 12.7 %collective-permute-start.2 = (bf16[8,384]{1,0:T(8,128)(2,1)S(1)}, bf16[8,384]{1,0:T(8,128)(2,1)S(1)}, u32[]{:S(2)}, u32[]{:S(2)}) collective-permute-start(bf16[8,384]{1,0:T(8,128)(2,1)S(1)} %pad_maximum_fusion.5), channel_id=1, source_target_pairs={{0,16},{1,17},{2,18},{3,19},{4,20},{5,21},{6,22},{7,23},{8,24},{9,... | collective-permute-start | bytes 18440 | tf_op jit(solution)/shard_map/ppermute | solution.py:77
  38.5 11.8 %collective-permute-start.1 = (bf16[48,384]{1,0:T(8,128)(2,1)S(1)}, bf16[48,384]{1,0:T(8,128)(2,1)S(1)}, u32[]{:S(2)}, u32[]{:S(2)}) collective-permute-start(bf16[48,384]{1,0:T(8,128)(2,1)S(1)} %pad_maximum_fusion.4), channel_id=1, source_target_pairs={{0,16},{1,17},{2,18},{3,19},{4,20},{5,21},{6,22},{7,23},{8,24},{9,... | collective-permute-start | bytes 110600 | tf_op jit(solution)/shard_map/ppermute | solution.py:77
  52.4 5.5 %copy-start.5 = (bf16[8,216,384]{2,1,0:T(8,128)(2,1)}, bf16[8,216,384]{2,1,0:T(8,128)(2,1)S(1)}, u32[]{:S(2)}) copy-start(bf16[8,216,384]{2,1,0:T(8,128)(2,1)S(1)} %all-to-all-done.1.refs_4_) | copy-start | bytes 3981316
  54.0 30.7 %all-to-all-start.2 = ((bf16[8,328,384]{2,1,0:T(8,128)(2,1)}), bf16[8,328,384]{2,1,0:T(8,128)(2,1)S(1)}, u32[]{:S(2)}, u32[]{:S(2)}) async-start(bf16[8,328,384]{2,1,0:T(8,128)(2,1)} %broadcast_in_dim.179), calls=%async_computation.2 | async-start | bytes 4030464 | tf_op jit(solution)/shard_map/all_to_all | solution.py:85
  57.8 3.3 %collective-permute-start.6 = (bf16[8,216,384]{2,1,0:T(8,128)(2,1)S(1)}, bf16[8,216,384]{2,1,0:T(8,128)(2,1)}, u32[]{:S(2)}, u32[]{:S(2)}) collective-permute-start(bf16[8,216,384]{2,1,0:T(8,128)(2,1)S(1)} %all-to-all-done.1.refs_4_), channel_id=1, source_target_pairs={{0,1},{1,0},{2,3},{3,2},{4,5},{5,4},{6,7},{7,6},{8,9},{9,8},{10,11... | collective-permute-start | bytes 3981320 | tf_op jit(solution)/shard_map/ppermute | solution.py:77
  61.1 23.7 %copy-start.33 = (s32[8]{0:T(128)S(1)}, s32[8]{0:T(128)}, u32[]{:S(2)}) copy-start(s32[8]{0:T(128)} %param.22) | copy-start | bytes 100
  61.1 24.3 %copy-start.30 = (s32[8,2]{0,1:T(2,128)S(1)}, s32[8,2]{0,1:T(2,128)}, u32[]{:S(2)}) copy-start(s32[8,2]{0,1:T(2,128)} %param.23) | copy-start | bytes 196
  61.1 24.6 %copy-start.31 = (pred[2]{0:T(512)(128)(4,1)S(1)}, pred[2]{0:T(512)(128)(4,1)}, u32[]{:S(2)}) copy-start(pred[2]{0:T(512)(128)(4,1)} %get-tuple-element.237) | copy-start | bytes 10
  61.1 25.5 %copy-start.20 = (f32[8,1,56]{2,1,0:T(1,128)S(1)}, f32[8,1,56]{2,1,0:T(1,128)}, u32[]{:S(2)}) copy-start(f32[8,1,56]{2,1,0:T(1,128)} %copy-done.19) | copy-start | bytes 5380
  76.1 15.2 %copy-start.13 = (bf16[2,8,32,192]{3,2,1,0:T(8,128)(2,1)S(1)}, bf16[2,8,32,192]{3,2,1,0:T(8,128)(2,1)}, u32[]{:S(2)}) copy-start(bf16[2,8,32,192]{3,2,1,0:T(8,128)(2,1)} %get-tuple-element.59) | copy-start | bytes 589828
  76.2 15.2 %copy-start.12 = (bf16[2,8,32,192]{3,2,1,0:T(8,128)(2,1)S(1)}, bf16[2,8,32,192]{3,2,1,0:T(8,128)(2,1)}, u32[]{:S(2)}) copy-start(bf16[2,8,32,192]{3,2,1,0:T(8,128)(2,1)} %get-tuple-element.60) | copy-start | bytes 589828
  84.8 9.1 %copy-start = (bf16[8,328,384]{2,1,0:T(8,128)(2,1)}, bf16[8,328,384]{2,1,0:T(8,128)(2,1)S(1)}, u32[]{:S(2)}) copy-start(bf16[8,328,384]{2,1,0:T(8,128)(2,1)S(1)} %all-to-all-done.2.refs_0_) | copy-start | bytes 6045700
  84.8 4.2 %collective-permute-start.7 = (bf16[8,328,384]{2,1,0:T(8,128)(2,1)S(1)}, bf16[8,328,384]{2,1,0:T(8,128)(2,1)}, u32[]{:S(2)}, u32[]{:S(2)}) collective-permute-start(bf16[8,328,384]{2,1,0:T(8,128)(2,1)S(1)} %all-to-all-done.2.refs_0_), channel_id=1, source_target_pairs={{0,1},{1,0},{2,3},{3,2},{4,5},{5,4},{6,7},{7,6},{8,9},{9,8},{10,11... | collective-permute-start | bytes 6045704 | tf_op jit(solution)/shard_map/ppermute | solution.py:77
  90.9 19.7 %collective-permute-start.8 = (bf16[2,8,32,192]{3,2,1,0:T(8,128)(2,1)}, bf16[2,8,32,192]{3,2,1,0:T(8,128)(2,1)}, u32[]{:S(2)}, u32[]{:S(2)}) collective-permute-start(bf16[2,8,32,192]{3,2,1,0:T(8,128)(2,1)} %get-tuple-element.58), channel_id=1, source_target_pairs={{0,1},{1,0},{2,3},{3,2},{4,5},{5,4},{6,7},{7,6},{8,9},{9,8},{10,11... | collective-permute-start | bytes 589832 | tf_op jit(solution)/shard_map/ppermute | solution.py:113
  91.4 19.3 %collective-permute-start.9 = (bf16[2,8,32,192]{3,2,1,0:T(8,128)(2,1)S(1)}, bf16[2,8,32,192]{3,2,1,0:T(8,128)(2,1)}, u32[]{:S(2)}, u32[]{:S(2)}) collective-permute-start(bf16[2,8,32,192]{3,2,1,0:T(8,128)(2,1)S(1)} %copy-done.13), channel_id=1, source_target_pairs={{0,2},{1,3},{2,0},{3,1},{4,6},{5,7},{6,4},{7,5},{8,10},{9,11},{10,... | collective-permute-start | bytes 589832 | tf_op jit(solution)/shard_map/ppermute | solution.py:113
  91.4 19.3 %collective-permute-start.10 = (bf16[2,8,32,192]{3,2,1,0:T(8,128)(2,1)S(1)}, bf16[2,8,32,192]{3,2,1,0:T(8,128)(2,1)}, u32[]{:S(2)}, u32[]{:S(2)}) collective-permute-start(bf16[2,8,32,192]{3,2,1,0:T(8,128)(2,1)S(1)} %copy-done.12), channel_id=1, source_target_pairs={{0,3},{1,2},{2,1},{3,0},{4,7},{5,6},{6,5},{7,4},{8,11},{9,10},{10,... | collective-permute-start | bytes 589832 | tf_op jit(solution)/shard_map/ppermute | solution.py:113
  178.5 4.5 %collective-permute-start.11 = (bf16[8,312,384]{2,1,0:T(8,128)(2,1)}, bf16[8,312,384]{2,1,0:T(8,128)(2,1)S(1)}, u32[]{:S(2)}, u32[]{:S(2)}) collective-permute-start(bf16[8,312,384]{2,1,0:T(8,128)(2,1)} %get-tuple-element.65), channel_id=1, source_target_pairs={{0,1},{1,0},{2,3},{3,2},{4,5},{5,4},{6,7},{7,6},{8,9},{9,8},{10,11... | collective-permute-start | bytes 5750792 | tf_op jit(solution)/shard_map/ppermute | solution.py:77
  186.3 37.2 %all-to-all-start.3 = ((bf16[8,312,384]{2,1,0:T(8,128)(2,1)}), bf16[8,312,384]{2,1,0:T(8,128)(2,1)S(1)}, u32[]{:S(2)}, u32[]{:S(2)}) async-start(bf16[8,312,384]{2,1,0:T(8,128)(2,1)} %add_convert_fusion), calls=%async_computation.3 | async-start | bytes 3833856 | tf_op jit(solution)/shard_map/all_to_all | solution.py:85
  217.5 3.3 %collective-permute-start.12 = (bf16[8,216,384]{2,1,0:T(8,128)(2,1)}, bf16[8,216,384]{2,1,0:T(8,128)(2,1)S(1)}, u32[]{:S(2)}, u32[]{:S(2)}) collective-permute-start(bf16[8,216,384]{2,1,0:T(8,128)(2,1)} %get-tuple-element.73), channel_id=1, source_target_pairs={{0,1},{1,0},{2,3},{3,2},{4,5},{5,4},{6,7},{7,6},{8,9},{9,8},{10,11... | collective-permute-start | bytes 3981320 | tf_op jit(solution)/shard_map/ppermute | solution.py:77
  223.5 6.6 %copy-start.21 = (f32[2,8,384]{2,1,0:T(8,128)S(1)}, f32[2,8,384]{2,1,0:T(8,128)}, u32[]{:S(2)}) copy-start(f32[2,8,384]{2,1,0:T(8,128)} %get-tuple-element.68) | copy-start | bytes 73732
  223.5 7.9 %copy-start.26 = (f32[2,8,192]{2,1,0:T(8,128)S(1)}, f32[2,8,192]{2,1,0:T(8,128)}, u32[]{:S(2)}) copy-start(f32[2,8,192]{2,1,0:T(8,128)} %get-tuple-element.78) | copy-start | bytes 36868
  223.5 26.8 %all-to-all-start.4 = ((bf16[8,216,384]{2,1,0:T(8,128)(2,1)}), bf16[8,216,384]{2,1,0:T(8,128)(2,1)S(1)}, u32[]{:S(2)}, u32[]{:S(2)}) async-start(bf16[8,216,384]{2,1,0:T(8,128)(2,1)} %add_convert_fusion.1), calls=%async_computation.4 | async-start | bytes 2654208 | tf_op jit(solution)/shard_map/all_to_all | solution.py:85
  233.9 14.8 %collective-permute-start.13 = (bf16[264,384]{1,0:T(8,128)(2,1)S(1)}, bf16[264,384]{1,0:T(8,128)(2,1)S(1)}, u32[]{:S(2)}, u32[]{:S(2)}) collective-permute-start(bf16[264,384]{1,0:T(8,128)(2,1)S(1)} %pad_maximum_fusion.1), channel_id=1, source_target_pairs={{0,16},{1,17},{2,18},{3,19},{4,20},{5,21},{6,22},{7,23},{8,24},{9,... | collective-permute-start | bytes 608264 | tf_op jit(solution)/shard_map/ppermute | solution.py:77
  248.7 18.7 %copy-start.4 = (f32[312,384]{1,0:T(8,128)S(1)}, f32[312,384]{1,0:T(8,128)}, u32[]{:S(2)}) copy-start(f32[312,384]{1,0:T(8,128)} %copy-done.3) | copy-start | bytes 1437700
  250.8 36.6 %copy-start.11 = (f32[12,1152]{1,0:T(8,128)S(1)}, f32[12,1152]{1,0:T(8,128)}, u32[]{:S(2)}) copy-start(f32[12,1152]{1,0:T(8,128)} %param.26) | copy-start | bytes 165892
  250.8 36.6 %copy-start.15 = (f32[12,1152]{1,0:T(8,128)S(1)}, f32[12,1152]{1,0:T(8,128)}, u32[]{:S(2)}) copy-start(f32[12,1152]{1,0:T(8,128)} %param.33) | copy-start | bytes 165892
  250.8 36.6 %copy-start.16 = (f32[12,1152]{1,0:T(8,128)S(1)}, f32[12,1152]{1,0:T(8,128)}, u32[]{:S(2)}) copy-start(f32[12,1152]{1,0:T(8,128)} %param.34) | copy-start | bytes 165892
  251.4 10.9 %all-to-all-start.5 = ((f32[32,1,128]{2,1,0:T(1,128)}), f32[32,1,128]{2,1,0:T(1,128)S(1)}, u32[]{:S(2)}, u32[]{:S(2)}) async-start(f32[32,1,128]{2,1,0:T(1,128)} %bitcast.31), calls=%async_computation.5 | async-start | bytes 32768 | tf_op jit(solution)/shard_map/all_to_all | solution.py:102
  255.8 32.4 %copy-start.22 = (f32[12,384]{1,0:T(8,128)S(1)}, f32[12,384]{1,0:T(8,128)}, u32[]{:S(2)}) copy-start(f32[12,384]{1,0:T(8,128)} %param.35) | copy-start | bytes 55300
  255.8 32.4 %copy-start.23 = (f32[12,384]{1,0:T(8,128)S(1)}, f32[12,384]{1,0:T(8,128)}, u32[]{:S(2)}) copy-start(f32[12,384]{1,0:T(8,128)} %param.36) | copy-start | bytes 55300
  255.8 33.0 %copy-start.17 = (f32[24,768]{1,0:T(8,128)S(1)}, f32[24,768]{1,0:T(8,128)}, u32[]{:S(2)}) copy-start(f32[24,768]{1,0:T(8,128)} %param.29) | copy-start | bytes 221188
  255.8 33.0 %copy-start.18 = (f32[24,768]{1,0:T(8,128)S(1)}, f32[24,768]{1,0:T(8,128)}, u32[]{:S(2)}) copy-start(f32[24,768]{1,0:T(8,128)} %param.30) | copy-start | bytes 221188
  256.5 10.9 %collective-permute-start.14 = (bf16[216,384]{1,0:T(8,128)(2,1)S(1)}, bf16[216,384]{1,0:T(8,128)(2,1)S(1)}, u32[]{:S(2)}, u32[]{:S(2)}) collective-permute-start(bf16[216,384]{1,0:T(8,128)(2,1)S(1)} %convert_element_type.127), channel_id=1, source_target_pairs={{0,16},{1,17},{2,18},{3,19},{4,20},{5,21},{6,22},{7,23},{8,24},{9,... | collective-permute-start | bytes 497672 | tf_op jit(solution)/shard_map/ppermute | solution.py:77
  263.9 25.6 %copy-start.2 = (f32[216,384]{1,0:T(8,128)S(1)}, f32[216,384]{1,0:T(8,128)}, u32[]{:S(2)}) copy-start(f32[216,384]{1,0:T(8,128)} %param.25) | copy-start | bytes 995332
  263.9 25.6 %copy-start.7 = (f32[216,384]{1,0:T(8,128)S(1)}, f32[216,384]{1,0:T(8,128)}, u32[]{:S(2)}) copy-start(f32[216,384]{1,0:T(8,128)} %param.31) | copy-start | bytes 995332
  263.9 25.6 %copy-start.8 = (f32[216,384]{1,0:T(8,128)S(1)}, f32[216,384]{1,0:T(8,128)}, u32[]{:S(2)}) copy-start(f32[216,384]{1,0:T(8,128)} %param.32) | copy-start | bytes 995332
  272.0 13.8 %all-to-all-start.6 = ((f32[32,8,128]{2,1,0:T(8,128)}), f32[32,8,128]{2,1,0:T(8,128)S(1)}, u32[]{:S(2)}, u32[]{:S(2)}) async-start(f32[32,8,128]{2,1,0:T(8,128)} %broadcast_in_dim.194), calls=%async_computation.6 | async-start | bytes 262144 | tf_op jit(solution)/shard_map/all_to_all | solution.py:102
  (11 other events, 24.0 us)
